TPU v7x, 512 devices: a whole 4x8x8 slice. The times are simulated.
512 devices in a mesh: group: 8 (over x, core), leaf: 64 (over y, z).
Axes of the slice: x: 4, y: 8, z: 8, core: 2. Of those that a mesh axis runs over, the one named last changes fastest.
Arguments:
- points: float32 [4096, 3, 256], P(('group', 'leaf')), may hold values from 0 to 3
- charges: float32 [4096, 8, 256], P(('group', 'leaf')), may hold values from -0.4 to 0.4
- up_op: float32 [4096, 128, 256], P(('group', 'leaf')), may hold values from -0.375 to 0.375
- skel_pts: float32 [4096, 3, 128], P(('group', 'leaf')), may hold values from 0 to 3
- upward_transfer_matrix: float32 [4096, 128, 128], P(('group', 'leaf')), may hold values from -0.1875 to 0.1875
- cell_pts: float32 [512, 3, 128], P(('group', 'leaf')), may hold values from 0 to 3
- near_list: int32 [4096, 9], P(('group', 'leaf')), may hold values from -1 to 4095, as said below
- leaf_list: int32 [4096, 16], P(('group', 'leaf')), may hold values from 0 to 4095, as said below
- top_list: int32 [512, 16], P(('group', 'leaf')), may hold values from 0 to 511, as said below
Outputs:
- potential: float32 [4096, 8, 256], P(('group', 'leaf'))
Inputs may be any that keep to these rules, and one draw needn't show every extreme that they name: `near_list`: row i starts with i itself; its other entries are distinct leaves i + o with 0 < |o| <= 4 inside 0 to 4095, or -1 for padding; the number of live entries varies by leaf, and the first leaf of each device lists every such neighbour that lies inside 0 to 4095. `leaf_list`: entries of a row are distinct leaves of the same subtree of 512 leaves, none within 4 of the row's leaf in the subtree's cyclic order. `top_list`: entries of a row are distinct cells of other subtrees.
All inputs are finite; a program needn't handle non-finite values.
Results may differ from a plain program's by a relative error of at most 0.0003.
Values sent between devices are 32-bit elements; how exact they have to be, the bound alone decides.
No kernel may reach another device: no remote copies, remote signals or barrier semaphores. Data moves between devices by JAX's collectives and lax.ppermute only.
A program may use at most 64 MiB of HBM per device.

v0:
```python
import jax
import jax.numpy as jnp
from jax import lax
from jax.sharding import PartitionSpec as P

WINDOW = 4


root_three = 1.7320508075688772
finest_level = lax.Precision.HIGHEST


def extended_2(shard, sides, width):
    for axis, dim in sides:
        count, length = (lax.axis_size(axis), shard.shape[dim])
        up = [(i, (i + 1) % count) for i in range(count - 1)]
        down = [(j, i) for i, j in up]
        last = lax.slice_in_dim(shard, length - width, length, axis=dim)
        first = lax.slice_in_dim(shard, 0, width, axis=dim)
        before = lax.ppermute(last, axis, up)
        after = lax.ppermute(first, axis, down)
        shard = jnp.concatenate([before, shard, after], axis=dim)
    return shard


def matern(left_pts, right_pts):
    square = None
    for comp in range(3):
        diff = left_pts[..., comp, :, None] - right_pts[..., comp, None, :]
        square = diff * diff if square is None else square + diff * diff
    scaled = root_three * jnp.sqrt(square)
    return (1.0 + scaled) * jnp.exp(-scaled)


def body(
    points,
    charges,
    up_op,
    skel_pts,
    upward_transfer_matrix,
    cell_pts,
    near_list,
    leaf_list,
    top_list,
):
    local_leaves = points.shape[0]
    base = (lax.axis_index("group") * lax.axis_size("leaf") + lax.axis_index("leaf")) * local_leaves
    slab = jnp.concatenate([points, charges], axis=1)
    extended = extended_2(slab, ((("group", "leaf"), 0),), WINDOW)
    ext_pts = extended[:, :3]
    ext_vals = extended[:, 3:]
    near = jnp.zeros(charges.shape, jnp.float32)
    for slot in range(near_list.shape[1]):
        ids = near_list[:, slot]
        local = jnp.where(ids >= 0, ids - base + WINDOW, 0)
        kernel = matern(points, ext_pts[local])
        term = jnp.einsum("lab,lpb->lpa", kernel, ext_vals[local], precision=finest_level)
        near = near + jnp.where((ids >= 0)[:, None, None], term, 0.0)
    source_weights = jnp.einsum("lrb,lpb->lpr", up_op, charges, precision=finest_level)
    skeleton_slab = jnp.concatenate([skel_pts, source_weights], axis=1)
    subtree = lax.all_gather(skeleton_slab, "leaf", axis=0, tiled=True)
    group_start = lax.axis_index("group") * subtree.shape[0]
    leaf_distant_field = jnp.zeros(source_weights.shape, jnp.float32)
    for slot in range(leaf_list.shape[1]):
        local = leaf_list[:, slot] - group_start
        source = subtree[local]
        kernel = matern(skel_pts, source[:, :3])
        leaf_distant_field = leaf_distant_field + jnp.einsum(
            "lab,lpb->lpa", kernel, source[:, 3:], precision=finest_level
        )
    cell_skeleton_weights = jnp.einsum(
        "fhm,fnm->nh", upward_transfer_matrix, source_weights, precision=finest_level
    )
    cell_slab = jnp.concatenate([cell_pts[0], cell_skeleton_weights], axis=0)[None]
    every_cell = lax.all_gather(cell_slab, ("group", "leaf"), axis=0, tiled=True)
    source = every_cell[top_list[0]]
    kernel = matern(cell_pts[0], source[:, :3])
    cell_distant_field = jnp.einsum("tab,tpb->pa", kernel, source[:, 3:], precision=finest_level)
    received_field = leaf_distant_field + jnp.einsum(
        "yqm,wq->ywm", upward_transfer_matrix, cell_distant_field, precision=finest_level
    )
    return near + jnp.einsum("lrb,lpr->lpb", up_op, received_field, precision=finest_level)


def solution(mesh):
    in_specs = (
        P(("group", "leaf"), None, None),
        P(("group", "leaf"), None, None),
        P(("group", "leaf"), None, None),
        P(("group", "leaf"), None, None),
        P(("group", "leaf"), None, None),
        P(("group", "leaf"), None, None),
        P(("group", "leaf"), None),
        P(("group", "leaf"), None),
        P(("group", "leaf"), None),
    )
    out_specs = P(("group", "leaf"), None, None)
    return jax.shard_map(body, mesh=mesh, in_specs=in_specs, out_specs=out_specs, check_vma=False)
```

profile of v0, /device:TPU:1, one launch (start us, length us, event | category | flops | bytes accessed | tf_op | source)
XLA Modules:
  0.0 234.4 jit_solution(3100403155620104077)
XLA Ops:
  7.8 1.8 fusion.766
  11.9 4.8 %collective-permute-start = (f32[4,11,256]{2,1,0:T(8,128)S(1)}, f32[4,11,256]{2,1,0:T(8,128)S(1)}, u32[]{:S(2)}, u32[]{:S(2)}) collective-permute-start(f32[4,11,256]{2,1,0:T(8,128)S(1)} %get-tuple-element.51), channel_id=1, source_target_pairs={{0,1},{1,2},{2,3},{3,4},{4,5},{5,6},{6,7},{7,8},{8,9},{9,10},{10,1... | collective-permute-start | bytes 135176 | tf_op jit(solution)/shard_map/ppermute | solution.py:20
  16.8 12.1 %collective-permute-start.1 = (f32[4,11,256]{2,1,0:T(8,128)S(1)}, f32[4,11,256]{2,1,0:T(8,128)S(1)}, u32[]{:S(2)}, u32[]{:S(2)}) collective-permute-start(f32[4,11,256]{2,1,0:T(8,128)S(1)} %get-tuple-element.52), channel_id=1, source_target_pairs={{1,0},{2,1},{3,2},{4,3},{5,4},{6,5},{7,6},{8,7},{9,8},{10,9},{11,1... | collective-permute-start | bytes 135176 | tf_op jit(solution)/shard_map/ppermute | solution.py:21
  44.0 3.8 %fusion.162 = f32[8,8,256]{2,1,0:T(8,128)S(1)} fusion(f32[8,8,256]{2,1,0:T(8,128)S(1)} %gather_fusion.2, f32[8,256]{1,0:T(8,128)S(1)} %bitcast.182, f32[8,256]{1,0:T(8,128)S(1)} %bitcast.183, f32[8,256]{1,0:T(8,128)S(1)} %bitcast.184, f32[8,256]{1,0:T(8,128)S(1)} %get-tuple-element.129, f32[8,256]{1,0:T(8,128)S(1)} %get-tuple-element.130, ...), kind=kOutput, calls=%fused_computation.180 | convolution fusion | flops 56639488 | bytes 180232 | tf_op jit(solution)/shard_map/lab,lpb->lpa/dot_general | solution.py:57
  47.8 3.8 %fusion.165 = f32[8,8,256]{2,1,0:T(8,128)S(1)} fusion(f32[8,8,256]{2,1,0:T(8,128)S(1)} %gather_fusion.4, f32[8,256]{1,0:T(8,128)S(1)} %bitcast.185, f32[8,256]{1,0:T(8,128)S(1)} %bitcast.186, f32[8,256]{1,0:T(8,128)S(1)} %bitcast.187, f32[8,256]{1,0:T(8,128)S(1)} %get-tuple-element.129, f32[8,256]{1,0:T(8,128)S(1)} %get-tuple-element.130, ...), kind=kOutput, calls=%fused_computation.181 | convolution fusion | flops 56639488 | bytes 180232 | tf_op jit(solution)/shard_map/lab,lpb->lpa/dot_general | solution.py:57
  51.5 3.8 %fusion.168 = f32[8,8,256]{2,1,0:T(8,128)S(1)} fusion(f32[8,8,256]{2,1,0:T(8,128)S(1)} %gather_fusion.6, f32[8,256]{1,0:T(8,128)S(1)} %bitcast.188, f32[8,256]{1,0:T(8,128)S(1)} %bitcast.189, f32[8,256]{1,0:T(8,128)S(1)} %bitcast.190, f32[8,256]{1,0:T(8,128)S(1)} %get-tuple-element.129, f32[8,256]{1,0:T(8,128)S(1)} %get-tuple-element.130, ...), kind=kOutput, calls=%fused_computation.182 | convolution fusion | flops 56639488 | bytes 180232 | tf_op jit(solution)/shard_map/lab,lpb->lpa/dot_general | solution.py:57
  55.3 3.8 %fusion.171 = f32[8,8,256]{2,1,0:T(8,128)S(1)} fusion(f32[8,8,256]{2,1,0:T(8,128)S(1)} %gather_fusion.8, f32[8,256]{1,0:T(8,128)S(1)} %bitcast.191, f32[8,256]{1,0:T(8,128)S(1)} %bitcast.192, f32[8,256]{1,0:T(8,128)S(1)} %bitcast.193, f32[8,256]{1,0:T(8,128)S(1)} %get-tuple-element.129, f32[8,256]{1,0:T(8,128)S(1)} %get-tuple-element.130, ...), kind=kOutput, calls=%fused_computation.183 | convolution fusion | flops 56639488 | bytes 180232 | tf_op jit(solution)/shard_map/lab,lpb->lpa/dot_general | solution.py:57
  59.1 3.8 %fusion.174 = f32[8,8,256]{2,1,0:T(8,128)S(1)} fusion(f32[8,8,256]{2,1,0:T(8,128)S(1)} %gather_fusion.10, f32[8,256]{1,0:T(8,128)S(1)} %bitcast.194, f32[8,256]{1,0:T(8,128)S(1)} %bitcast.195, f32[8,256]{1,0:T(8,128)S(1)} %bitcast.196, f32[8,256]{1,0:T(8,128)S(1)} %get-tuple-element.129, f32[8,256]{1,0:T(8,128)S(1)} %get-tuple-element.130, ...), kind=kOutput, calls=%fused_computation.184 | convolution fusion | flops 56639488 | bytes 180232 | tf_op jit(solution)/shard_map/lab,lpb->lpa/dot_general | solution.py:57
  62.8 3.8 %fusion.177 = f32[8,8,256]{2,1,0:T(8,128)S(1)} fusion(f32[8,8,256]{2,1,0:T(8,128)S(1)} %gather_fusion.12, f32[8,256]{1,0:T(8,128)S(1)} %bitcast.197, f32[8,256]{1,0:T(8,128)S(1)} %bitcast.198, f32[8,256]{1,0:T(8,128)S(1)} %bitcast.199, f32[8,256]{1,0:T(8,128)S(1)} %get-tuple-element.129, f32[8,256]{1,0:T(8,128)S(1)} %get-tuple-element.130, ...), kind=kOutput, calls=%fused_computation.185 | convolution fusion | flops 56639488 | bytes 180232 | tf_op jit(solution)/shard_map/lab,lpb->lpa/dot_general | solution.py:57
  66.6 3.8 %fusion.180 = f32[8,8,256]{2,1,0:T(8,128)S(1)} fusion(f32[8,8,256]{2,1,0:T(8,128)S(1)} %gather_fusion.14, f32[8,256]{1,0:T(8,128)S(1)} %bitcast.200, f32[8,256]{1,0:T(8,128)S(1)} %bitcast.201, f32[8,256]{1,0:T(8,128)S(1)} %bitcast.202, f32[8,256]{1,0:T(8,128)S(1)} %get-tuple-element.129, f32[8,256]{1,0:T(8,128)S(1)} %get-tuple-element.130, ...), kind=kOutput, calls=%fused_computation.186 | convolution fusion | flops 56639488 | bytes 180232 | tf_op jit(solution)/shard_map/lab,lpb->lpa/dot_general | solution.py:57
  70.3 3.8 %fusion.183 = f32[8,8,256]{2,1,0:T(8,128)S(1)} fusion(f32[8,8,256]{2,1,0:T(8,128)S(1)} %gather_fusion.16, f32[8,256]{1,0:T(8,128)S(1)} %bitcast.203, f32[8,256]{1,0:T(8,128)S(1)} %bitcast.204, f32[8,256]{1,0:T(8,128)S(1)} %bitcast.206, f32[8,256]{1,0:T(8,128)S(1)} %get-tuple-element.129, f32[8,256]{1,0:T(8,128)S(1)} %get-tuple-element.130, ...), kind=kOutput, calls=%fused_computation.187 | convolution fusion | flops 56639488 | bytes 180232 | tf_op jit(solution)/shard_map/lab,lpb->lpa/dot_general | solution.py:57
  74.1 4.1 %fusion.159 = f32[8,8,256]{2,1,0:T(8,128)S(1)} fusion(f32[8,8,256]{2,1,0:T(8,128)S(1)} %fusion.183, f32[8,8,256]{2,1,0:T(8,128)S(1)} %fusion.180, f32[8,8,256]{2,1,0:T(8,128)S(1)} %fusion.177, f32[8,8,256]{2,1,0:T(8,128)S(1)} %fusion.174, f32[8,8,256]{2,1,0:T(8,128)S(1)} %fusion.171, f32[8,8,256]{2,1,0:T(8,128)S(1)} %fusion.168, ...), kind=kOutput, calls=%fused_computation.179 | convolution fusion | flops 56770560 | bytes 704520 | tf_op jit(solution)/shard_map/lab,lpb->lpa/dot_general | solution.py:57
  78.2 20.5 %all-gather.5.cloned.1.call-done = f32[512,11,128]{2,0,1:T(8,128)} async-done(((f32[8,11,128]{2,0,1:T(8,128)}), f32[512,11,128]{2,0,1:T(8,128)}) %all-gather.5.cloned.1.call-update) | async-done | bytes 2883600 | tf_op jit(solution)/shard_map/all_gather | solution.py:61
  98.7 5.5 %copy.18 = f32[512,11,128]{2,1,0:T(8,128)} copy(f32[512,11,128]{2,0,1:T(8,128)} %all-gather.5.cloned.1.call-done) | data formatting | bytes 5767168 | tf_op jit(solution)/shard_map/all_gather | solution.py:61
  104.2 2.7 %gather_fusion.18 = f32[8,11,128]{2,1,0:T(8,128)S(1)} fusion(f32[512,11,128]{2,1,0:T(8,128)} %copy.18, s32[1024]{0:T(1024)S(1)} %get-tuple-element.176), kind=kCustom, calls=%fused_computation.18 | custom fusion | bytes 90144 | tf_op jit(solution)/shard_map/gather | solution.py:66
  107.0 2.7 %gather_fusion.19 = f32[8,11,128]{2,1,0:T(8,128)S(1)} fusion(f32[512,11,128]{2,1,0:T(8,128)} %copy.18, s32[1024]{0:T(1024)S(1)} %get-tuple-element.175), kind=kCustom, calls=%fused_computation.19 | custom fusion | bytes 90144 | tf_op jit(solution)/shard_map/gather | solution.py:66
  109.7 2.7 %gather_fusion.20 = f32[8,11,128]{2,1,0:T(8,128)S(1)} fusion(f32[512,11,128]{2,1,0:T(8,128)} %copy.18, s32[1024]{0:T(1024)S(1)} %get-tuple-element.174), kind=kCustom, calls=%fused_computation.20 | custom fusion | bytes 90144 | tf_op jit(solution)/shard_map/gather | solution.py:66
  112.5 2.7 %gather_fusion.21 = f32[8,11,128]{2,1,0:T(8,128)S(1)} fusion(f32[512,11,128]{2,1,0:T(8,128)} %copy.18, s32[1024]{0:T(1024)S(1)} %get-tuple-element.173), kind=kCustom, calls=%fused_computation.21 | custom fusion | bytes 90144 | tf_op jit(solution)/shard_map/gather | solution.py:66
  115.3 2.7 %gather_fusion.22 = f32[8,11,128]{2,1,0:T(8,128)S(1)} fusion(f32[512,11,128]{2,1,0:T(8,128)} %copy.18, s32[1024]{0:T(1024)S(1)} %get-tuple-element.172), kind=kCustom, calls=%fused_computation.22 | custom fusion | bytes 90144 | tf_op jit(solution)/shard_map/gather | solution.py:66
  118.0 2.7 %gather_fusion.23 = f32[8,11,128]{2,1,0:T(8,128)S(1)} fusion(f32[512,11,128]{2,1,0:T(8,128)} %copy.18, s32[1024]{0:T(1024)S(1)} %get-tuple-element.171), kind=kCustom, calls=%fused_computation.23 | custom fusion | bytes 90144 | tf_op jit(solution)/shard_map/gather | solution.py:66
  120.8 2.7 %gather_fusion.24 = f32[8,11,128]{2,1,0:T(8,128)S(1)} fusion(f32[512,11,128]{2,1,0:T(8,128)} %copy.18, s32[1024]{0:T(1024)S(1)} %get-tuple-element.170), kind=kCustom, calls=%fused_computation.24 | custom fusion | bytes 90144 | tf_op jit(solution)/shard_map/gather | solution.py:66
  123.6 2.7 %gather_fusion.25 = f32[8,11,128]{2,1,0:T(8,128)S(1)} fusion(f32[512,11,128]{2,1,0:T(8,128)} %copy.18, s32[1024]{0:T(1024)S(1)} %get-tuple-element.169), kind=kCustom, calls=%fused_computation.25 | custom fusion | bytes 90144 | tf_op jit(solution)/shard_map/gather | solution.py:66
  126.3 2.7 %gather_fusion.26 = f32[8,11,128]{2,1,0:T(8,128)S(1)} fusion(f32[512,11,128]{2,1,0:T(8,128)} %copy.18, s32[1024]{0:T(1024)S(1)} %get-tuple-element.168), kind=kCustom, calls=%fused_computation.26 | custom fusion | bytes 90144 | tf_op jit(solution)/shard_map/gather | solution.py:66
  129.1 2.7 %gather_fusion.27 = f32[8,11,128]{2,1,0:T(8,128)S(1)} fusion(f32[512,11,128]{2,1,0:T(8,128)} %copy.18, s32[1024]{0:T(1024)S(1)} %get-tuple-element.167), kind=kCustom, calls=%fused_computation.27 | custom fusion | bytes 90144 | tf_op jit(solution)/shard_map/gather | solution.py:66
  131.8 2.7 %gather_fusion.28 = f32[8,11,128]{2,1,0:T(8,128)S(1)} fusion(f32[512,11,128]{2,1,0:T(8,128)} %copy.18, s32[1024]{0:T(1024)S(1)} %get-tuple-element.166), kind=kCustom, calls=%fused_computation.28 | custom fusion | bytes 90144 | tf_op jit(solution)/shard_map/gather | solution.py:66
  134.6 2.7 %gather_fusion.29 = f32[8,11,128]{2,1,0:T(8,128)S(1)} fusion(f32[512,11,128]{2,1,0:T(8,128)} %copy.18, s32[1024]{0:T(1024)S(1)} %get-tuple-element.165), kind=kCustom, calls=%fused_computation.29 | custom fusion | bytes 90144 | tf_op jit(solution)/shard_map/gather | solution.py:66
  137.3 2.7 %gather_fusion.30 = f32[8,11,128]{2,1,0:T(8,128)S(1)} fusion(f32[512,11,128]{2,1,0:T(8,128)} %copy.18, s32[1024]{0:T(1024)S(1)} %get-tuple-element.164), kind=kCustom, calls=%fused_computation.30 | custom fusion | bytes 90144 | tf_op jit(solution)/shard_map/gather | solution.py:66
  140.0 2.7 %gather_fusion.31 = f32[8,11,128]{2,1,0:T(8,128)S(1)} fusion(f32[512,11,128]{2,1,0:T(8,128)} %copy.18, s32[1024]{0:T(1024)S(1)} %get-tuple-element.163), kind=kCustom, calls=%fused_computation.31 | custom fusion | bytes 90144 | tf_op jit(solution)/shard_map/gather | solution.py:66
  142.8 2.7 %gather_fusion.32 = f32[8,11,128]{2,1,0:T(8,128)S(1)} fusion(f32[512,11,128]{2,1,0:T(8,128)} %copy.18, s32[1024]{0:T(1024)S(1)} %get-tuple-element.162), kind=kCustom, calls=%fused_computation.32 | custom fusion | bytes 90144 | tf_op jit(solution)/shard_map/gather | solution.py:66
  145.5 2.7 %gather_fusion.33 = f32[8,11,128]{2,1,0:T(8,128)S(1)} fusion(f32[512,11,128]{2,1,0:T(8,128)} %copy.18, s32[1024]{0:T(1024)S(1)} %get-tuple-element.161), kind=kCustom, calls=%fused_computation.33 | custom fusion | bytes 90144 | tf_op jit(solution)/shard_map/gather | solution.py:66
  169.3 52.3 %all-gather.7.cloned.1.call-done = f32[512,11,128]{2,1,0:T(8,128)} async-done(((f32[1,11,128]{2,1,0:T(8,128)}), f32[512,11,128]{2,1,0:T(8,128)}) %all-gather.7.cloned.1.call-update) | async-done | bytes 2883600 | tf_op jit(solution)/shard_map/all_gather | solution.py:75
  221.6 2.7 %gather_fusion.34 = f32[16,11,128]{2,1,0:T(8,128)S(1)} fusion(f32[512,11,128]{2,1,0:T(8,128)} %all-gather.7.cloned.1.call-done, s32[1024]{0:T(1024)S(1)} %pad_clamp_fusion), kind=kCustom, calls=%fused_computation.34 | custom fusion | bytes 180288 | tf_op jit(solution)/shard_map/gather | solution.py:76
  (145 shorter events, 42.3 us)
Async XLA Ops:
  6.5 1.3 copy-start
  6.5 25.2 %copy-start.6 = (f32[8,3,128]{2,0,1:T(8,128)S(1)}, f32[8,3,128]{2,0,1:T(8,128)}, u32[]{:S(2)}) copy-start(f32[8,3,128]{2,0,1:T(8,128)} %param.12) | copy-start | bytes 36868
  6.5 26.6 %copy-start.3 = (f32[8,8,256]{2,1,0:T(8,128)S(1)}, f32[8,8,256]{2,1,0:T(8,128)}, u32[]{:S(2)}) copy-start(f32[8,8,256]{2,1,0:T(8,128)} %param.10) | copy-start | bytes 196612
  6.5 25.2 %copy-start.5 = (f32[8,3,256]{2,0,1:T(8,128)S(1)}, f32[8,3,256]{2,0,1:T(8,128)}, u32[]{:S(2)}) copy-start(f32[8,3,256]{2,0,1:T(8,128)} %param.9) | copy-start | bytes 73732
  6.5 25.2 %copy-start.7 = (f32[1,3,128]{2,0,1:T(1,128)S(1)}, f32[1,3,128]{2,0,1:T(1,128)}, u32[]{:S(2)}) copy-start(f32[1,3,128]{2,0,1:T(1,128)} %param.14) | copy-start | bytes 4612
  6.6 25.2 %copy-start.8 = (s32[1,16]{1,0:T(1,128)S(1)}, s32[1,16]{1,0:T(1,128)}, u32[]{:S(2)}) copy-start(s32[1,16]{1,0:T(1,128)} %param.17) | copy-start | bytes 196
  6.6 25.3 %copy-start.2 = (s32[8,9]{1,0:T(8,128)S(1)}, s32[8,9]{1,0:T(8,128)}, u32[]{:S(2)}) copy-start(s32[8,9]{1,0:T(8,128)} %param.15) | copy-start | bytes 868
  6.6 25.6 %copy-start.4 = (s32[8,16]{1,0:T(8,128)S(1)}, s32[8,16]{1,0:T(8,128)}, u32[]{:S(2)}) copy-start(s32[8,16]{1,0:T(8,128)} %param.16) | copy-start | bytes 1540
  6.6 92.1 %all-gather.5.cloned.1.call-start = ((), (), s32[]{:S(2)}) async-start(), calls=%async_computation | async-start | bytes 2928640 | tf_op jit(solution)/shard_map/all_gather | solution.py:61
  10.3 211.2 %all-gather.7.cloned.1.call-start = ((), (), s32[]{:S(2)}) async-start(), calls=%async_computation.1 | async-start | bytes 4202496 | tf_op jit(solution)/shard_map/all_gather | solution.py:75
  11.9 21.2 %collective-permute-start = (f32[4,11,256]{2,1,0:T(8,128)S(1)}, f32[4,11,256]{2,1,0:T(8,128)S(1)}, u32[]{:S(2)}, u32[]{:S(2)}) collective-permute-start(f32[4,11,256]{2,1,0:T(8,128)S(1)} %get-tuple-element.51), channel_id=1, source_target_pairs={{0,1},{1,2},{2,3},{3,4},{4,5},{5,6},{6,7},{7,8},{8,9},{9,10},{10,1... | collective-permute-start | bytes 135176 | tf_op jit(solution)/shard_map/ppermute | solution.py:20
  16.8 16.3 %collective-permute-start.1 = (f32[4,11,256]{2,1,0:T(8,128)S(1)}, f32[4,11,256]{2,1,0:T(8,128)S(1)}, u32[]{:S(2)}, u32[]{:S(2)}) collective-permute-start(f32[4,11,256]{2,1,0:T(8,128)S(1)} %get-tuple-element.52), channel_id=1, source_target_pairs={{1,0},{2,1},{3,2},{4,3},{5,4},{6,5},{7,6},{8,7},{9,8},{10,9},{11,1... | collective-permute-start | bytes 135176 | tf_op jit(solution)/shard_map/ppermute | solution.py:21
  169.3 56.6 %copy-start.1 = (f32[8,128,128]{2,1,0:T(8,128)S(1)}, f32[8,128,128]{2,1,0:T(8,128)}, u32[]{:S(2)}) copy-start(f32[8,128,128]{2,1,0:T(8,128)} %param.13) | copy-start | bytes 1572868
Sparse Core Ops, SparseCore 0:
  10.4 88.2 all-gather.4
  102.9 118.5 all-gather.6
where the time goes:
time: 235 us; the launch traced here: 234 us
  waiting for transfers between devices  72.8 us (31%)
  local copies, waits for them, and re-layouts  66 us (28%)
  matrix products  61.5 us (26%)
  starting transfers between devices  17 us (7%)
  between operations  14.4 us (6%)
  other arithmetic  2.65 us (1%)
    all_gather x1, waiting for transfers between devices, body(): lax.all_gather(cell_slab, ('group', 'leaf'), axis=0, tiled=True)  52.3 us
    gather x16, local copies, waits for them, and re-layouts, body(): source = subtree[local]  43.8 us
    dot_general x9, matrix products, body(): jnp.einsum('lab,lpb->lpa', kernel, ext_vals[local], precision=finest_level)  34.2 us
    dot_general x16, matrix products, body(): jnp.einsum('lab,lpb->lpa', kernel, source[:, 3:], precision=finest_level)  20.8 us
    all_gather x1, waiting for transfers between devices, body(): subtree = lax.all_gather(skeleton_slab, 'leaf', axis=0, tiled=True)  20.5 us
    ppermute x1, starting transfers between devices, extended_2(): after = lax.ppermute(first, axis, down)  12.1 us
    all_gather x1, local copies, waits for them, and re-layouts, body(): subtree = lax.all_gather(skeleton_slab, 'leaf', axis=0, tiled=True)  5.5 us
    gather x9, local copies, waits for them, and re-layouts, body(): kernel = matern(points, ext_pts[local])  5.19 us
  transfers between devices with their start and end apart: 4, of which 2 were waited for; matrix products, arithmetic and copies ran while one was open for 51% of the time, Pallas kernels for 0%

commit v1 on v0

v1 whole, which is shorter than its diff:
```python
import functools
import math

import jax
import jax.numpy as jnp
from jax import lax
from jax.experimental import pallas as pl
from jax.experimental.pallas import tpu as pltpu
from jax.sharding import Mesh, PartitionSpec as P

F32 = jnp.float32
BF16 = jnp.bfloat16
KAPPA = math.sqrt(3.0) * math.log2(math.e)
LN2 = math.log(2.0)
CENTER = 1.5
FEAT = 32
REACH = 4
OWN = 8
NBR = 9
UNROLL = 8
EXACT = lax.Precision.HIGHEST

SMEM = pl.BlockSpec(memory_space=pltpu.SMEM)
VMEM = pl.BlockSpec(memory_space=pltpu.VMEM)


def split3(x):
    a = x.astype(BF16)
    r = x - a.astype(F32)
    b = r.astype(BF16)
    c = (r - b.astype(F32)).astype(BF16)
    return a.astype(F32), b.astype(F32), c.astype(F32)


def features(pts):
    x = (pts - CENTER) * KAPPA
    n = jnp.sum(x * x, axis=0, keepdims=True)
    x1, x2, x3 = split3(x)
    n1, n2, n3 = split3(n)
    one = jnp.ones_like(n)
    pad = jnp.zeros((FEAT - 24, pts.shape[1]), F32)
    src = jnp.concatenate([x1, x1, x2, x2, x1, x3, n1, n2, n3, one, one, one, pad], 0)
    tgt = jnp.concatenate([-2 * x1, -2 * x2, -2 * x1, -2 * x2, -2 * x3, -2 * x1, one, one, one, n1, n2, n3, pad], 0)
    return src, tgt


def two_halves(vals):
    v = vals * LN2
    high = v.astype(BF16).astype(F32)
    return jnp.concatenate([high, v - high], 0).astype(BF16)


def matern_over_ln2(t):
    m = jnp.maximum(t, 1e-12)
    s = m * lax.rsqrt(m)
    return (s + 1.0 / LN2) * jnp.exp2(-s)


def product(src_feat, tgt_feat, vals):
    t = jnp.dot(src_feat, tgt_feat, preferred_element_type=F32)
    k = matern_over_ln2(t)
    high = k.astype(BF16)
    low = (k - high.astype(F32)).astype(BF16)
    out = jnp.dot(vals, high, preferred_element_type=F32) + jnp.dot(vals, low, preferred_element_type=F32)
    return out


def nt(a, b):
    return lax.dot_general(a, b, (((1,), (1,)), ((), ())), precision=EXACT, preferred_element_type=F32)


def pack_kernel(pts, chg, up, skel, utm, cpts, llist, tlist, m1, m0, first, last):
    f32 = F32
    for l in range(OWN):
        w = nt(chg[l], up[l])
        cw = nt(w, utm[l])
        total = cw if l == 0 else total + cw
        for d in range(8):
            m1[d, 8 * l : 8 * l + 8, :] = w
            m1[d, 64 + 3 * l : 67 + 3 * l, :] = skel[l]
            m0[d, 3 * l : 3 * l + 3, :] = skel[l]
    for d in range(8):
        m1[d, 88:96, :] = total
        m1[d, 96:99, :] = cpts[0]
        m1[d, 99:104, :] = jnp.zeros((5, 128), f32)
        m0[d, 24:27, :] = cpts[0]
        m0[d, 29:32, :] = jnp.zeros((3, 128), f32)
    for slab, start in ((first, 0), (last, OWN - REACH)):
        for i in range(REACH):
            slab[8 * i : 8 * i + 8, :] = chg[start + i]
            slab[32 + 3 * i : 35 + 3 * i, :] = pts[start + i]
        slab[44:48, :] = jnp.zeros((4, 256), f32)
    lane = lax.broadcasted_iota(jnp.int32, (1, 128), 1)
    sub8 = lax.broadcasted_iota(jnp.int32, (8, 128), 0)
    row = lax.broadcasted_iota(jnp.int32, (128, 128), 0)
    col = lax.broadcasted_iota(jnp.int32, (128, 128), 1)
    before = (row < col).astype(f32).astype(BF16)
    ll = llist[...]
    tl = tlist[...]
    leaf_hit = ((ll >> 3) & 7) == sub8
    top_hit = ((tl & 7) == sub8) & (lane < 16)
    leaf_one = leaf_hit.astype(f32)
    top_one = top_hit.astype(f32)
    leaf_pos = jnp.dot(leaf_one.astype(BF16), before, preferred_element_type=f32)
    top_pos = jnp.dot(top_one.astype(BF16), before, preferred_element_type=f32) + 16.0
    leaf_n = jnp.sum(leaf_one, axis=1, keepdims=True)
    top_n = jnp.sum(top_one, axis=1, keepdims=True)
    leaf_pos = jnp.where(leaf_hit, leaf_pos, -1.0)
    top_pos = jnp.where(top_hit, top_pos, -1.0)
    local = (ll & 7) + ((ll >> 6) & 7) * 8
    codes = jnp.where(sub8 == 0, lane >> 4, jnp.where(sub8 == 1, local, 0)).astype(f32).astype(BF16)
    tcodes = jnp.where(sub8 == 0, tl >> 3, 0).astype(f32).astype(BF16)
    rowf = row.astype(f32)
    for d in range(8):
        oh = (leaf_pos[d : d + 1] == rowf).astype(f32).astype(BF16)
        got = lax.dot_general(codes, oh, (((1,), (1,)), ((), ())), preferred_element_type=f32)
        m0[d, 27:28, :] = got[0:1] * 64.0 + got[1:2]
        oh = (top_pos[d : d + 1] == rowf).astype(f32).astype(BF16)
        got = lax.dot_general(tcodes, oh, (((1,), (1,)), ((), ())), preferred_element_type=f32)[0:1]
        got = got + jnp.where(lane == 0, leaf_n[d : d + 1], 0.0) + jnp.where(lane == 1, top_n[d : d + 1], 0.0)
        m0[d, 28:29, :] = got


def pack(pts, chg, up, skel, utm, cpts, llist, tlist):
    sd = jax.ShapeDtypeStruct
    return pl.pallas_call(
        pack_kernel,
        in_specs=[VMEM] * 8,
        out_specs=[VMEM] * 4,
        out_shape=[sd((8, 104, 128), F32), sd((8, 32, 128), F32), sd((48, 256), F32), sd((48, 256), F32)],
        compiler_params=pltpu.CompilerParams(vmem_limit_bytes=32 << 20),
        name="pack",
    )(pts, chg, up, skel, utm, cpts, llist, tlist)


def near_kernel(lo, hi, ids, pts, chg, before, after, out, fs, ft, vals):
    me = (lax.axis_index("g") * lax.axis_size("y") + lax.axis_index("y")) * lax.axis_size("z") + lax.axis_index("z")
    base = me * OWN - REACH
    for e in range(lo, hi + 2 * REACH):
        if e < REACH:
            p, c = before[32 + 3 * e : 35 + 3 * e, :], before[8 * e : 8 * e + 8, :]
        elif e < REACH + OWN:
            p, c = pts[e - REACH], chg[e - REACH]
        else:
            i = e - REACH - OWN
            p, c = after[32 + 3 * i : 35 + 3 * i, :], after[8 * i : 8 * i + 8, :]
        src, tgt = features(p)
        fs[e - lo] = src.T.astype(BF16)
        if lo <= e - REACH < hi:
            ft[e - REACH - lo] = tgt.astype(BF16)
        vals[e - lo] = two_halves(c)
    dead = hi - lo + 2 * REACH
    vals[dead] = jnp.zeros((16, 256), BF16)

    def leaf(i, carry):
        tgt = ft[i]
        acc = jnp.zeros((16, 256), F32)
        for n in range(NBR):
            ident = ids[i + lo, n]
            live = ident >= 0
            e = jnp.where(live, ident - base - lo, 0)
            acc = acc + product(fs[e], tgt, vals[jnp.where(live, e, dead)])
        out[i] = acc[0:8] + acc[8:16]
        return carry

    lax.fori_loop(0, hi - lo, leaf, 0)


def near_part(lo, hi, ids, pts, chg, before, after):
    n = hi - lo
    return pl.pallas_call(
        functools.partial(near_kernel, lo, hi),
        in_specs=[SMEM] + [VMEM] * 4,
        out_specs=VMEM,
        out_shape=jax.ShapeDtypeStruct((n, 8, 256), F32),
        scratch_shapes=[
            pltpu.VMEM((n + 8, 256, FEAT), BF16),
            pltpu.VMEM((n, FEAT, 256), BF16),
            pltpu.VMEM((n + 9, 16, 256), BF16),
        ],
        cost_estimate=pl.CostEstimate(flops=n * 9 * 256 * 256 * 1000, bytes_accessed=300000, transcendentals=n * 9 * 65536 * 2),
        compiler_params=pltpu.CompilerParams(vmem_limit_bytes=32 << 20),
        name="near",
    )(ids, pts, chg, before, after)


def far_leaf_kernel(req, src, tgt, out, fs, ft, vals):
    for y in range(8):
        for l in range(OWN):
            i = 8 * y + l
            f, _ = features(src[y, 64 + 3 * l : 67 + 3 * l, :])
            fs[i] = f.T.astype(BF16)
            vals[i] = two_halves(src[y, 8 * l : 8 * l + 8, :])
            _, f = features(tgt[y, 3 * l : 3 * l + 3, :])
            ft[i] = f.astype(BF16)
    vals[64] = jnp.zeros((16, 128), BF16)
    out[...] = jnp.zeros_like(out)

    def of_device(d, carry):
        n = req[d, 1, 0]

        def chunk(i, c):
            for u in range(UNROLL):
                at = i * UNROLL + u
                code = req[d, 0, at]
                t = code >> 6
                s = code & 63
                r = product(fs[s], ft[d * 8 + t], vals[jnp.where(at < n, s, 64)])
                out[d, t] += r[0:8] + r[8:16]
            return c

        lax.fori_loop(0, (n + UNROLL - 1) // UNROLL, chunk, 0)
        return carry

    lax.fori_loop(0, 8, of_device, 0)


def far_leaf(req, src, tgt):
    return pl.pallas_call(
        far_leaf_kernel,
        in_specs=[SMEM, VMEM, VMEM],
        out_specs=VMEM,
        out_shape=jax.ShapeDtypeStruct((8, 9, 8, 128), F32),
        scratch_shapes=[
            pltpu.VMEM((64, 128, FEAT), BF16),
            pltpu.VMEM((64, FEAT, 128), BF16),
            pltpu.VMEM((65, 16, 128), BF16),
        ],
        cost_estimate=pl.CostEstimate(flops=128 * 128 * 128 * 1000, bytes_accessed=900000, transcendentals=128 * 16384 * 2),
        compiler_params=pltpu.CompilerParams(vmem_limit_bytes=32 << 20),
        name="far_leaf",
    )(req, src, tgt)


def far_top_kernel(req, src, tgt, part, out, fs, vals):
    for g in range(8):
        for y in range(8):
            i = 8 * g + y
            f, _ = features(src[g, 16 * y + 8 : 16 * y + 11, :])
            fs[i] = f.T.astype(BF16)
            vals[i] = two_halves(src[g, 16 * y : 16 * y + 8, :])
    out[...] = part[...]

    def of_device(d, carry):
        n = req[d, 1, 1]
        _, f = features(tgt[d, 24:27, :])
        ft = f.astype(BF16)

        def one(i, acc):
            s = req[d, 1, 16 + i]
            return acc + product(fs[s], ft, vals[s])

        acc = lax.fori_loop(0, n, one, jnp.zeros((16, 128), F32))
        out[d, 8] = acc[0:8] + acc[8:16]
        return carry

    lax.fori_loop(0, 8, of_device, 0)


def far_top(req, src, tgt, part):
    return pl.pallas_call(
        far_top_kernel,
        in_specs=[SMEM, VMEM, VMEM, VMEM],
        out_specs=VMEM,
        out_shape=jax.ShapeDtypeStruct((8, 9, 8, 128), F32),
        scratch_shapes=[pltpu.VMEM((64, 128, FEAT), BF16), pltpu.VMEM((64, 16, 128), BF16)],
        compiler_params=pltpu.CompilerParams(vmem_limit_bytes=32 << 20),
        name="far_top",
    )(req, src, tgt, part)


def final_kernel(got, utm, up, near1, near2, out):
    tot = got[0]
    for d in range(1, 8):
        tot = tot + got[d]
    cell = tot[8]
    for l in range(OWN):
        incoming = tot[l] + jnp.dot(cell, utm[l], precision=EXACT, preferred_element_type=F32)
        near = near1[l] if l < OWN // 2 else near2[l - OWN // 2]
        out[l] = near + jnp.dot(incoming, up[l], precision=EXACT, preferred_element_type=F32)


def final(got, utm, up, near1, near2):
    return pl.pallas_call(
        final_kernel,
        in_specs=[VMEM] * 5,
        out_specs=VMEM,
        out_shape=jax.ShapeDtypeStruct((8, 8, 256), F32),
        compiler_params=pltpu.CompilerParams(vmem_limit_bytes=32 << 20),
        name="final",
    )(got, utm, up, near1, near2)


def body(points, charges, up_op, skel_pts, utm, cell_pts, near_list, leaf_list, top_list):
    every = ("g", "y", "z")
    llist = leaf_list.reshape(1, 128)
    tlist = jnp.pad(top_list, ((0, 0), (0, 112)), constant_values=0)
    m1, m0, first, last = pack(points, charges, up_op, skel_pts, utm, cell_pts, llist, tlist)
    count = lax.axis_size("g") * lax.axis_size("y") * lax.axis_size("z")
    up = [(i, i + 1) for i in range(count - 1)]
    down = [(i + 1, i) for i in range(count - 1)]
    got1 = lax.all_to_all(m1, "y", 0, 0, tiled=True)
    got0 = lax.all_to_all(m0, "z", 0, 0, tiled=True)
    before = lax.ppermute(last, every, up)
    after = lax.ppermute(first, every, down)
    near1 = near_part(0, 4, near_list, points, charges, before, after)
    got1, near1 = lax.optimization_barrier((got1, near1))
    cells = jnp.broadcast_to(got1[:, 88:104, :].reshape(1, 128, 128), (8, 128, 128))
    gotg = lax.all_to_all(cells, "g", 0, 0, tiled=True)
    req = got0[:, 27:29, :].astype(jnp.int32)
    part = far_leaf(req, got1, got0)
    part = far_top(req, gotg, got0, part)
    part, charges2 = lax.optimization_barrier((part, charges))
    gotr = lax.all_to_all(part, "z", 0, 0, tiled=True)
    near2 = near_part(4, 8, near_list, points, charges2, before, after)
    return final(gotr, utm, up_op, near1, near2)


def solution(mesh):
    fine = Mesh(mesh.devices.reshape(mesh.shape["group"], 8, 8), ("g", "y", "z"))
    row = ("g", "y", "z")
    specs = tuple(P(row, *([None] * k)) for k in (2, 2, 2, 2, 2, 2, 1, 1, 1))
    return jax.shard_map(body, mesh=fine, in_specs=specs, out_specs=P(row, None, None), check_vma=False)
```

time: 235 us -> 103 us (0.44)
  waiting for transfers between devices: 72.8 us -> 9.64 us
  matrix products: 61.5 us -> 0 us
  local copies, waits for them, and re-layouts: 66 us -> 5.3 us
  Pallas kernels: 0 us -> 41.8 us
  starting transfers between devices: 17 us -> 45.8 us
  between operations: 14.4 us -> 0.11 us
  other arithmetic: 2.65 us -> 0.01 us
    all_gather x2 -> x0, waiting for transfers between devices: 72.8 us -> none  [the longest x1 52.3 us: body(): lax.all_gather(cell_slab, ('group', 'leaf'), axis=0, tiled=True)]
    dot_general x30 -> x0, matrix products: 61.5 us -> none  [the longest x9 34.2 us: body(): jnp.einsum('lab,lpb->lpa', kernel, ext_vals[local], precision=finest_level)]
    gather x35 -> x0, local copies, waits for them, and re-layouts: 56.7 us -> none  [the longest x16 43.8 us: body(): source = subtree[local]]
    pallas_call x0 -> x6, Pallas kernels: none -> 41.8 us  [the longest x1 21.2 us: far_leaf(): pl.pallas_call(far_leaf_kernel, in_specs=[SMEM, VMEM, VMEM], out_specs=VM...]
    all_to_all x0 -> x4, starting transfers between devices: none -> 29.7 us  [the longest x1 9.14 us: body(): got0 = lax.all_to_all(m0, 'z', 0, 0, tiled=True)]
    all_to_all x0 -> x4, waiting for transfers between devices: none -> 9.63 us  [the longest x1 7.33 us: body(): gotr = lax.all_to_all(part, 'z', 0, 0, tiled=True)]
    all_gather x1 -> x0, local copies, waits for them, and re-layouts: 5.5 us -> none  [body(): subtree = lax.all_gather(skeleton_slab, 'leaf', axis=0, tiled=True)]
  transfers between devices with their start and end apart: 4 -> 6, of which waited for: 2 -> 2; matrix products, arithmetic and copies ran while one was open for 51% -> 0% of each run, Pallas kernels for 0% -> 32%
where the time goes in v1:
time: 103 us
  starting transfers between devices  45.8 us (44%)
  Pallas kernels  41.8 us (41%)
  waiting for transfers between devices  9.64 us (9%)
  local copies, waits for them, and re-layouts  5.3 us (5%)
    pallas_call x1, Pallas kernels, far_leaf(): pl.pallas_call(far_leaf_kernel, in_specs=[SMEM, VMEM, VMEM], out_specs=VM...  21.2 us
    ppermute x1, starting transfers between devices, body(): after = lax.ppermute(first, every, down)  12.1 us
    pallas_call x2, Pallas kernels, near_part(): pl.pallas_call(functools.partial(near_kernel, lo, hi), in_specs=[SMEM] +...  11.1 us
    all_to_all x1, starting transfers between devices, body(): got0 = lax.all_to_all(m0, 'z', 0, 0, tiled=True)  9.14 us
    all_to_all x1, starting transfers between devices, body(): got1 = lax.all_to_all(m1, 'y', 0, 0, tiled=True)  7.65 us
    all_to_all x1, waiting for transfers between devices, body(): gotr = lax.all_to_all(part, 'z', 0, 0, tiled=True)  7.33 us
    all_to_all x1, starting transfers between devices, body(): gotg = lax.all_to_all(cells, 'g', 0, 0, tiled=True)  7.24 us
    all_to_all x1, starting transfers between devices, body(): gotr = lax.all_to_all(part, 'z', 0, 0, tiled=True)  5.71 us
  transfers between devices with their start and end apart: 6, of which 2 were waited for; matrix products, arithmetic and copies ran while one was open for 0% of the time, Pallas kernels for 32%

profile of v1, /device:TPU:1, one launch (start us, length us, event | category | flops | bytes accessed | tf_op | source)
XLA Modules:
  0.0 102.7 jit_solution(16770963037351618836)
XLA Ops:
  0.0 0.8 reshape.5.llist
  0.8 0.0 copy-done.7
  0.8 0.7 copy.11.skel
  1.5 0.0 copy-done.6
  1.6 0.6 copy-done.8
  2.2 0.0 copy-done.4
  2.2 1.2 %copy-done = f32[8,128,256]{2,1,0:T(8,128)S(1)} copy-done((f32[8,128,256]{2,1,0:T(8,128)S(1)}, f32[8,128,256]{2,1,0:T(8,128)}, u32[]{:S(2)}) %copy-start) | copy-done | bytes 1048600
  3.4 1.0 %copy-done.2 = f32[8,128,128]{2,1,0:T(8,128)S(1)} copy-done((f32[8,128,128]{2,1,0:T(8,128)S(1)}, f32[8,128,128]{2,1,0:T(8,128)}, u32[]{:S(2)}) %copy-start.2) | copy-done | bytes 524312
  4.5 2.8 %pack.1 = (f32[8,104,128]{2,1,0:T(8,128)}, f32[8,32,128]{2,1,0:T(8,128)}, f32[48,256]{1,0:T(8,128)S(1)}, f32[48,256]{1,0:T(8,128)S(1)}) custom-call(f32[8,3,256]{2,1,0:T(4,128)S(1)} %copy.10.pts, f32[8,8,256]{2,1,0:T(8,128)S(1)} %copy-done.4, f32[8,128,256]{2,1,0:T(8,128)S(1)} %copy-done, f32[8,3,128]{2,1,0:T(4,128)S(1)} %copy.11.skel, ...), custom_call_target="tpu_custom_call" | custom-call | tf_op jit(solution)/shard_map/pack/pallas_call | solution.py:126
  7.3 7.7 %all-to-all-start.1 = ((f32[8,104,128]{2,1,0:T(8,128)}), f32[8,104,128]{2,1,0:T(8,128)S(1)}, u32[]{:S(2)}, u32[]{:S(2)}) async-start(f32[8,104,128]{2,1,0:T(8,128)} %get-tuple-element.14), calls=%async_computation.1 | async-start | bytes 851968 | tf_op jit(solution)/shard_map/all_to_all | solution.py:302
  15.0 4.0 %collective-permute-start = (f32[48,256]{1,0:T(8,128)S(1)}, f32[48,256]{1,0:T(8,128)S(1)}, u32[]{:S(2)}, u32[]{:S(2)}) collective-permute-start(f32[48,256]{1,0:T(8,128)S(1)} %get-tuple-element.15), channel_id=1, source_target_pairs={{0,1},{1,2},{2,3},{3,4},{4,5},{5,6},{6,7},{7,8},{8,9},{9,10},{10,1... | collective-permute-start | bytes 147464 | tf_op jit(solution)/shard_map/ppermute | solution.py:304
  19.0 12.1 %collective-permute-start.1 = (f32[48,256]{1,0:T(8,128)S(1)}, f32[48,256]{1,0:T(8,128)S(1)}, u32[]{:S(2)}, u32[]{:S(2)}) collective-permute-start(f32[48,256]{1,0:T(8,128)S(1)} %get-tuple-element.16), channel_id=1, source_target_pairs={{1,0},{2,1},{3,2},{4,3},{5,4},{6,5},{7,6},{8,7},{9,8},{10,9},{11,1... | collective-permute-start | bytes 147464 | tf_op jit(solution)/shard_map/ppermute | solution.py:305
  31.1 0.0 all-to-all-done.1.src
  31.1 0.0 copy-start.5
  31.1 9.1 %all-to-all-start = ((f32[8,32,128]{2,1,0:T(8,128)}), f32[8,32,128]{2,1,0:T(8,128)S(1)}, u32[]{:S(2)}, u32[]{:S(2)}) async-start(f32[8,32,128]{2,1,0:T(8,128)} %get-tuple-element.13), calls=%async_computation | async-start | bytes 262144 | tf_op jit(solution)/shard_map/all_to_all | solution.py:303
  40.2 0.0 collective-permute-done.before
  40.2 0.0 collective-permute-done.1.after
  40.3 0.0 copy-done.5
  40.3 5.6 %near.2.near1 = f32[4,8,256]{2,1,0:T(8,128)S(1)} custom-call(s32[8,9]{1,0:T(8,128)S(1)} %copy-done.5, f32[8,3,256]{2,1,0:T(4,128)S(1)} %copy.10.pts, f32[8,8,256]{2,1,0:T(8,128)S(1)} %copy-done.4, f32[48,256]{1,0:T(8,128)S(1)} %collective-permute-done.before, f32[48,256]{1,0:T(8,128)S(1)} %collective-permute-done.1.after), custom_call_target="tpu_custom_call" | custom-call | flops 2359296000 | bytes 300000 | tf_op jit(solution)/shard_map/near/pallas_call | solution.py:171
  45.9 2.3 %all-to-all-done.tgt = f32[8,32,128]{2,1,0:T(8,128)S(1)} async-done(((f32[8,32,128]{2,1,0:T(8,128)}), f32[8,32,128]{2,1,0:T(8,128)S(1)}, u32[]{:S(2)}, u32[]{:S(2)}) %all-to-all-start) | async-done | bytes 131104 | tf_op jit(solution)/shard_map/all_to_all | solution.py:303
  48.2 0.8 broadcast_in_dim.8
  49.0 7.2 %all-to-all-start.2 = ((f32[8,128,128]{2,1,0:T(8,128)}), f32[8,128,128]{2,1,0:T(8,128)S(1)}, u32[]{:S(2)}, u32[]{:S(2)}) async-start(f32[8,128,128]{2,1,0:T(8,128)} %broadcast_in_dim.8), calls=%async_computation.2 | async-start | bytes 1048576 | tf_op jit(solution)/shard_map/all_to_all | solution.py:309
  56.3 21.2 %far_leaf.1.part = f32[8,9,8,128]{3,2,1,0:T(8,128)S(1)} custom-call(s32[8,2,128]{2,1,0:T(2,128)S(1)} %slice_convert_fusion.req, f32[8,104,128]{2,1,0:T(8,128)S(1)} %all-to-all-done.1.src, f32[8,32,128]{2,1,0:T(8,128)S(1)} %all-to-all-done.tgt), custom_call_target="tpu_custom_call" | custom-call | flops 2097152000 | bytes 900000 | tf_op jit(solution)/shard_map/far_leaf/pallas_call | solution.py:219
  77.5 0.0 all-to-all-done.2.src
  77.5 4.8 %far_top.1 = f32[8,9,8,128]{3,2,1,0:T(8,128)} custom-call(s32[8,2,128]{2,1,0:T(2,128)S(1)} %slice_convert_fusion.req, f32[8,128,128]{2,1,0:T(8,128)S(1)} %all-to-all-done.2.src, f32[8,32,128]{2,1,0:T(8,128)S(1)} %all-to-all-done.tgt, f32[8,9,8,128]{3,2,1,0:T(8,128)S(1)} %far_leaf.1.part), custom_call_target="tpu_custom_call" | custom-call | tf_op jit(solution)/shard_map/far_top/pallas_call | solution.py:261
  82.3 5.7 %all-to-all-start.3 = ((f32[8,9,8,128]{3,2,1,0:T(8,128)}), f32[8,9,8,128]{3,2,1,0:T(8,128)S(1)}, u32[]{:S(2)}, u32[]{:S(2)}) async-start(f32[8,9,8,128]{3,2,1,0:T(8,128)} %far_top.1), calls=%async_computation.3 | async-start | bytes 589824 | tf_op jit(solution)/shard_map/all_to_all | solution.py:314
  88.0 0.0 copy-start.3
  88.1 5.6 %near.3.near2 = f32[4,8,256]{2,1,0:T(8,128)S(1)} custom-call(s32[8,9]{1,0:T(8,128)S(1)} %copy-done.5, f32[8,3,256]{2,1,0:T(4,128)S(1)} %copy.10.pts, f32[8,8,256]{2,1,0:T(8,128)S(1)} %copy-done.4, f32[48,256]{1,0:T(8,128)S(1)} %collective-permute-done.before, f32[48,256]{1,0:T(8,128)S(1)} %collective-permute-done.1.after), custom_call_target="tpu_custom_call" | custom-call | flops 2359296000 | bytes 300000 | tf_op jit(solution)/shard_map/near/pallas_call | solution.py:171
  93.6 7.3 %all-to-all-done.3.got = f32[8,9,8,128]{3,2,1,0:T(8,128)S(1)} async-done(((f32[8,9,8,128]{3,2,1,0:T(8,128)}), f32[8,9,8,128]{3,2,1,0:T(8,128)S(1)}, u32[]{:S(2)}, u32[]{:S(2)}) %all-to-all-start.3) | async-done | bytes 294944 | tf_op jit(solution)/shard_map/all_to_all | solution.py:314
  101.0 0.0 copy-done.1
  101.0 0.0 copy-done.3
  101.0 1.8 %final.1 = f32[8,8,256]{2,1,0:T(8,128)} custom-call(f32[8,9,8,128]{3,2,1,0:T(8,128)S(1)} %all-to-all-done.3.got, f32[8,128,128]{2,1,0:T(8,128)S(1)} %copy-done.3, f32[8,128,256]{2,1,0:T(8,128)S(1)} %copy-done.1, f32[4,8,256]{2,1,0:T(8,128)S(1)} %near.2.near1, f32[4,8,256]{2,1,0:T(8,128)S(1)} %near.3.near2), custom_call_target="tpu_custom_call" | custom-call | tf_op jit(solution)/shard_map/final/pallas_call | solution.py:284
  (12 shorter events, 0.1 us)
Async XLA Ops:
  0.0 0.8 copy-start.7
  0.0 1.5 %copy-start.6 = (f32[8,3,256]{2,0,1:T(8,128)S(1)}, f32[8,3,256]{2,0,1:T(8,128)}, u32[]{:S(2)}) copy-start(f32[8,3,256]{2,0,1:T(8,128)} %param.9) | copy-start | bytes 73732
  0.0 2.2 %copy-start.4 = (f32[8,8,256]{2,1,0:T(8,128)S(1)}, f32[8,8,256]{2,1,0:T(8,128)}, u32[]{:S(2)}) copy-start(f32[8,8,256]{2,1,0:T(8,128)} %chg.4) | copy-start | bytes 196612
  1.5 0.7 copy-start.8
  2.2 1.2 %copy-start = (f32[8,128,256]{2,1,0:T(8,128)S(1)}, f32[8,128,256]{2,1,0:T(8,128)}, u32[]{:S(2)}) copy-start(f32[8,128,256]{2,1,0:T(8,128)} %up.3) | copy-start | bytes 3145732
  3.4 1.0 %copy-start.2 = (f32[8,128,128]{2,1,0:T(8,128)S(1)}, f32[8,128,128]{2,1,0:T(8,128)}, u32[]{:S(2)}) copy-start(f32[8,128,128]{2,1,0:T(8,128)} %utm.3) | copy-start | bytes 1572868
  7.3 23.8 %all-to-all-start.1 = ((f32[8,104,128]{2,1,0:T(8,128)}), f32[8,104,128]{2,1,0:T(8,128)S(1)}, u32[]{:S(2)}, u32[]{:S(2)}) async-start(f32[8,104,128]{2,1,0:T(8,128)} %get-tuple-element.14), calls=%async_computation.1 | async-start | bytes 851968 | tf_op jit(solution)/shard_map/all_to_all | solution.py:302
  15.0 25.3 %collective-permute-start = (f32[48,256]{1,0:T(8,128)S(1)}, f32[48,256]{1,0:T(8,128)S(1)}, u32[]{:S(2)}, u32[]{:S(2)}) collective-permute-start(f32[48,256]{1,0:T(8,128)S(1)} %get-tuple-element.15), channel_id=1, source_target_pairs={{0,1},{1,2},{2,3},{3,4},{4,5},{5,6},{6,7},{7,8},{8,9},{9,10},{10,1... | collective-permute-start | bytes 147464 | tf_op jit(solution)/shard_map/ppermute | solution.py:304
  19.0 21.3 %collective-permute-start.1 = (f32[48,256]{1,0:T(8,128)S(1)}, f32[48,256]{1,0:T(8,128)S(1)}, u32[]{:S(2)}, u32[]{:S(2)}) collective-permute-start(f32[48,256]{1,0:T(8,128)S(1)} %get-tuple-element.16), channel_id=1, source_target_pairs={{1,0},{2,1},{3,2},{4,3},{5,4},{6,5},{7,6},{8,7},{9,8},{10,9},{11,1... | collective-permute-start | bytes 147464 | tf_op jit(solution)/shard_map/ppermute | solution.py:305
  31.1 9.2 %copy-start.5 = (s32[8,9]{1,0:T(8,128)S(1)}, s32[8,9]{1,0:T(8,128)}, u32[]{:S(2)}) copy-start(s32[8,9]{1,0:T(8,128)} %ids.3) | copy-start | bytes 868
  31.1 17.1 %all-to-all-start = ((f32[8,32,128]{2,1,0:T(8,128)}), f32[8,32,128]{2,1,0:T(8,128)S(1)}, u32[]{:S(2)}, u32[]{:S(2)}) async-start(f32[8,32,128]{2,1,0:T(8,128)} %get-tuple-element.13), calls=%async_computation | async-start | bytes 262144 | tf_op jit(solution)/shard_map/all_to_all | solution.py:303
  49.0 28.5 %all-to-all-start.2 = ((f32[8,128,128]{2,1,0:T(8,128)}), f32[8,128,128]{2,1,0:T(8,128)S(1)}, u32[]{:S(2)}, u32[]{:S(2)}) async-start(f32[8,128,128]{2,1,0:T(8,128)} %broadcast_in_dim.8), calls=%async_computation.2 | async-start | bytes 1048576 | tf_op jit(solution)/shard_map/all_to_all | solution.py:309
  82.3 18.6 %all-to-all-start.3 = ((f32[8,9,8,128]{3,2,1,0:T(8,128)}), f32[8,9,8,128]{3,2,1,0:T(8,128)S(1)}, u32[]{:S(2)}, u32[]{:S(2)}) async-start(f32[8,9,8,128]{3,2,1,0:T(8,128)} %far_top.1), calls=%async_computation.3 | async-start | bytes 589824 | tf_op jit(solution)/shard_map/all_to_all | solution.py:314
  88.0 12.9 %copy-start.1 = (f32[8,128,256]{2,1,0:T(8,128)S(1)}, f32[8,128,256]{2,1,0:T(8,128)}, u32[]{:S(2)}) copy-start(f32[8,128,256]{2,1,0:T(8,128)} %up.3) | copy-start | bytes 3145732
  88.0 12.9 %copy-start.3 = (f32[8,128,128]{2,1,0:T(8,128)S(1)}, f32[8,128,128]{2,1,0:T(8,128)}, u32[]{:S(2)}) copy-start(f32[8,128,128]{2,1,0:T(8,128)} %utm.3) | copy-start | bytes 1572868

commit v2 on v1

v2 whole, which is shorter than its diff:
```python
import functools
import math

import jax
import jax.numpy as jnp
from jax import lax
from jax.experimental import pallas as pl
from jax.experimental.pallas import tpu as pltpu
from jax.sharding import Mesh, PartitionSpec as P

F32 = jnp.float32
BF16 = jnp.bfloat16
KAPPA = math.sqrt(3.0) * math.log2(math.e)
LN2 = math.log(2.0)
CENTER = 1.5
FEAT = 32
REACH = 4
OWN = 8
NBR = 9
PAIRS = 8
DUMMY = 64
EXACT = lax.Precision.HIGHEST

SMEM = pl.BlockSpec(memory_space=pltpu.SMEM)
VMEM = pl.BlockSpec(memory_space=pltpu.VMEM)
PARAMS = pltpu.CompilerParams(vmem_limit_bytes=40 << 20)


def split2(x):
    a = x.astype(BF16).astype(F32)
    return a, (x - a).astype(BF16).astype(F32)


def split3(x):
    a = x.astype(BF16).astype(F32)
    b, c = split2(x - a)
    return a, b, c


def dense_features(xyz):
    parts = [split2((x - CENTER) * KAPPA) for x in xyz]
    n = None
    for a, b in parts:
        r = a + b
        n = r * r if n is None else n + r * r
    n1, n2, n3 = split3(n)
    one = jnp.ones_like(n)
    zero = jnp.zeros_like(n)
    high = [a for a, _ in parts]
    low = [b for _, b in parts]
    high2 = [-2.0 * a for a in high]
    low2 = [-2.0 * b for b in low]
    s0 = high + [n1, n2, n3, one, one]
    s1 = low + [one, zero, zero, zero, zero]
    t0 = high2 + [one, one, one, n1, n2]
    t1 = low2 + [zero] * 5
    t2 = high2 + [n3] + [zero] * 4
    return s0, s1, t0, t1, t2


def spread(rows, tmp):
    n, width = rows[0].shape
    halves = width // 128
    for r, v in enumerate(rows):
        for h in range(halves):
            tmp[h, n * r : n * r + n, :] = v[:, 128 * h : 128 * h + 128]

    def load(leaf):
        return jnp.concatenate([tmp[h, pl.ds(leaf, 8, stride=n), :] for h in range(halves)], 1)

    return load


def two_halves(vals):
    v = vals * LN2
    high = v.astype(BF16).astype(F32)
    return jnp.concatenate([high, v - high], 0).astype(BF16)


def matern_over_ln2(t):
    m = jnp.maximum(t, 1e-12)
    s = m * lax.rsqrt(m)
    return (s + 1.0 / LN2) * jnp.exp2(-s)


def product(src_feat, tgt_feat, vals):
    t = jnp.dot(src_feat, tgt_feat, preferred_element_type=F32)
    k = matern_over_ln2(t)
    high = k.astype(BF16)
    low = (k - high.astype(F32)).astype(BF16)
    return jnp.dot(vals, high, preferred_element_type=F32) + jnp.dot(vals, low, preferred_element_type=F32)


def nt(a, b):
    return lax.dot_general(a, b, (((1,), (1,)), ((), ())), precision=EXACT, preferred_element_type=F32)


def request_kernel(pts, chg, skel, cpts, llist, tlist, m0, first, last, row16):
    lane = lax.broadcasted_iota(jnp.int32, (1, 128), 1)
    sub8 = lax.broadcasted_iota(jnp.int32, (8, 128), 0)
    lane8 = lax.broadcasted_iota(jnp.int32, (8, 128), 1)
    row = lax.broadcasted_iota(jnp.int32, (128, 128), 0)
    col = lax.broadcasted_iota(jnp.int32, (128, 128), 1)
    before = (row < col).astype(F32).astype(BF16)
    pick = (lax.broadcasted_iota(jnp.int32, (16, 128), 0) == (lax.broadcasted_iota(jnp.int32, (16, 128), 1) & 15))
    pick = pick.astype(F32).astype(BF16)
    ll = llist[...]
    mine = sub8 == (lane8 >> 4)

    def flat(v):
        w = jnp.dot(v.astype(F32).astype(BF16), pick, preferred_element_type=F32)
        return jnp.sum(jnp.where(mine, w, 0.0), axis=0, keepdims=True).astype(jnp.int32)

    upper = flat(ll >> 6)
    lower = flat(ll & 63)
    row16[...] = jnp.zeros((8, 128), jnp.int32)
    row16[0:1, 0:16] = tlist[...]
    tl = row16[0:1, :]
    leaf_hit = (lower >> 3) == sub8
    top_hit = ((tl & 7) == sub8) & (lane < 16)
    leaf_one = leaf_hit.astype(F32)
    top_one = top_hit.astype(F32)
    leaf_pos = jnp.dot(leaf_one.astype(BF16), before, preferred_element_type=F32)
    top_pos = jnp.dot(top_one.astype(BF16), before, preferred_element_type=F32) + 16.0
    leaf_n = jnp.sum(leaf_one, axis=1, keepdims=True)
    top_n = jnp.sum(top_one, axis=1, keepdims=True)
    leaf_pos = jnp.where(leaf_hit, leaf_pos, -1.0)
    top_pos = jnp.where(top_hit, top_pos, -1.0)
    local = (lower & 7) + (upper & 7) * 8
    codes = jnp.where(sub8 == 0, lane >> 4, jnp.where(sub8 == 1, local, 0)).astype(F32).astype(BF16)
    tcodes = jnp.where(sub8 == 0, tl >> 3, 0).astype(F32).astype(BF16)
    rowf = row.astype(F32)
    for d in range(8):
        for c in range(3):
            m0[d, 8 * c : 8 * c + 8, :] = skel[c]
            m0[d, 24 + c : 25 + c, :] = cpts[c]
        m0[d, 29:32, :] = jnp.zeros((3, 128), F32)
        oh = (leaf_pos[d : d + 1] == rowf).astype(F32).astype(BF16)
        got = lax.dot_general(codes, oh, (((1,), (1,)), ((), ())), preferred_element_type=F32)
        m0[d, 27:28, :] = got[0:1] * 128.0 + got[1:2]
        oh = (top_pos[d : d + 1] == rowf).astype(F32).astype(BF16)
        got = lax.dot_general(tcodes, oh, (((1,), (1,)), ((), ())), preferred_element_type=F32)[0:1]
        got = got + jnp.where(lane == 0, leaf_n[d : d + 1], 0.0) + jnp.where(lane == 1, top_n[d : d + 1], 0.0)
        m0[d, 28:29, :] = got
    for slab, start in ((first, 0), (last, OWN - REACH)):
        for i in range(REACH):
            slab[8 * i : 8 * i + 8, :] = chg[start + i]
        for c in range(3):
            slab[32 + 4 * c : 36 + 4 * c, :] = pts[c, start : start + REACH, :]
        slab[44:48, :] = jnp.zeros((4, 256), F32)


def request(pts, chg, skel, cpts, llist, tlist):
    sd = jax.ShapeDtypeStruct
    return pl.pallas_call(
        request_kernel,
        in_specs=[VMEM] * 6,
        out_specs=[VMEM] * 3,
        out_shape=[sd((8, 32, 128), F32), sd((48, 256), F32), sd((48, 256), F32)],
        scratch_shapes=[pltpu.VMEM((8, 128), jnp.int32)],
        compiler_params=PARAMS,
        name="request",
    )(pts, chg, skel, cpts, llist, tlist)


def weights_kernel(chg, up, skel, utm, cpts, m1):
    for l in range(OWN):
        w = nt(chg[l], up[l])
        cw = nt(w, utm[l])
        total = cw if l == 0 else total + cw
        for d in range(8):
            m1[d, 8 * l : 8 * l + 8, :] = w
    for d in range(8):
        m1[d, 88:96, :] = total
        for c in range(3):
            m1[d, 64 + 8 * c : 72 + 8 * c, :] = skel[c]
            m1[d, 96 + c : 97 + c, :] = cpts[c]
        m1[d, 99:104, :] = jnp.zeros((5, 128), F32)


def weights(chg, up, skel, utm, cpts):
    return pl.pallas_call(
        weights_kernel,
        in_specs=[VMEM] * 5,
        out_specs=VMEM,
        out_shape=jax.ShapeDtypeStruct((8, 104, 128), F32),
        compiler_params=PARAMS,
        name="weights",
    )(chg, up, skel, utm, cpts)


def near_kernel(lo, hi, ids, pts, chg, before, after, out, fs, ft, vals, xyz, ts, tl):
    me = (lax.axis_index("g") * lax.axis_size("y") + lax.axis_index("y")) * lax.axis_size("z") + lax.axis_index("z")
    base = me * OWN - REACH
    for c in range(3):
        xyz[c, 0:4, :] = before[32 + 4 * c : 36 + 4 * c, :]
        xyz[c, 4:12, :] = pts[c]
        xyz[c, 12:16, :] = after[32 + 4 * c : 36 + 4 * c, :]
    s0, s1, t0, t1, t2 = dense_features([xyz[0], xyz[1], xyz[2]])
    s0 = spread(s0, ts)
    s1 = spread(s1, tl)
    for e in range(lo, hi + 2 * REACH):
        a, b = s0(e), s1(e)
        fs[e - lo] = jnp.concatenate([a, b, a, b], 0).T.astype(BF16)
        if e < REACH:
            c = before[8 * e : 8 * e + 8, :]
        elif e < REACH + OWN:
            c = chg[e - REACH]
        else:
            c = after[8 * (e - REACH - OWN) : 8 * (e - REACH - OWN) + 8, :]
        vals[e - lo] = two_halves(c)
    for i, rows in enumerate((t0, t2, t1, t1)):
        load = spread(rows, ts)
        for e in range(lo + REACH, hi + REACH):
            ft[e - REACH - lo, 8 * i : 8 * i + 8, :] = load(e)
    dead = hi - lo + 2 * REACH
    vals[dead] = jnp.zeros((16, 256), BF16)

    def leaf(i, carry):
        tgt = ft[i].astype(BF16)
        acc = jnp.zeros((16, 256), F32)
        for n in range(NBR):
            ident = ids[i + lo, n]
            live = ident >= 0
            e = jnp.where(live, ident - base - lo, 0)
            acc = acc + product(fs[e], tgt, vals[jnp.where(live, e, dead)])
        out[i] = acc[0:8] + acc[8:16]
        return carry

    lax.fori_loop(0, hi - lo, leaf, 0)


def near_part(lo, hi, ids, pts, chg, before, after):
    n = hi - lo
    return pl.pallas_call(
        functools.partial(near_kernel, lo, hi),
        in_specs=[SMEM] + [VMEM] * 4,
        out_specs=VMEM,
        out_shape=jax.ShapeDtypeStruct((n, 8, 256), F32),
        scratch_shapes=[
            pltpu.VMEM((n + 8, 256, FEAT), BF16),
            pltpu.VMEM((n, FEAT, 256), F32),
            pltpu.VMEM((n + 9, 16, 256), BF16),
            pltpu.VMEM((3, 16, 256), F32),
            pltpu.VMEM((2, 128, 128), F32),
            pltpu.VMEM((2, 128, 128), F32),
        ],
        cost_estimate=pl.CostEstimate(flops=n * 9 * 65536000, bytes_accessed=300000, transcendentals=n * 9 * 131072),
        compiler_params=PARAMS,
        name="near",
    )(ids, pts, chg, before, after)


def prepare_sources(i, xyz, t0, t1, even, odd):
    s0, s1, _, _, _ = dense_features(xyz)
    s0 = spread(s0, t0)
    s1 = spread(s1, t1)
    rows = []
    for l in range(8):
        a, b = s0(l), s1(l)
        rows.append(jnp.concatenate([a, b, a, b], 0))
    zero = jnp.zeros((64, 128), F32)
    left = lax.broadcasted_iota(jnp.int32, (128, 128), 1) < FEAT
    for l in range(0, 8, 2):
        for a, b in ((l, l + 1), (l + 1, l)):
            both = jnp.concatenate([rows[a], rows[b], zero], 0).T
            even[8 * i + a] = jnp.where(left, both, 0.0).astype(BF16)[:, 0:64]
            odd[8 * i + b] = jnp.where(left, 0.0, both).astype(BF16)[:, 0:64]


def prepare_targets(i, xyz, tmp, ft):
    _, _, t0, t1, t2 = dense_features(xyz)
    for j, rows in enumerate((t0, t2, t1, t1)):
        load = spread(rows, tmp.at[j])
        for l in range(8):
            ft[8 * i + l, 8 * j : 8 * j + 8, :] = load(l)


def flatten(req, flat, row, start, slot):
    off = 0
    for d in range(8):
        n = req[d, 1, slot]

        def copy(j, carry, d=d, off=off):
            for u in range(8):
                flat[off + j * 8 + u] = req[d, row, start + j * 8 + u] + d * (1024 if row == 0 else 128)
            return carry

        lax.fori_loop(0, (n + 7) // 8, copy, 0)
        off = off + n
    for u in range(2 * PAIRS):
        flat[off + u] = DUMMY
    return off


def interact(total, flat, even, odd, ft, vals, add):
    zero = jnp.zeros((FEAT, 128), BF16)

    def chunk(i, carry):
        for u in range(PAIRS):
            ca = flat[i * (2 * PAIRS) + 2 * u]
            cb = flat[i * (2 * PAIRS) + 2 * u + 1]
            ta, sa = ca >> 7, ca & 127
            tb, sb = cb >> 7, cb & 127
            fa = ft[ta].astype(BF16)
            fb = ft[tb].astype(BF16)
            tgt = jnp.concatenate([jnp.concatenate([fa, zero], 1), jnp.concatenate([zero, fb], 1)], 0)
            r = product(even[sa] + odd[sb], tgt, jnp.concatenate([vals[sa], vals[sb]], 0))
            add(ta, r[0:8, 0:128] + r[8:16, 0:128])
            add(tb, r[16:24, 128:256] + r[24:32, 128:256])
        return carry

    lax.fori_loop(0, (total + 2 * PAIRS - 1) // (2 * PAIRS), chunk, 0)


def clear_dummy(even, odd, vals):
    even[DUMMY] = jnp.zeros((128, 64), BF16)
    odd[DUMMY] = jnp.zeros((128, 64), BF16)
    vals[DUMMY] = jnp.zeros((16, 128), BF16)


def far_leaf_kernel(req, src, tgt, out, flat, even, odd, ft, vals, t0, t1, t2):
    for y in range(8):
        prepare_sources(y, [src[y, 64 + 8 * c : 72 + 8 * c, :] for c in range(3)], t0.at[y], t1.at[y], even, odd)
        prepare_targets(y, [tgt[32 * y + 8 * c : 32 * y + 8 * c + 8, :] for c in range(3)], t2.at[y], ft)
        for l in range(OWN):
            vals[8 * y + l] = two_halves(src[y, 8 * l : 8 * l + 8, :])
    clear_dummy(even, odd, vals)
    out[...] = jnp.zeros_like(out)
    total = flatten(req, flat, 0, 0, 0)

    def add(t, v):
        out[t >> 3, t & 7] += v

    interact(total, flat, even, odd, ft, vals, add)


FAR_SCRATCH = [
    pltpu.SMEM((1024 + 64,), jnp.int32),
    pltpu.VMEM((65, 128, 64), BF16),
    pltpu.VMEM((65, 128, 64), BF16),
    pltpu.VMEM((64, FEAT, 128), F32),
    pltpu.VMEM((65, 16, 128), BF16),
    pltpu.VMEM((8, 1, 64, 128), F32),
    pltpu.VMEM((8, 1, 64, 128), F32),
    pltpu.VMEM((8, 4, 1, 64, 128), F32),
]


def far_leaf(req, src, tgt):
    return pl.pallas_call(
        far_leaf_kernel,
        in_specs=[SMEM, VMEM, VMEM],
        out_specs=VMEM,
        out_shape=jax.ShapeDtypeStruct((8, 9, 8, 128), F32),
        scratch_shapes=FAR_SCRATCH,
        cost_estimate=pl.CostEstimate(flops=2097152000, bytes_accessed=900000, transcendentals=4194304),
        compiler_params=PARAMS,
        name="far_leaf",
    )(req, src, tgt.reshape(256, 128))


def far_top_kernel(req, src, tgt, part, out, flat, even, odd, ft, vals, t0, t1, t2):
    for g in range(8):
        xyz = [src[pl.ds(128 * g + 8 + c, 8, stride=16), :] for c in range(3)]
        prepare_sources(g, xyz, t0.at[g], t1.at[g], even, odd)
        for y in range(8):
            vals[8 * g + y] = two_halves(src[128 * g + 16 * y : 128 * g + 16 * y + 8, :])
    prepare_targets(0, [tgt[pl.ds(24 + c, 8, stride=32), :] for c in range(3)], t2.at[0], ft)
    clear_dummy(even, odd, vals)
    out[...] = part[...]
    total = flatten(req, flat, 1, 16, 1)

    def add(t, v):
        out[t, 8] += v

    interact(total, flat, even, odd, ft, vals, add)


def far_top(req, src, tgt, part):
    return pl.pallas_call(
        far_top_kernel,
        in_specs=[SMEM, VMEM, VMEM, VMEM],
        out_specs=VMEM,
        out_shape=jax.ShapeDtypeStruct((8, 9, 8, 128), F32),
        scratch_shapes=FAR_SCRATCH,
        compiler_params=PARAMS,
        name="far_top",
    )(req, src.reshape(1024, 128), tgt.reshape(256, 128), part)


def final_kernel(got, utm, up, near1, near2, out):
    tot = got[0]
    for d in range(1, 8):
        tot = tot + got[d]
    cell = tot[8]
    half = near1.shape[0]
    for l in range(OWN):
        incoming = tot[l] + jnp.dot(cell, utm[l], precision=EXACT, preferred_element_type=F32)
        near = near1[l] if l < half else near2[l - half]
        out[l] = near + jnp.dot(incoming, up[l], precision=EXACT, preferred_element_type=F32)


def final(got, utm, up, near1, near2):
    return pl.pallas_call(
        final_kernel,
        in_specs=[VMEM] * 5,
        out_specs=VMEM,
        out_shape=jax.ShapeDtypeStruct((8, 8, 256), F32),
        compiler_params=PARAMS,
        name="final",
    )(got, utm, up, near1, near2)


def body(points, charges, up_op, skel_pts, utm, cell_pts, near_list, leaf_list, top_list):
    every = ("g", "y", "z")
    pts = jnp.transpose(points, (1, 0, 2))
    skel = jnp.transpose(skel_pts, (1, 0, 2))
    cpts = jnp.transpose(cell_pts, (1, 0, 2))
    count = lax.axis_size("g") * lax.axis_size("y") * lax.axis_size("z")
    up = [(i, i + 1) for i in range(count - 1)]
    down = [(i + 1, i) for i in range(count - 1)]
    m0, first, last = request(pts, charges, skel, cpts, leaf_list, top_list)
    got0 = lax.all_to_all(m0, "z", 0, 0, tiled=True)
    before = lax.ppermute(last, every, up)
    after = lax.ppermute(first, every, down)
    m1 = weights(charges, up_op, skel, utm, cpts)
    m1, got0 = lax.optimization_barrier((m1, got0))
    got1 = lax.all_to_all(m1, "y", 0, 0, tiled=True)
    req = got0[:, 27:29, :].astype(jnp.int32)
    near1 = near_part(0, 4, near_list, pts, charges, before, after)
    got1, near1 = lax.optimization_barrier((got1, near1))
    cells = jnp.broadcast_to(got1[:, 88:104, :].reshape(1, 128, 128), (8, 128, 128))
    gotg = lax.all_to_all(cells, "g", 0, 0, tiled=True)
    part = far_leaf(req, got1, got0)
    part = far_top(req, gotg, got0, part)
    part, charges2 = lax.optimization_barrier((part, charges))
    gotr = lax.all_to_all(part, "z", 0, 0, tiled=True)
    near2 = near_part(4, 8, near_list, pts, charges2, before, after)
    return final(gotr, utm, up_op, near1, near2)


def solution(mesh):
    fine = Mesh(mesh.devices.reshape(mesh.shape["group"], 8, 8), ("g", "y", "z"))
    row = ("g", "y", "z")
    specs = tuple(P(row, *([None] * k)) for k in (2, 2, 2, 2, 2, 2, 1, 1, 1))
    return jax.shard_map(body, mesh=fine, in_specs=specs, out_specs=P(row, None, None), check_vma=False)
```

time: 103 us -> 90 us (0.87)
  the two profiles are of different devices: /device:TPU:1 before, /device:TPU:25 now
where the time goes in v2:
time: 90 us; the launch traced here: 89.1 us
  starting transfers between devices  37.9 us (42%)
  Pallas kernels  29.2 us (32%)
  waiting for transfers between devices  15.1 us (17%)
  local copies, waits for them, and re-layouts  6.78 us (8%)
    pallas_call x2, Pallas kernels, near_part(): pl.pallas_call(functools.partial(near_kernel, lo, hi), in_specs=[SMEM] +...  11.2 us
    all_to_all x1, starting transfers between devices, body(): got0 = lax.all_to_all(m0, 'z', 0, 0, tiled=True)  10.2 us
    pallas_call x1, Pallas kernels, far_leaf(): pl.pallas_call(far_leaf_kernel, in_specs=[SMEM, VMEM, VMEM], out_specs=VM...  7.93 us
    all_to_all x1, starting transfers between devices, body(): gotr = lax.all_to_all(part, 'z', 0, 0, tiled=True)  7.84 us
    all_to_all x1, waiting for transfers between devices, body(): gotr = lax.all_to_all(part, 'z', 0, 0, tiled=True)  7.46 us
    all_to_all x1, starting transfers between devices, body(): got1 = lax.all_to_all(m1, 'y', 0, 0, tiled=True)  6.76 us
    unnamed x28, local copies, waits for them, and re-layouts  5.92 us
    all_to_all x1, starting transfers between devices, body(): gotg = lax.all_to_all(cells, 'g', 0, 0, tiled=True)  5.8 us
  transfers between devices with their start and end apart: 6, of which 4 were waited for; matrix products, arithmetic and copies ran while one was open for 0% of the time, Pallas kernels for 25%

profile of v2, /device:TPU:25, one launch (start us, length us, event | category | flops | bytes accessed | tf_op | source)
XLA Modules:
  0.0 89.1 jit_solution(6880881214605636976)
XLA Ops:
  0.0 0.7 copy-done.11
  0.7 0.0 copy-done.10
  0.7 0.8 copy-done.4
  1.5 0.7 copy-done.6
  2.2 0.7 copy-done.8
  3.0 0.7 copy-done.12
  3.6 1.3 %request.1 = (f32[8,32,128]{2,1,0:T(8,128)}, f32[48,256]{1,0:T(8,128)S(1)}, f32[48,256]{1,0:T(8,128)S(1)}) custom-call(f32[3,8,256]{2,1,0:T(8,128)S(1)} %bitcast.11, f32[8,8,256]{2,1,0:T(8,128)S(1)} %copy-done.4, f32[3,8,128]{2,1,0:T(8,128)S(1)} %bitcast.9, f32[3,1,128]{2,1,0:T(1,128)S(1)} %bitcast.14, s32[8,16]{1,0:T(8,128)S(1)} %copy-done.11, ...), custom_call_target="tpu_custom_call" | custom-call | tf_op jit(solution)/shard_map/request/pallas_call | solution.py:155
  4.9 10.2 %all-to-all-start = ((f32[8,32,128]{2,1,0:T(8,128)}), f32[8,32,128]{2,1,0:T(8,128)S(1)}, u32[]{:S(2)}, u32[]{:S(2)}) async-start(f32[8,32,128]{2,1,0:T(8,128)} %get-tuple-element.14), calls=%async_computation | async-start | bytes 262144 | tf_op jit(solution)/shard_map/all_to_all | solution.py:424
  15.1 0.0 copy-done.5
  15.1 0.0 copy-start
  15.1 1.2 %copy-done = f32[8,128,256]{2,1,0:T(8,128)S(1)} copy-done((f32[8,128,256]{2,1,0:T(8,128)S(1)}, f32[8,128,256]{2,1,0:T(8,128)}, u32[]{:S(2)}) %copy-start) | copy-done | bytes 1048600
  16.3 1.0 %copy-done.2 = f32[8,128,128]{2,1,0:T(8,128)S(1)} copy-done((f32[8,128,128]{2,1,0:T(8,128)S(1)}, f32[8,128,128]{2,1,0:T(8,128)}, u32[]{:S(2)}) %copy-start.2) | copy-done | bytes 524312
  17.4 3.0 %weights.1 = f32[8,104,128]{2,1,0:T(8,128)} custom-call(f32[8,8,256]{2,1,0:T(8,128)S(1)} %copy-done.5, f32[8,128,256]{2,1,0:T(8,128)S(1)} %copy-done, f32[3,8,128]{2,1,0:T(8,128)S(1)} %bitcast.10, f32[8,128,128]{2,1,0:T(8,128)S(1)} %copy-done.2, f32[3,1,128]{2,1,0:T(1,128)S(1)} %bitcast.15), custom_call_target="tpu_custom_call" | custom-call | tf_op jit(solution)/shard_map/weights/pallas_call | solution.py:182
  20.4 2.5 %all-to-all-done = f32[8,32,128]{2,1,0:T(8,128)S(1)} async-done(((f32[8,32,128]{2,1,0:T(8,128)}), f32[8,32,128]{2,1,0:T(8,128)S(1)}, u32[]{:S(2)}, u32[]{:S(2)}) %all-to-all-start) | async-done | bytes 131104 | tf_op jit(solution)/shard_map/all_to_all | solution.py:424
  22.9 6.8 %all-to-all-start.1 = ((f32[8,104,128]{2,1,0:T(8,128)}), f32[8,104,128]{2,1,0:T(8,128)S(1)}, u32[]{:S(2)}, u32[]{:S(2)}) async-start(f32[8,104,128]{2,1,0:T(8,128)} %weights.1), calls=%async_computation.1 | async-start | bytes 851968 | tf_op jit(solution)/shard_map/all_to_all | solution.py:429
  29.6 2.3 %collective-permute-start = (f32[48,256]{1,0:T(8,128)S(1)}, f32[48,256]{1,0:T(8,128)S(1)}, u32[]{:S(2)}, u32[]{:S(2)}) collective-permute-start(f32[48,256]{1,0:T(8,128)S(1)} %get-tuple-element.17), channel_id=1, source_target_pairs={{0,1},{1,2},{2,3},{3,4},{4,5},{5,6},{6,7},{7,8},{8,9},{9,10},{10,1... | collective-permute-start | bytes 147464 | tf_op jit(solution)/shard_map/ppermute | solution.py:425
  32.0 5.0 %collective-permute-start.1 = (f32[48,256]{1,0:T(8,128)S(1)}, f32[48,256]{1,0:T(8,128)S(1)}, u32[]{:S(2)}, u32[]{:S(2)}) collective-permute-start(f32[48,256]{1,0:T(8,128)S(1)} %get-tuple-element.18), channel_id=1, source_target_pairs={{1,0},{2,1},{3,2},{4,3},{5,4},{6,5},{7,6},{8,7},{9,8},{10,9},{11,1... | collective-permute-start | bytes 147464 | tf_op jit(solution)/shard_map/ppermute | solution.py:426
  37.0 3.6 %collective-permute-done.before = f32[48,256]{1,0:T(8,128)S(1)} collective-permute-done((f32[48,256]{1,0:T(8,128)S(1)}, f32[48,256]{1,0:T(8,128)S(1)}, u32[]{:S(2)}, u32[]{:S(2)}) %collective-permute-start) | collective-permute-done | bytes 49184 | tf_op jit(solution)/shard_map/ppermute | solution.py:425
  40.6 0.0 collective-permute-done.1.after
  40.7 5.6 %near.2.near1 = f32[4,8,256]{2,1,0:T(8,128)S(1)} custom-call(s32[8,9]{1,0:T(8,128)S(1)} %copy-done.13, f32[3,8,256]{2,1,0:T(8,128)S(1)} %bitcast.12, f32[8,8,256]{2,1,0:T(8,128)S(1)} %copy-done.5, f32[48,256]{1,0:T(8,128)S(1)} %collective-permute-done.before, f32[48,256]{1,0:T(8,128)S(1)} %collective-permute-done.1.after), custom_call_target="tpu_custom_call" | custom-call | flops 2359296000 | bytes 300000 | tf_op jit(solution)/shard_map/near/pallas_call | solution.py:235
  46.2 0.0 all-to-all-done.1.src
  46.3 0.8 broadcast_in_dim.8
  47.1 5.8 %all-to-all-start.2 = ((f32[8,128,128]{2,1,0:T(8,128)}), f32[8,128,128]{2,1,0:T(8,128)S(1)}, u32[]{:S(2)}, u32[]{:S(2)}) async-start(f32[8,128,128]{2,1,0:T(8,128)} %broadcast_in_dim.8), calls=%async_computation.2 | async-start | bytes 1048576 | tf_op jit(solution)/shard_map/all_to_all | solution.py:434
  52.9 7.9 %far_leaf.1.part = f32[8,9,8,128]{3,2,1,0:T(8,128)S(1)} custom-call(s32[8,2,128]{2,1,0:T(2,128)S(1)} %slice_convert_fusion.req, f32[8,104,128]{2,1,0:T(8,128)S(1)} %all-to-all-done.1.src, f32[256,128]{1,0:T(8,128)S(1)} %bitcast.7), custom_call_target="tpu_custom_call" | custom-call | flops 2097152000 | bytes 900000 | tf_op jit(solution)/shard_map/far_leaf/pallas_call | solution.py:351
  60.8 1.5 %all-to-all-done.2 = f32[8,128,128]{2,1,0:T(8,128)S(1)} async-done(((f32[8,128,128]{2,1,0:T(8,128)}), f32[8,128,128]{2,1,0:T(8,128)S(1)}, u32[]{:S(2)}, u32[]{:S(2)}) %all-to-all-start.2) | async-done | bytes 524320 | tf_op jit(solution)/shard_map/all_to_all | solution.py:434
  62.4 4.1 %far_top.1 = f32[8,9,8,128]{3,2,1,0:T(8,128)} custom-call(s32[8,2,128]{2,1,0:T(2,128)S(1)} %slice_convert_fusion.req, f32[1024,128]{1,0:T(8,128)S(1)} %bitcast.6, f32[256,128]{1,0:T(8,128)S(1)} %bitcast.8, f32[8,9,8,128]{3,2,1,0:T(8,128)S(1)} %far_leaf.1.part), custom_call_target="tpu_custom_call" | custom-call | tf_op jit(solution)/shard_map/far_top/pallas_call | solution.py:381
  66.5 7.8 %all-to-all-start.3 = ((f32[8,9,8,128]{3,2,1,0:T(8,128)}), f32[8,9,8,128]{3,2,1,0:T(8,128)S(1)}, u32[]{:S(2)}, u32[]{:S(2)}) async-start(f32[8,9,8,128]{3,2,1,0:T(8,128)} %far_top.1), calls=%async_computation.3 | async-start | bytes 589824 | tf_op jit(solution)/shard_map/all_to_all | solution.py:438
  74.3 0.0 copy-start.3
  74.3 5.6 %near.3.near2 = f32[4,8,256]{2,1,0:T(8,128)S(1)} custom-call(s32[8,9]{1,0:T(8,128)S(1)} %copy-done.13, f32[3,8,256]{2,1,0:T(8,128)S(1)} %bitcast.13, f32[8,8,256]{2,1,0:T(8,128)S(1)} %copy-done.5, f32[48,256]{1,0:T(8,128)S(1)} %collective-permute-done.before, f32[48,256]{1,0:T(8,128)S(1)} %collective-permute-done.1.after), custom_call_target="tpu_custom_call" | custom-call | flops 2359296000 | bytes 300000 | tf_op jit(solution)/shard_map/near/pallas_call | solution.py:235
  79.9 7.5 %all-to-all-done.3.got = f32[8,9,8,128]{3,2,1,0:T(8,128)S(1)} async-done(((f32[8,9,8,128]{3,2,1,0:T(8,128)}), f32[8,9,8,128]{3,2,1,0:T(8,128)S(1)}, u32[]{:S(2)}, u32[]{:S(2)}) %all-to-all-start.3) | async-done | bytes 294944 | tf_op jit(solution)/shard_map/all_to_all | solution.py:438
  87.4 0.0 copy-done.1
  87.4 1.8 %final.1 = f32[8,8,256]{2,1,0:T(8,128)} custom-call(f32[8,9,8,128]{3,2,1,0:T(8,128)S(1)} %all-to-all-done.3.got, f32[8,128,128]{2,1,0:T(8,128)S(1)} %copy-done.3, f32[8,128,256]{2,1,0:T(8,128)S(1)} %copy-done.1, f32[4,8,256]{2,1,0:T(8,128)S(1)} %near.2.near1, f32[4,8,256]{2,1,0:T(8,128)S(1)} %near.3.near2), custom_call_target="tpu_custom_call" | custom-call | tf_op jit(solution)/shard_map/final/pallas_call | solution.py:405
  (18 shorter events, 0.1 us)
Async XLA Ops:
  0.0 0.7 copy-start.11
  0.0 0.7 copy-start.10
  0.7 0.8 copy-start.4
  1.5 0.7 copy-start.6
  2.2 0.7 copy-start.8
  3.0 0.7 copy-start.12
  4.9 10.2 %copy-start.5 = (f32[8,8,256]{2,1,0:T(8,128)S(1)}, f32[8,8,256]{2,1,0:T(8,128)}, u32[]{:S(2)}) copy-start(f32[8,8,256]{2,1,0:T(8,128)} %chg.6) | copy-start | bytes 196612
  4.9 10.2 %copy-start.7 = (f32[8,3,128]{2,0,1:T(8,128)S(1)}, f32[8,3,128]{2,0,1:T(8,128)}, u32[]{:S(2)}) copy-start(f32[8,3,128]{2,0,1:T(8,128)} %param.12) | copy-start | bytes 36868
  4.9 17.9 %all-to-all-start = ((f32[8,32,128]{2,1,0:T(8,128)}), f32[8,32,128]{2,1,0:T(8,128)S(1)}, u32[]{:S(2)}, u32[]{:S(2)}) async-start(f32[8,32,128]{2,1,0:T(8,128)} %get-tuple-element.14), calls=%async_computation | async-start | bytes 262144 | tf_op jit(solution)/shard_map/all_to_all | solution.py:424
  15.1 1.2 %copy-start = (f32[8,128,256]{2,1,0:T(8,128)S(1)}, f32[8,128,256]{2,1,0:T(8,128)}, u32[]{:S(2)}) copy-start(f32[8,128,256]{2,1,0:T(8,128)} %up.3) | copy-start | bytes 3145732
  16.3 1.0 %copy-start.2 = (f32[8,128,128]{2,1,0:T(8,128)S(1)}, f32[8,128,128]{2,1,0:T(8,128)}, u32[]{:S(2)}) copy-start(f32[8,128,128]{2,1,0:T(8,128)} %utm.3) | copy-start | bytes 1572868
  20.4 20.3 %copy-start.9 = (f32[8,3,256]{2,0,1:T(8,128)S(1)}, f32[8,3,256]{2,0,1:T(8,128)}, u32[]{:S(2)}) copy-start(f32[8,3,256]{2,0,1:T(8,128)} %param.9) | copy-start | bytes 73732
  20.4 20.3 %copy-start.13 = (s32[8,9]{1,0:T(8,128)S(1)}, s32[8,9]{1,0:T(8,128)}, u32[]{:S(2)}) copy-start(s32[8,9]{1,0:T(8,128)} %ids.3) | copy-start | bytes 868
  22.9 23.4 %all-to-all-start.1 = ((f32[8,104,128]{2,1,0:T(8,128)}), f32[8,104,128]{2,1,0:T(8,128)S(1)}, u32[]{:S(2)}, u32[]{:S(2)}) async-start(f32[8,104,128]{2,1,0:T(8,128)} %weights.1), calls=%async_computation.1 | async-start | bytes 851968 | tf_op jit(solution)/shard_map/all_to_all | solution.py:429
  29.6 11.0 %collective-permute-start = (f32[48,256]{1,0:T(8,128)S(1)}, f32[48,256]{1,0:T(8,128)S(1)}, u32[]{:S(2)}, u32[]{:S(2)}) collective-permute-start(f32[48,256]{1,0:T(8,128)S(1)} %get-tuple-element.17), channel_id=1, source_target_pairs={{0,1},{1,2},{2,3},{3,4},{4,5},{5,6},{6,7},{7,8},{8,9},{9,10},{10,1... | collective-permute-start | bytes 147464 | tf_op jit(solution)/shard_map/ppermute | solution.py:425
  32.0 8.7 %collective-permute-start.1 = (f32[48,256]{1,0:T(8,128)S(1)}, f32[48,256]{1,0:T(8,128)S(1)}, u32[]{:S(2)}, u32[]{:S(2)}) collective-permute-start(f32[48,256]{1,0:T(8,128)S(1)} %get-tuple-element.18), channel_id=1, source_target_pairs={{1,0},{2,1},{3,2},{4,3},{5,4},{6,5},{7,6},{8,7},{9,8},{10,9},{11,1... | collective-permute-start | bytes 147464 | tf_op jit(solution)/shard_map/ppermute | solution.py:426
  47.1 15.3 %all-to-all-start.2 = ((f32[8,128,128]{2,1,0:T(8,128)}), f32[8,128,128]{2,1,0:T(8,128)S(1)}, u32[]{:S(2)}, u32[]{:S(2)}) async-start(f32[8,128,128]{2,1,0:T(8,128)} %broadcast_in_dim.8), calls=%async_computation.2 | async-start | bytes 1048576 | tf_op jit(solution)/shard_map/all_to_all | solution.py:434
  66.5 20.9 %all-to-all-start.3 = ((f32[8,9,8,128]{3,2,1,0:T(8,128)}), f32[8,9,8,128]{3,2,1,0:T(8,128)S(1)}, u32[]{:S(2)}, u32[]{:S(2)}) async-start(f32[8,9,8,128]{3,2,1,0:T(8,128)} %far_top.1), calls=%async_computation.3 | async-start | bytes 589824 | tf_op jit(solution)/shard_map/all_to_all | solution.py:438
  74.3 13.0 %copy-start.1 = (f32[8,128,256]{2,1,0:T(8,128)S(1)}, f32[8,128,256]{2,1,0:T(8,128)}, u32[]{:S(2)}) copy-start(f32[8,128,256]{2,1,0:T(8,128)} %up.3) | copy-start | bytes 3145732
  74.3 13.0 %copy-start.3 = (f32[8,128,128]{2,1,0:T(8,128)S(1)}, f32[8,128,128]{2,1,0:T(8,128)}, u32[]{:S(2)}) copy-start(f32[8,128,128]{2,1,0:T(8,128)} %utm.3) | copy-start | bytes 1572868

commit v3 on v2

--- a/solution.py
+++ b/solution.py
@@ -19,11 +19,12 @@
 NBR = 9
 PAIRS = 8
 DUMMY = 64
-EXACT = lax.Precision.HIGHEST
 
 SMEM = pl.BlockSpec(memory_space=pltpu.SMEM)
+HBM = pl.BlockSpec(memory_space=pltpu.HBM)
 VMEM = pl.BlockSpec(memory_space=pltpu.VMEM)
 PARAMS = pltpu.CompilerParams(vmem_limit_bytes=40 << 20)
+WIDE = pltpu.CompilerParams(vmem_limit_bytes=60 << 20)
 
 
 def split2(x):
@@ -91,11 +92,29 @@
     return jnp.dot(vals, high, preferred_element_type=F32) + jnp.dot(vals, low, preferred_element_type=F32)
 
 
-def nt(a, b):
-    return lax.dot_general(a, b, (((1,), (1,)), ((), ())), precision=EXACT, preferred_element_type=F32)
-
-
-def request_kernel(pts, chg, skel, cpts, llist, tlist, m0, first, last, row16):
+def dot3(a, b, transposed=False):
+    ah = a.astype(BF16).astype(F32)
+    both = jnp.concatenate([ah, a - ah], 0).astype(BF16)
+    bh = b.astype(BF16)
+    bl = (b - bh.astype(F32)).astype(BF16)
+    dims = (((1,), (1 if transposed else 0,)), ((), ()))
+    r = lax.dot_general(both, bh, dims, preferred_element_type=F32)
+    r = r + lax.dot_general(both, bl, dims, preferred_element_type=F32)
+    return r[0:8] + r[8:16]
+
+
+def fetch(pairs, sems):
+    copies = [pltpu.make_async_copy(a, b, sems.at[i]) for i, (a, b) in enumerate(pairs)]
+    for c in copies:
+        c.start()
+    return copies
+
+
+def request_kernel(pts_h, chg_h, skel_h, cpts_h, llist_h, tlist_h, m0, first, last, row16, pts, chg, skel, cpts, llist, tlist, sems):
+    ins = ((llist_h, llist), (tlist_h, tlist), (skel_h, skel), (cpts_h, cpts), (pts_h, pts), (chg_h, chg))
+    copies = fetch(ins, sems)
+    for c in copies[0:2]:
+        c.wait()
     lane = lax.broadcasted_iota(jnp.int32, (1, 128), 1)
     sub8 = lax.broadcasted_iota(jnp.int32, (8, 128), 0)
     lane8 = lax.broadcasted_iota(jnp.int32, (8, 128), 1)
@@ -130,6 +149,8 @@
     codes = jnp.where(sub8 == 0, lane >> 4, jnp.where(sub8 == 1, local, 0)).astype(F32).astype(BF16)
     tcodes = jnp.where(sub8 == 0, tl >> 3, 0).astype(F32).astype(BF16)
     rowf = row.astype(F32)
+    for c in copies[2:6]:
+        c.wait()
     for d in range(8):
         for c in range(3):
             m0[d, 8 * c : 8 * c + 8, :] = skel[c]
@@ -154,22 +175,34 @@
     sd = jax.ShapeDtypeStruct
     return pl.pallas_call(
         request_kernel,
-        in_specs=[VMEM] * 6,
+        in_specs=[HBM] * 6,
         out_specs=[VMEM] * 3,
         out_shape=[sd((8, 32, 128), F32), sd((48, 256), F32), sd((48, 256), F32)],
-        scratch_shapes=[pltpu.VMEM((8, 128), jnp.int32)],
-        compiler_params=PARAMS,
+        scratch_shapes=[pltpu.VMEM((8, 128), jnp.int32)]
+        + [pltpu.VMEM(a.shape, a.dtype) for a in (pts, chg, skel, cpts, llist, tlist)]
+        + [pltpu.SemaphoreType.DMA((6,))],
+        compiler_params=WIDE,
         name="request",
     )(pts, chg, skel, cpts, llist, tlist)
 
 
-def weights_kernel(chg, up, skel, utm, cpts, m1):
+def weights_kernel(chg_h, up_h, skel_h, utm_h, cpts_h, m1, chg, up, skel, utm, cpts, sems):
+    ins = [(chg_h, chg)]
     for l in range(OWN):
-        w = nt(chg[l], up[l])
-        cw = nt(w, utm[l])
+        ins += [(up_h.at[l], up.at[l]), (utm_h.at[l], utm.at[l])]
+    ins += [(skel_h, skel), (cpts_h, cpts)]
+    copies = fetch(ins, sems)
+    copies[0].wait()
+    for l in range(OWN):
+        copies[1 + 2 * l].wait()
+        w = dot3(chg[l], up[l], True)
+        copies[2 + 2 * l].wait()
+        cw = dot3(w, utm[l], True)
         total = cw if l == 0 else total + cw
         for d in range(8):
             m1[d, 8 * l : 8 * l + 8, :] = w
+    copies[17].wait()
+    copies[18].wait()
     for d in range(8):
         m1[d, 88:96, :] = total
         for c in range(3):
@@ -181,10 +214,11 @@
 def weights(chg, up, skel, utm, cpts):
     return pl.pallas_call(
         weights_kernel,
-        in_specs=[VMEM] * 5,
+        in_specs=[HBM] * 5,
         out_specs=VMEM,
         out_shape=jax.ShapeDtypeStruct((8, 104, 128), F32),
-        compiler_params=PARAMS,
+        scratch_shapes=[pltpu.VMEM(a.shape, a.dtype) for a in (chg, up, skel, utm, cpts)] + [pltpu.SemaphoreType.DMA((19,))],
+        compiler_params=WIDE,
         name="weights",
     )(chg, up, skel, utm, cpts)
 
@@ -396,9 +430,9 @@
     cell = tot[8]
     half = near1.shape[0]
     for l in range(OWN):
-        incoming = tot[l] + jnp.dot(cell, utm[l], precision=EXACT, preferred_element_type=F32)
+        incoming = tot[l] + dot3(cell, utm[l])
         near = near1[l] if l < half else near2[l - half]
-        out[l] = near + jnp.dot(incoming, up[l], precision=EXACT, preferred_element_type=F32)
+        out[l] = near + dot3(incoming, up[l])
 
 
 def final(got, utm, up, near1, near2):
@@ -424,7 +458,8 @@
     got0 = lax.all_to_all(m0, "z", 0, 0, tiled=True)
     before = lax.ppermute(last, every, up)
     after = lax.ppermute(first, every, down)
-    m1 = weights(charges, up_op, skel, utm, cpts)
+    skel1, before, after = lax.optimization_barrier((skel, before, after))
+    m1 = weights(charges, up_op, skel1, utm, cpts)
     m1, got0 = lax.optimization_barrier((m1, got0))
     got1 = lax.all_to_all(m1, "y", 0, 0, tiled=True)
     req = got0[:, 27:29, :].astype(jnp.int32)

time: 90 us -> 89.7 us (level)
  the two profiles are of different devices: /device:TPU:25 before, /device:TPU:1 now
where the time goes in v3:
time: 89.7 us; the launch traced here: 89.1 us
  starting transfers between devices  40.3 us (45%)
  Pallas kernels  32 us (36%)
  waiting for transfers between devices  15.8 us (18%)
    pallas_call x2, Pallas kernels, near_part(): pl.pallas_call(functools.partial(near_kernel, lo, hi), in_specs=[SMEM] +...  11.2 us
    all_to_all x1, starting transfers between devices, body(): got0 = lax.all_to_all(m0, 'z', 0, 0, tiled=True)  11 us
    pallas_call x1, Pallas kernels, far_leaf(): pl.pallas_call(far_leaf_kernel, in_specs=[SMEM, VMEM, VMEM], out_specs=VM...  9.38 us
    all_to_all x1, starting transfers between devices, body(): gotg = lax.all_to_all(cells, 'g', 0, 0, tiled=True)  7.94 us
    all_to_all x1, waiting for transfers between devices, body(): gotr = lax.all_to_all(part, 'z', 0, 0, tiled=True)  7.43 us
    ppermute x1, starting transfers between devices, body(): after = lax.ppermute(first, every, down)  7.16 us
    all_to_all x1, waiting for transfers between devices, body(): got1 = lax.all_to_all(m1, 'y', 0, 0, tiled=True)  7.09 us
    all_to_all x1, starting transfers between devices, body(): gotr = lax.all_to_all(part, 'z', 0, 0, tiled=True)  5.8 us
  transfers between devices with their start and end apart: 6, of which 5 were waited for; matrix products, arithmetic and copies ran while one was open for 0% of the time, Pallas kernels for 29%

profile of v3, /device:TPU:1, one launch (start us, length us, event | category | flops | bytes accessed | tf_op | source)
XLA Modules:
  0.0 89.1 jit_solution(11146991347931610940)
XLA Ops:
  0.0 2.0 %request.1 = (f32[8,32,128]{2,1,0:T(8,128)}, f32[48,256]{1,0:T(8,128)}, f32[48,256]{1,0:T(8,128)}) custom-call(f32[3,8,256]{2,1,0:T(8,128)} %bitcast.9, f32[8,8,256]{2,1,0:T(8,128)} %chg.2, f32[3,8,128]{2,1,0:T(8,128)} %bitcast.13, f32[3,1,128]{2,1,0:T(1,128)} %bitcast.15, s32[8,16]{1,0:T(8,128)} %llist_h.1, s32[1,16]{1,0:T(1,128)} %tlist_h.1), custom_call_target="tpu_custom_call" | custom-call | tf_op jit(solution)/shard_map/request/pallas_call | solution.py:176
  2.0 0.0 copy-start.6
  2.0 0.0 copy-start.5
  2.1 11.0 %all-to-all-start = ((f32[8,32,128]{2,1,0:T(8,128)}), f32[8,32,128]{2,1,0:T(8,128)S(1)}, u32[]{:S(2)}, u32[]{:S(2)}) async-start(f32[8,32,128]{2,1,0:T(8,128)} %get-tuple-element.20), calls=%async_computation | async-start | bytes 262144 | tf_op jit(solution)/shard_map/all_to_all | solution.py:458
  13.1 0.0 copy-done.6
  13.1 3.4 %collective-permute-start = (f32[48,256]{1,0:T(8,128)S(1)}, f32[48,256]{1,0:T(8,128)S(1)}, u32[]{:S(2)}, u32[]{:S(2)}) collective-permute-start(f32[48,256]{1,0:T(8,128)S(1)} %copy-done.6), channel_id=1, source_target_pairs={{0,1},{1,2},{2,3},{3,4},{4,5},{5,6},{6,7},{7,8},{8,9},{9,10},{10,1... | collective-permute-start | bytes 147464 | tf_op jit(solution)/shard_map/ppermute | solution.py:459
  16.4 0.0 copy-done.5
  16.4 7.2 %collective-permute-start.1 = (f32[48,256]{1,0:T(8,128)S(1)}, f32[48,256]{1,0:T(8,128)S(1)}, u32[]{:S(2)}, u32[]{:S(2)}) collective-permute-start(f32[48,256]{1,0:T(8,128)S(1)} %copy-done.5), channel_id=1, source_target_pairs={{1,0},{2,1},{3,2},{4,3},{5,4},{6,5},{7,6},{8,7},{9,8},{10,9},{11,1... | collective-permute-start | bytes 147464 | tf_op jit(solution)/shard_map/ppermute | solution.py:460
  23.6 0.1 collective-permute-done.before
  23.7 1.1 %collective-permute-done.1.after = f32[48,256]{1,0:T(8,128)S(1)} collective-permute-done((f32[48,256]{1,0:T(8,128)S(1)}, f32[48,256]{1,0:T(8,128)S(1)}, u32[]{:S(2)}, u32[]{:S(2)}) %collective-permute-start.1) | collective-permute-done | bytes 49184 | tf_op jit(solution)/shard_map/ppermute | solution.py:460
  24.8 4.9 %weights.1 = f32[8,104,128]{2,1,0:T(8,128)} custom-call(f32[8,8,256]{2,1,0:T(8,128)} %chg.2, f32[8,128,256]{2,1,0:T(8,128)} %up.1, f32[3,8,128]{2,1,0:T(8,128)} %bitcast.14, f32[8,128,128]{2,1,0:T(8,128)} %utm.1, f32[3,1,128]{2,1,0:T(1,128)} %bitcast.16), custom_call_target="tpu_custom_call" | custom-call | tf_op jit(solution)/shard_map/weights/pallas_call | solution.py:215
  29.7 0.0 copy-start.2
  29.7 0.0 copy-start.3
  29.7 0.0 copy-start.4
  29.7 0.0 all-to-all-done
  29.7 5.1 %all-to-all-start.1 = ((f32[8,104,128]{2,1,0:T(8,128)}), f32[8,104,128]{2,1,0:T(8,128)S(1)}, u32[]{:S(2)}, u32[]{:S(2)}) async-start(f32[8,104,128]{2,1,0:T(8,128)} %weights.1), calls=%async_computation.1 | async-start | bytes 851968 | tf_op jit(solution)/shard_map/all_to_all | solution.py:464
  34.8 0.0 copy-done.2
  34.8 0.0 copy-done.3
  34.8 0.0 copy-done.4
  34.8 5.6 %near.2.near1 = f32[4,8,256]{2,1,0:T(8,128)S(1)} custom-call(s32[8,9]{1,0:T(8,128)S(1)} %copy-done.4, f32[3,8,256]{2,1,0:T(8,128)S(1)} %bitcast.10, f32[8,8,256]{2,1,0:T(8,128)S(1)} %copy-done.2, f32[48,256]{1,0:T(8,128)S(1)} %collective-permute-done.before, f32[48,256]{1,0:T(8,128)S(1)} %collective-permute-done.1.after), custom_call_target="tpu_custom_call" | custom-call | flops 2359296000 | bytes 300000 | tf_op jit(solution)/shard_map/near/pallas_call | solution.py:269
  40.4 7.1 %all-to-all-done.1.src = f32[8,104,128]{2,1,0:T(8,128)S(1)} async-done(((f32[8,104,128]{2,1,0:T(8,128)}), f32[8,104,128]{2,1,0:T(8,128)S(1)}, u32[]{:S(2)}, u32[]{:S(2)}) %all-to-all-start.1) | async-done | bytes 426016 | tf_op jit(solution)/shard_map/all_to_all | solution.py:464
  47.5 0.8 broadcast_in_dim.8
  48.3 7.9 %all-to-all-start.2 = ((f32[8,128,128]{2,1,0:T(8,128)}), f32[8,128,128]{2,1,0:T(8,128)S(1)}, u32[]{:S(2)}, u32[]{:S(2)}) async-start(f32[8,128,128]{2,1,0:T(8,128)} %broadcast_in_dim.8), calls=%async_computation.2 | async-start | bytes 1048576 | tf_op jit(solution)/shard_map/all_to_all | solution.py:469
  56.3 9.4 %far_leaf.1.part = f32[8,9,8,128]{3,2,1,0:T(8,128)S(1)} custom-call(s32[8,2,128]{2,1,0:T(2,128)S(1)} %slice_convert_fusion.req, f32[8,104,128]{2,1,0:T(8,128)S(1)} %all-to-all-done.1.src, f32[256,128]{1,0:T(8,128)S(1)} %bitcast.7), custom_call_target="tpu_custom_call" | custom-call | flops 2097152000 | bytes 900000 | tf_op jit(solution)/shard_map/far_leaf/pallas_call | solution.py:385
  65.6 0.1 all-to-all-done.2
  65.7 3.3 %far_top.1 = f32[8,9,8,128]{3,2,1,0:T(8,128)} custom-call(s32[8,2,128]{2,1,0:T(2,128)S(1)} %slice_convert_fusion.req, f32[1024,128]{1,0:T(8,128)S(1)} %bitcast.6, f32[256,128]{1,0:T(8,128)S(1)} %bitcast.8, f32[8,9,8,128]{3,2,1,0:T(8,128)S(1)} %far_leaf.1.part), custom_call_target="tpu_custom_call" | custom-call | tf_op jit(solution)/shard_map/far_top/pallas_call | solution.py:415
  69.1 5.8 %all-to-all-start.3 = ((f32[8,9,8,128]{3,2,1,0:T(8,128)}), f32[8,9,8,128]{3,2,1,0:T(8,128)S(1)}, u32[]{:S(2)}, u32[]{:S(2)}) async-start(f32[8,9,8,128]{3,2,1,0:T(8,128)} %far_top.1), calls=%async_computation.3 | async-start | bytes 589824 | tf_op jit(solution)/shard_map/all_to_all | solution.py:473
  74.9 0.0 copy-start.1
  74.9 5.6 %near.3.near2 = f32[4,8,256]{2,1,0:T(8,128)S(1)} custom-call(s32[8,9]{1,0:T(8,128)S(1)} %copy-done.4, f32[3,8,256]{2,1,0:T(8,128)S(1)} %bitcast.11, f32[8,8,256]{2,1,0:T(8,128)S(1)} %copy-done.2, f32[48,256]{1,0:T(8,128)S(1)} %collective-permute-done.before, f32[48,256]{1,0:T(8,128)S(1)} %collective-permute-done.1.after), custom_call_target="tpu_custom_call" | custom-call | flops 2359296000 | bytes 300000 | tf_op jit(solution)/shard_map/near/pallas_call | solution.py:269
  80.5 7.4 %all-to-all-done.3.got = f32[8,9,8,128]{3,2,1,0:T(8,128)S(1)} async-done(((f32[8,9,8,128]{3,2,1,0:T(8,128)}), f32[8,9,8,128]{3,2,1,0:T(8,128)S(1)}, u32[]{:S(2)}, u32[]{:S(2)}) %all-to-all-start.3) | async-done | bytes 294944 | tf_op jit(solution)/shard_map/all_to_all | solution.py:473
  87.9 0.0 copy-done
  87.9 1.2 %final.1 = f32[8,8,256]{2,1,0:T(8,128)} custom-call(f32[8,9,8,128]{3,2,1,0:T(8,128)S(1)} %all-to-all-done.3.got, f32[8,128,128]{2,1,0:T(8,128)S(1)} %copy-done.1, f32[8,128,256]{2,1,0:T(8,128)S(1)} %copy-done, f32[4,8,256]{2,1,0:T(8,128)S(1)} %near.2.near1, f32[4,8,256]{2,1,0:T(8,128)S(1)} %near.3.near2), custom_call_target="tpu_custom_call" | custom-call | tf_op jit(solution)/shard_map/final/pallas_call | solution.py:439
  (4 shorter events, 0.0 us)
Async XLA Ops:
  2.0 11.0 %copy-start.6 = (f32[48,256]{1,0:T(8,128)S(1)}, f32[48,256]{1,0:T(8,128)}, u32[]{:S(2)}) copy-start(f32[48,256]{1,0:T(8,128)} %get-tuple-element.17) | copy-start | bytes 147460
  2.0 14.4 %copy-start.5 = (f32[48,256]{1,0:T(8,128)S(1)}, f32[48,256]{1,0:T(8,128)}, u32[]{:S(2)}) copy-start(f32[48,256]{1,0:T(8,128)} %get-tuple-element.18) | copy-start | bytes 147460
  2.1 27.7 %all-to-all-start = ((f32[8,32,128]{2,1,0:T(8,128)}), f32[8,32,128]{2,1,0:T(8,128)S(1)}, u32[]{:S(2)}, u32[]{:S(2)}) async-start(f32[8,32,128]{2,1,0:T(8,128)} %get-tuple-element.20), calls=%async_computation | async-start | bytes 262144 | tf_op jit(solution)/shard_map/all_to_all | solution.py:458
  13.1 10.6 %collective-permute-start = (f32[48,256]{1,0:T(8,128)S(1)}, f32[48,256]{1,0:T(8,128)S(1)}, u32[]{:S(2)}, u32[]{:S(2)}) collective-permute-start(f32[48,256]{1,0:T(8,128)S(1)} %copy-done.6), channel_id=1, source_target_pairs={{0,1},{1,2},{2,3},{3,4},{4,5},{5,6},{6,7},{7,8},{8,9},{9,10},{10,1... | collective-permute-start | bytes 147464 | tf_op jit(solution)/shard_map/ppermute | solution.py:459
  16.4 8.3 %collective-permute-start.1 = (f32[48,256]{1,0:T(8,128)S(1)}, f32[48,256]{1,0:T(8,128)S(1)}, u32[]{:S(2)}, u32[]{:S(2)}) collective-permute-start(f32[48,256]{1,0:T(8,128)S(1)} %copy-done.5), channel_id=1, source_target_pairs={{1,0},{2,1},{3,2},{4,3},{5,4},{6,5},{7,6},{8,7},{9,8},{10,9},{11,1... | collective-permute-start | bytes 147464 | tf_op jit(solution)/shard_map/ppermute | solution.py:460
  29.7 5.1 %copy-start.2 = (f32[8,8,256]{2,1,0:T(8,128)S(1)}, f32[8,8,256]{2,1,0:T(8,128)}, u32[]{:S(2)}) copy-start(f32[8,8,256]{2,1,0:T(8,128)} %chg.2) | copy-start | bytes 196612
  29.7 5.1 %copy-start.3 = (f32[8,3,256]{2,0,1:T(8,128)S(1)}, f32[8,3,256]{2,0,1:T(8,128)}, u32[]{:S(2)}) copy-start(f32[8,3,256]{2,0,1:T(8,128)} %param.9) | copy-start | bytes 73732
  29.7 5.1 %copy-start.4 = (s32[8,9]{1,0:T(8,128)S(1)}, s32[8,9]{1,0:T(8,128)}, u32[]{:S(2)}) copy-start(s32[8,9]{1,0:T(8,128)} %ids.3) | copy-start | bytes 868
  29.7 17.8 %all-to-all-start.1 = ((f32[8,104,128]{2,1,0:T(8,128)}), f32[8,104,128]{2,1,0:T(8,128)S(1)}, u32[]{:S(2)}, u32[]{:S(2)}) async-start(f32[8,104,128]{2,1,0:T(8,128)} %weights.1), calls=%async_computation.1 | async-start | bytes 851968 | tf_op jit(solution)/shard_map/all_to_all | solution.py:464
  48.3 17.4 %all-to-all-start.2 = ((f32[8,128,128]{2,1,0:T(8,128)}), f32[8,128,128]{2,1,0:T(8,128)S(1)}, u32[]{:S(2)}, u32[]{:S(2)}) async-start(f32[8,128,128]{2,1,0:T(8,128)} %broadcast_in_dim.8), calls=%async_computation.2 | async-start | bytes 1048576 | tf_op jit(solution)/shard_map/all_to_all | solution.py:469
  69.1 18.8 %all-to-all-start.3 = ((f32[8,9,8,128]{3,2,1,0:T(8,128)}), f32[8,9,8,128]{3,2,1,0:T(8,128)S(1)}, u32[]{:S(2)}, u32[]{:S(2)}) async-start(f32[8,9,8,128]{3,2,1,0:T(8,128)} %far_top.1), calls=%async_computation.3 | async-start | bytes 589824 | tf_op jit(solution)/shard_map/all_to_all | solution.py:473
  74.9 13.0 %copy-start = (f32[8,128,256]{2,1,0:T(8,128)S(1)}, f32[8,128,256]{2,1,0:T(8,128)}, u32[]{:S(2)}) copy-start(f32[8,128,256]{2,1,0:T(8,128)} %up.1) | copy-start | bytes 3145732
  74.9 13.0 %copy-start.1 = (f32[8,128,128]{2,1,0:T(8,128)S(1)}, f32[8,128,128]{2,1,0:T(8,128)}, u32[]{:S(2)}) copy-start(f32[8,128,128]{2,1,0:T(8,128)} %utm.1) | copy-start | bytes 1572868

commit v4 on v3

--- a/solution.py
+++ b/solution.py
@@ -186,38 +186,38 @@
     )(pts, chg, skel, cpts, llist, tlist)
 
 
-def weights_kernel(chg_h, up_h, skel_h, utm_h, cpts_h, m1, chg, up, skel, utm, cpts, sems):
-    ins = [(chg_h, chg)]
+def weights_kernel(chg_h, up_h, skel_h, utm_h, cpts_h, m1, chg, up, skel, utm, cpts, slab, sems):
+    ins = ((chg_h, chg), (up_h, up), (utm_h, utm), (skel_h, skel), (cpts_h, cpts))
+    copies = fetch(ins, sems)
+    slab[96:104, :] = jnp.zeros((8, 128), F32)
+    for c in copies[3:5]:
+        c.wait()
+    for c in range(3):
+        slab[64 + 8 * c : 72 + 8 * c, :] = skel[c]
+        slab[96 + c : 97 + c, :] = cpts[c]
+    copies[0].wait()
+    copies[1].wait()
+    own = [dot3(chg[l], up[l], True) for l in range(OWN)]
     for l in range(OWN):
-        ins += [(up_h.at[l], up.at[l]), (utm_h.at[l], utm.at[l])]
-    ins += [(skel_h, skel), (cpts_h, cpts)]
-    copies = fetch(ins, sems)
-    copies[0].wait()
-    for l in range(OWN):
-        copies[1 + 2 * l].wait()
-        w = dot3(chg[l], up[l], True)
-        copies[2 + 2 * l].wait()
-        cw = dot3(w, utm[l], True)
-        total = cw if l == 0 else total + cw
-        for d in range(8):
-            m1[d, 8 * l : 8 * l + 8, :] = w
-    copies[17].wait()
-    copies[18].wait()
-    for d in range(8):
-        m1[d, 88:96, :] = total
-        for c in range(3):
-            m1[d, 64 + 8 * c : 72 + 8 * c, :] = skel[c]
-            m1[d, 96 + c : 97 + c, :] = cpts[c]
-        m1[d, 99:104, :] = jnp.zeros((5, 128), F32)
+        slab[8 * l : 8 * l + 8, :] = own[l]
+    copies[2].wait()
+    total = dot3(own[0], utm[0], True)
+    for l in range(1, OWN):
+        total = total + dot3(own[l], utm[l], True)
+    slab[88:96, :] = total
+    for c in fetch([(slab, m1.at[d]) for d in range(8)], sems):
+        c.wait()
 
 
 def weights(chg, up, skel, utm, cpts):
     return pl.pallas_call(
         weights_kernel,
         in_specs=[HBM] * 5,
-        out_specs=VMEM,
+        out_specs=HBM,
         out_shape=jax.ShapeDtypeStruct((8, 104, 128), F32),
-        scratch_shapes=[pltpu.VMEM(a.shape, a.dtype) for a in (chg, up, skel, utm, cpts)] + [pltpu.SemaphoreType.DMA((19,))],
+        scratch_shapes=[pltpu.VMEM(a.shape, a.dtype) for a in (chg, up, skel, utm, cpts)]
+        + [pltpu.VMEM((104, 128), F32), pltpu.SemaphoreType.DMA((8,))],
+        cost_estimate=pl.CostEstimate(flops=50000000, bytes_accessed=8000000, transcendentals=0),
         compiler_params=WIDE,
         name="weights",
     )(chg, up, skel, utm, cpts)
@@ -285,21 +285,13 @@
     )(ids, pts, chg, before, after)
 
 
-def prepare_sources(i, xyz, t0, t1, even, odd):
+def prepare_sources(i, xyz, t0, t1, feat):
     s0, s1, _, _, _ = dense_features(xyz)
     s0 = spread(s0, t0)
     s1 = spread(s1, t1)
-    rows = []
     for l in range(8):
-        a, b = s0(l), s1(l)
-        rows.append(jnp.concatenate([a, b, a, b], 0))
-    zero = jnp.zeros((64, 128), F32)
-    left = lax.broadcasted_iota(jnp.int32, (128, 128), 1) < FEAT
-    for l in range(0, 8, 2):
-        for a, b in ((l, l + 1), (l + 1, l)):
-            both = jnp.concatenate([rows[a], rows[b], zero], 0).T
-            even[8 * i + a] = jnp.where(left, both, 0.0).astype(BF16)[:, 0:64]
-            odd[8 * i + b] = jnp.where(left, 0.0, both).astype(BF16)[:, 0:64]
+        feat[8 * i + l, 0:8, :] = s0(l)
+        feat[8 * i + l, 8:16, :] = s1(l)
 
 
 def prepare_targets(i, xyz, tmp, ft):
@@ -327,7 +319,7 @@
     return off
 
 
-def interact(total, flat, even, odd, ft, vals, add):
+def interact(total, flat, fs, ft, vals, add):
     zero = jnp.zeros((FEAT, 128), BF16)
 
     def chunk(i, carry):
@@ -339,7 +331,9 @@
             fa = ft[ta].astype(BF16)
             fb = ft[tb].astype(BF16)
             tgt = jnp.concatenate([jnp.concatenate([fa, zero], 1), jnp.concatenate([zero, fb], 1)], 0)
-            r = product(even[sa] + odd[sb], tgt, jnp.concatenate([vals[sa], vals[sb]], 0))
+            ra, rb = fs[sa], fs[sb]
+            src = jnp.concatenate([ra, ra, rb, rb], 0).T.astype(BF16)
+            r = product(src, tgt, jnp.concatenate([vals[sa], vals[sb]], 0))
             add(ta, r[0:8, 0:128] + r[8:16, 0:128])
             add(tb, r[16:24, 128:256] + r[24:32, 128:256])
         return carry
@@ -347,32 +341,30 @@
     lax.fori_loop(0, (total + 2 * PAIRS - 1) // (2 * PAIRS), chunk, 0)
 
 
-def clear_dummy(even, odd, vals):
-    even[DUMMY] = jnp.zeros((128, 64), BF16)
-    odd[DUMMY] = jnp.zeros((128, 64), BF16)
+def clear_dummy(fs, vals):
+    fs[DUMMY] = jnp.zeros((16, 128), F32)
     vals[DUMMY] = jnp.zeros((16, 128), BF16)
 
 
-def far_leaf_kernel(req, src, tgt, out, flat, even, odd, ft, vals, t0, t1, t2):
+def far_leaf_kernel(req, src, tgt, out, flat, fs, ft, vals, t0, t1, t2):
     for y in range(8):
-        prepare_sources(y, [src[y, 64 + 8 * c : 72 + 8 * c, :] for c in range(3)], t0.at[y], t1.at[y], even, odd)
+        prepare_sources(y, [src[y, 64 + 8 * c : 72 + 8 * c, :] for c in range(3)], t0.at[y], t1.at[y], fs)
         prepare_targets(y, [tgt[32 * y + 8 * c : 32 * y + 8 * c + 8, :] for c in range(3)], t2.at[y], ft)
         for l in range(OWN):
             vals[8 * y + l] = two_halves(src[y, 8 * l : 8 * l + 8, :])
-    clear_dummy(even, odd, vals)
+    clear_dummy(fs, vals)
     out[...] = jnp.zeros_like(out)
     total = flatten(req, flat, 0, 0, 0)
 
     def add(t, v):
         out[t >> 3, t & 7] += v
 
-    interact(total, flat, even, odd, ft, vals, add)
+    interact(total, flat, fs, ft, vals, add)
 
 
 FAR_SCRATCH = [
     pltpu.SMEM((1024 + 64,), jnp.int32),
-    pltpu.VMEM((65, 128, 64), BF16),
-    pltpu.VMEM((65, 128, 64), BF16),
+    pltpu.VMEM((65, 16, 128), F32),
     pltpu.VMEM((64, FEAT, 128), F32),
     pltpu.VMEM((65, 16, 128), BF16),
     pltpu.VMEM((8, 1, 64, 128), F32),
@@ -394,21 +386,21 @@
     )(req, src, tgt.reshape(256, 128))
 
 
-def far_top_kernel(req, src, tgt, part, out, flat, even, odd, ft, vals, t0, t1, t2):
+def far_top_kernel(req, src, tgt, part, out, flat, fs, ft, vals, t0, t1, t2):
     for g in range(8):
         xyz = [src[pl.ds(128 * g + 8 + c, 8, stride=16), :] for c in range(3)]
-        prepare_sources(g, xyz, t0.at[g], t1.at[g], even, odd)
+        prepare_sources(g, xyz, t0.at[g], t1.at[g], fs)
         for y in range(8):
             vals[8 * g + y] = two_halves(src[128 * g + 16 * y : 128 * g + 16 * y + 8, :])
     prepare_targets(0, [tgt[pl.ds(24 + c, 8, stride=32), :] for c in range(3)], t2.at[0], ft)
-    clear_dummy(even, odd, vals)
+    clear_dummy(fs, vals)
     out[...] = part[...]
     total = flatten(req, flat, 1, 16, 1)
 
     def add(t, v):
         out[t, 8] += v
 
-    interact(total, flat, even, odd, ft, vals, add)
+    interact(total, flat, fs, ft, vals, add)
 
 
 def far_top(req, src, tgt, part):
@@ -458,9 +450,8 @@
     got0 = lax.all_to_all(m0, "z", 0, 0, tiled=True)
     before = lax.ppermute(last, every, up)
     after = lax.ppermute(first, every, down)
-    skel1, before, after = lax.optimization_barrier((skel, before, after))
-    m1 = weights(charges, up_op, skel1, utm, cpts)
-    m1, got0 = lax.optimization_barrier((m1, got0))
+    m1 = weights(charges, up_op, skel, utm, cpts)
+    m1, got0, before, after = lax.optimization_barrier((m1, got0, before, after))
     got1 = lax.all_to_all(m1, "y", 0, 0, tiled=True)
     req = got0[:, 27:29, :].astype(jnp.int32)
     near1 = near_part(0, 4, near_list, pts, charges, before, after)

time: 89.7 us -> 85.2 us (0.950)
  Pallas kernels: 32 us -> 27.5 us
  waiting for transfers between devices: 15.8 us -> 17 us
  starting transfers between devices: 40.3 us -> 39.1 us
    pallas_call x1, Pallas kernels: 4.89 us -> 2.88 us  [weights(): pl.pallas_call(weights_kernel, in_specs=[HBM] * 5, out_specs=HBM, out_sha...]
    all_to_all x1, waiting for transfers between devices: 0.09 us -> 1.87 us  [body(): gotg = lax.all_to_all(cells, 'g', 0, 0, tiled=True)]
    pallas_call x1, Pallas kernels: 9.38 us -> 7.59 us  [far_leaf(): pl.pallas_call(far_leaf_kernel, in_specs=[SMEM, VMEM, VMEM], out_specs=VM...]
    ppermute x1, waiting for transfers between devices: 1.07 us -> 0.01 us  [body(): after = lax.ppermute(first, every, down)]
  transfers between devices with their start and end apart: 6 -> 6, of which waited for: 5 -> 3; matrix products, arithmetic and copies ran while one was open for 0% -> 0% of each run, Pallas kernels for 29% -> 26%
where the time goes in v4:
time: 85.2 us; the launch traced here: 84.6 us
  starting transfers between devices  39.1 us (46%)
  Pallas kernels  27.5 us (32%)
  waiting for transfers between devices  17 us (20%)
  local copies, waits for them, and re-layouts  0.87 us (1%)
    pallas_call x2, Pallas kernels, near_part(): pl.pallas_call(functools.partial(near_kernel, lo, hi), in_specs=[SMEM] +...  11.2 us
    all_to_all x1, starting transfers between devices, body(): got0 = lax.all_to_all(m0, 'z', 0, 0, tiled=True)  11 us
    all_to_all x1, waiting for transfers between devices, body(): got1 = lax.all_to_all(m1, 'y', 0, 0, tiled=True)  7.64 us
    pallas_call x1, Pallas kernels, far_leaf(): pl.pallas_call(far_leaf_kernel, in_specs=[SMEM, VMEM, VMEM], out_specs=VM...  7.59 us
    all_to_all x1, waiting for transfers between devices, body(): gotr = lax.all_to_all(part, 'z', 0, 0, tiled=True)  7.48 us
    all_to_all x1, starting transfers between devices, body(): gotg = lax.all_to_all(cells, 'g', 0, 0, tiled=True)  7.39 us
    ppermute x1, starting transfers between devices, body(): after = lax.ppermute(first, every, down)  7.16 us
    all_to_all x1, starting transfers between devices, body(): gotr = lax.all_to_all(part, 'z', 0, 0, tiled=True)  5.28 us
  transfers between devices with their start and end apart: 6, of which 3 were waited for; matrix products, arithmetic and copies ran while one was open for 0% of the time, Pallas kernels for 26%

profile of v4, /device:TPU:1, one launch (start us, length us, event | category | flops | bytes accessed | tf_op | source)
XLA Modules:
  0.0 84.6 jit_solution(12409789891401422649)
XLA Ops:
  0.0 2.0 %request.1 = (f32[8,32,128]{2,1,0:T(8,128)}, f32[48,256]{1,0:T(8,128)}, f32[48,256]{1,0:T(8,128)}) custom-call(f32[3,8,256]{2,1,0:T(8,128)} %bitcast.9, f32[8,8,256]{2,1,0:T(8,128)} %chg.2, f32[3,8,128]{2,1,0:T(8,128)} %bitcast.13, f32[3,1,128]{2,1,0:T(1,128)} %bitcast.15, s32[8,16]{1,0:T(8,128)} %llist_h.1, s32[1,16]{1,0:T(1,128)} %tlist_h.1), custom_call_target="tpu_custom_call" | custom-call | tf_op jit(solution)/shard_map/request/pallas_call | solution.py:176
  2.0 0.0 copy-start.6
  2.0 0.0 copy-start.5
  2.1 11.0 %all-to-all-start = ((f32[8,32,128]{2,1,0:T(8,128)}), f32[8,32,128]{2,1,0:T(8,128)S(1)}, u32[]{:S(2)}, u32[]{:S(2)}) async-start(f32[8,32,128]{2,1,0:T(8,128)} %get-tuple-element.16), calls=%async_computation | async-start | bytes 262144 | tf_op jit(solution)/shard_map/all_to_all | solution.py:450
  13.1 0.0 copy-done.6
  13.1 3.4 %collective-permute-start = (f32[48,256]{1,0:T(8,128)S(1)}, f32[48,256]{1,0:T(8,128)S(1)}, u32[]{:S(2)}, u32[]{:S(2)}) collective-permute-start(f32[48,256]{1,0:T(8,128)S(1)} %copy-done.6), channel_id=1, source_target_pairs={{0,1},{1,2},{2,3},{3,4},{4,5},{5,6},{6,7},{7,8},{8,9},{9,10},{10,1... | collective-permute-start | bytes 147464 | tf_op jit(solution)/shard_map/ppermute | solution.py:451
  16.4 0.0 copy-done.5
  16.4 7.2 %collective-permute-start.1 = (f32[48,256]{1,0:T(8,128)S(1)}, f32[48,256]{1,0:T(8,128)S(1)}, u32[]{:S(2)}, u32[]{:S(2)}) collective-permute-start(f32[48,256]{1,0:T(8,128)S(1)} %copy-done.5), channel_id=1, source_target_pairs={{1,0},{2,1},{3,2},{4,3},{5,4},{6,5},{7,6},{8,7},{9,8},{10,9},{11,1... | collective-permute-start | bytes 147464 | tf_op jit(solution)/shard_map/ppermute | solution.py:452
  23.6 2.9 %weights.1 = f32[8,104,128]{2,1,0:T(8,128)} custom-call(f32[8,8,256]{2,1,0:T(8,128)} %chg.2, f32[8,128,256]{2,1,0:T(8,128)} %up.1, f32[3,8,128]{2,1,0:T(8,128)} %bitcast.14, f32[8,128,128]{2,1,0:T(8,128)} %utm.1, f32[3,1,128]{2,1,0:T(1,128)} %bitcast.16), custom_call_target="tpu_custom_call" | custom-call | flops 50000000 | bytes 8000000 | tf_op jit(solution)/shard_map/weights/pallas_call | solution.py:213
  26.5 0.0 copy-start.2
  26.5 0.0 copy-start.3
  26.5 0.0 copy-start.4
  26.5 0.0 collective-permute-done.before
  26.5 0.0 collective-permute-done.1.after
  26.6 0.0 all-to-all-done
  26.6 4.9 %all-to-all-start.1 = ((f32[8,104,128]{2,1,0:T(8,128)}), f32[8,104,128]{2,1,0:T(8,128)S(1)}, u32[]{:S(2)}, u32[]{:S(2)}) async-start(f32[8,104,128]{2,1,0:T(8,128)} %weights.1), calls=%async_computation.1 | async-start | bytes 851968 | tf_op jit(solution)/shard_map/all_to_all | solution.py:455
  31.5 0.0 copy-done.2
  31.5 0.0 copy-done.3
  31.5 0.0 copy-done.4
  31.5 5.6 %near.2.near1 = f32[4,8,256]{2,1,0:T(8,128)S(1)} custom-call(s32[8,9]{1,0:T(8,128)S(1)} %copy-done.4, f32[3,8,256]{2,1,0:T(8,128)S(1)} %bitcast.10, f32[8,8,256]{2,1,0:T(8,128)S(1)} %copy-done.2, f32[48,256]{1,0:T(8,128)S(1)} %collective-permute-done.before, f32[48,256]{1,0:T(8,128)S(1)} %collective-permute-done.1.after), custom_call_target="tpu_custom_call" | custom-call | flops 2359296000 | bytes 300000 | tf_op jit(solution)/shard_map/near/pallas_call | solution.py:269
  37.1 7.6 %all-to-all-done.1.src = f32[8,104,128]{2,1,0:T(8,128)S(1)} async-done(((f32[8,104,128]{2,1,0:T(8,128)}), f32[8,104,128]{2,1,0:T(8,128)S(1)}, u32[]{:S(2)}, u32[]{:S(2)}) %all-to-all-start.1) | async-done | bytes 426016 | tf_op jit(solution)/shard_map/all_to_all | solution.py:455
  44.7 0.8 broadcast_in_dim.8
  45.6 7.4 %all-to-all-start.2 = ((f32[8,128,128]{2,1,0:T(8,128)}), f32[8,128,128]{2,1,0:T(8,128)S(1)}, u32[]{:S(2)}, u32[]{:S(2)}) async-start(f32[8,128,128]{2,1,0:T(8,128)} %broadcast_in_dim.8), calls=%async_computation.2 | async-start | bytes 1048576 | tf_op jit(solution)/shard_map/all_to_all | solution.py:460
  53.0 7.6 %far_leaf.1.part = f32[8,9,8,128]{3,2,1,0:T(8,128)S(1)} custom-call(s32[8,2,128]{2,1,0:T(2,128)S(1)} %slice_convert_fusion.req, f32[8,104,128]{2,1,0:T(8,128)S(1)} %all-to-all-done.1.src, f32[256,128]{1,0:T(8,128)S(1)} %bitcast.7), custom_call_target="tpu_custom_call" | custom-call | flops 2097152000 | bytes 900000 | tf_op jit(solution)/shard_map/far_leaf/pallas_call | solution.py:377
  60.6 1.9 %all-to-all-done.2 = f32[8,128,128]{2,1,0:T(8,128)S(1)} async-done(((f32[8,128,128]{2,1,0:T(8,128)}), f32[8,128,128]{2,1,0:T(8,128)S(1)}, u32[]{:S(2)}, u32[]{:S(2)}) %all-to-all-start.2) | async-done | bytes 524320 | tf_op jit(solution)/shard_map/all_to_all | solution.py:460
  62.4 2.7 %far_top.1 = f32[8,9,8,128]{3,2,1,0:T(8,128)} custom-call(s32[8,2,128]{2,1,0:T(2,128)S(1)} %slice_convert_fusion.req, f32[1024,128]{1,0:T(8,128)S(1)} %bitcast.6, f32[256,128]{1,0:T(8,128)S(1)} %bitcast.8, f32[8,9,8,128]{3,2,1,0:T(8,128)S(1)} %far_leaf.1.part), custom_call_target="tpu_custom_call" | custom-call | tf_op jit(solution)/shard_map/far_top/pallas_call | solution.py:407
  65.1 5.3 %all-to-all-start.3 = ((f32[8,9,8,128]{3,2,1,0:T(8,128)}), f32[8,9,8,128]{3,2,1,0:T(8,128)S(1)}, u32[]{:S(2)}, u32[]{:S(2)}) async-start(f32[8,9,8,128]{3,2,1,0:T(8,128)} %far_top.1), calls=%async_computation.3 | async-start | bytes 589824 | tf_op jit(solution)/shard_map/all_to_all | solution.py:464
  70.4 0.0 copy-start.1
  70.4 5.6 %near.3.near2 = f32[4,8,256]{2,1,0:T(8,128)S(1)} custom-call(s32[8,9]{1,0:T(8,128)S(1)} %copy-done.4, f32[3,8,256]{2,1,0:T(8,128)S(1)} %bitcast.11, f32[8,8,256]{2,1,0:T(8,128)S(1)} %copy-done.2, f32[48,256]{1,0:T(8,128)S(1)} %collective-permute-done.before, f32[48,256]{1,0:T(8,128)S(1)} %collective-permute-done.1.after), custom_call_target="tpu_custom_call" | custom-call | flops 2359296000 | bytes 300000 | tf_op jit(solution)/shard_map/near/pallas_call | solution.py:269
  76.0 7.5 %all-to-all-done.3.got = f32[8,9,8,128]{3,2,1,0:T(8,128)S(1)} async-done(((f32[8,9,8,128]{3,2,1,0:T(8,128)}), f32[8,9,8,128]{3,2,1,0:T(8,128)S(1)}, u32[]{:S(2)}, u32[]{:S(2)}) %all-to-all-start.3) | async-done | bytes 294944 | tf_op jit(solution)/shard_map/all_to_all | solution.py:464
  83.4 0.0 copy-done.1
  83.4 1.2 %final.1 = f32[8,8,256]{2,1,0:T(8,128)} custom-call(f32[8,9,8,128]{3,2,1,0:T(8,128)S(1)} %all-to-all-done.3.got, f32[8,128,128]{2,1,0:T(8,128)S(1)} %copy-done.1, f32[8,128,256]{2,1,0:T(8,128)S(1)} %copy-done, f32[4,8,256]{2,1,0:T(8,128)S(1)} %near.2.near1, f32[4,8,256]{2,1,0:T(8,128)S(1)} %near.3.near2), custom_call_target="tpu_custom_call" | custom-call | tf_op jit(solution)/shard_map/final/pallas_call | solution.py:431
  (4 shorter events, 0.0 us)
Async XLA Ops:
  2.0 11.0 %copy-start.6 = (f32[48,256]{1,0:T(8,128)S(1)}, f32[48,256]{1,0:T(8,128)}, u32[]{:S(2)}) copy-start(f32[48,256]{1,0:T(8,128)} %get-tuple-element.17) | copy-start | bytes 147460
  2.0 14.4 %copy-start.5 = (f32[48,256]{1,0:T(8,128)S(1)}, f32[48,256]{1,0:T(8,128)}, u32[]{:S(2)}) copy-start(f32[48,256]{1,0:T(8,128)} %get-tuple-element.18) | copy-start | bytes 147460
  2.1 24.5 %all-to-all-start = ((f32[8,32,128]{2,1,0:T(8,128)}), f32[8,32,128]{2,1,0:T(8,128)S(1)}, u32[]{:S(2)}, u32[]{:S(2)}) async-start(f32[8,32,128]{2,1,0:T(8,128)} %get-tuple-element.16), calls=%async_computation | async-start | bytes 262144 | tf_op jit(solution)/shard_map/all_to_all | solution.py:450
  13.1 13.5 %collective-permute-start = (f32[48,256]{1,0:T(8,128)S(1)}, f32[48,256]{1,0:T(8,128)S(1)}, u32[]{:S(2)}, u32[]{:S(2)}) collective-permute-start(f32[48,256]{1,0:T(8,128)S(1)} %copy-done.6), channel_id=1, source_target_pairs={{0,1},{1,2},{2,3},{3,4},{4,5},{5,6},{6,7},{7,8},{8,9},{9,10},{10,1... | collective-permute-start | bytes 147464 | tf_op jit(solution)/shard_map/ppermute | solution.py:451
  16.4 10.1 %collective-permute-start.1 = (f32[48,256]{1,0:T(8,128)S(1)}, f32[48,256]{1,0:T(8,128)S(1)}, u32[]{:S(2)}, u32[]{:S(2)}) collective-permute-start(f32[48,256]{1,0:T(8,128)S(1)} %copy-done.5), channel_id=1, source_target_pairs={{1,0},{2,1},{3,2},{4,3},{5,4},{6,5},{7,6},{8,7},{9,8},{10,9},{11,1... | collective-permute-start | bytes 147464 | tf_op jit(solution)/shard_map/ppermute | solution.py:452
  26.5 5.0 %copy-start.2 = (f32[8,8,256]{2,1,0:T(8,128)S(1)}, f32[8,8,256]{2,1,0:T(8,128)}, u32[]{:S(2)}) copy-start(f32[8,8,256]{2,1,0:T(8,128)} %chg.2) | copy-start | bytes 196612
  26.5 5.0 %copy-start.3 = (f32[8,3,256]{2,0,1:T(8,128)S(1)}, f32[8,3,256]{2,0,1:T(8,128)}, u32[]{:S(2)}) copy-start(f32[8,3,256]{2,0,1:T(8,128)} %param.9) | copy-start | bytes 73732
  26.5 5.0 %copy-start.4 = (s32[8,9]{1,0:T(8,128)S(1)}, s32[8,9]{1,0:T(8,128)}, u32[]{:S(2)}) copy-start(s32[8,9]{1,0:T(8,128)} %ids.3) | copy-start | bytes 868
  26.6 18.2 %all-to-all-start.1 = ((f32[8,104,128]{2,1,0:T(8,128)}), f32[8,104,128]{2,1,0:T(8,128)S(1)}, u32[]{:S(2)}, u32[]{:S(2)}) async-start(f32[8,104,128]{2,1,0:T(8,128)} %weights.1), calls=%async_computation.1 | async-start | bytes 851968 | tf_op jit(solution)/shard_map/all_to_all | solution.py:455
  45.6 16.9 %all-to-all-start.2 = ((f32[8,128,128]{2,1,0:T(8,128)}), f32[8,128,128]{2,1,0:T(8,128)S(1)}, u32[]{:S(2)}, u32[]{:S(2)}) async-start(f32[8,128,128]{2,1,0:T(8,128)} %broadcast_in_dim.8), calls=%async_computation.2 | async-start | bytes 1048576 | tf_op jit(solution)/shard_map/all_to_all | solution.py:460
  65.1 18.3 %all-to-all-start.3 = ((f32[8,9,8,128]{3,2,1,0:T(8,128)}), f32[8,9,8,128]{3,2,1,0:T(8,128)S(1)}, u32[]{:S(2)}, u32[]{:S(2)}) async-start(f32[8,9,8,128]{3,2,1,0:T(8,128)} %far_top.1), calls=%async_computation.3 | async-start | bytes 589824 | tf_op jit(solution)/shard_map/all_to_all | solution.py:464
  70.4 13.1 %copy-start = (f32[8,128,256]{2,1,0:T(8,128)S(1)}, f32[8,128,256]{2,1,0:T(8,128)}, u32[]{:S(2)}) copy-start(f32[8,128,256]{2,1,0:T(8,128)} %up.1) | copy-start | bytes 3145732
  70.4 13.1 %copy-start.1 = (f32[8,128,128]{2,1,0:T(8,128)S(1)}, f32[8,128,128]{2,1,0:T(8,128)}, u32[]{:S(2)}) copy-start(f32[8,128,128]{2,1,0:T(8,128)} %utm.1) | copy-start | bytes 1572868

commit v5 on v4

--- a/solution.py
+++ b/solution.py
@@ -19,6 +19,9 @@
 NBR = 9
 PAIRS = 8
 DUMMY = 64
+CHUNK = 8
+EARLY = 32
+NEAR_DUMMY = 16
 
 SMEM = pl.BlockSpec(memory_space=pltpu.SMEM)
 HBM = pl.BlockSpec(memory_space=pltpu.HBM)
@@ -223,66 +226,107 @@
     )(chg, up, skel, utm, cpts)
 
 
-def near_kernel(lo, hi, ids, pts, chg, before, after, out, fs, ft, vals, xyz, ts, tl):
+def near_blocks(ids, flat, base, early):
+    pos = jnp.int32(0)
+    seen = jnp.int32(0)
+    for l in range(OWN):
+        for n in range(NBR):
+            ident = ids[l, n]
+            e = ident - base
+            own = (e >= REACH) & (e < REACH + OWN)
+            first = own & (seen < EARLY)
+            flat[pos] = l * 32 + e
+            take = first if early else (ident >= 0) & jnp.logical_not(first)
+            pos = pos + take.astype(jnp.int32)
+            seen = seen + own.astype(jnp.int32)
+    for u in range(CHUNK):
+        flat[pos + u] = NEAR_DUMMY
+    return pos
+
+
+def near_setup(sources, xyz, vals_of, fs, ft, vals, ts, tl):
+    s0, s1, t0, t1, t2 = dense_features(xyz)
+    load0, load1 = spread(s0, ts.at[0]), spread(s1, tl)
+    for e in sources:
+        a, b = load0(e), load1(e)
+        fs[e] = jnp.concatenate([a, b, a, b], 0).T.astype(BF16)
+        vals[e] = two_halves(vals_of(e))
+    vals[NEAR_DUMMY] = jnp.zeros((16, 256), BF16)
+    fs[NEAR_DUMMY] = jnp.zeros((256, FEAT), BF16)
+    load0, load1, load2 = spread(t0, ts.at[1]), spread(t1, ts.at[2]), spread(t2, ts.at[3])
+    for l in range(OWN):
+        e = l + REACH
+        one = load1(e)
+        ft[l, 0:16, :] = jnp.concatenate([load0(e), load2(e)], 0).astype(BF16)
+        ft[l, 16:32, :] = jnp.concatenate([one, one], 0).astype(BF16)
+
+
+def near_run(count, flat, out, fs, ft, vals):
+    out[...] = jnp.zeros_like(out)
+
+    def chunk(i, carry):
+        for u in range(CHUNK):
+            code = flat[i * CHUNK + u]
+            l, e = code >> 5, code & 31
+            r = product(fs[e], ft[l], vals[e])
+            out[l] += r[0:8] + r[8:16]
+        return carry
+
+    lax.fori_loop(0, (count + CHUNK - 1) // CHUNK, chunk, 0)
+
+
+def near_base():
     me = (lax.axis_index("g") * lax.axis_size("y") + lax.axis_index("y")) * lax.axis_size("z") + lax.axis_index("z")
-    base = me * OWN - REACH
+    return me * OWN - REACH
+
+
+def near_early_kernel(ids, pts, chg, out, flat, fs, ft, vals, xyz, ts, tl):
+    count = near_blocks(ids, flat, near_base(), True)
+    for c in range(3):
+        xyz[c] = jnp.zeros((16, 256), F32)
+        xyz[c, 4:12, :] = pts[c]
+    own = range(REACH, REACH + OWN)
+    near_setup(own, [xyz[0], xyz[1], xyz[2]], lambda e: chg[e - REACH], fs, ft, vals, ts, tl)
+    near_run(count, flat, out, fs, ft, vals)
+
+
+def near_late_kernel(ids, pts, chg, before, after, out, flat, fs, ft, vals, xyz, ts, tl):
+    count = near_blocks(ids, flat, near_base(), False)
     for c in range(3):
         xyz[c, 0:4, :] = before[32 + 4 * c : 36 + 4 * c, :]
         xyz[c, 4:12, :] = pts[c]
         xyz[c, 12:16, :] = after[32 + 4 * c : 36 + 4 * c, :]
-    s0, s1, t0, t1, t2 = dense_features([xyz[0], xyz[1], xyz[2]])
-    s0 = spread(s0, ts)
-    s1 = spread(s1, tl)
-    for e in range(lo, hi + 2 * REACH):
-        a, b = s0(e), s1(e)
-        fs[e - lo] = jnp.concatenate([a, b, a, b], 0).T.astype(BF16)
+
+    def vals_of(e):
         if e < REACH:
-            c = before[8 * e : 8 * e + 8, :]
-        elif e < REACH + OWN:
-            c = chg[e - REACH]
-        else:
-            c = after[8 * (e - REACH - OWN) : 8 * (e - REACH - OWN) + 8, :]
-        vals[e - lo] = two_halves(c)
-    for i, rows in enumerate((t0, t2, t1, t1)):
-        load = spread(rows, ts)
-        for e in range(lo + REACH, hi + REACH):
-            ft[e - REACH - lo, 8 * i : 8 * i + 8, :] = load(e)
-    dead = hi - lo + 2 * REACH
-    vals[dead] = jnp.zeros((16, 256), BF16)
-
-    def leaf(i, carry):
-        tgt = ft[i].astype(BF16)
-        acc = jnp.zeros((16, 256), F32)
-        for n in range(NBR):
-            ident = ids[i + lo, n]
-            live = ident >= 0
-            e = jnp.where(live, ident - base - lo, 0)
-            acc = acc + product(fs[e], tgt, vals[jnp.where(live, e, dead)])
-        out[i] = acc[0:8] + acc[8:16]
-        return carry
-
-    lax.fori_loop(0, hi - lo, leaf, 0)
-
-
-def near_part(lo, hi, ids, pts, chg, before, after):
-    n = hi - lo
+            return before[8 * e : 8 * e + 8, :]
+        if e < REACH + OWN:
+            return chg[e - REACH]
+        return after[8 * (e - REACH - OWN) : 8 * (e - REACH - OWN) + 8, :]
+
+    near_setup(range(16), [xyz[0], xyz[1], xyz[2]], vals_of, fs, ft, vals, ts, tl)
+    near_run(count, flat, out, fs, ft, vals)
+
+
+def near_part(early, *args):
     return pl.pallas_call(
-        functools.partial(near_kernel, lo, hi),
-        in_specs=[SMEM] + [VMEM] * 4,
+        near_early_kernel if early else near_late_kernel,
+        in_specs=[SMEM] + [VMEM] * (len(args) - 1),
         out_specs=VMEM,
-        out_shape=jax.ShapeDtypeStruct((n, 8, 256), F32),
+        out_shape=jax.ShapeDtypeStruct((OWN, 8, 256), F32),
         scratch_shapes=[
-            pltpu.VMEM((n + 8, 256, FEAT), BF16),
-            pltpu.VMEM((n, FEAT, 256), F32),
-            pltpu.VMEM((n + 9, 16, 256), BF16),
+            pltpu.SMEM((OWN * NBR + CHUNK + 8,), jnp.int32),
+            pltpu.VMEM((17, 256, FEAT), BF16),
+            pltpu.VMEM((OWN, FEAT, 256), BF16),
+            pltpu.VMEM((17, 16, 256), BF16),
             pltpu.VMEM((3, 16, 256), F32),
-            pltpu.VMEM((2, 128, 128), F32),
+            pltpu.VMEM((4, 2, 128, 128), F32),
             pltpu.VMEM((2, 128, 128), F32),
         ],
-        cost_estimate=pl.CostEstimate(flops=n * 9 * 65536000, bytes_accessed=300000, transcendentals=n * 9 * 131072),
+        cost_estimate=pl.CostEstimate(flops=2000000000, bytes_accessed=300000, transcendentals=4194304),
         compiler_params=PARAMS,
         name="near",
-    )(ids, pts, chg, before, after)
+    )(*args)
 
 
 def prepare_sources(i, xyz, t0, t1, feat):
@@ -296,10 +340,11 @@
 
 def prepare_targets(i, xyz, tmp, ft):
     _, _, t0, t1, t2 = dense_features(xyz)
-    for j, rows in enumerate((t0, t2, t1, t1)):
-        load = spread(rows, tmp.at[j])
-        for l in range(8):
-            ft[8 * i + l, 8 * j : 8 * j + 8, :] = load(l)
+    load0, load1, load2 = spread(t0, tmp.at[0]), spread(t1, tmp.at[1]), spread(t2, tmp.at[2])
+    for l in range(8):
+        one = load1(l)
+        ft[8 * i + l, 0:16, :] = jnp.concatenate([load0(l), load2(l)], 0).astype(BF16)
+        ft[8 * i + l, 16:32, :] = jnp.concatenate([one, one], 0).astype(BF16)
 
 
 def flatten(req, flat, row, start, slot):
@@ -328,8 +373,8 @@
             cb = flat[i * (2 * PAIRS) + 2 * u + 1]
             ta, sa = ca >> 7, ca & 127
             tb, sb = cb >> 7, cb & 127
-            fa = ft[ta].astype(BF16)
-            fb = ft[tb].astype(BF16)
+            fa = ft[ta]
+            fb = ft[tb]
             tgt = jnp.concatenate([jnp.concatenate([fa, zero], 1), jnp.concatenate([zero, fb], 1)], 0)
             ra, rb = fs[sa], fs[sb]
             src = jnp.concatenate([ra, ra, rb, rb], 0).T.astype(BF16)
@@ -365,11 +410,11 @@
 FAR_SCRATCH = [
     pltpu.SMEM((1024 + 64,), jnp.int32),
     pltpu.VMEM((65, 16, 128), F32),
-    pltpu.VMEM((64, FEAT, 128), F32),
+    pltpu.VMEM((64, FEAT, 128), BF16),
     pltpu.VMEM((65, 16, 128), BF16),
     pltpu.VMEM((8, 1, 64, 128), F32),
     pltpu.VMEM((8, 1, 64, 128), F32),
-    pltpu.VMEM((8, 4, 1, 64, 128), F32),
+    pltpu.VMEM((8, 3, 1, 64, 128), F32),
 ]
 
 
@@ -420,11 +465,9 @@
     for d in range(1, 8):
         tot = tot + got[d]
     cell = tot[8]
-    half = near1.shape[0]
     for l in range(OWN):
         incoming = tot[l] + dot3(cell, utm[l])
-        near = near1[l] if l < half else near2[l - half]
-        out[l] = near + dot3(incoming, up[l])
+        out[l] = near1[l] + near2[l] + dot3(incoming, up[l])
 
 
 def final(got, utm, up, near1, near2):
@@ -448,21 +491,22 @@
     down = [(i + 1, i) for i in range(count - 1)]
     m0, first, last = request(pts, charges, skel, cpts, leaf_list, top_list)
     got0 = lax.all_to_all(m0, "z", 0, 0, tiled=True)
+    m1 = weights(charges, up_op, skel, utm, cpts)
+    m1, got0 = lax.optimization_barrier((m1, got0))
+    got1 = lax.all_to_all(m1, "y", 0, 0, tiled=True)
+    req = got0[:, 27:29, :].astype(jnp.int32)
+    near1 = near_part(True, near_list, pts, charges)
+    near1, first, last = lax.optimization_barrier((near1, first, last))
     before = lax.ppermute(last, every, up)
     after = lax.ppermute(first, every, down)
-    m1 = weights(charges, up_op, skel, utm, cpts)
-    m1, got0, before, after = lax.optimization_barrier((m1, got0, before, after))
-    got1 = lax.all_to_all(m1, "y", 0, 0, tiled=True)
-    req = got0[:, 27:29, :].astype(jnp.int32)
-    near1 = near_part(0, 4, near_list, pts, charges, before, after)
-    got1, near1 = lax.optimization_barrier((got1, near1))
+    got1, near1, before, after = lax.optimization_barrier((got1, near1, before, after))
     cells = jnp.broadcast_to(got1[:, 88:104, :].reshape(1, 128, 128), (8, 128, 128))
     gotg = lax.all_to_all(cells, "g", 0, 0, tiled=True)
     part = far_leaf(req, got1, got0)
     part = far_top(req, gotg, got0, part)
     part, charges2 = lax.optimization_barrier((part, charges))
     gotr = lax.all_to_all(part, "z", 0, 0, tiled=True)
-    near2 = near_part(4, 8, near_list, pts, charges2, before, after)
+    near2 = near_part(False, near_list, pts, charges2, before, after)
     return final(gotr, utm, up_op, near1, near2)
 
 

time: 85.2 us -> 84.2 us (0.988)
  the two profiles are of different devices: /device:TPU:1 before, /device:TPU:24 now
where the time goes in v5:
time: 84.2 us; the launch traced here: 83.6 us
  starting transfers between devices  38 us (45%)
  Pallas kernels  25.5 us (30%)
  waiting for transfers between devices  19.1 us (23%)
  local copies, waits for them, and re-layouts  0.87 us (1%)
    all_to_all x1, starting transfers between devices, body(): got0 = lax.all_to_all(m0, 'z', 0, 0, tiled=True)  10.3 us
    all_to_all x1, waiting for transfers between devices, body(): gotr = lax.all_to_all(part, 'z', 0, 0, tiled=True)  9.12 us
    pallas_call x2, Pallas kernels, near_part(): pl.pallas_call(near_early_kernel if early else near_late_kernel, in_specs...  8.47 us
    pallas_call x1, Pallas kernels, far_leaf(): pl.pallas_call(far_leaf_kernel, in_specs=[SMEM, VMEM, VMEM], out_specs=VM...  8.31 us
    all_to_all x1, starting transfers between devices, body(): gotr = lax.all_to_all(part, 'z', 0, 0, tiled=True)  8.14 us
    all_to_all x1, starting transfers between devices, body(): got1 = lax.all_to_all(m1, 'y', 0, 0, tiled=True)  7.32 us
    all_to_all x1, waiting for transfers between devices, body(): got0 = lax.all_to_all(m0, 'z', 0, 0, tiled=True)  6.18 us
    ppermute x1, starting transfers between devices, body(): after = lax.ppermute(first, every, down)  5.68 us
  transfers between devices with their start and end apart: 6, of which 5 were waited for; matrix products, arithmetic and copies ran while one was open for 0% of the time, Pallas kernels for 24%

profile of v5, /device:TPU:24, one launch (start us, length us, event | category | flops | bytes accessed | tf_op | source)
XLA Modules:
  0.0 83.6 jit_solution(4005625299291481930)
XLA Ops:
  0.0 2.0 %request.1 = (f32[8,32,128]{2,1,0:T(8,128)}, f32[48,256]{1,0:T(8,128)}, f32[48,256]{1,0:T(8,128)}) custom-call(f32[3,8,256]{2,1,0:T(8,128)} %bitcast.9, f32[8,8,256]{2,1,0:T(8,128)} %chg.2, f32[3,8,128]{2,1,0:T(8,128)} %bitcast.13, f32[3,1,128]{2,1,0:T(1,128)} %bitcast.15, s32[8,16]{1,0:T(8,128)} %llist_h.1, s32[1,16]{1,0:T(1,128)} %tlist_h.1), custom_call_target="tpu_custom_call" | custom-call | tf_op jit(solution)/shard_map/request/pallas_call | solution.py:179
  2.0 10.3 %all-to-all-start = ((f32[8,32,128]{2,1,0:T(8,128)}), f32[8,32,128]{2,1,0:T(8,128)S(1)}, u32[]{:S(2)}, u32[]{:S(2)}) async-start(f32[8,32,128]{2,1,0:T(8,128)} %get-tuple-element.19), calls=%async_computation | async-start | bytes 262144 | tf_op jit(solution)/shard_map/all_to_all | solution.py:493
  12.4 2.9 %weights.1 = f32[8,104,128]{2,1,0:T(8,128)} custom-call(f32[8,8,256]{2,1,0:T(8,128)} %chg.2, f32[8,128,256]{2,1,0:T(8,128)} %up.1, f32[3,8,128]{2,1,0:T(8,128)} %bitcast.14, f32[8,128,128]{2,1,0:T(8,128)} %utm.1, f32[3,1,128]{2,1,0:T(1,128)} %bitcast.16), custom_call_target="tpu_custom_call" | custom-call | flops 50000000 | bytes 8000000 | tf_op jit(solution)/shard_map/weights/pallas_call | solution.py:216
  15.2 0.0 copy-start.2
  15.3 0.0 copy-start.3
  15.3 0.0 copy-start.4
  15.3 6.2 %all-to-all-done = f32[8,32,128]{2,1,0:T(8,128)S(1)} async-done(((f32[8,32,128]{2,1,0:T(8,128)}), f32[8,32,128]{2,1,0:T(8,128)S(1)}, u32[]{:S(2)}, u32[]{:S(2)}) %all-to-all-start) | async-done | bytes 131104 | tf_op jit(solution)/shard_map/all_to_all | solution.py:493
  21.5 7.3 %all-to-all-start.1 = ((f32[8,104,128]{2,1,0:T(8,128)}), f32[8,104,128]{2,1,0:T(8,128)S(1)}, u32[]{:S(2)}, u32[]{:S(2)}) async-start(f32[8,104,128]{2,1,0:T(8,128)} %weights.1), calls=%async_computation.1 | async-start | bytes 851968 | tf_op jit(solution)/shard_map/all_to_all | solution.py:496
  28.8 0.0 copy-done.2
  28.8 0.0 copy-done.3
  28.8 0.0 copy-done.4
  28.8 0.0 copy-start.6
  28.8 0.0 copy-start.5
  28.8 5.2 %near.2.near1 = f32[8,8,256]{2,1,0:T(8,128)S(1)} custom-call(s32[8,9]{1,0:T(8,128)S(1)} %copy-done.4, f32[3,8,256]{2,1,0:T(8,128)S(1)} %bitcast.10, f32[8,8,256]{2,1,0:T(8,128)S(1)} %copy-done.2), custom_call_target="tpu_custom_call" | custom-call | flops 2000000000 | bytes 300000 | tf_op jit(solution)/shard_map/near/pallas_call | solution.py:312
  34.1 0.0 copy-done.6
  34.1 2.3 %collective-permute-start = (f32[48,256]{1,0:T(8,128)S(1)}, f32[48,256]{1,0:T(8,128)S(1)}, u32[]{:S(2)}, u32[]{:S(2)}) collective-permute-start(f32[48,256]{1,0:T(8,128)S(1)} %copy-done.6), channel_id=1, source_target_pairs={{0,1},{1,2},{2,3},{3,4},{4,5},{5,6},{6,7},{7,8},{8,9},{9,10},{10,1... | collective-permute-start | bytes 147464 | tf_op jit(solution)/shard_map/ppermute | solution.py:500
  36.4 0.0 copy-done.5
  36.4 5.7 %collective-permute-start.1 = (f32[48,256]{1,0:T(8,128)S(1)}, f32[48,256]{1,0:T(8,128)S(1)}, u32[]{:S(2)}, u32[]{:S(2)}) collective-permute-start(f32[48,256]{1,0:T(8,128)S(1)} %copy-done.5), channel_id=1, source_target_pairs={{1,0},{2,1},{3,2},{4,3},{5,4},{6,5},{7,6},{8,7},{9,8},{10,9},{11,1... | collective-permute-start | bytes 147464 | tf_op jit(solution)/shard_map/ppermute | solution.py:501
  42.1 0.1 collective-permute-done.before
  42.2 1.6 %collective-permute-done.1.after = f32[48,256]{1,0:T(8,128)S(1)} collective-permute-done((f32[48,256]{1,0:T(8,128)S(1)}, f32[48,256]{1,0:T(8,128)S(1)}, u32[]{:S(2)}, u32[]{:S(2)}) %collective-permute-start.1) | collective-permute-done | bytes 49184 | tf_op jit(solution)/shard_map/ppermute | solution.py:501
  43.8 0.0 all-to-all-done.1.src
  43.8 0.8 broadcast_in_dim.8
  44.6 4.3 %all-to-all-start.2 = ((f32[8,128,128]{2,1,0:T(8,128)}), f32[8,128,128]{2,1,0:T(8,128)S(1)}, u32[]{:S(2)}, u32[]{:S(2)}) async-start(f32[8,128,128]{2,1,0:T(8,128)} %broadcast_in_dim.8), calls=%async_computation.2 | async-start | bytes 1048576 | tf_op jit(solution)/shard_map/all_to_all | solution.py:504
  48.9 8.3 %far_leaf.1.part = f32[8,9,8,128]{3,2,1,0:T(8,128)S(1)} custom-call(s32[8,2,128]{2,1,0:T(2,128)S(1)} %slice_convert_fusion.req, f32[8,104,128]{2,1,0:T(8,128)S(1)} %all-to-all-done.1.src, f32[256,128]{1,0:T(8,128)S(1)} %bitcast.7), custom_call_target="tpu_custom_call" | custom-call | flops 2097152000 | bytes 900000 | tf_op jit(solution)/shard_map/far_leaf/pallas_call | solution.py:422
  57.2 2.0 %all-to-all-done.2 = f32[8,128,128]{2,1,0:T(8,128)S(1)} async-done(((f32[8,128,128]{2,1,0:T(8,128)}), f32[8,128,128]{2,1,0:T(8,128)S(1)}, u32[]{:S(2)}, u32[]{:S(2)}) %all-to-all-start.2) | async-done | bytes 524320 | tf_op jit(solution)/shard_map/all_to_all | solution.py:504
  59.3 2.6 %far_top.1 = f32[8,9,8,128]{3,2,1,0:T(8,128)} custom-call(s32[8,2,128]{2,1,0:T(2,128)S(1)} %slice_convert_fusion.req, f32[1024,128]{1,0:T(8,128)S(1)} %bitcast.6, f32[256,128]{1,0:T(8,128)S(1)} %bitcast.8, f32[8,9,8,128]{3,2,1,0:T(8,128)S(1)} %far_leaf.1.part), custom_call_target="tpu_custom_call" | custom-call | tf_op jit(solution)/shard_map/far_top/pallas_call | solution.py:452
  61.9 8.1 %all-to-all-start.3 = ((f32[8,9,8,128]{3,2,1,0:T(8,128)}), f32[8,9,8,128]{3,2,1,0:T(8,128)S(1)}, u32[]{:S(2)}, u32[]{:S(2)}) async-start(f32[8,9,8,128]{3,2,1,0:T(8,128)} %far_top.1), calls=%async_computation.3 | async-start | bytes 589824 | tf_op jit(solution)/shard_map/all_to_all | solution.py:508
  70.1 0.0 copy-start.1
  70.1 3.2 %near.3.near2 = f32[8,8,256]{2,1,0:T(8,128)S(1)} custom-call(s32[8,9]{1,0:T(8,128)S(1)} %copy-done.4, f32[3,8,256]{2,1,0:T(8,128)S(1)} %bitcast.11, f32[8,8,256]{2,1,0:T(8,128)S(1)} %copy-done.2, f32[48,256]{1,0:T(8,128)S(1)} %collective-permute-done.before, f32[48,256]{1,0:T(8,128)S(1)} %collective-permute-done.1.after), custom_call_target="tpu_custom_call" | custom-call | flops 2000000000 | bytes 300000 | tf_op jit(solution)/shard_map/near/pallas_call | solution.py:312
  73.3 9.1 %all-to-all-done.3.got = f32[8,9,8,128]{3,2,1,0:T(8,128)S(1)} async-done(((f32[8,9,8,128]{3,2,1,0:T(8,128)}), f32[8,9,8,128]{3,2,1,0:T(8,128)S(1)}, u32[]{:S(2)}, u32[]{:S(2)}) %all-to-all-start.3) | async-done | bytes 294944 | tf_op jit(solution)/shard_map/all_to_all | solution.py:508
  82.4 0.0 copy-done.1
  82.4 1.2 %final.1 = f32[8,8,256]{2,1,0:T(8,128)} custom-call(f32[8,9,8,128]{3,2,1,0:T(8,128)S(1)} %all-to-all-done.3.got, f32[8,128,128]{2,1,0:T(8,128)S(1)} %copy-done.1, f32[8,128,256]{2,1,0:T(8,128)S(1)} %copy-done, f32[8,8,256]{2,1,0:T(8,128)S(1)} %near.2.near1, f32[8,8,256]{2,1,0:T(8,128)S(1)} %near.3.near2), custom_call_target="tpu_custom_call" | custom-call | tf_op jit(solution)/shard_map/final/pallas_call | solution.py:474
  (4 shorter events, 0.0 us)
Async XLA Ops:
  2.0 19.4 %all-to-all-start = ((f32[8,32,128]{2,1,0:T(8,128)}), f32[8,32,128]{2,1,0:T(8,128)S(1)}, u32[]{:S(2)}, u32[]{:S(2)}) async-start(f32[8,32,128]{2,1,0:T(8,128)} %get-tuple-element.19), calls=%async_computation | async-start | bytes 262144 | tf_op jit(solution)/shard_map/all_to_all | solution.py:493
  15.2 13.5 %copy-start.2 = (f32[8,8,256]{2,1,0:T(8,128)S(1)}, f32[8,8,256]{2,1,0:T(8,128)}, u32[]{:S(2)}) copy-start(f32[8,8,256]{2,1,0:T(8,128)} %chg.2) | copy-start | bytes 196612
  15.3 13.5 %copy-start.3 = (f32[8,3,256]{2,0,1:T(8,128)S(1)}, f32[8,3,256]{2,0,1:T(8,128)}, u32[]{:S(2)}) copy-start(f32[8,3,256]{2,0,1:T(8,128)} %param.9) | copy-start | bytes 73732
  15.3 13.5 %copy-start.4 = (s32[8,9]{1,0:T(8,128)S(1)}, s32[8,9]{1,0:T(8,128)}, u32[]{:S(2)}) copy-start(s32[8,9]{1,0:T(8,128)} %ids.3) | copy-start | bytes 868
  21.5 22.3 %all-to-all-start.1 = ((f32[8,104,128]{2,1,0:T(8,128)}), f32[8,104,128]{2,1,0:T(8,128)S(1)}, u32[]{:S(2)}, u32[]{:S(2)}) async-start(f32[8,104,128]{2,1,0:T(8,128)} %weights.1), calls=%async_computation.1 | async-start | bytes 851968 | tf_op jit(solution)/shard_map/all_to_all | solution.py:496
  28.8 5.3 %copy-start.6 = (f32[48,256]{1,0:T(8,128)S(1)}, f32[48,256]{1,0:T(8,128)}, u32[]{:S(2)}) copy-start(f32[48,256]{1,0:T(8,128)} %get-tuple-element.25) | copy-start | bytes 147460
  28.8 7.6 %copy-start.5 = (f32[48,256]{1,0:T(8,128)S(1)}, f32[48,256]{1,0:T(8,128)}, u32[]{:S(2)}) copy-start(f32[48,256]{1,0:T(8,128)} %get-tuple-element.26) | copy-start | bytes 147460
  34.1 8.1 %collective-permute-start = (f32[48,256]{1,0:T(8,128)S(1)}, f32[48,256]{1,0:T(8,128)S(1)}, u32[]{:S(2)}, u32[]{:S(2)}) collective-permute-start(f32[48,256]{1,0:T(8,128)S(1)} %copy-done.6), channel_id=1, source_target_pairs={{0,1},{1,2},{2,3},{3,4},{4,5},{5,6},{6,7},{7,8},{8,9},{9,10},{10,1... | collective-permute-start | bytes 147464 | tf_op jit(solution)/shard_map/ppermute | solution.py:500
  36.4 7.4 %collective-permute-start.1 = (f32[48,256]{1,0:T(8,128)S(1)}, f32[48,256]{1,0:T(8,128)S(1)}, u32[]{:S(2)}, u32[]{:S(2)}) collective-permute-start(f32[48,256]{1,0:T(8,128)S(1)} %copy-done.5), channel_id=1, source_target_pairs={{1,0},{2,1},{3,2},{4,3},{5,4},{6,5},{7,6},{8,7},{9,8},{10,9},{11,1... | collective-permute-start | bytes 147464 | tf_op jit(solution)/shard_map/ppermute | solution.py:501
  44.6 14.6 %all-to-all-start.2 = ((f32[8,128,128]{2,1,0:T(8,128)}), f32[8,128,128]{2,1,0:T(8,128)S(1)}, u32[]{:S(2)}, u32[]{:S(2)}) async-start(f32[8,128,128]{2,1,0:T(8,128)} %broadcast_in_dim.8), calls=%async_computation.2 | async-start | bytes 1048576 | tf_op jit(solution)/shard_map/all_to_all | solution.py:504
  61.9 20.5 %all-to-all-start.3 = ((f32[8,9,8,128]{3,2,1,0:T(8,128)}), f32[8,9,8,128]{3,2,1,0:T(8,128)S(1)}, u32[]{:S(2)}, u32[]{:S(2)}) async-start(f32[8,9,8,128]{3,2,1,0:T(8,128)} %far_top.1), calls=%async_computation.3 | async-start | bytes 589824 | tf_op jit(solution)/shard_map/all_to_all | solution.py:508
  70.1 12.4 %copy-start = (f32[8,128,256]{2,1,0:T(8,128)S(1)}, f32[8,128,256]{2,1,0:T(8,128)}, u32[]{:S(2)}) copy-start(f32[8,128,256]{2,1,0:T(8,128)} %up.1) | copy-start | bytes 3145732
  70.1 12.4 %copy-start.1 = (f32[8,128,128]{2,1,0:T(8,128)S(1)}, f32[8,128,128]{2,1,0:T(8,128)}, u32[]{:S(2)}) copy-start(f32[8,128,128]{2,1,0:T(8,128)} %utm.1) | copy-start | bytes 1572868

commit v6 on v5

--- a/solution.py
+++ b/solution.py
@@ -20,7 +20,7 @@
 PAIRS = 8
 DUMMY = 64
 CHUNK = 8
-EARLY = 32
+EARLY = 48
 NEAR_DUMMY = 16
 
 SMEM = pl.BlockSpec(memory_space=pltpu.SMEM)
@@ -391,73 +391,94 @@
     vals[DUMMY] = jnp.zeros((16, 128), BF16)
 
 
-def far_leaf_kernel(req, src, tgt, out, flat, fs, ft, vals, t0, t1, t2):
+def far_prep_kernel(req, tgt, ft, ftop, leaf_flat, top_flat, counts, tmp):
+    for d in range(8):
+        prepare_targets(d, [tgt[32 * d + 8 * c : 32 * d + 8 * c + 8, :] for c in range(3)], tmp.at[d], ft)
+    prepare_targets(0, [tgt[pl.ds(24 + c, 8, stride=32), :] for c in range(3)], tmp.at[8], ftop)
+    counts[0] = flatten(req, leaf_flat, 0, 0, 0)
+    counts[1] = flatten(req, top_flat, 1, 16, 1)
+
+
+def far_prep(req, tgt):
+    sd = jax.ShapeDtypeStruct
+    return pl.pallas_call(
+        far_prep_kernel,
+        in_specs=[SMEM, VMEM],
+        out_specs=[VMEM, VMEM, SMEM, SMEM, SMEM],
+        out_shape=[
+            sd((64, FEAT, 128), BF16),
+            sd((8, FEAT, 128), BF16),
+            sd((1024 + 64,), jnp.int32),
+            sd((256,), jnp.int32),
+            sd((2,), jnp.int32),
+        ],
+        scratch_shapes=[pltpu.VMEM((9, 3, 1, 64, 128), F32)],
+        cost_estimate=pl.CostEstimate(flops=100000000, bytes_accessed=900000, transcendentals=0),
+        compiler_params=PARAMS,
+        name="far_prep",
+    )(req, tgt.reshape(256, 128))
+
+
+def far_leaf_kernel(counts, flat, src, ft, out, fs, vals, t0, t1):
     for y in range(8):
         prepare_sources(y, [src[y, 64 + 8 * c : 72 + 8 * c, :] for c in range(3)], t0.at[y], t1.at[y], fs)
-        prepare_targets(y, [tgt[32 * y + 8 * c : 32 * y + 8 * c + 8, :] for c in range(3)], t2.at[y], ft)
         for l in range(OWN):
             vals[8 * y + l] = two_halves(src[y, 8 * l : 8 * l + 8, :])
     clear_dummy(fs, vals)
     out[...] = jnp.zeros_like(out)
-    total = flatten(req, flat, 0, 0, 0)
 
     def add(t, v):
         out[t >> 3, t & 7] += v
 
-    interact(total, flat, fs, ft, vals, add)
+    interact(counts[0], flat, fs, ft, vals, add)
 
 
 FAR_SCRATCH = [
-    pltpu.SMEM((1024 + 64,), jnp.int32),
     pltpu.VMEM((65, 16, 128), F32),
-    pltpu.VMEM((64, FEAT, 128), BF16),
     pltpu.VMEM((65, 16, 128), BF16),
     pltpu.VMEM((8, 1, 64, 128), F32),
     pltpu.VMEM((8, 1, 64, 128), F32),
-    pltpu.VMEM((8, 3, 1, 64, 128), F32),
 ]
 
 
-def far_leaf(req, src, tgt):
+def far_leaf(counts, flat, src, ft):
     return pl.pallas_call(
         far_leaf_kernel,
-        in_specs=[SMEM, VMEM, VMEM],
+        in_specs=[SMEM, SMEM, VMEM, VMEM],
         out_specs=VMEM,
         out_shape=jax.ShapeDtypeStruct((8, 9, 8, 128), F32),
         scratch_shapes=FAR_SCRATCH,
         cost_estimate=pl.CostEstimate(flops=2097152000, bytes_accessed=900000, transcendentals=4194304),
         compiler_params=PARAMS,
         name="far_leaf",
-    )(req, src, tgt.reshape(256, 128))
-
-
-def far_top_kernel(req, src, tgt, part, out, flat, fs, ft, vals, t0, t1, t2):
+    )(counts, flat, src, ft)
+
+
+def far_top_kernel(counts, flat, src, ft, part, out, fs, vals, t0, t1):
     for g in range(8):
         xyz = [src[pl.ds(128 * g + 8 + c, 8, stride=16), :] for c in range(3)]
         prepare_sources(g, xyz, t0.at[g], t1.at[g], fs)
         for y in range(8):
             vals[8 * g + y] = two_halves(src[128 * g + 16 * y : 128 * g + 16 * y + 8, :])
-    prepare_targets(0, [tgt[pl.ds(24 + c, 8, stride=32), :] for c in range(3)], t2.at[0], ft)
     clear_dummy(fs, vals)
     out[...] = part[...]
-    total = flatten(req, flat, 1, 16, 1)
 
     def add(t, v):
         out[t, 8] += v
 
-    interact(total, flat, fs, ft, vals, add)
-
-
-def far_top(req, src, tgt, part):
+    interact(counts[1], flat, fs, ft, vals, add)
+
+
+def far_top(counts, flat, src, ft, part):
     return pl.pallas_call(
         far_top_kernel,
-        in_specs=[SMEM, VMEM, VMEM, VMEM],
+        in_specs=[SMEM, SMEM, VMEM, VMEM, VMEM],
         out_specs=VMEM,
         out_shape=jax.ShapeDtypeStruct((8, 9, 8, 128), F32),
         scratch_shapes=FAR_SCRATCH,
         compiler_params=PARAMS,
         name="far_top",
-    )(req, src.reshape(1024, 128), tgt.reshape(256, 128), part)
+    )(counts, flat, src.reshape(1024, 128), ft, part)
 
 
 def final_kernel(got, utm, up, near1, near2, out):
@@ -495,18 +516,18 @@
     m1, got0 = lax.optimization_barrier((m1, got0))
     got1 = lax.all_to_all(m1, "y", 0, 0, tiled=True)
     req = got0[:, 27:29, :].astype(jnp.int32)
+    ft, ftop, leaf_flat, top_flat, counts = far_prep(req, got0)
     near1 = near_part(True, near_list, pts, charges)
-    near1, first, last = lax.optimization_barrier((near1, first, last))
+    got1, near1, ft, counts = lax.optimization_barrier((got1, near1, ft, counts))
+    cells = jnp.broadcast_to(got1[:, 88:104, :].reshape(1, 128, 128), (8, 128, 128))
+    gotg = lax.all_to_all(cells, "g", 0, 0, tiled=True)
+    part = far_leaf(counts, leaf_flat, got1, ft)
+    part = far_top(counts, top_flat, gotg, ftop, part)
+    part, first, last = lax.optimization_barrier((part, first, last))
+    gotr = lax.all_to_all(part, "z", 0, 0, tiled=True)
     before = lax.ppermute(last, every, up)
     after = lax.ppermute(first, every, down)
-    got1, near1, before, after = lax.optimization_barrier((got1, near1, before, after))
-    cells = jnp.broadcast_to(got1[:, 88:104, :].reshape(1, 128, 128), (8, 128, 128))
-    gotg = lax.all_to_all(cells, "g", 0, 0, tiled=True)
-    part = far_leaf(req, got1, got0)
-    part = far_top(req, gotg, got0, part)
-    part, charges2 = lax.optimization_barrier((part, charges))
-    gotr = lax.all_to_all(part, "z", 0, 0, tiled=True)
-    near2 = near_part(False, near_list, pts, charges2, before, after)
+    near2 = near_part(False, near_list, pts, charges, before, after)
     return final(gotr, utm, up_op, near1, near2)
 
 

time: 84.2 us -> 80.3 us (0.954)
  the two profiles are of different devices: /device:TPU:24 before, /device:TPU:1 now
where the time goes in v6:
time: 80.3 us; the launch traced here: 79.7 us
  starting transfers between devices  38.4 us (48%)
  Pallas kernels  26.7 us (33%)
  waiting for transfers between devices  13.5 us (17%)
  local copies, waits for them, and re-layouts  0.9 us (1%)
    all_to_all x1, starting transfers between devices, body(): got0 = lax.all_to_all(m0, 'z', 0, 0, tiled=True)  10.9 us
    pallas_call x2, Pallas kernels, near_part(): pl.pallas_call(near_early_kernel if early else near_late_kernel, in_specs...  8.5 us
    all_to_all x1, starting transfers between devices, body(): gotg = lax.all_to_all(cells, 'g', 0, 0, tiled=True)  8.09 us
    all_to_all x1, starting transfers between devices, body(): got1 = lax.all_to_all(m1, 'y', 0, 0, tiled=True)  6.82 us
    pallas_call x1, Pallas kernels, far_leaf(): pl.pallas_call(far_leaf_kernel, in_specs=[SMEM, SMEM, VMEM, VMEM], out_sp...  6.74 us
    ppermute x1, starting transfers between devices, body(): after = lax.ppermute(first, every, down)  5.64 us
    all_to_all x1, waiting for transfers between devices, body(): got0 = lax.all_to_all(m0, 'z', 0, 0, tiled=True)  4.84 us
    all_to_all x1, waiting for transfers between devices, body(): got1 = lax.all_to_all(m1, 'y', 0, 0, tiled=True)  4.81 us
  transfers between devices with their start and end apart: 6, of which 5 were waited for; matrix products, arithmetic and copies ran while one was open for 0% of the time, Pallas kernels for 26%

profile of v6, /device:TPU:1, one launch (start us, length us, event | category | flops | bytes accessed | tf_op | source)
XLA Modules:
  0.0 79.7 jit_solution(12954309999557558386)
XLA Ops:
  0.0 2.0 %request.1 = (f32[8,32,128]{2,1,0:T(8,128)}, f32[48,256]{1,0:T(8,128)}, f32[48,256]{1,0:T(8,128)}) custom-call(f32[3,8,256]{2,1,0:T(8,128)} %bitcast.8, f32[8,8,256]{2,1,0:T(8,128)} %chg.3, f32[3,8,128]{2,1,0:T(8,128)} %bitcast.12, f32[3,1,128]{2,1,0:T(1,128)} %bitcast.14, s32[8,16]{1,0:T(8,128)} %llist_h.1, s32[1,16]{1,0:T(1,128)} %tlist_h.1), custom_call_target="tpu_custom_call" | custom-call | tf_op jit(solution)/shard_map/request/pallas_call | solution.py:179
  2.0 10.9 %all-to-all-start = ((f32[8,32,128]{2,1,0:T(8,128)}), f32[8,32,128]{2,1,0:T(8,128)S(1)}, u32[]{:S(2)}, u32[]{:S(2)}) async-start(f32[8,32,128]{2,1,0:T(8,128)} %get-tuple-element.22), calls=%async_computation | async-start | bytes 262144 | tf_op jit(solution)/shard_map/all_to_all | solution.py:514
  12.9 2.9 %weights.1 = f32[8,104,128]{2,1,0:T(8,128)} custom-call(f32[8,8,256]{2,1,0:T(8,128)} %chg.3, f32[8,128,256]{2,1,0:T(8,128)} %up.1, f32[3,8,128]{2,1,0:T(8,128)} %bitcast.13, f32[8,128,128]{2,1,0:T(8,128)} %utm.1, f32[3,1,128]{2,1,0:T(1,128)} %bitcast.15), custom_call_target="tpu_custom_call" | custom-call | flops 50000000 | bytes 8000000 | tf_op jit(solution)/shard_map/weights/pallas_call | solution.py:216
  15.8 0.0 copy-start.2
  15.8 0.0 copy-start.3
  15.8 0.0 copy-start.4
  15.9 4.8 %all-to-all-done = f32[8,32,128]{2,1,0:T(8,128)S(1)} async-done(((f32[8,32,128]{2,1,0:T(8,128)}), f32[8,32,128]{2,1,0:T(8,128)S(1)}, u32[]{:S(2)}, u32[]{:S(2)}) %all-to-all-start) | async-done | bytes 131104 | tf_op jit(solution)/shard_map/all_to_all | solution.py:514
  20.7 6.8 %all-to-all-start.1 = ((f32[8,104,128]{2,1,0:T(8,128)}), f32[8,104,128]{2,1,0:T(8,128)S(1)}, u32[]{:S(2)}, u32[]{:S(2)}) async-start(f32[8,104,128]{2,1,0:T(8,128)} %weights.1), calls=%async_computation.1 | async-start | bytes 851968 | tf_op jit(solution)/shard_map/all_to_all | solution.py:517
  27.5 0.0 copy-done.2
  27.5 0.0 copy-done.3
  27.5 0.0 copy-done.4
  27.5 5.3 %near.2.near1 = f32[8,8,256]{2,1,0:T(8,128)S(1)} custom-call(s32[8,9]{1,0:T(8,128)S(1)} %copy-done.4, f32[3,8,256]{2,1,0:T(8,128)S(1)} %bitcast.9, f32[8,8,256]{2,1,0:T(8,128)S(1)} %copy-done.2), custom_call_target="tpu_custom_call" | custom-call | flops 2000000000 | bytes 300000 | tf_op jit(solution)/shard_map/near/pallas_call | solution.py:312
  32.8 2.4 %far_prep.1 = (bf16[64,32,128]{2,1,0:T(8,128)(2,1)S(1)}, bf16[8,32,128]{2,1,0:T(8,128)(2,1)S(1)}, s32[1088]{0:T(1024)S(1)}, s32[256]{0:T(256)S(1)}, s32[2]{0:T(128)S(1)}) custom-call(s32[8,2,128]{2,1,0:T(2,128)S(1)} %slice_convert_fusion.req, f32[256,128]{1,0:T(8,128)S(1)} %bitcast.7), custom_call_target="tpu_custom_call" | custom-call | flops 100000000 | bytes 900000 | tf_op jit(solution)/shard_map/far_prep/pallas_call | solution.py:404
  35.3 4.8 %all-to-all-done.1.src = f32[8,104,128]{2,1,0:T(8,128)S(1)} async-done(((f32[8,104,128]{2,1,0:T(8,128)}), f32[8,104,128]{2,1,0:T(8,128)S(1)}, u32[]{:S(2)}, u32[]{:S(2)}) %all-to-all-start.1) | async-done | bytes 426016 | tf_op jit(solution)/shard_map/all_to_all | solution.py:517
  40.1 0.8 %broadcast_in_dim.8 = f32[8,128,128]{2,1,0:T(8,128)} broadcast(f32[128,128]{1,0:T(8,128)S(1)} %bitcast.11), dimensions={1,2} | broadcast | bytes 589824 | tf_op jit(solution)/shard_map/broadcast_in_dim | solution.py:522
  40.9 8.1 %all-to-all-start.2 = ((f32[8,128,128]{2,1,0:T(8,128)}), f32[8,128,128]{2,1,0:T(8,128)S(1)}, u32[]{:S(2)}, u32[]{:S(2)}) async-start(f32[8,128,128]{2,1,0:T(8,128)} %broadcast_in_dim.8), calls=%async_computation.2 | async-start | bytes 1048576 | tf_op jit(solution)/shard_map/all_to_all | solution.py:523
  49.0 6.7 %far_leaf.1.part = f32[8,9,8,128]{3,2,1,0:T(8,128)S(1)} custom-call(s32[2]{0:T(128)S(1)} %get-tuple-element.27.counts, s32[1088]{0:T(1024)S(1)} %get-tuple-element.31.flat, f32[8,104,128]{2,1,0:T(8,128)S(1)} %all-to-all-done.1.src, bf16[64,32,128]{2,1,0:T(8,128)(2,1)S(1)} %get-tuple-element.32.ft), custom_call_target="tpu_custom_call" | custom-call | flops 2097152000 | bytes 900000 | tf_op jit(solution)/shard_map/far_leaf/pallas_call | solution.py:445
  55.7 2.7 %all-to-all-done.2 = f32[8,128,128]{2,1,0:T(8,128)S(1)} async-done(((f32[8,128,128]{2,1,0:T(8,128)}), f32[8,128,128]{2,1,0:T(8,128)S(1)}, u32[]{:S(2)}, u32[]{:S(2)}) %all-to-all-start.2) | async-done | bytes 524320 | tf_op jit(solution)/shard_map/all_to_all | solution.py:523
  58.5 2.9 %far_top.1 = f32[8,9,8,128]{3,2,1,0:T(8,128)} custom-call(s32[2]{0:T(128)S(1)} %get-tuple-element.27.counts, s32[256]{0:T(256)S(1)} %get-tuple-element.28.flat, f32[1024,128]{1,0:T(8,128)S(1)} %bitcast.6, bf16[8,32,128]{2,1,0:T(8,128)(2,1)S(1)} %get-tuple-element.30.ft, f32[8,9,8,128]{3,2,1,0:T(8,128)S(1)} %far_leaf.1.part), custom_call_target="tpu_custom_call" | custom-call | tf_op jit(solution)/shard_map/far_top/pallas_call | solution.py:473
  61.4 3.6 %all-to-all-start.3 = ((f32[8,9,8,128]{3,2,1,0:T(8,128)}), f32[8,9,8,128]{3,2,1,0:T(8,128)S(1)}, u32[]{:S(2)}, u32[]{:S(2)}) async-start(f32[8,9,8,128]{3,2,1,0:T(8,128)} %far_top.1), calls=%async_computation.3 | async-start | bytes 589824 | tf_op jit(solution)/shard_map/all_to_all | solution.py:527
  65.0 0.0 copy-done.6
  65.0 0.0 copy-start
  65.0 0.0 copy-start.1
  65.0 3.4 %collective-permute-start = (f32[48,256]{1,0:T(8,128)S(1)}, f32[48,256]{1,0:T(8,128)S(1)}, u32[]{:S(2)}, u32[]{:S(2)}) collective-permute-start(f32[48,256]{1,0:T(8,128)S(1)} %copy-done.6), channel_id=1, source_target_pairs={{0,1},{1,2},{2,3},{3,4},{4,5},{5,6},{6,7},{7,8},{8,9},{9,10},{10,1... | collective-permute-start | bytes 147464 | tf_op jit(solution)/shard_map/ppermute | solution.py:528
  68.4 0.0 copy-done.5
  68.4 5.6 %collective-permute-start.1 = (f32[48,256]{1,0:T(8,128)S(1)}, f32[48,256]{1,0:T(8,128)S(1)}, u32[]{:S(2)}, u32[]{:S(2)}) collective-permute-start(f32[48,256]{1,0:T(8,128)S(1)} %copy-done.5), channel_id=1, source_target_pairs={{1,0},{2,1},{3,2},{4,3},{5,4},{6,5},{7,6},{8,7},{9,8},{10,9},{11,1... | collective-permute-start | bytes 147464 | tf_op jit(solution)/shard_map/ppermute | solution.py:529
  74.1 0.5 collective-permute-done.before
  74.5 0.7 collective-permute-done.1.after
  75.2 3.2 %near.3.near2 = f32[8,8,256]{2,1,0:T(8,128)S(1)} custom-call(s32[8,9]{1,0:T(8,128)S(1)} %copy-done.4, f32[3,8,256]{2,1,0:T(8,128)S(1)} %bitcast.10, f32[8,8,256]{2,1,0:T(8,128)S(1)} %copy-done.2, f32[48,256]{1,0:T(8,128)S(1)} %collective-permute-done.before, f32[48,256]{1,0:T(8,128)S(1)} %collective-permute-done.1.after), custom_call_target="tpu_custom_call" | custom-call | flops 2000000000 | bytes 300000 | tf_op jit(solution)/shard_map/near/pallas_call | solution.py:312
  78.5 0.0 all-to-all-done.3.got
  78.5 0.0 copy-done
  78.5 1.2 %final.1 = f32[8,8,256]{2,1,0:T(8,128)} custom-call(f32[8,9,8,128]{3,2,1,0:T(8,128)S(1)} %all-to-all-done.3.got, f32[8,128,128]{2,1,0:T(8,128)S(1)} %copy-done.1, f32[8,128,256]{2,1,0:T(8,128)S(1)} %copy-done, f32[8,8,256]{2,1,0:T(8,128)S(1)} %near.2.near1, f32[8,8,256]{2,1,0:T(8,128)S(1)} %near.3.near2), custom_call_target="tpu_custom_call" | custom-call | tf_op jit(solution)/shard_map/final/pallas_call | solution.py:495
  (5 shorter events, 0.0 us)
Async XLA Ops:
  2.0 18.6 %all-to-all-start = ((f32[8,32,128]{2,1,0:T(8,128)}), f32[8,32,128]{2,1,0:T(8,128)S(1)}, u32[]{:S(2)}, u32[]{:S(2)}) async-start(f32[8,32,128]{2,1,0:T(8,128)} %get-tuple-element.22), calls=%async_computation | async-start | bytes 262144 | tf_op jit(solution)/shard_map/all_to_all | solution.py:514
  15.8 11.7 %copy-start.2 = (f32[8,8,256]{2,1,0:T(8,128)S(1)}, f32[8,8,256]{2,1,0:T(8,128)}, u32[]{:S(2)}) copy-start(f32[8,8,256]{2,1,0:T(8,128)} %chg.3) | copy-start | bytes 196612
  15.8 11.7 %copy-start.3 = (f32[8,3,256]{2,0,1:T(8,128)S(1)}, f32[8,3,256]{2,0,1:T(8,128)}, u32[]{:S(2)}) copy-start(f32[8,3,256]{2,0,1:T(8,128)} %param.9) | copy-start | bytes 73732
  15.8 11.7 %copy-start.4 = (s32[8,9]{1,0:T(8,128)S(1)}, s32[8,9]{1,0:T(8,128)}, u32[]{:S(2)}) copy-start(s32[8,9]{1,0:T(8,128)} %ids.3) | copy-start | bytes 868
  20.7 19.4 %all-to-all-start.1 = ((f32[8,104,128]{2,1,0:T(8,128)}), f32[8,104,128]{2,1,0:T(8,128)S(1)}, u32[]{:S(2)}, u32[]{:S(2)}) async-start(f32[8,104,128]{2,1,0:T(8,128)} %weights.1), calls=%async_computation.1 | async-start | bytes 851968 | tf_op jit(solution)/shard_map/all_to_all | solution.py:517
  40.9 17.6 %all-to-all-start.2 = ((f32[8,128,128]{2,1,0:T(8,128)}), f32[8,128,128]{2,1,0:T(8,128)S(1)}, u32[]{:S(2)}, u32[]{:S(2)}) async-start(f32[8,128,128]{2,1,0:T(8,128)} %broadcast_in_dim.8), calls=%async_computation.2 | async-start | bytes 1048576 | tf_op jit(solution)/shard_map/all_to_all | solution.py:523
  61.4 3.6 %copy-start.6 = (f32[48,256]{1,0:T(8,128)S(1)}, f32[48,256]{1,0:T(8,128)}, u32[]{:S(2)}) copy-start(f32[48,256]{1,0:T(8,128)} %get-tuple-element.37) | copy-start | bytes 147460
  61.4 7.0 %copy-start.5 = (f32[48,256]{1,0:T(8,128)S(1)}, f32[48,256]{1,0:T(8,128)}, u32[]{:S(2)}) copy-start(f32[48,256]{1,0:T(8,128)} %get-tuple-element.38) | copy-start | bytes 147460
  61.4 17.0 %all-to-all-start.3 = ((f32[8,9,8,128]{3,2,1,0:T(8,128)}), f32[8,9,8,128]{3,2,1,0:T(8,128)S(1)}, u32[]{:S(2)}, u32[]{:S(2)}) async-start(f32[8,9,8,128]{3,2,1,0:T(8,128)} %far_top.1), calls=%async_computation.3 | async-start | bytes 589824 | tf_op jit(solution)/shard_map/all_to_all | solution.py:527
  65.0 13.5 %copy-start = (f32[8,128,256]{2,1,0:T(8,128)S(1)}, f32[8,128,256]{2,1,0:T(8,128)}, u32[]{:S(2)}) copy-start(f32[8,128,256]{2,1,0:T(8,128)} %up.1) | copy-start | bytes 3145732
  65.0 13.5 %copy-start.1 = (f32[8,128,128]{2,1,0:T(8,128)S(1)}, f32[8,128,128]{2,1,0:T(8,128)}, u32[]{:S(2)}) copy-start(f32[8,128,128]{2,1,0:T(8,128)} %utm.1) | copy-start | bytes 1572868
  65.0 9.5 %collective-permute-start = (f32[48,256]{1,0:T(8,128)S(1)}, f32[48,256]{1,0:T(8,128)S(1)}, u32[]{:S(2)}, u32[]{:S(2)}) collective-permute-start(f32[48,256]{1,0:T(8,128)S(1)} %copy-done.6), channel_id=1, source_target_pairs={{0,1},{1,2},{2,3},{3,4},{4,5},{5,6},{6,7},{7,8},{8,9},{9,10},{10,1... | collective-permute-start | bytes 147464 | tf_op jit(solution)/shard_map/ppermute | solution.py:528
  68.4 6.8 %collective-permute-start.1 = (f32[48,256]{1,0:T(8,128)S(1)}, f32[48,256]{1,0:T(8,128)S(1)}, u32[]{:S(2)}, u32[]{:S(2)}) collective-permute-start(f32[48,256]{1,0:T(8,128)S(1)} %copy-done.5), channel_id=1, source_target_pairs={{1,0},{2,1},{3,2},{4,3},{5,4},{6,5},{7,6},{8,7},{9,8},{10,9},{11,1... | collective-permute-start | bytes 147464 | tf_op jit(solution)/shard_map/ppermute | solution.py:529

commit v7 on v6

--- a/solution.py
+++ b/solution.py
@@ -20,7 +20,6 @@
 PAIRS = 8
 DUMMY = 64
 CHUNK = 8
-EARLY = 48
 NEAR_DUMMY = 16
 
 SMEM = pl.BlockSpec(memory_space=pltpu.SMEM)
@@ -226,25 +225,21 @@
     )(chg, up, skel, utm, cpts)
 
 
-def near_blocks(ids, flat, base, early):
+def near_blocks(ids, flat, base, first_leaf, early):
     pos = jnp.int32(0)
-    seen = jnp.int32(0)
-    for l in range(OWN):
+    for l in range(first_leaf, OWN):
         for n in range(NBR):
             ident = ids[l, n]
             e = ident - base
-            own = (e >= REACH) & (e < REACH + OWN)
-            first = own & (seen < EARLY)
             flat[pos] = l * 32 + e
-            take = first if early else (ident >= 0) & jnp.logical_not(first)
+            take = (ident >= 0) & (e < REACH + OWN) if early else e >= REACH + OWN
             pos = pos + take.astype(jnp.int32)
-            seen = seen + own.astype(jnp.int32)
     for u in range(CHUNK):
-        flat[pos + u] = NEAR_DUMMY
+        flat[pos + u] = (OWN - 1) * 32 + NEAR_DUMMY
     return pos
 
 
-def near_setup(sources, xyz, vals_of, fs, ft, vals, ts, tl):
+def near_setup(sources, leaves, xyz, vals_of, fs, ft, vals, ts, tl):
     s0, s1, t0, t1, t2 = dense_features(xyz)
     load0, load1 = spread(s0, ts.at[0]), spread(s1, tl)
     for e in sources:
@@ -254,7 +249,7 @@
     vals[NEAR_DUMMY] = jnp.zeros((16, 256), BF16)
     fs[NEAR_DUMMY] = jnp.zeros((256, FEAT), BF16)
     load0, load1, load2 = spread(t0, ts.at[1]), spread(t1, ts.at[2]), spread(t2, ts.at[3])
-    for l in range(OWN):
+    for l in leaves:
         e = l + REACH
         one = load1(e)
         ft[l, 0:16, :] = jnp.concatenate([load0(e), load2(e)], 0).astype(BF16)
@@ -280,31 +275,32 @@
     return me * OWN - REACH
 
 
-def near_early_kernel(ids, pts, chg, out, flat, fs, ft, vals, xyz, ts, tl):
-    count = near_blocks(ids, flat, near_base(), True)
-    for c in range(3):
-        xyz[c] = jnp.zeros((16, 256), F32)
-        xyz[c, 4:12, :] = pts[c]
-    own = range(REACH, REACH + OWN)
-    near_setup(own, [xyz[0], xyz[1], xyz[2]], lambda e: chg[e - REACH], fs, ft, vals, ts, tl)
-    near_run(count, flat, out, fs, ft, vals)
-
-
-def near_late_kernel(ids, pts, chg, before, after, out, flat, fs, ft, vals, xyz, ts, tl):
-    count = near_blocks(ids, flat, near_base(), False)
+def near_early_kernel(ids, pts, chg, before, out, flat, fs, ft, vals, xyz, ts, tl):
+    count = near_blocks(ids, flat, near_base(), 0, True)
     for c in range(3):
         xyz[c, 0:4, :] = before[32 + 4 * c : 36 + 4 * c, :]
         xyz[c, 4:12, :] = pts[c]
+        xyz[c, 12:16, :] = jnp.zeros((4, 256), F32)
+
+    def vals_of(e):
+        return before[8 * e : 8 * e + 8, :] if e < REACH else chg[e - REACH]
+
+    near_setup(range(REACH + OWN), range(OWN), [xyz[0], xyz[1], xyz[2]], vals_of, fs, ft, vals, ts, tl)
+    near_run(count, flat, out, fs, ft, vals)
+
+
+def near_late_kernel(ids, pts, after, out, flat, fs, ft, vals, xyz, ts, tl):
+    count = near_blocks(ids, flat, near_base(), OWN - REACH, False)
+    for c in range(3):
+        xyz[c, 0:4, :] = jnp.zeros((4, 256), F32)
+        xyz[c, 4:12, :] = pts[c]
         xyz[c, 12:16, :] = after[32 + 4 * c : 36 + 4 * c, :]
 
     def vals_of(e):
-        if e < REACH:
-            return before[8 * e : 8 * e + 8, :]
-        if e < REACH + OWN:
-            return chg[e - REACH]
         return after[8 * (e - REACH - OWN) : 8 * (e - REACH - OWN) + 8, :]
 
-    near_setup(range(16), [xyz[0], xyz[1], xyz[2]], vals_of, fs, ft, vals, ts, tl)
+    halo = range(REACH + OWN, 2 * REACH + OWN)
+    near_setup(halo, range(OWN - REACH, OWN), [xyz[0], xyz[1], xyz[2]], vals_of, fs, ft, vals, ts, tl)
     near_run(count, flat, out, fs, ft, vals)
 
 
@@ -454,12 +450,31 @@
     )(counts, flat, src, ft)
 
 
+def cells_kernel(src, out):
+    for y in range(8):
+        for d in range(8):
+            out[d, 8 * y : 8 * y + 8, :] = src[y, 88:96, :]
+            for c in range(3):
+                out[d, 64 + 8 * c + y : 65 + 8 * c + y, :] = src[y, 96 + c : 97 + c, :]
+
+
+def cells_message(src):
+    return pl.pallas_call(
+        cells_kernel,
+        in_specs=[VMEM],
+        out_specs=VMEM,
+        out_shape=jax.ShapeDtypeStruct((8, 88, 128), F32),
+        compiler_params=PARAMS,
+        name="cells",
+    )(src)
+
+
 def far_top_kernel(counts, flat, src, ft, part, out, fs, vals, t0, t1):
     for g in range(8):
-        xyz = [src[pl.ds(128 * g + 8 + c, 8, stride=16), :] for c in range(3)]
+        xyz = [src[g, 64 + 8 * c : 72 + 8 * c, :] for c in range(3)]
         prepare_sources(g, xyz, t0.at[g], t1.at[g], fs)
         for y in range(8):
-            vals[8 * g + y] = two_halves(src[128 * g + 16 * y : 128 * g + 16 * y + 8, :])
+            vals[8 * g + y] = two_halves(src[g, 8 * y : 8 * y + 8, :])
     clear_dummy(fs, vals)
     out[...] = part[...]
 
@@ -478,7 +493,7 @@
         scratch_shapes=FAR_SCRATCH,
         compiler_params=PARAMS,
         name="far_top",
-    )(counts, flat, src.reshape(1024, 128), ft, part)
+    )(counts, flat, src, ft, part)
 
 
 def final_kernel(got, utm, up, near1, near2, out):
@@ -512,22 +527,21 @@
     down = [(i + 1, i) for i in range(count - 1)]
     m0, first, last = request(pts, charges, skel, cpts, leaf_list, top_list)
     got0 = lax.all_to_all(m0, "z", 0, 0, tiled=True)
+    before = lax.ppermute(last, every, up)
     m1 = weights(charges, up_op, skel, utm, cpts)
-    m1, got0 = lax.optimization_barrier((m1, got0))
+    m1, got0, before = lax.optimization_barrier((m1, got0, before))
     got1 = lax.all_to_all(m1, "y", 0, 0, tiled=True)
     req = got0[:, 27:29, :].astype(jnp.int32)
     ft, ftop, leaf_flat, top_flat, counts = far_prep(req, got0)
-    near1 = near_part(True, near_list, pts, charges)
+    near1 = near_part(True, near_list, pts, charges, before)
     got1, near1, ft, counts = lax.optimization_barrier((got1, near1, ft, counts))
-    cells = jnp.broadcast_to(got1[:, 88:104, :].reshape(1, 128, 128), (8, 128, 128))
-    gotg = lax.all_to_all(cells, "g", 0, 0, tiled=True)
+    gotg = lax.all_to_all(cells_message(got1), "g", 0, 0, tiled=True)
     part = far_leaf(counts, leaf_flat, got1, ft)
     part = far_top(counts, top_flat, gotg, ftop, part)
-    part, first, last = lax.optimization_barrier((part, first, last))
+    part, first = lax.optimization_barrier((part, first))
     gotr = lax.all_to_all(part, "z", 0, 0, tiled=True)
-    before = lax.ppermute(last, every, up)
     after = lax.ppermute(first, every, down)
-    near2 = near_part(False, near_list, pts, charges, before, after)
+    near2 = near_part(False, near_list, pts, after)
     return final(gotr, utm, up_op, near1, near2)
 
 

time: 80.3 us -> 78.3 us (0.975)
  the two profiles are of different devices: /device:TPU:1 before, /device:TPU:6 now
where the time goes in v7:
time: 78.3 us; the launch traced here: 77.6 us
  starting transfers between devices  35.3 us (45%)
  Pallas kernels  27.5 us (35%)
  waiting for transfers between devices  14.7 us (19%)
    all_to_all x1, starting transfers between devices, body(): got0 = lax.all_to_all(m0, 'z', 0, 0, tiled=True)  10.5 us
    pallas_call x2, Pallas kernels, near_part(): pl.pallas_call(near_early_kernel if early else near_late_kernel, in_specs...  9.31 us
    all_to_all x1, starting transfers between devices, body(): got1 = lax.all_to_all(m1, 'y', 0, 0, tiled=True)  6.83 us
    pallas_call x1, Pallas kernels, far_leaf(): pl.pallas_call(far_leaf_kernel, in_specs=[SMEM, SMEM, VMEM, VMEM], out_sp...  6.75 us
    ppermute x1, waiting for transfers between devices, body(): after = lax.ppermute(first, every, down)  6.65 us
    all_to_all x1, starting transfers between devices, body(): gotr = lax.all_to_all(part, 'z', 0, 0, tiled=True)  6.29 us
    all_to_all x1, starting transfers between devices, body(): gotg = lax.all_to_all(cells_message(got1), 'g', 0, 0, tiled=True)  4.78 us
    all_to_all x1, waiting for transfers between devices, body(): got1 = lax.all_to_all(m1, 'y', 0, 0, tiled=True)  4.08 us
  transfers between devices with their start and end apart: 6, of which 4 were waited for; matrix products, arithmetic and copies ran while one was open for 0% of the time, Pallas kernels for 27%

profile of v7, /device:TPU:6, one launch (start us, length us, event | category | flops | bytes accessed | tf_op | source)
XLA Modules:
  0.0 77.6 jit_solution(6512355320002593350)
XLA Ops:
  0.0 2.0 %request.1 = (f32[8,32,128]{2,1,0:T(8,128)}, f32[48,256]{1,0:T(8,128)}, f32[48,256]{1,0:T(8,128)}) custom-call(f32[3,8,256]{2,1,0:T(8,128)} %bitcast.5, f32[8,8,256]{2,1,0:T(8,128)} %chg.1, f32[3,8,128]{2,1,0:T(8,128)} %bitcast.8, f32[3,1,128]{2,1,0:T(1,128)} %bitcast.10, s32[8,16]{1,0:T(8,128)} %llist_h.1, s32[1,16]{1,0:T(1,128)} %tlist_h.1), custom_call_target="tpu_custom_call" | custom-call | tf_op jit(solution)/shard_map/request/pallas_call | solution.py:178
  2.0 0.0 copy-start.6
  2.1 10.5 %all-to-all-start = ((f32[8,32,128]{2,1,0:T(8,128)}), f32[8,32,128]{2,1,0:T(8,128)S(1)}, u32[]{:S(2)}, u32[]{:S(2)}) async-start(f32[8,32,128]{2,1,0:T(8,128)} %get-tuple-element.22), calls=%async_computation | async-start | bytes 262144 | tf_op jit(solution)/shard_map/all_to_all | solution.py:529
  12.5 0.0 copy-done.6
  12.5 3.9 %collective-permute-start = (f32[48,256]{1,0:T(8,128)S(1)}, f32[48,256]{1,0:T(8,128)S(1)}, u32[]{:S(2)}, u32[]{:S(2)}) collective-permute-start(f32[48,256]{1,0:T(8,128)S(1)} %copy-done.6), channel_id=1, source_target_pairs={{0,1},{1,2},{2,3},{3,4},{4,5},{5,6},{6,7},{7,8},{8,9},{9,10},{10,1... | collective-permute-start | bytes 147464 | tf_op jit(solution)/shard_map/ppermute | solution.py:530
  16.4 2.9 %weights.1 = f32[8,104,128]{2,1,0:T(8,128)} custom-call(f32[8,8,256]{2,1,0:T(8,128)} %chg.1, f32[8,128,256]{2,1,0:T(8,128)} %up.1, f32[3,8,128]{2,1,0:T(8,128)} %bitcast.9, f32[8,128,128]{2,1,0:T(8,128)} %utm.1, f32[3,1,128]{2,1,0:T(1,128)} %bitcast.11), custom_call_target="tpu_custom_call" | custom-call | flops 50000000 | bytes 8000000 | tf_op jit(solution)/shard_map/weights/pallas_call | solution.py:215
  19.3 2.9 %collective-permute-done.before = f32[48,256]{1,0:T(8,128)S(1)} collective-permute-done((f32[48,256]{1,0:T(8,128)S(1)}, f32[48,256]{1,0:T(8,128)S(1)}, u32[]{:S(2)}, u32[]{:S(2)}) %collective-permute-start) | collective-permute-done | bytes 49184 | tf_op jit(solution)/shard_map/ppermute | solution.py:530
  22.3 0.0 all-to-all-done
  22.3 6.8 %all-to-all-start.1 = ((f32[8,104,128]{2,1,0:T(8,128)}), f32[8,104,128]{2,1,0:T(8,128)S(1)}, u32[]{:S(2)}, u32[]{:S(2)}) async-start(f32[8,104,128]{2,1,0:T(8,128)} %weights.1), calls=%async_computation.1 | async-start | bytes 851968 | tf_op jit(solution)/shard_map/all_to_all | solution.py:533
  29.1 0.0 copy-start.2
  29.1 0.0 copy-start.3
  29.1 0.0 copy-start.4
  29.2 2.3 %far_prep.1 = (bf16[64,32,128]{2,1,0:T(8,128)(2,1)S(1)}, bf16[8,32,128]{2,1,0:T(8,128)(2,1)S(1)}, s32[1088]{0:T(1024)S(1)}, s32[256]{0:T(256)S(1)}, s32[2]{0:T(128)S(1)}) custom-call(s32[8,2,128]{2,1,0:T(2,128)S(1)} %slice_convert_fusion.req, f32[256,128]{1,0:T(8,128)S(1)} %bitcast.4), custom_call_target="tpu_custom_call" | custom-call | flops 100000000 | bytes 900000 | tf_op jit(solution)/shard_map/far_prep/pallas_call | solution.py:400
  31.5 0.0 copy-done.2
  31.5 0.0 copy-done.3
  31.5 0.0 copy-done.4
  31.5 7.4 %near.2.near1 = f32[8,8,256]{2,1,0:T(8,128)S(1)} custom-call(s32[8,9]{1,0:T(8,128)S(1)} %copy-done.4, f32[3,8,256]{2,1,0:T(8,128)S(1)} %bitcast.6, f32[8,8,256]{2,1,0:T(8,128)S(1)} %copy-done.2, f32[48,256]{1,0:T(8,128)S(1)} %collective-permute-done.before), custom_call_target="tpu_custom_call" | custom-call | flops 2000000000 | bytes 300000 | tf_op jit(solution)/shard_map/near/pallas_call | solution.py:308
  39.0 4.1 %all-to-all-done.1.src = f32[8,104,128]{2,1,0:T(8,128)S(1)} async-done(((f32[8,104,128]{2,1,0:T(8,128)}), f32[8,104,128]{2,1,0:T(8,128)S(1)}, u32[]{:S(2)}, u32[]{:S(2)}) %all-to-all-start.1) | async-done | bytes 426016 | tf_op jit(solution)/shard_map/all_to_all | solution.py:533
  43.0 0.8 %cells.1 = f32[8,88,128]{2,1,0:T(8,128)} custom-call(f32[8,104,128]{2,1,0:T(8,128)S(1)} %all-to-all-done.1.src), custom_call_target="tpu_custom_call" | custom-call | tf_op jit(solution)/shard_map/cells/pallas_call | solution.py:462
  43.9 4.8 %all-to-all-start.2 = ((f32[8,88,128]{2,1,0:T(8,128)}), f32[8,88,128]{2,1,0:T(8,128)S(1)}, u32[]{:S(2)}, u32[]{:S(2)}) async-start(f32[8,88,128]{2,1,0:T(8,128)} %cells.1), calls=%async_computation.2 | async-start | bytes 720896 | tf_op jit(solution)/shard_map/all_to_all | solution.py:538
  48.6 6.8 %far_leaf.1.part = f32[8,9,8,128]{3,2,1,0:T(8,128)S(1)} custom-call(s32[2]{0:T(128)S(1)} %get-tuple-element.29.counts, s32[1088]{0:T(1024)S(1)} %get-tuple-element.33.flat, f32[8,104,128]{2,1,0:T(8,128)S(1)} %all-to-all-done.1.src, bf16[64,32,128]{2,1,0:T(8,128)(2,1)S(1)} %get-tuple-element.34.ft), custom_call_target="tpu_custom_call" | custom-call | flops 2097152000 | bytes 900000 | tf_op jit(solution)/shard_map/far_leaf/pallas_call | solution.py:441
  55.4 0.0 all-to-all-done.2.src
  55.4 2.2 %far_top.1 = f32[8,9,8,128]{3,2,1,0:T(8,128)} custom-call(s32[2]{0:T(128)S(1)} %get-tuple-element.29.counts, s32[256]{0:T(256)S(1)} %get-tuple-element.30.flat, f32[8,88,128]{2,1,0:T(8,128)S(1)} %all-to-all-done.2.src, bf16[8,32,128]{2,1,0:T(8,128)(2,1)S(1)} %get-tuple-element.32.ft, f32[8,9,8,128]{3,2,1,0:T(8,128)S(1)} %far_leaf.1.part), custom_call_target="tpu_custom_call" | custom-call | tf_op jit(solution)/shard_map/far_top/pallas_call | solution.py:488
  57.6 6.3 %all-to-all-start.3 = ((f32[8,9,8,128]{3,2,1,0:T(8,128)}), f32[8,9,8,128]{3,2,1,0:T(8,128)S(1)}, u32[]{:S(2)}, u32[]{:S(2)}) async-start(f32[8,9,8,128]{3,2,1,0:T(8,128)} %far_top.1), calls=%async_computation.3 | async-start | bytes 589824 | tf_op jit(solution)/shard_map/all_to_all | solution.py:542
  63.9 0.0 copy-done.5
  63.9 0.0 copy-start
  63.9 0.0 copy-start.1
  63.9 3.0 %collective-permute-start.1 = (f32[48,256]{1,0:T(8,128)S(1)}, f32[48,256]{1,0:T(8,128)S(1)}, u32[]{:S(2)}, u32[]{:S(2)}) collective-permute-start(f32[48,256]{1,0:T(8,128)S(1)} %copy-done.5), channel_id=1, source_target_pairs={{1,0},{2,1},{3,2},{4,3},{5,4},{6,5},{7,6},{8,7},{9,8},{10,9},{11,1... | collective-permute-start | bytes 147464 | tf_op jit(solution)/shard_map/ppermute | solution.py:543
  66.9 6.7 %collective-permute-done.1.after = f32[48,256]{1,0:T(8,128)S(1)} collective-permute-done((f32[48,256]{1,0:T(8,128)S(1)}, f32[48,256]{1,0:T(8,128)S(1)}, u32[]{:S(2)}, u32[]{:S(2)}) %collective-permute-start.1) | collective-permute-done | bytes 49184 | tf_op jit(solution)/shard_map/ppermute | solution.py:543
  73.6 1.9 %near.3.near2 = f32[8,8,256]{2,1,0:T(8,128)S(1)} custom-call(s32[8,9]{1,0:T(8,128)S(1)} %copy-done.4, f32[3,8,256]{2,1,0:T(8,128)S(1)} %bitcast.7, f32[48,256]{1,0:T(8,128)S(1)} %collective-permute-done.1.after), custom_call_target="tpu_custom_call" | custom-call | flops 2000000000 | bytes 300000 | tf_op jit(solution)/shard_map/near/pallas_call | solution.py:308
  75.5 1.0 %all-to-all-done.3.got = f32[8,9,8,128]{3,2,1,0:T(8,128)S(1)} async-done(((f32[8,9,8,128]{3,2,1,0:T(8,128)}), f32[8,9,8,128]{3,2,1,0:T(8,128)S(1)}, u32[]{:S(2)}, u32[]{:S(2)}) %all-to-all-start.3) | async-done | bytes 294944 | tf_op jit(solution)/shard_map/all_to_all | solution.py:542
  76.5 1.2 %final.1 = f32[8,8,256]{2,1,0:T(8,128)} custom-call(f32[8,9,8,128]{3,2,1,0:T(8,128)S(1)} %all-to-all-done.3.got, f32[8,128,128]{2,1,0:T(8,128)S(1)} %copy-done.1, f32[8,128,256]{2,1,0:T(8,128)S(1)} %copy-done, f32[8,8,256]{2,1,0:T(8,128)S(1)} %near.2.near1, f32[8,8,256]{2,1,0:T(8,128)S(1)} %near.3.near2), custom_call_target="tpu_custom_call" | custom-call | tf_op jit(solution)/shard_map/final/pallas_call | solution.py:510
  (4 shorter events, 0.0 us)
Async XLA Ops:
  2.0 10.5 %copy-start.6 = (f32[48,256]{1,0:T(8,128)S(1)}, f32[48,256]{1,0:T(8,128)}, u32[]{:S(2)}) copy-start(f32[48,256]{1,0:T(8,128)} %get-tuple-element.23) | copy-start | bytes 147460
  2.1 20.2 %all-to-all-start = ((f32[8,32,128]{2,1,0:T(8,128)}), f32[8,32,128]{2,1,0:T(8,128)S(1)}, u32[]{:S(2)}, u32[]{:S(2)}) async-start(f32[8,32,128]{2,1,0:T(8,128)} %get-tuple-element.22), calls=%async_computation | async-start | bytes 262144 | tf_op jit(solution)/shard_map/all_to_all | solution.py:529
  12.5 9.7 %collective-permute-start = (f32[48,256]{1,0:T(8,128)S(1)}, f32[48,256]{1,0:T(8,128)S(1)}, u32[]{:S(2)}, u32[]{:S(2)}) collective-permute-start(f32[48,256]{1,0:T(8,128)S(1)} %copy-done.6), channel_id=1, source_target_pairs={{0,1},{1,2},{2,3},{3,4},{4,5},{5,6},{6,7},{7,8},{8,9},{9,10},{10,1... | collective-permute-start | bytes 147464 | tf_op jit(solution)/shard_map/ppermute | solution.py:530
  22.3 20.8 %all-to-all-start.1 = ((f32[8,104,128]{2,1,0:T(8,128)}), f32[8,104,128]{2,1,0:T(8,128)S(1)}, u32[]{:S(2)}, u32[]{:S(2)}) async-start(f32[8,104,128]{2,1,0:T(8,128)} %weights.1), calls=%async_computation.1 | async-start | bytes 851968 | tf_op jit(solution)/shard_map/all_to_all | solution.py:533
  29.1 2.4 %copy-start.2 = (f32[8,8,256]{2,1,0:T(8,128)S(1)}, f32[8,8,256]{2,1,0:T(8,128)}, u32[]{:S(2)}) copy-start(f32[8,8,256]{2,1,0:T(8,128)} %chg.1) | copy-start | bytes 196612
  29.1 2.4 %copy-start.3 = (f32[8,3,256]{2,0,1:T(8,128)S(1)}, f32[8,3,256]{2,0,1:T(8,128)}, u32[]{:S(2)}) copy-start(f32[8,3,256]{2,0,1:T(8,128)} %param.9) | copy-start | bytes 73732
  29.1 2.4 %copy-start.4 = (s32[8,9]{1,0:T(8,128)S(1)}, s32[8,9]{1,0:T(8,128)}, u32[]{:S(2)}) copy-start(s32[8,9]{1,0:T(8,128)} %ids.3) | copy-start | bytes 868
  43.9 11.5 %all-to-all-start.2 = ((f32[8,88,128]{2,1,0:T(8,128)}), f32[8,88,128]{2,1,0:T(8,128)S(1)}, u32[]{:S(2)}, u32[]{:S(2)}) async-start(f32[8,88,128]{2,1,0:T(8,128)} %cells.1), calls=%async_computation.2 | async-start | bytes 720896 | tf_op jit(solution)/shard_map/all_to_all | solution.py:538
  57.6 6.3 %copy-start.5 = (f32[48,256]{1,0:T(8,128)S(1)}, f32[48,256]{1,0:T(8,128)}, u32[]{:S(2)}) copy-start(f32[48,256]{1,0:T(8,128)} %get-tuple-element.38) | copy-start | bytes 147460
  57.6 18.9 %all-to-all-start.3 = ((f32[8,9,8,128]{3,2,1,0:T(8,128)}), f32[8,9,8,128]{3,2,1,0:T(8,128)S(1)}, u32[]{:S(2)}, u32[]{:S(2)}) async-start(f32[8,9,8,128]{3,2,1,0:T(8,128)} %far_top.1), calls=%async_computation.3 | async-start | bytes 589824 | tf_op jit(solution)/shard_map/all_to_all | solution.py:542
  63.9 12.6 %copy-start = (f32[8,128,256]{2,1,0:T(8,128)S(1)}, f32[8,128,256]{2,1,0:T(8,128)}, u32[]{:S(2)}) copy-start(f32[8,128,256]{2,1,0:T(8,128)} %up.1) | copy-start | bytes 3145732
  63.9 12.6 %copy-start.1 = (f32[8,128,128]{2,1,0:T(8,128)S(1)}, f32[8,128,128]{2,1,0:T(8,128)}, u32[]{:S(2)}) copy-start(f32[8,128,128]{2,1,0:T(8,128)} %utm.1) | copy-start | bytes 1572868
  63.9 9.7 %collective-permute-start.1 = (f32[48,256]{1,0:T(8,128)S(1)}, f32[48,256]{1,0:T(8,128)S(1)}, u32[]{:S(2)}, u32[]{:S(2)}) collective-permute-start(f32[48,256]{1,0:T(8,128)S(1)} %copy-done.5), channel_id=1, source_target_pairs={{1,0},{2,1},{3,2},{4,3},{5,4},{6,5},{7,6},{8,7},{9,8},{10,9},{11,1... | collective-permute-start | bytes 147464 | tf_op jit(solution)/shard_map/ppermute | solution.py:543

commit v8 on v7

--- a/solution.py
+++ b/solution.py
@@ -17,9 +17,9 @@
 REACH = 4
 OWN = 8
 NBR = 9
-PAIRS = 8
+PAIRS = 16
 DUMMY = 64
-CHUNK = 8
+CHUNK = 16
 NEAR_DUMMY = 16
 
 SMEM = pl.BlockSpec(memory_space=pltpu.SMEM)
@@ -92,6 +92,22 @@
     high = k.astype(BF16)
     low = (k - high.astype(F32)).astype(BF16)
     return jnp.dot(vals, high, preferred_element_type=F32) + jnp.dot(vals, low, preferred_element_type=F32)
+
+
+def in_chunks(n, size, step):
+    half = size // 2
+    big = (n + half - 1) // size
+
+    def full(i, carry):
+        step(i * size, size)
+        return carry
+
+    def rest(i, carry):
+        step(big * size, half)
+        return carry
+
+    lax.fori_loop(0, big, full, 0)
+    lax.fori_loop(0, (n > big * size).astype(jnp.int32), rest, 0)
 
 
 def dot3(a, b, transposed=False):
@@ -259,15 +275,14 @@
 def near_run(count, flat, out, fs, ft, vals):
     out[...] = jnp.zeros_like(out)
 
-    def chunk(i, carry):
-        for u in range(CHUNK):
-            code = flat[i * CHUNK + u]
+    def step(start, size):
+        for u in range(size):
+            code = flat[start + u]
             l, e = code >> 5, code & 31
             r = product(fs[e], ft[l], vals[e])
             out[l] += r[0:8] + r[8:16]
-        return carry
-
-    lax.fori_loop(0, (count + CHUNK - 1) // CHUNK, chunk, 0)
+
+    in_chunks(count, CHUNK, step)
 
 
 def near_base():
@@ -363,10 +378,10 @@
 def interact(total, flat, fs, ft, vals, add):
     zero = jnp.zeros((FEAT, 128), BF16)
 
-    def chunk(i, carry):
-        for u in range(PAIRS):
-            ca = flat[i * (2 * PAIRS) + 2 * u]
-            cb = flat[i * (2 * PAIRS) + 2 * u + 1]
+    def step(start, size):
+        for u in range(size // 2):
+            ca = flat[start + 2 * u]
+            cb = flat[start + 2 * u + 1]
             ta, sa = ca >> 7, ca & 127
             tb, sb = cb >> 7, cb & 127
             fa = ft[ta]
@@ -377,9 +392,8 @@
             r = product(src, tgt, jnp.concatenate([vals[sa], vals[sb]], 0))
             add(ta, r[0:8, 0:128] + r[8:16, 0:128])
             add(tb, r[16:24, 128:256] + r[24:32, 128:256])
-        return carry
-
-    lax.fori_loop(0, (total + 2 * PAIRS - 1) // (2 * PAIRS), chunk, 0)
+
+    in_chunks(total, 2 * PAIRS, step)
 
 
 def clear_dummy(fs, vals):
@@ -450,12 +464,14 @@
     )(counts, flat, src, ft)
 
 
-def cells_kernel(src, out):
+def cells_kernel(src, out, slab):
     for y in range(8):
-        for d in range(8):
+        for c in range(3):
+            slab[8 * c + y : 8 * c + y + 1, :] = src[y, 96 + c : 97 + c, :]
+    for d in range(8):
+        for y in range(8):
             out[d, 8 * y : 8 * y + 8, :] = src[y, 88:96, :]
-            for c in range(3):
-                out[d, 64 + 8 * c + y : 65 + 8 * c + y, :] = src[y, 96 + c : 97 + c, :]
+        out[d, 64:88, :] = slab[...]
 
 
 def cells_message(src):
@@ -464,6 +480,7 @@
         in_specs=[VMEM],
         out_specs=VMEM,
         out_shape=jax.ShapeDtypeStruct((8, 88, 128), F32),
+        scratch_shapes=[pltpu.VMEM((24, 128), F32)],
         compiler_params=PARAMS,
         name="cells",
     )(src)

time: 78.3 us -> 78.1 us (level)
  the two profiles are of different devices: /device:TPU:6 before, /device:TPU:1 now
where the time goes in v8:
time: 78.1 us; the launch traced here: 77.4 us
  starting transfers between devices  36.2 us (46%)
  Pallas kernels  25.4 us (33%)
  waiting for transfers between devices  15.7 us (20%)
    all_to_all x1, starting transfers between devices, body(): got0 = lax.all_to_all(m0, 'z', 0, 0, tiled=True)  11 us
    pallas_call x2, Pallas kernels, near_part(): pl.pallas_call(near_early_kernel if early else near_late_kernel, in_specs...  8.51 us
    all_to_all x1, starting transfers between devices, body(): gotg = lax.all_to_all(cells_message(got1), 'g', 0, 0, tiled=True)  7.97 us
    pallas_call x1, Pallas kernels, far_leaf(): pl.pallas_call(far_leaf_kernel, in_specs=[SMEM, SMEM, VMEM, VMEM], out_sp...  5.04 us
    ppermute x1, starting transfers between devices, body(): after = lax.ppermute(first, every, down)  4.81 us
    all_to_all x1, starting transfers between devices, body(): gotr = lax.all_to_all(part, 'z', 0, 0, tiled=True)  4.52 us
    all_to_all x1, starting transfers between devices, body(): got1 = lax.all_to_all(m1, 'y', 0, 0, tiled=True)  4.49 us
    ppermute x1, waiting for transfers between devices, body(): before = lax.ppermute(last, every, up)  4.36 us
  transfers between devices with their start and end apart: 6, of which 5 were waited for; matrix products, arithmetic and copies ran while one was open for 0% of the time, Pallas kernels for 24%

profile of v8, /device:TPU:1, one launch (start us, length us, event | category | flops | bytes accessed | tf_op | source)
XLA Modules:
  0.0 77.4 jit_solution(13158970785117588984)
XLA Ops:
  0.0 2.0 %request.1 = (f32[8,32,128]{2,1,0:T(8,128)}, f32[48,256]{1,0:T(8,128)}, f32[48,256]{1,0:T(8,128)}) custom-call(f32[3,8,256]{2,1,0:T(8,128)} %bitcast.5, f32[8,8,256]{2,1,0:T(8,128)} %chg.1, f32[3,8,128]{2,1,0:T(8,128)} %bitcast.8, f32[3,1,128]{2,1,0:T(1,128)} %bitcast.10, s32[8,16]{1,0:T(8,128)} %llist_h.1, s32[1,16]{1,0:T(1,128)} %tlist_h.1), custom_call_target="tpu_custom_call" | custom-call | tf_op jit(solution)/shard_map/request/pallas_call | solution.py:194
  2.0 0.0 copy-start.6
  2.1 11.0 %all-to-all-start = ((f32[8,32,128]{2,1,0:T(8,128)}), f32[8,32,128]{2,1,0:T(8,128)S(1)}, u32[]{:S(2)}, u32[]{:S(2)}) async-start(f32[8,32,128]{2,1,0:T(8,128)} %get-tuple-element.22), calls=%async_computation | async-start | bytes 262144 | tf_op jit(solution)/shard_map/all_to_all | solution.py:546
  13.1 0.0 copy-done.6
  13.1 3.4 %collective-permute-start = (f32[48,256]{1,0:T(8,128)S(1)}, f32[48,256]{1,0:T(8,128)S(1)}, u32[]{:S(2)}, u32[]{:S(2)}) collective-permute-start(f32[48,256]{1,0:T(8,128)S(1)} %copy-done.6), channel_id=1, source_target_pairs={{0,1},{1,2},{2,3},{3,4},{4,5},{5,6},{6,7},{7,8},{8,9},{9,10},{10,1... | collective-permute-start | bytes 147464 | tf_op jit(solution)/shard_map/ppermute | solution.py:547
  16.4 2.9 %weights.1 = f32[8,104,128]{2,1,0:T(8,128)} custom-call(f32[8,8,256]{2,1,0:T(8,128)} %chg.1, f32[8,128,256]{2,1,0:T(8,128)} %up.1, f32[3,8,128]{2,1,0:T(8,128)} %bitcast.9, f32[8,128,128]{2,1,0:T(8,128)} %utm.1, f32[3,1,128]{2,1,0:T(1,128)} %bitcast.11), custom_call_target="tpu_custom_call" | custom-call | flops 50000000 | bytes 8000000 | tf_op jit(solution)/shard_map/weights/pallas_call | solution.py:231
  19.3 4.4 %collective-permute-done.before = f32[48,256]{1,0:T(8,128)S(1)} collective-permute-done((f32[48,256]{1,0:T(8,128)S(1)}, f32[48,256]{1,0:T(8,128)S(1)}, u32[]{:S(2)}, u32[]{:S(2)}) %collective-permute-start) | collective-permute-done | bytes 49184 | tf_op jit(solution)/shard_map/ppermute | solution.py:547
  23.7 0.0 all-to-all-done
  23.7 4.5 %all-to-all-start.1 = ((f32[8,104,128]{2,1,0:T(8,128)}), f32[8,104,128]{2,1,0:T(8,128)S(1)}, u32[]{:S(2)}, u32[]{:S(2)}) async-start(f32[8,104,128]{2,1,0:T(8,128)} %weights.1), calls=%async_computation.1 | async-start | bytes 851968 | tf_op jit(solution)/shard_map/all_to_all | solution.py:550
  28.2 0.0 copy-start.2
  28.2 0.0 copy-start.3
  28.2 0.0 copy-start.4
  28.2 2.4 %far_prep.1 = (bf16[64,32,128]{2,1,0:T(8,128)(2,1)S(1)}, bf16[8,32,128]{2,1,0:T(8,128)(2,1)S(1)}, s32[1088]{0:T(1024)S(1)}, s32[256]{0:T(256)S(1)}, s32[2]{0:T(128)S(1)}) custom-call(s32[8,2,128]{2,1,0:T(2,128)S(1)} %slice_convert_fusion.req, f32[256,128]{1,0:T(8,128)S(1)} %bitcast.4), custom_call_target="tpu_custom_call" | custom-call | flops 100000000 | bytes 900000 | tf_op jit(solution)/shard_map/far_prep/pallas_call | solution.py:414
  30.6 0.0 copy-done.2
  30.6 0.0 copy-done.3
  30.7 6.6 %near.2.near1 = f32[8,8,256]{2,1,0:T(8,128)S(1)} custom-call(s32[8,9]{1,0:T(8,128)S(1)} %copy-done.4, f32[3,8,256]{2,1,0:T(8,128)S(1)} %bitcast.6, f32[8,8,256]{2,1,0:T(8,128)S(1)} %copy-done.2, f32[48,256]{1,0:T(8,128)S(1)} %collective-permute-done.before), custom_call_target="tpu_custom_call" | custom-call | flops 2000000000 | bytes 300000 | tf_op jit(solution)/shard_map/near/pallas_call | solution.py:323
  37.3 3.6 %all-to-all-done.1.src = f32[8,104,128]{2,1,0:T(8,128)S(1)} async-done(((f32[8,104,128]{2,1,0:T(8,128)}), f32[8,104,128]{2,1,0:T(8,128)S(1)}, u32[]{:S(2)}, u32[]{:S(2)}) %all-to-all-start.1) | async-done | bytes 426016 | tf_op jit(solution)/shard_map/all_to_all | solution.py:550
  40.9 0.8 %cells.1 = f32[8,88,128]{2,1,0:T(8,128)} custom-call(f32[8,104,128]{2,1,0:T(8,128)S(1)} %all-to-all-done.1.src), custom_call_target="tpu_custom_call" | custom-call | tf_op jit(solution)/shard_map/cells/pallas_call | solution.py:478
  41.7 8.0 %all-to-all-start.2 = ((f32[8,88,128]{2,1,0:T(8,128)}), f32[8,88,128]{2,1,0:T(8,128)S(1)}, u32[]{:S(2)}, u32[]{:S(2)}) async-start(f32[8,88,128]{2,1,0:T(8,128)} %cells.1), calls=%async_computation.2 | async-start | bytes 720896 | tf_op jit(solution)/shard_map/all_to_all | solution.py:555
  49.6 5.0 %far_leaf.1.part = f32[8,9,8,128]{3,2,1,0:T(8,128)S(1)} custom-call(s32[2]{0:T(128)S(1)} %get-tuple-element.29.counts, s32[1088]{0:T(1024)S(1)} %get-tuple-element.33.flat, f32[8,104,128]{2,1,0:T(8,128)S(1)} %all-to-all-done.1.src, bf16[64,32,128]{2,1,0:T(8,128)(2,1)S(1)} %get-tuple-element.34.ft), custom_call_target="tpu_custom_call" | custom-call | flops 2097152000 | bytes 900000 | tf_op jit(solution)/shard_map/far_leaf/pallas_call | solution.py:455
  54.7 2.7 %all-to-all-done.2.src = f32[8,88,128]{2,1,0:T(8,128)S(1)} async-done(((f32[8,88,128]{2,1,0:T(8,128)}), f32[8,88,128]{2,1,0:T(8,128)S(1)}, u32[]{:S(2)}, u32[]{:S(2)}) %all-to-all-start.2) | async-done | bytes 360480 | tf_op jit(solution)/shard_map/all_to_all | solution.py:555
  57.3 2.6 %far_top.1 = f32[8,9,8,128]{3,2,1,0:T(8,128)} custom-call(s32[2]{0:T(128)S(1)} %get-tuple-element.29.counts, s32[256]{0:T(256)S(1)} %get-tuple-element.30.flat, f32[8,88,128]{2,1,0:T(8,128)S(1)} %all-to-all-done.2.src, bf16[8,32,128]{2,1,0:T(8,128)(2,1)S(1)} %get-tuple-element.32.ft, f32[8,9,8,128]{3,2,1,0:T(8,128)S(1)} %far_leaf.1.part), custom_call_target="tpu_custom_call" | custom-call | tf_op jit(solution)/shard_map/far_top/pallas_call | solution.py:505
  60.0 4.5 %all-to-all-start.3 = ((f32[8,9,8,128]{3,2,1,0:T(8,128)}), f32[8,9,8,128]{3,2,1,0:T(8,128)S(1)}, u32[]{:S(2)}, u32[]{:S(2)}) async-start(f32[8,9,8,128]{3,2,1,0:T(8,128)} %far_top.1), calls=%async_computation.3 | async-start | bytes 589824 | tf_op jit(solution)/shard_map/all_to_all | solution.py:559
  64.5 0.0 copy-done.5
  64.5 0.0 copy-start
  64.5 0.0 copy-start.1
  64.5 4.8 %collective-permute-start.1 = (f32[48,256]{1,0:T(8,128)S(1)}, f32[48,256]{1,0:T(8,128)S(1)}, u32[]{:S(2)}, u32[]{:S(2)}) collective-permute-start(f32[48,256]{1,0:T(8,128)S(1)} %copy-done.5), channel_id=1, source_target_pairs={{1,0},{2,1},{3,2},{4,3},{5,4},{6,5},{7,6},{8,7},{9,8},{10,9},{11,1... | collective-permute-start | bytes 147464 | tf_op jit(solution)/shard_map/ppermute | solution.py:560
  69.3 3.0 %collective-permute-done.1.after = f32[48,256]{1,0:T(8,128)S(1)} collective-permute-done((f32[48,256]{1,0:T(8,128)S(1)}, f32[48,256]{1,0:T(8,128)S(1)}, u32[]{:S(2)}, u32[]{:S(2)}) %collective-permute-start.1) | collective-permute-done | bytes 49184 | tf_op jit(solution)/shard_map/ppermute | solution.py:560
  72.4 1.9 %near.3.near2 = f32[8,8,256]{2,1,0:T(8,128)S(1)} custom-call(s32[8,9]{1,0:T(8,128)S(1)} %copy-done.4, f32[3,8,256]{2,1,0:T(8,128)S(1)} %bitcast.7, f32[48,256]{1,0:T(8,128)S(1)} %collective-permute-done.1.after), custom_call_target="tpu_custom_call" | custom-call | flops 2000000000 | bytes 300000 | tf_op jit(solution)/shard_map/near/pallas_call | solution.py:323
  74.2 2.0 %all-to-all-done.3.got = f32[8,9,8,128]{3,2,1,0:T(8,128)S(1)} async-done(((f32[8,9,8,128]{3,2,1,0:T(8,128)}), f32[8,9,8,128]{3,2,1,0:T(8,128)S(1)}, u32[]{:S(2)}, u32[]{:S(2)}) %all-to-all-start.3) | async-done | bytes 294944 | tf_op jit(solution)/shard_map/all_to_all | solution.py:559
  76.3 0.0 copy-done.1
  76.3 1.2 %final.1 = f32[8,8,256]{2,1,0:T(8,128)} custom-call(f32[8,9,8,128]{3,2,1,0:T(8,128)S(1)} %all-to-all-done.3.got, f32[8,128,128]{2,1,0:T(8,128)S(1)} %copy-done.1, f32[8,128,256]{2,1,0:T(8,128)S(1)} %copy-done, f32[8,8,256]{2,1,0:T(8,128)S(1)} %near.2.near1, f32[8,8,256]{2,1,0:T(8,128)S(1)} %near.3.near2), custom_call_target="tpu_custom_call" | custom-call | tf_op jit(solution)/shard_map/final/pallas_call | solution.py:527
  (4 shorter events, 0.0 us)
Async XLA Ops:
  2.0 11.0 %copy-start.6 = (f32[48,256]{1,0:T(8,128)S(1)}, f32[48,256]{1,0:T(8,128)}, u32[]{:S(2)}) copy-start(f32[48,256]{1,0:T(8,128)} %get-tuple-element.23) | copy-start | bytes 147460
  2.1 21.6 %all-to-all-start = ((f32[8,32,128]{2,1,0:T(8,128)}), f32[8,32,128]{2,1,0:T(8,128)S(1)}, u32[]{:S(2)}, u32[]{:S(2)}) async-start(f32[8,32,128]{2,1,0:T(8,128)} %get-tuple-element.22), calls=%async_computation | async-start | bytes 262144 | tf_op jit(solution)/shard_map/all_to_all | solution.py:546
  13.1 10.6 %collective-permute-start = (f32[48,256]{1,0:T(8,128)S(1)}, f32[48,256]{1,0:T(8,128)S(1)}, u32[]{:S(2)}, u32[]{:S(2)}) collective-permute-start(f32[48,256]{1,0:T(8,128)S(1)} %copy-done.6), channel_id=1, source_target_pairs={{0,1},{1,2},{2,3},{3,4},{4,5},{5,6},{6,7},{7,8},{8,9},{9,10},{10,1... | collective-permute-start | bytes 147464 | tf_op jit(solution)/shard_map/ppermute | solution.py:547
  23.7 17.2 %all-to-all-start.1 = ((f32[8,104,128]{2,1,0:T(8,128)}), f32[8,104,128]{2,1,0:T(8,128)S(1)}, u32[]{:S(2)}, u32[]{:S(2)}) async-start(f32[8,104,128]{2,1,0:T(8,128)} %weights.1), calls=%async_computation.1 | async-start | bytes 851968 | tf_op jit(solution)/shard_map/all_to_all | solution.py:550
  28.2 2.4 %copy-start.2 = (f32[8,8,256]{2,1,0:T(8,128)S(1)}, f32[8,8,256]{2,1,0:T(8,128)}, u32[]{:S(2)}) copy-start(f32[8,8,256]{2,1,0:T(8,128)} %chg.1) | copy-start | bytes 196612
  28.2 2.4 %copy-start.3 = (f32[8,3,256]{2,0,1:T(8,128)S(1)}, f32[8,3,256]{2,0,1:T(8,128)}, u32[]{:S(2)}) copy-start(f32[8,3,256]{2,0,1:T(8,128)} %param.9) | copy-start | bytes 73732
  28.2 2.4 %copy-start.4 = (s32[8,9]{1,0:T(8,128)S(1)}, s32[8,9]{1,0:T(8,128)}, u32[]{:S(2)}) copy-start(s32[8,9]{1,0:T(8,128)} %ids.3) | copy-start | bytes 868
  41.7 15.7 %all-to-all-start.2 = ((f32[8,88,128]{2,1,0:T(8,128)}), f32[8,88,128]{2,1,0:T(8,128)S(1)}, u32[]{:S(2)}, u32[]{:S(2)}) async-start(f32[8,88,128]{2,1,0:T(8,128)} %cells.1), calls=%async_computation.2 | async-start | bytes 720896 | tf_op jit(solution)/shard_map/all_to_all | solution.py:555
  59.9 4.5 %copy-start.5 = (f32[48,256]{1,0:T(8,128)S(1)}, f32[48,256]{1,0:T(8,128)}, u32[]{:S(2)}) copy-start(f32[48,256]{1,0:T(8,128)} %get-tuple-element.38) | copy-start | bytes 147460
  60.0 16.3 %all-to-all-start.3 = ((f32[8,9,8,128]{3,2,1,0:T(8,128)}), f32[8,9,8,128]{3,2,1,0:T(8,128)S(1)}, u32[]{:S(2)}, u32[]{:S(2)}) async-start(f32[8,9,8,128]{3,2,1,0:T(8,128)} %far_top.1), calls=%async_computation.3 | async-start | bytes 589824 | tf_op jit(solution)/shard_map/all_to_all | solution.py:559
  64.5 11.8 %copy-start = (f32[8,128,256]{2,1,0:T(8,128)S(1)}, f32[8,128,256]{2,1,0:T(8,128)}, u32[]{:S(2)}) copy-start(f32[8,128,256]{2,1,0:T(8,128)} %up.1) | copy-start | bytes 3145732
  64.5 11.8 %copy-start.1 = (f32[8,128,128]{2,1,0:T(8,128)S(1)}, f32[8,128,128]{2,1,0:T(8,128)}, u32[]{:S(2)}) copy-start(f32[8,128,128]{2,1,0:T(8,128)} %utm.1) | copy-start | bytes 1572868
  64.5 7.9 %collective-permute-start.1 = (f32[48,256]{1,0:T(8,128)S(1)}, f32[48,256]{1,0:T(8,128)S(1)}, u32[]{:S(2)}, u32[]{:S(2)}) collective-permute-start(f32[48,256]{1,0:T(8,128)S(1)} %copy-done.5), channel_id=1, source_target_pairs={{1,0},{2,1},{3,2},{4,3},{5,4},{6,5},{7,6},{8,7},{9,8},{10,9},{11,1... | collective-permute-start | bytes 147464 | tf_op jit(solution)/shard_map/ppermute | solution.py:560

commit v9 on v8

--- a/solution.py
+++ b/solution.py
@@ -148,13 +148,19 @@
         w = jnp.dot(v.astype(F32).astype(BF16), pick, preferred_element_type=F32)
         return jnp.sum(jnp.where(mine, w, 0.0), axis=0, keepdims=True).astype(jnp.int32)
 
-    upper = flat(ll >> 6)
+    upper = flat(ll >> 6) & 7
     lower = flat(ll & 63)
+    odd = ((lax.axis_index("d") >> 6) & 1) == 1
+    leaf_u = jnp.where(odd, lower >> 3, upper)
+    leaf_v = jnp.where(odd, upper, lower >> 3)
     row16[...] = jnp.zeros((8, 128), jnp.int32)
     row16[0:1, 0:16] = tlist[...]
     tl = row16[0:1, :]
-    leaf_hit = (lower >> 3) == sub8
-    top_hit = ((tl & 7) == sub8) & (lane < 16)
+    top_odd = ((tl >> 6) & 1) == 1
+    top_u = jnp.where(top_odd, tl & 7, (tl >> 3) & 7)
+    top_v = jnp.where(top_odd, (tl >> 3) & 7, tl & 7)
+    leaf_hit = leaf_v == sub8
+    top_hit = (top_v == sub8) & (lane < 16)
     leaf_one = leaf_hit.astype(F32)
     top_one = top_hit.astype(F32)
     leaf_pos = jnp.dot(leaf_one.astype(BF16), before, preferred_element_type=F32)
@@ -163,9 +169,9 @@
     top_n = jnp.sum(top_one, axis=1, keepdims=True)
     leaf_pos = jnp.where(leaf_hit, leaf_pos, -1.0)
     top_pos = jnp.where(top_hit, top_pos, -1.0)
-    local = (lower & 7) + (upper & 7) * 8
+    local = (lower & 7) + leaf_u * 8
     codes = jnp.where(sub8 == 0, lane >> 4, jnp.where(sub8 == 1, local, 0)).astype(F32).astype(BF16)
-    tcodes = jnp.where(sub8 == 0, tl >> 3, 0).astype(F32).astype(BF16)
+    tcodes = jnp.where(sub8 == 0, (tl >> 6) * 8 + top_u, 0).astype(F32).astype(BF16)
     rowf = row.astype(F32)
     for c in copies[2:6]:
         c.wait()
@@ -286,8 +292,7 @@
 
 
 def near_base():
-    me = (lax.axis_index("g") * lax.axis_size("y") + lax.axis_index("y")) * lax.axis_size("z") + lax.axis_index("z")
-    return me * OWN - REACH
+    return lax.axis_index("d") * OWN - REACH
 
 
 def near_early_kernel(ids, pts, chg, before, out, flat, fs, ft, vals, xyz, ts, tl):
@@ -534,36 +539,46 @@
     )(got, utm, up, near1, near2)
 
 
+def device(g, u, v):
+    return g * 64 + (v * 8 + u if g % 2 else u * 8 + v)
+
+
 def body(points, charges, up_op, skel_pts, utm, cell_pts, near_list, leaf_list, top_list):
-    every = ("g", "y", "z")
+    r = range(8)
+    along_u = [[device(g, u, v) for u in r] for g in r for v in r]
+    along_v = [[device(g, u, v) for v in r] for g in r for u in r]
+    along_g = [[device(g, u, v) for g in r] for u in r for v in r]
+
+    def exchange(x, groups):
+        return lax.all_to_all(x, "d", 0, 0, axis_index_groups=groups, tiled=True)
+
     pts = jnp.transpose(points, (1, 0, 2))
     skel = jnp.transpose(skel_pts, (1, 0, 2))
     cpts = jnp.transpose(cell_pts, (1, 0, 2))
-    count = lax.axis_size("g") * lax.axis_size("y") * lax.axis_size("z")
+    count = lax.axis_size("d")
     up = [(i, i + 1) for i in range(count - 1)]
     down = [(i + 1, i) for i in range(count - 1)]
     m0, first, last = request(pts, charges, skel, cpts, leaf_list, top_list)
-    got0 = lax.all_to_all(m0, "z", 0, 0, tiled=True)
-    before = lax.ppermute(last, every, up)
+    got0 = exchange(m0, along_v)
+    before = lax.ppermute(last, "d", up)
     m1 = weights(charges, up_op, skel, utm, cpts)
     m1, got0, before = lax.optimization_barrier((m1, got0, before))
-    got1 = lax.all_to_all(m1, "y", 0, 0, tiled=True)
+    got1 = exchange(m1, along_u)
     req = got0[:, 27:29, :].astype(jnp.int32)
     ft, ftop, leaf_flat, top_flat, counts = far_prep(req, got0)
     near1 = near_part(True, near_list, pts, charges, before)
     got1, near1, ft, counts = lax.optimization_barrier((got1, near1, ft, counts))
-    gotg = lax.all_to_all(cells_message(got1), "g", 0, 0, tiled=True)
+    gotg = exchange(cells_message(got1), along_g)
     part = far_leaf(counts, leaf_flat, got1, ft)
     part = far_top(counts, top_flat, gotg, ftop, part)
     part, first = lax.optimization_barrier((part, first))
-    gotr = lax.all_to_all(part, "z", 0, 0, tiled=True)
-    after = lax.ppermute(first, every, down)
+    gotr = exchange(part, along_v)
+    after = lax.ppermute(first, "d", down)
     near2 = near_part(False, near_list, pts, after)
     return final(gotr, utm, up_op, near1, near2)
 
 
 def solution(mesh):
-    fine = Mesh(mesh.devices.reshape(mesh.shape["group"], 8, 8), ("g", "y", "z"))
-    row = ("g", "y", "z")
-    specs = tuple(P(row, *([None] * k)) for k in (2, 2, 2, 2, 2, 2, 1, 1, 1))
-    return jax.shard_map(body, mesh=fine, in_specs=specs, out_specs=P(row, None, None), check_vma=False)
+    line = Mesh(mesh.devices.reshape(-1), ("d",))
+    specs = tuple(P("d", *([None] * k)) for k in (2, 2, 2, 2, 2, 2, 1, 1, 1))
+    return jax.shard_map(body, mesh=line, in_specs=specs, out_specs=P("d", None, None), check_vma=False)

time: 78.1 us -> 86 us (1.10)
  starting transfers between devices: 36.2 us -> 46.3 us
  waiting for transfers between devices: 15.7 us -> 12.6 us
    all_to_all x4, starting transfers between devices: 28 us -> 35.9 us  [exchange(): return lax.all_to_all(x, 'd', 0, 0, axis_index_groups=groups, tiled=True)]
    all_to_all x4, waiting for transfers between devices: 8.3 us -> 3.94 us  [exchange(): return lax.all_to_all(x, 'd', 0, 0, axis_index_groups=groups, tiled=True)]
    ppermute x2, starting transfers between devices: 8.17 us -> 10.4 us  [the longest x1 6.45 us: body(): after = lax.ppermute(first, 'd', down)]
    ppermute x2, waiting for transfers between devices: 7.4 us -> 8.64 us  [the longest x1 7.49 us: body(): before = lax.ppermute(last, 'd', up)]
    pallas_call x1, Pallas kernels: 5.04 us -> 6.22 us  [far_leaf(): pl.pallas_call(far_leaf_kernel, in_specs=[SMEM, SMEM, VMEM, VMEM], out_sp...]
  transfers between devices with their start and end apart: 6 -> 6, of which waited for: 5 -> 5; matrix products, arithmetic and copies ran while one was open for 0% -> 0% of each run, Pallas kernels for 24% -> 23%
where the time goes in v9:
time: 86 us; the launch traced here: 85.3 us
  starting transfers between devices  46.3 us (54%)
  Pallas kernels  26.2 us (30%)
  waiting for transfers between devices  12.6 us (15%)
    all_to_all x4, starting transfers between devices, exchange(): return lax.all_to_all(x, 'd', 0, 0, axis_index_groups=groups, tiled=True)  35.9 us
    pallas_call x2, Pallas kernels, near_part(): pl.pallas_call(near_early_kernel if early else near_late_kernel, in_specs...  8.5 us
    ppermute x1, waiting for transfers between devices, body(): before = lax.ppermute(last, 'd', up)  7.49 us
    ppermute x1, starting transfers between devices, body(): after = lax.ppermute(first, 'd', down)  6.45 us
    pallas_call x1, Pallas kernels, far_leaf(): pl.pallas_call(far_leaf_kernel, in_specs=[SMEM, SMEM, VMEM, VMEM], out_sp...  6.22 us
    ppermute x1, starting transfers between devices, body(): before = lax.ppermute(last, 'd', up)  4 us
    all_to_all x4, waiting for transfers between devices, exchange(): return lax.all_to_all(x, 'd', 0, 0, axis_index_groups=groups, tiled=True)  3.94 us
    pallas_call x1, Pallas kernels, weights(): pl.pallas_call(weights_kernel, in_specs=[HBM] * 5, out_specs=HBM, out_sha...  2.9 us
  transfers between devices with their start and end apart: 6, of which 5 were waited for; matrix products, arithmetic and copies ran while one was open for 0% of the time, Pallas kernels for 23%

profile of v9, /device:TPU:1, one launch (start us, length us, event | category | flops | bytes accessed | tf_op | source)
XLA Modules:
  0.0 85.3 jit_solution(15414697169234949919)
XLA Ops:
  0.0 2.0 %request.1 = (f32[8,32,128]{2,1,0:T(8,128)}, f32[48,256]{1,0:T(8,128)}, f32[48,256]{1,0:T(8,128)}) custom-call(f32[3,8,256]{2,1,0:T(8,128)} %bitcast.5, f32[8,8,256]{2,1,0:T(8,128)} %chg.1, f32[3,8,128]{2,1,0:T(8,128)} %bitcast.8, f32[3,1,128]{2,1,0:T(1,128)} %bitcast.10, s32[8,16]{1,0:T(8,128)} %llist_h.1, s32[1,16]{1,0:T(1,128)} %tlist_h.1), custom_call_target="tpu_custom_call" | custom-call | tf_op jit(solution)/shard_map/request/pallas_call | solution.py:200
  2.0 0.0 copy-start.6
  2.1 7.8 %all-to-all-start = ((f32[8,32,128]{2,1,0:T(8,128)}), f32[8,32,128]{2,1,0:T(8,128)S(1)}, u32[]{:S(2)}, u32[]{:S(2)}) async-start(f32[8,32,128]{2,1,0:T(8,128)} %get-tuple-element.22), calls=%async_computation | async-start | bytes 262144 | tf_op jit(solution)/shard_map/all_to_all | solution.py:553
  9.9 0.0 copy-done.6
  9.9 4.0 %collective-permute-start = (f32[48,256]{1,0:T(8,128)S(1)}, f32[48,256]{1,0:T(8,128)S(1)}, u32[]{:S(2)}, u32[]{:S(2)}) collective-permute-start(f32[48,256]{1,0:T(8,128)S(1)} %copy-done.6), channel_id=1, source_target_pairs={{0,1},{1,2},{2,3},{3,4},{4,5},{5,6},{6,7},{7,8},{8,9},{9,10},{10,1... | collective-permute-start | bytes 147464 | tf_op jit(solution)/shard_map/ppermute | solution.py:563
  13.9 2.9 %weights.1 = f32[8,104,128]{2,1,0:T(8,128)} custom-call(f32[8,8,256]{2,1,0:T(8,128)} %chg.1, f32[8,128,256]{2,1,0:T(8,128)} %up.1, f32[3,8,128]{2,1,0:T(8,128)} %bitcast.9, f32[8,128,128]{2,1,0:T(8,128)} %utm.1, f32[3,1,128]{2,1,0:T(1,128)} %bitcast.11), custom_call_target="tpu_custom_call" | custom-call | flops 50000000 | bytes 8000000 | tf_op jit(solution)/shard_map/weights/pallas_call | solution.py:237
  16.8 7.5 %collective-permute-done.before = f32[48,256]{1,0:T(8,128)S(1)} collective-permute-done((f32[48,256]{1,0:T(8,128)S(1)}, f32[48,256]{1,0:T(8,128)S(1)}, u32[]{:S(2)}, u32[]{:S(2)}) %collective-permute-start) | collective-permute-done | bytes 49184 | tf_op jit(solution)/shard_map/ppermute | solution.py:563
  24.3 0.0 all-to-all-done
  24.3 4.0 %all-to-all-start.1 = ((f32[8,104,128]{2,1,0:T(8,128)}), f32[8,104,128]{2,1,0:T(8,128)S(1)}, u32[]{:S(2)}, u32[]{:S(2)}) async-start(f32[8,104,128]{2,1,0:T(8,128)} %weights.1), calls=%async_computation.1 | async-start | bytes 851968 | tf_op jit(solution)/shard_map/all_to_all | solution.py:553
  28.2 0.0 copy-start.2
  28.2 0.0 copy-start.3
  28.2 0.0 copy-start.4
  28.3 2.4 %far_prep.1 = (bf16[64,32,128]{2,1,0:T(8,128)(2,1)S(1)}, bf16[8,32,128]{2,1,0:T(8,128)(2,1)S(1)}, s32[1088]{0:T(1024)S(1)}, s32[256]{0:T(256)S(1)}, s32[2]{0:T(128)S(1)}) custom-call(s32[8,2,128]{2,1,0:T(2,128)S(1)} %slice_convert_fusion.req, f32[256,128]{1,0:T(8,128)S(1)} %bitcast.4), custom_call_target="tpu_custom_call" | custom-call | flops 100000000 | bytes 900000 | tf_op jit(solution)/shard_map/far_prep/pallas_call | solution.py:419
  30.7 0.0 copy-done.2
  30.7 0.0 copy-done.3
  30.7 0.0 copy-done.4
  30.7 6.6 %near.2.near1 = f32[8,8,256]{2,1,0:T(8,128)S(1)} custom-call(s32[8,9]{1,0:T(8,128)S(1)} %copy-done.4, f32[3,8,256]{2,1,0:T(8,128)S(1)} %bitcast.6, f32[8,8,256]{2,1,0:T(8,128)S(1)} %copy-done.2, f32[48,256]{1,0:T(8,128)S(1)} %collective-permute-done.before), custom_call_target="tpu_custom_call" | custom-call | flops 2000000000 | bytes 300000 | tf_op jit(solution)/shard_map/near/pallas_call | solution.py:328
  37.3 2.0 %all-to-all-done.1.src = f32[8,104,128]{2,1,0:T(8,128)S(1)} async-done(((f32[8,104,128]{2,1,0:T(8,128)}), f32[8,104,128]{2,1,0:T(8,128)S(1)}, u32[]{:S(2)}, u32[]{:S(2)}) %all-to-all-start.1) | async-done | bytes 426016 | tf_op jit(solution)/shard_map/all_to_all | solution.py:553
  39.3 0.8 cells.1
  40.1 7.8 %all-to-all-start.2 = ((f32[8,88,128]{2,1,0:T(8,128)}), f32[8,88,128]{2,1,0:T(8,128)S(1)}, u32[]{:S(2)}, u32[]{:S(2)}) async-start(f32[8,88,128]{2,1,0:T(8,128)} %cells.1), calls=%async_computation.2 | async-start | bytes 720896 | tf_op jit(solution)/shard_map/all_to_all | solution.py:553
  47.9 6.2 %far_leaf.1.part = f32[8,9,8,128]{3,2,1,0:T(8,128)S(1)} custom-call(s32[2]{0:T(128)S(1)} %get-tuple-element.29.counts, s32[1088]{0:T(1024)S(1)} %get-tuple-element.33.flat, f32[8,104,128]{2,1,0:T(8,128)S(1)} %all-to-all-done.1.src, bf16[64,32,128]{2,1,0:T(8,128)(2,1)S(1)} %get-tuple-element.34.ft), custom_call_target="tpu_custom_call" | custom-call | flops 2097152000 | bytes 900000 | tf_op jit(solution)/shard_map/far_leaf/pallas_call | solution.py:460
  54.1 1.5 %all-to-all-done.2.src = f32[8,88,128]{2,1,0:T(8,128)S(1)} async-done(((f32[8,88,128]{2,1,0:T(8,128)}), f32[8,88,128]{2,1,0:T(8,128)S(1)}, u32[]{:S(2)}, u32[]{:S(2)}) %all-to-all-start.2) | async-done | bytes 360480 | tf_op jit(solution)/shard_map/all_to_all | solution.py:553
  55.6 2.2 %far_top.1 = f32[8,9,8,128]{3,2,1,0:T(8,128)} custom-call(s32[2]{0:T(128)S(1)} %get-tuple-element.29.counts, s32[256]{0:T(256)S(1)} %get-tuple-element.30.flat, f32[8,88,128]{2,1,0:T(8,128)S(1)} %all-to-all-done.2.src, bf16[8,32,128]{2,1,0:T(8,128)(2,1)S(1)} %get-tuple-element.32.ft, f32[8,9,8,128]{3,2,1,0:T(8,128)S(1)} %far_leaf.1.part), custom_call_target="tpu_custom_call" | custom-call | tf_op jit(solution)/shard_map/far_top/pallas_call | solution.py:510
  57.8 16.3 %all-to-all-start.3 = ((f32[8,9,8,128]{3,2,1,0:T(8,128)}), f32[8,9,8,128]{3,2,1,0:T(8,128)S(1)}, u32[]{:S(2)}, u32[]{:S(2)}) async-start(f32[8,9,8,128]{3,2,1,0:T(8,128)} %far_top.1), calls=%async_computation.3 | async-start | bytes 589824 | tf_op jit(solution)/shard_map/all_to_all | solution.py:553
  74.1 0.0 copy-done.5
  74.1 0.0 copy-start
  74.1 0.0 copy-start.1
  74.1 6.4 %collective-permute-start.1 = (f32[48,256]{1,0:T(8,128)S(1)}, f32[48,256]{1,0:T(8,128)S(1)}, u32[]{:S(2)}, u32[]{:S(2)}) collective-permute-start(f32[48,256]{1,0:T(8,128)S(1)} %copy-done.5), channel_id=1, source_target_pairs={{1,0},{2,1},{3,2},{4,3},{5,4},{6,5},{7,6},{8,7},{9,8},{10,9},{11,1... | collective-permute-start | bytes 147464 | tf_op jit(solution)/shard_map/ppermute | solution.py:576
  80.6 1.2 %collective-permute-done.1.after = f32[48,256]{1,0:T(8,128)S(1)} collective-permute-done((f32[48,256]{1,0:T(8,128)S(1)}, f32[48,256]{1,0:T(8,128)S(1)}, u32[]{:S(2)}, u32[]{:S(2)}) %collective-permute-start.1) | collective-permute-done | bytes 49184 | tf_op jit(solution)/shard_map/ppermute | solution.py:576
  81.8 1.9 %near.3.near2 = f32[8,8,256]{2,1,0:T(8,128)S(1)} custom-call(s32[8,9]{1,0:T(8,128)S(1)} %copy-done.4, f32[3,8,256]{2,1,0:T(8,128)S(1)} %bitcast.7, f32[48,256]{1,0:T(8,128)S(1)} %collective-permute-done.1.after), custom_call_target="tpu_custom_call" | custom-call | flops 2000000000 | bytes 300000 | tf_op jit(solution)/shard_map/near/pallas_call | solution.py:328
  83.6 0.5 all-to-all-done.3.got
  84.1 1.2 %final.1 = f32[8,8,256]{2,1,0:T(8,128)} custom-call(f32[8,9,8,128]{3,2,1,0:T(8,128)S(1)} %all-to-all-done.3.got, f32[8,128,128]{2,1,0:T(8,128)S(1)} %copy-done.1, f32[8,128,256]{2,1,0:T(8,128)S(1)} %copy-done, f32[8,8,256]{2,1,0:T(8,128)S(1)} %near.2.near1, f32[8,8,256]{2,1,0:T(8,128)S(1)} %near.3.near2), custom_call_target="tpu_custom_call" | custom-call | tf_op jit(solution)/shard_map/final/pallas_call | solution.py:532
  (4 shorter events, 0.0 us)
Async XLA Ops:
  2.0 7.8 %copy-start.6 = (f32[48,256]{1,0:T(8,128)S(1)}, f32[48,256]{1,0:T(8,128)}, u32[]{:S(2)}) copy-start(f32[48,256]{1,0:T(8,128)} %get-tuple-element.23) | copy-start | bytes 147460
  2.1 22.2 %all-to-all-start = ((f32[8,32,128]{2,1,0:T(8,128)}), f32[8,32,128]{2,1,0:T(8,128)S(1)}, u32[]{:S(2)}, u32[]{:S(2)}) async-start(f32[8,32,128]{2,1,0:T(8,128)} %get-tuple-element.22), calls=%async_computation | async-start | bytes 262144 | tf_op jit(solution)/shard_map/all_to_all | solution.py:553
  9.9 14.4 %collective-permute-start = (f32[48,256]{1,0:T(8,128)S(1)}, f32[48,256]{1,0:T(8,128)S(1)}, u32[]{:S(2)}, u32[]{:S(2)}) collective-permute-start(f32[48,256]{1,0:T(8,128)S(1)} %copy-done.6), channel_id=1, source_target_pairs={{0,1},{1,2},{2,3},{3,4},{4,5},{5,6},{6,7},{7,8},{8,9},{9,10},{10,1... | collective-permute-start | bytes 147464 | tf_op jit(solution)/shard_map/ppermute | solution.py:563
  24.3 15.0 %all-to-all-start.1 = ((f32[8,104,128]{2,1,0:T(8,128)}), f32[8,104,128]{2,1,0:T(8,128)S(1)}, u32[]{:S(2)}, u32[]{:S(2)}) async-start(f32[8,104,128]{2,1,0:T(8,128)} %weights.1), calls=%async_computation.1 | async-start | bytes 851968 | tf_op jit(solution)/shard_map/all_to_all | solution.py:553
  28.2 2.5 %copy-start.2 = (f32[8,8,256]{2,1,0:T(8,128)S(1)}, f32[8,8,256]{2,1,0:T(8,128)}, u32[]{:S(2)}) copy-start(f32[8,8,256]{2,1,0:T(8,128)} %chg.1) | copy-start | bytes 196612
  28.2 2.4 %copy-start.3 = (f32[8,3,256]{2,0,1:T(8,128)S(1)}, f32[8,3,256]{2,0,1:T(8,128)}, u32[]{:S(2)}) copy-start(f32[8,3,256]{2,0,1:T(8,128)} %param.9) | copy-start | bytes 73732
  28.2 2.4 %copy-start.4 = (s32[8,9]{1,0:T(8,128)S(1)}, s32[8,9]{1,0:T(8,128)}, u32[]{:S(2)}) copy-start(s32[8,9]{1,0:T(8,128)} %ids.3) | copy-start | bytes 868
  40.1 15.5 %all-to-all-start.2 = ((f32[8,88,128]{2,1,0:T(8,128)}), f32[8,88,128]{2,1,0:T(8,128)S(1)}, u32[]{:S(2)}, u32[]{:S(2)}) async-start(f32[8,88,128]{2,1,0:T(8,128)} %cells.1), calls=%async_computation.2 | async-start | bytes 720896 | tf_op jit(solution)/shard_map/all_to_all | solution.py:553
  57.8 16.3 %copy-start.5 = (f32[48,256]{1,0:T(8,128)S(1)}, f32[48,256]{1,0:T(8,128)}, u32[]{:S(2)}) copy-start(f32[48,256]{1,0:T(8,128)} %get-tuple-element.38) | copy-start | bytes 147460
  57.8 26.3 %all-to-all-start.3 = ((f32[8,9,8,128]{3,2,1,0:T(8,128)}), f32[8,9,8,128]{3,2,1,0:T(8,128)S(1)}, u32[]{:S(2)}, u32[]{:S(2)}) async-start(f32[8,9,8,128]{3,2,1,0:T(8,128)} %far_top.1), calls=%async_computation.3 | async-start | bytes 589824 | tf_op jit(solution)/shard_map/all_to_all | solution.py:553
  74.1 10.0 %copy-start = (f32[8,128,256]{2,1,0:T(8,128)S(1)}, f32[8,128,256]{2,1,0:T(8,128)}, u32[]{:S(2)}) copy-start(f32[8,128,256]{2,1,0:T(8,128)} %up.1) | copy-start | bytes 3145732
  74.1 10.0 %copy-start.1 = (f32[8,128,128]{2,1,0:T(8,128)S(1)}, f32[8,128,128]{2,1,0:T(8,128)}, u32[]{:S(2)}) copy-start(f32[8,128,128]{2,1,0:T(8,128)} %utm.1) | copy-start | bytes 1572868
  74.1 7.6 %collective-permute-start.1 = (f32[48,256]{1,0:T(8,128)S(1)}, f32[48,256]{1,0:T(8,128)S(1)}, u32[]{:S(2)}, u32[]{:S(2)}) collective-permute-start(f32[48,256]{1,0:T(8,128)S(1)} %copy-done.5), channel_id=1, source_target_pairs={{1,0},{2,1},{3,2},{4,3},{5,4},{6,5},{7,6},{8,7},{9,8},{10,9},{11,1... | collective-permute-start | bytes 147464 | tf_op jit(solution)/shard_map/ppermute | solution.py:576

commit v10 on v9

--- a/solution.py
+++ b/solution.py
@@ -121,16 +121,24 @@
     return r[0:8] + r[8:16]
 
 
-def fetch(pairs, sems):
-    copies = [pltpu.make_async_copy(a, b, sems.at[i]) for i, (a, b) in enumerate(pairs)]
+def odd_group():
+    return (lax.axis_index("d") >> 6) & 1
+
+
+def fetch(pairs, sems, at):
+    copies = [pltpu.make_async_copy(a, b, sems.at[at + i]) for i, (a, b) in enumerate(pairs)]
     for c in copies:
         c.start()
     return copies
 
 
-def request_kernel(pts_h, chg_h, skel_h, cpts_h, llist_h, tlist_h, m0, first, last, row16, pts, chg, skel, cpts, llist, tlist, sems):
-    ins = ((llist_h, llist), (tlist_h, tlist), (skel_h, skel), (cpts_h, cpts), (pts_h, pts), (chg_h, chg))
-    copies = fetch(ins, sems)
+def pack_kernel(
+    pts_h, chg_h, skel_h, cpts_h, llist_h, tlist_h, up_h, utm_h,
+    m0_h, m1_h, first_h, last_h,
+    pts, chg, skel, cpts, llist, tlist, up, utm, m0, m1, first, last, row16, sems,
+):
+    ins = ((llist_h, llist), (tlist_h, tlist), (skel_h, skel), (cpts_h, cpts), (chg_h, chg), (pts_h, pts), (up_h, up), (utm_h, utm))
+    copies = fetch(ins, sems, 0)
     for c in copies[0:2]:
         c.wait()
     lane = lax.broadcasted_iota(jnp.int32, (1, 128), 1)
@@ -150,15 +158,14 @@
 
     upper = flat(ll >> 6) & 7
     lower = flat(ll & 63)
-    odd = ((lax.axis_index("d") >> 6) & 1) == 1
-    leaf_u = jnp.where(odd, lower >> 3, upper)
-    leaf_v = jnp.where(odd, upper, lower >> 3)
     row16[...] = jnp.zeros((8, 128), jnp.int32)
     row16[0:1, 0:16] = tlist[...]
     tl = row16[0:1, :]
-    top_odd = ((tl >> 6) & 1) == 1
-    top_u = jnp.where(top_odd, tl & 7, (tl >> 3) & 7)
-    top_v = jnp.where(top_odd, (tl >> 3) & 7, tl & 7)
+    odd = odd_group() == 1
+    leaf_u = jnp.where(odd, lower >> 3, upper)
+    leaf_v = jnp.where(odd, upper, lower >> 3)
+    top_u = jnp.where(odd, tl & 7, (tl >> 3) & 7)
+    top_v = jnp.where(odd, (tl >> 3) & 7, tl & 7)
     leaf_hit = leaf_v == sub8
     top_hit = (top_v == sub8) & (lane < 16)
     leaf_one = leaf_hit.astype(F32)
@@ -193,58 +200,41 @@
         for c in range(3):
             slab[32 + 4 * c : 36 + 4 * c, :] = pts[c, start : start + REACH, :]
         slab[44:48, :] = jnp.zeros((4, 256), F32)
-
-
-def request(pts, chg, skel, cpts, llist, tlist):
-    sd = jax.ShapeDtypeStruct
-    return pl.pallas_call(
-        request_kernel,
-        in_specs=[HBM] * 6,
-        out_specs=[VMEM] * 3,
-        out_shape=[sd((8, 32, 128), F32), sd((48, 256), F32), sd((48, 256), F32)],
-        scratch_shapes=[pltpu.VMEM((8, 128), jnp.int32)]
-        + [pltpu.VMEM(a.shape, a.dtype) for a in (pts, chg, skel, cpts, llist, tlist)]
-        + [pltpu.SemaphoreType.DMA((6,))],
-        compiler_params=WIDE,
-        name="request",
-    )(pts, chg, skel, cpts, llist, tlist)
-
-
-def weights_kernel(chg_h, up_h, skel_h, utm_h, cpts_h, m1, chg, up, skel, utm, cpts, slab, sems):
-    ins = ((chg_h, chg), (up_h, up), (utm_h, utm), (skel_h, skel), (cpts_h, cpts))
-    copies = fetch(ins, sems)
-    slab[96:104, :] = jnp.zeros((8, 128), F32)
-    for c in copies[3:5]:
-        c.wait()
+    outs = fetch(((first, first_h), (last, last_h)), sems, 8)
+    m1[96:104, :] = jnp.zeros((8, 128), F32)
     for c in range(3):
-        slab[64 + 8 * c : 72 + 8 * c, :] = skel[c]
-        slab[96 + c : 97 + c, :] = cpts[c]
-    copies[0].wait()
-    copies[1].wait()
+        m1[64 + 8 * c : 72 + 8 * c, :] = skel[c]
+        m1[96 + c : 97 + c, :] = cpts[c]
+    copies[6].wait()
     own = [dot3(chg[l], up[l], True) for l in range(OWN)]
     for l in range(OWN):
-        slab[8 * l : 8 * l + 8, :] = own[l]
-    copies[2].wait()
+        m1[8 * l : 8 * l + 8, :] = own[l]
+    copies[7].wait()
     total = dot3(own[0], utm[0], True)
     for l in range(1, OWN):
         total = total + dot3(own[l], utm[l], True)
-    slab[88:96, :] = total
-    for c in fetch([(slab, m1.at[d]) for d in range(8)], sems):
+    m1[88:96, :] = total
+    for d in range(8):
+        m0[d, 32:40, :] = total
+    outs += fetch([(m0, m0_h)] + [(m1, m1_h.at[d]) for d in range(8)], sems, 10)
+    for c in outs:
         c.wait()
 
 
-def weights(chg, up, skel, utm, cpts):
-    return pl.pallas_call(
-        weights_kernel,
-        in_specs=[HBM] * 5,
-        out_specs=HBM,
-        out_shape=jax.ShapeDtypeStruct((8, 104, 128), F32),
-        scratch_shapes=[pltpu.VMEM(a.shape, a.dtype) for a in (chg, up, skel, utm, cpts)]
-        + [pltpu.VMEM((104, 128), F32), pltpu.SemaphoreType.DMA((8,))],
-        cost_estimate=pl.CostEstimate(flops=50000000, bytes_accessed=8000000, transcendentals=0),
+def pack(*args):
+    sd = jax.ShapeDtypeStruct
+    shapes = [(8, 40, 128), (104, 128), (48, 256), (48, 256)]
+    return pl.pallas_call(
+        pack_kernel,
+        in_specs=[HBM] * 8,
+        out_specs=[HBM] * 4,
+        out_shape=[sd((8, 40, 128), F32), sd((8, 104, 128), F32), sd((48, 256), F32), sd((48, 256), F32)],
+        scratch_shapes=[pltpu.VMEM(a.shape, a.dtype) for a in args]
+        + [pltpu.VMEM(s, F32) for s in shapes]
+        + [pltpu.VMEM((8, 128), jnp.int32), pltpu.SemaphoreType.DMA((19,))],
         compiler_params=WIDE,
-        name="weights",
-    )(chg, up, skel, utm, cpts)
+        name="pack",
+    )(*args)
 
 
 def near_blocks(ids, flat, base, first_leaf, early):
@@ -408,8 +398,8 @@
 
 def far_prep_kernel(req, tgt, ft, ftop, leaf_flat, top_flat, counts, tmp):
     for d in range(8):
-        prepare_targets(d, [tgt[32 * d + 8 * c : 32 * d + 8 * c + 8, :] for c in range(3)], tmp.at[d], ft)
-    prepare_targets(0, [tgt[pl.ds(24 + c, 8, stride=32), :] for c in range(3)], tmp.at[8], ftop)
+        prepare_targets(d, [tgt[40 * d + 8 * c : 40 * d + 8 * c + 8, :] for c in range(3)], tmp.at[d], ft)
+    prepare_targets(0, [tgt[pl.ds(24 + c, 8, stride=40), :] for c in range(3)], tmp.at[8], ftop)
     counts[0] = flatten(req, leaf_flat, 0, 0, 0)
     counts[1] = flatten(req, top_flat, 1, 16, 1)
 
@@ -431,7 +421,7 @@
         cost_estimate=pl.CostEstimate(flops=100000000, bytes_accessed=900000, transcendentals=0),
         compiler_params=PARAMS,
         name="far_prep",
-    )(req, tgt.reshape(256, 128))
+    )(req, tgt.reshape(320, 128))
 
 
 def far_leaf_kernel(counts, flat, src, ft, out, fs, vals, t0, t1):
@@ -469,26 +459,28 @@
     )(counts, flat, src, ft)
 
 
-def cells_kernel(src, out, slab):
+def cells_kernel(along_u, along_v, out, slab):
     for y in range(8):
+        slab[0, 8 * y : 8 * y + 8, :] = along_u[y, 88:96, :]
+        slab[1, 8 * y : 8 * y + 8, :] = along_v[y, 32:40, :]
         for c in range(3):
-            slab[8 * c + y : 8 * c + y + 1, :] = src[y, 96 + c : 97 + c, :]
+            slab[0, 64 + 8 * c + y : 65 + 8 * c + y, :] = along_u[y, 96 + c : 97 + c, :]
+            slab[1, 64 + 8 * c + y : 65 + 8 * c + y, :] = along_v[y, 24 + c : 25 + c, :]
+    odd = odd_group()
     for d in range(8):
-        for y in range(8):
-            out[d, 8 * y : 8 * y + 8, :] = src[y, 88:96, :]
-        out[d, 64:88, :] = slab[...]
-
-
-def cells_message(src):
+        out[d] = slab[(d % 2) ^ odd]
+
+
+def cells_message(along_u, along_v):
     return pl.pallas_call(
         cells_kernel,
-        in_specs=[VMEM],
+        in_specs=[VMEM] * 2,
         out_specs=VMEM,
         out_shape=jax.ShapeDtypeStruct((8, 88, 128), F32),
-        scratch_shapes=[pltpu.VMEM((24, 128), F32)],
+        scratch_shapes=[pltpu.VMEM((2, 88, 128), F32)],
         compiler_params=PARAMS,
         name="cells",
-    )(src)
+    )(along_u, along_v)
 
 
 def far_top_kernel(counts, flat, src, ft, part, out, fs, vals, t0, t1):
@@ -547,7 +539,7 @@
     r = range(8)
     along_u = [[device(g, u, v) for u in r] for g in r for v in r]
     along_v = [[device(g, u, v) for v in r] for g in r for u in r]
-    along_g = [[device(g, u, v) for g in r] for u in r for v in r]
+    along_g = [[g * 64 + i for g in r] for i in range(64)]
 
     def exchange(x, groups):
         return lax.all_to_all(x, "d", 0, 0, axis_index_groups=groups, tiled=True)
@@ -558,17 +550,16 @@
     count = lax.axis_size("d")
     up = [(i, i + 1) for i in range(count - 1)]
     down = [(i + 1, i) for i in range(count - 1)]
-    m0, first, last = request(pts, charges, skel, cpts, leaf_list, top_list)
+    m0, m1, first, last = pack(pts, charges, skel, cpts, leaf_list, top_list, up_op, utm)
     got0 = exchange(m0, along_v)
     before = lax.ppermute(last, "d", up)
-    m1 = weights(charges, up_op, skel, utm, cpts)
     m1, got0, before = lax.optimization_barrier((m1, got0, before))
     got1 = exchange(m1, along_u)
     req = got0[:, 27:29, :].astype(jnp.int32)
     ft, ftop, leaf_flat, top_flat, counts = far_prep(req, got0)
     near1 = near_part(True, near_list, pts, charges, before)
     got1, near1, ft, counts = lax.optimization_barrier((got1, near1, ft, counts))
-    gotg = exchange(cells_message(got1), along_g)
+    gotg = exchange(cells_message(got1, got0), along_g)
     part = far_leaf(counts, leaf_flat, got1, ft)
     part = far_top(counts, top_flat, gotg, ftop, part)
     part, first = lax.optimization_barrier((part, first))

time: 86 us -> 75.5 us (0.88)
  the two profiles are of different devices: /device:TPU:1 before, /device:TPU:2 now
where the time goes in v10:
time: 75.5 us; the launch traced here: 74.9 us
  starting transfers between devices  31.7 us (42%)
  Pallas kernels  23.2 us (31%)
  waiting for transfers between devices  19.8 us (26%)
    all_to_all x4, starting transfers between devices, exchange(): return lax.all_to_all(x, 'd', 0, 0, axis_index_groups=groups, tiled=True)  25.4 us
    pallas_call x2, Pallas kernels, near_part(): pl.pallas_call(near_early_kernel if early else near_late_kernel, in_specs...  7.7 us
    ppermute x1, waiting for transfers between devices, body(): before = lax.ppermute(last, 'd', up)  7.55 us
    all_to_all x4, waiting for transfers between devices, exchange(): return lax.all_to_all(x, 'd', 0, 0, axis_index_groups=groups, tiled=True)  7.17 us
    pallas_call x1, Pallas kernels, far_leaf(): pl.pallas_call(far_leaf_kernel, in_specs=[SMEM, SMEM, VMEM, VMEM], out_sp...  5.45 us
    ppermute x1, waiting for transfers between devices, body(): after = lax.ppermute(first, 'd', down)  5.09 us
    ppermute x1, starting transfers between devices, body(): before = lax.ppermute(last, 'd', up)  3.92 us
    pallas_call x1, Pallas kernels, pack(): pl.pallas_call(pack_kernel, in_specs=[HBM] * 8, out_specs=[HBM] * 4, out_...  3.14 us
  transfers between devices with their start and end apart: 6, of which 5 were waited for; matrix products, arithmetic and copies ran while one was open for 0% of the time, Pallas kernels for 21%

profile of v10, /device:TPU:2, one launch (start us, length us, event | category | flops | bytes accessed | tf_op | source)
XLA Modules:
  0.0 74.9 jit_solution(2525983466961587007)
XLA Ops:
  0.0 3.1 %pack.1 = (f32[8,40,128]{2,1,0:T(8,128)}, f32[8,104,128]{2,1,0:T(8,128)}, f32[48,256]{1,0:T(8,128)}, f32[48,256]{1,0:T(8,128)}) custom-call(f32[3,8,256]{2,1,0:T(8,128)} %bitcast.5, f32[8,8,256]{2,1,0:T(8,128)} %chg.1, f32[3,8,128]{2,1,0:T(8,128)} %bitcast.8, f32[3,1,128]{2,1,0:T(1,128)} %bitcast.9, s32[8,16]{1,0:T(8,128)} %llist_h.1, s32[1,16]{1,0:T(1,128)} %tlist_h.1, ...), custom_call_target="tpu_custom_call" | custom-call | tf_op jit(solution)/shard_map/pack/pallas_call | solution.py:227
  3.1 0.0 copy-start.6
  3.2 10.5 %all-to-all-start = ((f32[8,40,128]{2,1,0:T(8,128)}), f32[8,40,128]{2,1,0:T(8,128)S(1)}, u32[]{:S(2)}, u32[]{:S(2)}) async-start(f32[8,40,128]{2,1,0:T(8,128)} %get-tuple-element.24), calls=%async_computation | async-start | bytes 327680 | tf_op jit(solution)/shard_map/all_to_all | solution.py:545
  13.6 0.0 copy-done.6
  13.6 3.9 %collective-permute-start = (f32[48,256]{1,0:T(8,128)S(1)}, f32[48,256]{1,0:T(8,128)S(1)}, u32[]{:S(2)}, u32[]{:S(2)}) collective-permute-start(f32[48,256]{1,0:T(8,128)S(1)} %copy-done.6), channel_id=1, source_target_pairs={{0,1},{1,2},{2,3},{3,4},{4,5},{5,6},{6,7},{7,8},{8,9},{9,10},{10,1... | collective-permute-start | bytes 147464 | tf_op jit(solution)/shard_map/ppermute | solution.py:555
  17.5 7.5 %collective-permute-done.before = f32[48,256]{1,0:T(8,128)S(1)} collective-permute-done((f32[48,256]{1,0:T(8,128)S(1)}, f32[48,256]{1,0:T(8,128)S(1)}, u32[]{:S(2)}, u32[]{:S(2)}) %collective-permute-start) | collective-permute-done | bytes 49184 | tf_op jit(solution)/shard_map/ppermute | solution.py:555
  25.1 0.0 all-to-all-done.along_v
  25.1 5.2 %all-to-all-start.1 = ((f32[8,104,128]{2,1,0:T(8,128)}), f32[8,104,128]{2,1,0:T(8,128)S(1)}, u32[]{:S(2)}, u32[]{:S(2)}) async-start(f32[8,104,128]{2,1,0:T(8,128)} %get-tuple-element.26), calls=%async_computation.1 | async-start | bytes 851968 | tf_op jit(solution)/shard_map/all_to_all | solution.py:545
  30.3 0.0 copy-start.2
  30.3 0.0 copy-start.3
  30.3 0.0 copy-start.4
  30.3 2.3 %far_prep.1 = (bf16[64,32,128]{2,1,0:T(8,128)(2,1)S(1)}, bf16[8,32,128]{2,1,0:T(8,128)(2,1)S(1)}, s32[1088]{0:T(1024)S(1)}, s32[256]{0:T(256)S(1)}, s32[2]{0:T(128)S(1)}) custom-call(s32[8,2,128]{2,1,0:T(2,128)S(1)} %slice_convert_fusion.req, f32[320,128]{1,0:T(8,128)S(1)} %bitcast.4), custom_call_target="tpu_custom_call" | custom-call | flops 100000000 | bytes 900000 | tf_op jit(solution)/shard_map/far_prep/pallas_call | solution.py:409
  32.6 0.0 copy-done.2
  32.7 0.0 copy-done.3
  32.7 0.0 copy-done.4
  32.7 5.8 %near.2.near1 = f32[8,8,256]{2,1,0:T(8,128)S(1)} custom-call(s32[8,9]{1,0:T(8,128)S(1)} %copy-done.4, f32[3,8,256]{2,1,0:T(8,128)S(1)} %bitcast.6, f32[8,8,256]{2,1,0:T(8,128)S(1)} %copy-done.2, f32[48,256]{1,0:T(8,128)S(1)} %collective-permute-done.before), custom_call_target="tpu_custom_call" | custom-call | flops 2000000000 | bytes 300000 | tf_op jit(solution)/shard_map/near/pallas_call | solution.py:318
  38.5 4.0 %all-to-all-done.1.along_u.src = f32[8,104,128]{2,1,0:T(8,128)S(1)} async-done(((f32[8,104,128]{2,1,0:T(8,128)}), f32[8,104,128]{2,1,0:T(8,128)S(1)}, u32[]{:S(2)}, u32[]{:S(2)}) %all-to-all-start.1) | async-done | bytes 426016 | tf_op jit(solution)/shard_map/all_to_all | solution.py:545
  42.5 0.8 %cells.1 = f32[8,88,128]{2,1,0:T(8,128)} custom-call(f32[8,104,128]{2,1,0:T(8,128)S(1)} %all-to-all-done.1.along_u.src, f32[8,40,128]{2,1,0:T(8,128)S(1)} %all-to-all-done.along_v), custom_call_target="tpu_custom_call" | custom-call | tf_op jit(solution)/shard_map/cells/pallas_call | solution.py:475
  43.3 4.8 %all-to-all-start.2 = ((f32[8,88,128]{2,1,0:T(8,128)}), f32[8,88,128]{2,1,0:T(8,128)S(1)}, u32[]{:S(2)}, u32[]{:S(2)}) async-start(f32[8,88,128]{2,1,0:T(8,128)} %cells.1), calls=%async_computation.2 | async-start | bytes 720896 | tf_op jit(solution)/shard_map/all_to_all | solution.py:545
  48.1 5.5 %far_leaf.1.part = f32[8,9,8,128]{3,2,1,0:T(8,128)S(1)} custom-call(s32[2]{0:T(128)S(1)} %get-tuple-element.31.counts, s32[1088]{0:T(1024)S(1)} %get-tuple-element.35.flat, f32[8,104,128]{2,1,0:T(8,128)S(1)} %all-to-all-done.1.along_u.src, bf16[64,32,128]{2,1,0:T(8,128)(2,1)S(1)} %get-tuple-element.36.ft), custom_call_target="tpu_custom_call" | custom-call | flops 2097152000 | bytes 900000 | tf_op jit(solution)/shard_map/far_leaf/pallas_call | solution.py:450
  53.6 1.7 %all-to-all-done.2.src = f32[8,88,128]{2,1,0:T(8,128)S(1)} async-done(((f32[8,88,128]{2,1,0:T(8,128)}), f32[8,88,128]{2,1,0:T(8,128)S(1)}, u32[]{:S(2)}, u32[]{:S(2)}) %all-to-all-start.2) | async-done | bytes 360480 | tf_op jit(solution)/shard_map/all_to_all | solution.py:545
  55.3 2.6 %far_top.1 = f32[8,9,8,128]{3,2,1,0:T(8,128)} custom-call(s32[2]{0:T(128)S(1)} %get-tuple-element.31.counts, s32[256]{0:T(256)S(1)} %get-tuple-element.32.flat, f32[8,88,128]{2,1,0:T(8,128)S(1)} %all-to-all-done.2.src, bf16[8,32,128]{2,1,0:T(8,128)(2,1)S(1)} %get-tuple-element.34.ft, f32[8,9,8,128]{3,2,1,0:T(8,128)S(1)} %far_leaf.1.part), custom_call_target="tpu_custom_call" | custom-call | tf_op jit(solution)/shard_map/far_top/pallas_call | solution.py:502
  57.9 5.0 %all-to-all-start.3 = ((f32[8,9,8,128]{3,2,1,0:T(8,128)}), f32[8,9,8,128]{3,2,1,0:T(8,128)S(1)}, u32[]{:S(2)}, u32[]{:S(2)}) async-start(f32[8,9,8,128]{3,2,1,0:T(8,128)} %far_top.1), calls=%async_computation.3 | async-start | bytes 589824 | tf_op jit(solution)/shard_map/all_to_all | solution.py:545
  62.9 0.0 copy-done.5
  62.9 0.0 copy-start
  62.9 0.0 copy-start.1
  62.9 2.3 %collective-permute-start.1 = (f32[48,256]{1,0:T(8,128)S(1)}, f32[48,256]{1,0:T(8,128)S(1)}, u32[]{:S(2)}, u32[]{:S(2)}) collective-permute-start(f32[48,256]{1,0:T(8,128)S(1)} %copy-done.5), channel_id=1, source_target_pairs={{1,0},{2,1},{3,2},{4,3},{5,4},{6,5},{7,6},{8,7},{9,8},{10,9},{11,1... | collective-permute-start | bytes 147464 | tf_op jit(solution)/shard_map/ppermute | solution.py:567
  65.2 5.1 %collective-permute-done.1.after = f32[48,256]{1,0:T(8,128)S(1)} collective-permute-done((f32[48,256]{1,0:T(8,128)S(1)}, f32[48,256]{1,0:T(8,128)S(1)}, u32[]{:S(2)}, u32[]{:S(2)}) %collective-permute-start.1) | collective-permute-done | bytes 49184 | tf_op jit(solution)/shard_map/ppermute | solution.py:567
  70.3 1.9 %near.3.near2 = f32[8,8,256]{2,1,0:T(8,128)S(1)} custom-call(s32[8,9]{1,0:T(8,128)S(1)} %copy-done.4, f32[3,8,256]{2,1,0:T(8,128)S(1)} %bitcast.7, f32[48,256]{1,0:T(8,128)S(1)} %collective-permute-done.1.after), custom_call_target="tpu_custom_call" | custom-call | flops 2000000000 | bytes 300000 | tf_op jit(solution)/shard_map/near/pallas_call | solution.py:318
  72.2 1.5 %all-to-all-done.3.got = f32[8,9,8,128]{3,2,1,0:T(8,128)S(1)} async-done(((f32[8,9,8,128]{3,2,1,0:T(8,128)}), f32[8,9,8,128]{3,2,1,0:T(8,128)S(1)}, u32[]{:S(2)}, u32[]{:S(2)}) %all-to-all-start.3) | async-done | bytes 294944 | tf_op jit(solution)/shard_map/all_to_all | solution.py:545
  73.7 0.0 copy-done
  73.7 1.2 %final.1 = f32[8,8,256]{2,1,0:T(8,128)} custom-call(f32[8,9,8,128]{3,2,1,0:T(8,128)S(1)} %all-to-all-done.3.got, f32[8,128,128]{2,1,0:T(8,128)S(1)} %copy-done.1, f32[8,128,256]{2,1,0:T(8,128)S(1)} %copy-done, f32[8,8,256]{2,1,0:T(8,128)S(1)} %near.2.near1, f32[8,8,256]{2,1,0:T(8,128)S(1)} %near.3.near2), custom_call_target="tpu_custom_call" | custom-call | tf_op jit(solution)/shard_map/final/pallas_call | solution.py:524
  (3 shorter events, 0.0 us)
Async XLA Ops:
  3.1 10.5 %copy-start.6 = (f32[48,256]{1,0:T(8,128)S(1)}, f32[48,256]{1,0:T(8,128)}, u32[]{:S(2)}) copy-start(f32[48,256]{1,0:T(8,128)} %get-tuple-element.25) | copy-start | bytes 147460
  3.2 21.9 %all-to-all-start = ((f32[8,40,128]{2,1,0:T(8,128)}), f32[8,40,128]{2,1,0:T(8,128)S(1)}, u32[]{:S(2)}, u32[]{:S(2)}) async-start(f32[8,40,128]{2,1,0:T(8,128)} %get-tuple-element.24), calls=%async_computation | async-start | bytes 327680 | tf_op jit(solution)/shard_map/all_to_all | solution.py:545
  13.6 11.5 %collective-permute-start = (f32[48,256]{1,0:T(8,128)S(1)}, f32[48,256]{1,0:T(8,128)S(1)}, u32[]{:S(2)}, u32[]{:S(2)}) collective-permute-start(f32[48,256]{1,0:T(8,128)S(1)} %copy-done.6), channel_id=1, source_target_pairs={{0,1},{1,2},{2,3},{3,4},{4,5},{5,6},{6,7},{7,8},{8,9},{9,10},{10,1... | collective-permute-start | bytes 147464 | tf_op jit(solution)/shard_map/ppermute | solution.py:555
  25.1 17.4 %all-to-all-start.1 = ((f32[8,104,128]{2,1,0:T(8,128)}), f32[8,104,128]{2,1,0:T(8,128)S(1)}, u32[]{:S(2)}, u32[]{:S(2)}) async-start(f32[8,104,128]{2,1,0:T(8,128)} %get-tuple-element.26), calls=%async_computation.1 | async-start | bytes 851968 | tf_op jit(solution)/shard_map/all_to_all | solution.py:545
  30.3 2.4 %copy-start.2 = (f32[8,8,256]{2,1,0:T(8,128)S(1)}, f32[8,8,256]{2,1,0:T(8,128)}, u32[]{:S(2)}) copy-start(f32[8,8,256]{2,1,0:T(8,128)} %chg.1) | copy-start | bytes 196612
  30.3 2.4 %copy-start.3 = (f32[8,3,256]{2,0,1:T(8,128)S(1)}, f32[8,3,256]{2,0,1:T(8,128)}, u32[]{:S(2)}) copy-start(f32[8,3,256]{2,0,1:T(8,128)} %param.9) | copy-start | bytes 73732
  30.3 2.4 %copy-start.4 = (s32[8,9]{1,0:T(8,128)S(1)}, s32[8,9]{1,0:T(8,128)}, u32[]{:S(2)}) copy-start(s32[8,9]{1,0:T(8,128)} %ids.3) | copy-start | bytes 868
  43.3 12.0 %all-to-all-start.2 = ((f32[8,88,128]{2,1,0:T(8,128)}), f32[8,88,128]{2,1,0:T(8,128)S(1)}, u32[]{:S(2)}, u32[]{:S(2)}) async-start(f32[8,88,128]{2,1,0:T(8,128)} %cells.1), calls=%async_computation.2 | async-start | bytes 720896 | tf_op jit(solution)/shard_map/all_to_all | solution.py:545
  57.9 5.0 %copy-start.5 = (f32[48,256]{1,0:T(8,128)S(1)}, f32[48,256]{1,0:T(8,128)}, u32[]{:S(2)}) copy-start(f32[48,256]{1,0:T(8,128)} %get-tuple-element.40) | copy-start | bytes 147460
  57.9 15.8 %all-to-all-start.3 = ((f32[8,9,8,128]{3,2,1,0:T(8,128)}), f32[8,9,8,128]{3,2,1,0:T(8,128)S(1)}, u32[]{:S(2)}, u32[]{:S(2)}) async-start(f32[8,9,8,128]{3,2,1,0:T(8,128)} %far_top.1), calls=%async_computation.3 | async-start | bytes 589824 | tf_op jit(solution)/shard_map/all_to_all | solution.py:545
  62.9 10.8 %copy-start = (f32[8,128,256]{2,1,0:T(8,128)S(1)}, f32[8,128,256]{2,1,0:T(8,128)}, u32[]{:S(2)}) copy-start(f32[8,128,256]{2,1,0:T(8,128)} %up.1) | copy-start | bytes 3145732
  62.9 10.8 %copy-start.1 = (f32[8,128,128]{2,1,0:T(8,128)S(1)}, f32[8,128,128]{2,1,0:T(8,128)}, u32[]{:S(2)}) copy-start(f32[8,128,128]{2,1,0:T(8,128)} %utm.1) | copy-start | bytes 1572868
  62.9 7.4 %collective-permute-start.1 = (f32[48,256]{1,0:T(8,128)S(1)}, f32[48,256]{1,0:T(8,128)S(1)}, u32[]{:S(2)}, u32[]{:S(2)}) collective-permute-start(f32[48,256]{1,0:T(8,128)S(1)} %copy-done.5), channel_id=1, source_target_pairs={{1,0},{2,1},{3,2},{4,3},{5,4},{6,5},{7,6},{8,7},{9,8},{10,9},{11,1... | collective-permute-start | bytes 147464 | tf_op jit(solution)/shard_map/ppermute | solution.py:567

commit v11 on v10

--- a/solution.py
+++ b/solution.py
@@ -21,6 +21,7 @@
 DUMMY = 64
 CHUNK = 16
 NEAR_DUMMY = 16
+FIRST_OWN = 16
 
 SMEM = pl.BlockSpec(memory_space=pltpu.SMEM)
 HBM = pl.BlockSpec(memory_space=pltpu.HBM)
@@ -237,14 +238,25 @@
     )(*args)
 
 
-def near_blocks(ids, flat, base, first_leaf, early):
+FIRST, MIDDLE, LAST = range(3)
+
+
+def near_blocks(ids, flat, base, first_leaf, stage):
     pos = jnp.int32(0)
+    seen = jnp.int32(0)
     for l in range(first_leaf, OWN):
         for n in range(NBR):
             ident = ids[l, n]
             e = ident - base
             flat[pos] = l * 32 + e
-            take = (ident >= 0) & (e < REACH + OWN) if early else e >= REACH + OWN
+            if stage == LAST:
+                take = e >= REACH + OWN
+            else:
+                own = (e >= REACH) & (e < REACH + OWN)
+                take = own & (seen < FIRST_OWN)
+                if stage == MIDDLE:
+                    take = (ident >= 0) & (e < REACH + OWN) & jnp.logical_not(take)
+                seen = seen + own.astype(jnp.int32)
             pos = pos + take.astype(jnp.int32)
     for u in range(CHUNK):
         flat[pos + u] = (OWN - 1) * 32 + NEAR_DUMMY
@@ -268,8 +280,8 @@
         ft[l, 16:32, :] = jnp.concatenate([one, one], 0).astype(BF16)
 
 
-def near_run(count, flat, out, fs, ft, vals):
-    out[...] = jnp.zeros_like(out)
+def near_run(count, flat, start, out, fs, ft, vals):
+    out[...] = jnp.zeros_like(out) if start is None else start[...]
 
     def step(start, size):
         for u in range(size):
@@ -285,8 +297,18 @@
     return lax.axis_index("d") * OWN - REACH
 
 
-def near_early_kernel(ids, pts, chg, before, out, flat, fs, ft, vals, xyz, ts, tl):
-    count = near_blocks(ids, flat, near_base(), 0, True)
+def near_first_kernel(ids, pts, chg, out, flat, fs, ft, vals, xyz, ts, tl):
+    count = near_blocks(ids, flat, near_base(), 0, FIRST)
+    for c in range(3):
+        xyz[c] = jnp.zeros((16, 256), F32)
+        xyz[c, 4:12, :] = pts[c]
+    own = range(REACH, REACH + OWN)
+    near_setup(own, range(OWN), [xyz[0], xyz[1], xyz[2]], lambda e: chg[e - REACH], fs, ft, vals, ts, tl)
+    near_run(count, flat, None, out, fs, ft, vals)
+
+
+def near_middle_kernel(ids, pts, chg, before, start, out, flat, fs, ft, vals, xyz, ts, tl):
+    count = near_blocks(ids, flat, near_base(), 0, MIDDLE)
     for c in range(3):
         xyz[c, 0:4, :] = before[32 + 4 * c : 36 + 4 * c, :]
         xyz[c, 4:12, :] = pts[c]
@@ -296,11 +318,11 @@
         return before[8 * e : 8 * e + 8, :] if e < REACH else chg[e - REACH]
 
     near_setup(range(REACH + OWN), range(OWN), [xyz[0], xyz[1], xyz[2]], vals_of, fs, ft, vals, ts, tl)
-    near_run(count, flat, out, fs, ft, vals)
-
-
-def near_late_kernel(ids, pts, after, out, flat, fs, ft, vals, xyz, ts, tl):
-    count = near_blocks(ids, flat, near_base(), OWN - REACH, False)
+    near_run(count, flat, start, out, fs, ft, vals)
+
+
+def near_last_kernel(ids, pts, after, out, flat, fs, ft, vals, xyz, ts, tl):
+    count = near_blocks(ids, flat, near_base(), OWN - REACH, LAST)
     for c in range(3):
         xyz[c, 0:4, :] = jnp.zeros((4, 256), F32)
         xyz[c, 4:12, :] = pts[c]
@@ -311,12 +333,12 @@
 
     halo = range(REACH + OWN, 2 * REACH + OWN)
     near_setup(halo, range(OWN - REACH, OWN), [xyz[0], xyz[1], xyz[2]], vals_of, fs, ft, vals, ts, tl)
-    near_run(count, flat, out, fs, ft, vals)
-
-
-def near_part(early, *args):
-    return pl.pallas_call(
-        near_early_kernel if early else near_late_kernel,
+    near_run(count, flat, None, out, fs, ft, vals)
+
+
+def near_part(stage, *args):
+    return pl.pallas_call(
+        (near_first_kernel, near_middle_kernel, near_last_kernel)[stage],
         in_specs=[SMEM] + [VMEM] * (len(args) - 1),
         out_specs=VMEM,
         out_shape=jax.ShapeDtypeStruct((OWN, 8, 256), F32),
@@ -551,13 +573,15 @@
     up = [(i, i + 1) for i in range(count - 1)]
     down = [(i + 1, i) for i in range(count - 1)]
     m0, m1, first, last = pack(pts, charges, skel, cpts, leaf_list, top_list, up_op, utm)
+    m0, charges1 = lax.optimization_barrier((m0, charges))
     got0 = exchange(m0, along_v)
     before = lax.ppermute(last, "d", up)
-    m1, got0, before = lax.optimization_barrier((m1, got0, before))
+    near0 = near_part(FIRST, near_list, pts, charges1)
+    m1, got0, before, near0 = lax.optimization_barrier((m1, got0, before, near0))
     got1 = exchange(m1, along_u)
     req = got0[:, 27:29, :].astype(jnp.int32)
     ft, ftop, leaf_flat, top_flat, counts = far_prep(req, got0)
-    near1 = near_part(True, near_list, pts, charges, before)
+    near1 = near_part(MIDDLE, near_list, pts, charges, before, near0)
     got1, near1, ft, counts = lax.optimization_barrier((got1, near1, ft, counts))
     gotg = exchange(cells_message(got1, got0), along_g)
     part = far_leaf(counts, leaf_flat, got1, ft)
@@ -565,7 +589,7 @@
     part, first = lax.optimization_barrier((part, first))
     gotr = exchange(part, along_v)
     after = lax.ppermute(first, "d", down)
-    near2 = near_part(False, near_list, pts, after)
+    near2 = near_part(LAST, near_list, pts, after)
     return final(gotr, utm, up_op, near1, near2)
 
 

time: 75.5 us -> 75.3 us (level)
  waiting for transfers between devices: 19.8 us -> 17.5 us
  Pallas kernels: 23.2 us -> 24.9 us
    ppermute x1, waiting for transfers between devices: 7.55 us -> 4.65 us  [body(): before = lax.ppermute(last, 'd', up)]
    pallas_call x2 -> x3, Pallas kernels: 7.7 us -> 9.61 us  [near_part(): pl.pallas_call((near_first_kernel, near_middle_kernel, near_last_kernel)[...]
    all_to_all x4, waiting for transfers between devices: 7.17 us -> 8.18 us  [exchange(): return lax.all_to_all(x, 'd', 0, 0, axis_index_groups=groups, tiled=True)]
  transfers between devices with their start and end apart: 6 -> 6, of which waited for: 5 -> 5; matrix products, arithmetic and copies ran while one was open for 0% -> 0% of each run, Pallas kernels for 21% -> 23%
where the time goes in v11:
time: 75.3 us; the launch traced here: 74.7 us
  starting transfers between devices  32.1 us (43%)
  Pallas kernels  24.9 us (33%)
  waiting for transfers between devices  17.5 us (23%)
    all_to_all x4, starting transfers between devices, exchange(): return lax.all_to_all(x, 'd', 0, 0, axis_index_groups=groups, tiled=True)  25.4 us
    pallas_call x3, Pallas kernels, near_part(): pl.pallas_call((near_first_kernel, near_middle_kernel, near_last_kernel)[...  9.61 us
    all_to_all x4, waiting for transfers between devices, exchange(): return lax.all_to_all(x, 'd', 0, 0, axis_index_groups=groups, tiled=True)  8.18 us
    pallas_call x1, Pallas kernels, far_leaf(): pl.pallas_call(far_leaf_kernel, in_specs=[SMEM, SMEM, VMEM, VMEM], out_sp...  5.46 us
    ppermute x1, waiting for transfers between devices, body(): after = lax.ppermute(first, 'd', down)  4.68 us
    ppermute x1, waiting for transfers between devices, body(): before = lax.ppermute(last, 'd', up)  4.65 us
    ppermute x1, starting transfers between devices, body(): before = lax.ppermute(last, 'd', up)  3.92 us
    pallas_call x1, Pallas kernels, pack(): pl.pallas_call(pack_kernel, in_specs=[HBM] * 8, out_specs=[HBM] * 4, out_...  3.14 us
  transfers between devices with their start and end apart: 6, of which 5 were waited for; matrix products, arithmetic and copies ran while one was open for 0% of the time, Pallas kernels for 23%

profile of v11, /device:TPU:2, one launch (start us, length us, event | category | flops | bytes accessed | tf_op | source)
XLA Modules:
  0.0 74.7 jit_solution(15280919758036560743)
XLA Ops:
  0.0 3.1 %pack.1 = (f32[8,40,128]{2,1,0:T(8,128)}, f32[8,104,128]{2,1,0:T(8,128)}, f32[48,256]{1,0:T(8,128)}, f32[48,256]{1,0:T(8,128)}) custom-call(f32[3,8,256]{2,1,0:T(8,128)} %bitcast.5, f32[8,8,256]{2,1,0:T(8,128)} %chg.2, f32[3,8,128]{2,1,0:T(8,128)} %bitcast.9, f32[3,1,128]{2,1,0:T(1,128)} %bitcast.10, s32[8,16]{1,0:T(8,128)} %llist_h.1, s32[1,16]{1,0:T(1,128)} %tlist_h.1, ...), custom_call_target="tpu_custom_call" | custom-call | tf_op jit(solution)/shard_map/pack/pallas_call | solution.py:228
  3.1 0.0 copy-start.6
  3.2 0.0 copy-start.2
  3.2 0.0 copy-start.3
  3.2 0.0 copy-start.4
  3.2 10.5 %all-to-all-start = ((f32[8,40,128]{2,1,0:T(8,128)}), f32[8,40,128]{2,1,0:T(8,128)S(1)}, u32[]{:S(2)}, u32[]{:S(2)}) async-start(f32[8,40,128]{2,1,0:T(8,128)} %get-tuple-element.28), calls=%async_computation | async-start | bytes 327680 | tf_op jit(solution)/shard_map/all_to_all | solution.py:567
  13.7 0.0 copy-done.6
  13.7 3.9 %collective-permute-start = (f32[48,256]{1,0:T(8,128)S(1)}, f32[48,256]{1,0:T(8,128)S(1)}, u32[]{:S(2)}, u32[]{:S(2)}) collective-permute-start(f32[48,256]{1,0:T(8,128)S(1)} %copy-done.6), channel_id=1, source_target_pairs={{0,1},{1,2},{2,3},{3,4},{4,5},{5,6},{6,7},{7,8},{8,9},{9,10},{10,1... | collective-permute-start | bytes 147464 | tf_op jit(solution)/shard_map/ppermute | solution.py:578
  17.6 0.0 copy-done.2
  17.6 0.0 copy-done.3
  17.6 2.9 %near.3.start = f32[8,8,256]{2,1,0:T(8,128)S(1)} custom-call(s32[8,9]{1,0:T(8,128)S(1)} %copy-done.4, f32[3,8,256]{2,1,0:T(8,128)S(1)} %bitcast.6, f32[8,8,256]{2,1,0:T(8,128)S(1)} %copy-done.2), custom_call_target="tpu_custom_call" | custom-call | flops 2000000000 | bytes 300000 | tf_op jit(solution)/shard_map/near/pallas_call | solution.py:340
  20.5 4.6 %collective-permute-done.before = f32[48,256]{1,0:T(8,128)S(1)} collective-permute-done((f32[48,256]{1,0:T(8,128)S(1)}, f32[48,256]{1,0:T(8,128)S(1)}, u32[]{:S(2)}, u32[]{:S(2)}) %collective-permute-start) | collective-permute-done | bytes 49184 | tf_op jit(solution)/shard_map/ppermute | solution.py:578
  25.1 0.0 all-to-all-done.along_v
  25.1 5.2 %all-to-all-start.1 = ((f32[8,104,128]{2,1,0:T(8,128)}), f32[8,104,128]{2,1,0:T(8,128)S(1)}, u32[]{:S(2)}, u32[]{:S(2)}) async-start(f32[8,104,128]{2,1,0:T(8,128)} %get-tuple-element.31), calls=%async_computation.1 | async-start | bytes 851968 | tf_op jit(solution)/shard_map/all_to_all | solution.py:567
  30.3 2.4 %far_prep.1 = (bf16[64,32,128]{2,1,0:T(8,128)(2,1)S(1)}, bf16[8,32,128]{2,1,0:T(8,128)(2,1)S(1)}, s32[1088]{0:T(1024)S(1)}, s32[256]{0:T(256)S(1)}, s32[2]{0:T(128)S(1)}) custom-call(s32[8,2,128]{2,1,0:T(2,128)S(1)} %slice_convert_fusion.req, f32[320,128]{1,0:T(8,128)S(1)} %bitcast.4), custom_call_target="tpu_custom_call" | custom-call | flops 100000000 | bytes 900000 | tf_op jit(solution)/shard_map/far_prep/pallas_call | solution.py:431
  32.7 4.9 %near.4.near1 = f32[8,8,256]{2,1,0:T(8,128)S(1)} custom-call(s32[8,9]{1,0:T(8,128)S(1)} %copy-done.4, f32[3,8,256]{2,1,0:T(8,128)S(1)} %bitcast.7, f32[8,8,256]{2,1,0:T(8,128)S(1)} %copy-done.2, f32[48,256]{1,0:T(8,128)S(1)} %collective-permute-done.before, f32[8,8,256]{2,1,0:T(8,128)S(1)} %near.3.start), custom_call_target="tpu_custom_call" | custom-call | flops 2000000000 | bytes 300000 | tf_op jit(solution)/shard_map/near/pallas_call | solution.py:340
  37.5 5.0 %all-to-all-done.1.along_u.src = f32[8,104,128]{2,1,0:T(8,128)S(1)} async-done(((f32[8,104,128]{2,1,0:T(8,128)}), f32[8,104,128]{2,1,0:T(8,128)S(1)}, u32[]{:S(2)}, u32[]{:S(2)}) %all-to-all-start.1) | async-done | bytes 426016 | tf_op jit(solution)/shard_map/all_to_all | solution.py:567
  42.5 0.8 %cells.1 = f32[8,88,128]{2,1,0:T(8,128)} custom-call(f32[8,104,128]{2,1,0:T(8,128)S(1)} %all-to-all-done.1.along_u.src, f32[8,40,128]{2,1,0:T(8,128)S(1)} %all-to-all-done.along_v), custom_call_target="tpu_custom_call" | custom-call | tf_op jit(solution)/shard_map/cells/pallas_call | solution.py:497
  43.3 4.8 %all-to-all-start.2 = ((f32[8,88,128]{2,1,0:T(8,128)}), f32[8,88,128]{2,1,0:T(8,128)S(1)}, u32[]{:S(2)}, u32[]{:S(2)}) async-start(f32[8,88,128]{2,1,0:T(8,128)} %cells.1), calls=%async_computation.2 | async-start | bytes 720896 | tf_op jit(solution)/shard_map/all_to_all | solution.py:567
  48.2 5.5 %far_leaf.1.part = f32[8,9,8,128]{3,2,1,0:T(8,128)S(1)} custom-call(s32[2]{0:T(128)S(1)} %get-tuple-element.37.counts, s32[1088]{0:T(1024)S(1)} %get-tuple-element.41.flat, f32[8,104,128]{2,1,0:T(8,128)S(1)} %all-to-all-done.1.along_u.src, bf16[64,32,128]{2,1,0:T(8,128)(2,1)S(1)} %get-tuple-element.42.ft), custom_call_target="tpu_custom_call" | custom-call | flops 2097152000 | bytes 900000 | tf_op jit(solution)/shard_map/far_leaf/pallas_call | solution.py:472
  53.6 1.7 %all-to-all-done.2.src = f32[8,88,128]{2,1,0:T(8,128)S(1)} async-done(((f32[8,88,128]{2,1,0:T(8,128)}), f32[8,88,128]{2,1,0:T(8,128)S(1)}, u32[]{:S(2)}, u32[]{:S(2)}) %all-to-all-start.2) | async-done | bytes 360480 | tf_op jit(solution)/shard_map/all_to_all | solution.py:567
  55.3 2.4 %far_top.1 = f32[8,9,8,128]{3,2,1,0:T(8,128)} custom-call(s32[2]{0:T(128)S(1)} %get-tuple-element.37.counts, s32[256]{0:T(256)S(1)} %get-tuple-element.38.flat, f32[8,88,128]{2,1,0:T(8,128)S(1)} %all-to-all-done.2.src, bf16[8,32,128]{2,1,0:T(8,128)(2,1)S(1)} %get-tuple-element.40.ft, f32[8,9,8,128]{3,2,1,0:T(8,128)S(1)} %far_leaf.1.part), custom_call_target="tpu_custom_call" | custom-call | tf_op jit(solution)/shard_map/far_top/pallas_call | solution.py:524
  57.7 5.0 %all-to-all-start.3 = ((f32[8,9,8,128]{3,2,1,0:T(8,128)}), f32[8,9,8,128]{3,2,1,0:T(8,128)S(1)}, u32[]{:S(2)}, u32[]{:S(2)}) async-start(f32[8,9,8,128]{3,2,1,0:T(8,128)} %far_top.1), calls=%async_computation.3 | async-start | bytes 589824 | tf_op jit(solution)/shard_map/all_to_all | solution.py:567
  62.7 0.0 copy-done.5
  62.7 0.0 copy-start
  62.7 0.0 copy-start.1
  62.7 2.7 %collective-permute-start.1 = (f32[48,256]{1,0:T(8,128)S(1)}, f32[48,256]{1,0:T(8,128)S(1)}, u32[]{:S(2)}, u32[]{:S(2)}) collective-permute-start(f32[48,256]{1,0:T(8,128)S(1)} %copy-done.5), channel_id=1, source_target_pairs={{1,0},{2,1},{3,2},{4,3},{5,4},{6,5},{7,6},{8,7},{9,8},{10,9},{11,1... | collective-permute-start | bytes 147464 | tf_op jit(solution)/shard_map/ppermute | solution.py:591
  65.4 4.7 %collective-permute-done.1.after = f32[48,256]{1,0:T(8,128)S(1)} collective-permute-done((f32[48,256]{1,0:T(8,128)S(1)}, f32[48,256]{1,0:T(8,128)S(1)}, u32[]{:S(2)}, u32[]{:S(2)}) %collective-permute-start.1) | collective-permute-done | bytes 49184 | tf_op jit(solution)/shard_map/ppermute | solution.py:591
  70.1 1.9 %near.5.near2 = f32[8,8,256]{2,1,0:T(8,128)S(1)} custom-call(s32[8,9]{1,0:T(8,128)S(1)} %copy-done.4, f32[3,8,256]{2,1,0:T(8,128)S(1)} %bitcast.8, f32[48,256]{1,0:T(8,128)S(1)} %collective-permute-done.1.after), custom_call_target="tpu_custom_call" | custom-call | flops 2000000000 | bytes 300000 | tf_op jit(solution)/shard_map/near/pallas_call | solution.py:340
  72.0 1.5 %all-to-all-done.3.got = f32[8,9,8,128]{3,2,1,0:T(8,128)S(1)} async-done(((f32[8,9,8,128]{3,2,1,0:T(8,128)}), f32[8,9,8,128]{3,2,1,0:T(8,128)S(1)}, u32[]{:S(2)}, u32[]{:S(2)}) %all-to-all-start.3) | async-done | bytes 294944 | tf_op jit(solution)/shard_map/all_to_all | solution.py:567
  73.5 0.0 copy-done.1
  73.5 1.2 %final.1 = f32[8,8,256]{2,1,0:T(8,128)} custom-call(f32[8,9,8,128]{3,2,1,0:T(8,128)S(1)} %all-to-all-done.3.got, f32[8,128,128]{2,1,0:T(8,128)S(1)} %copy-done.1, f32[8,128,256]{2,1,0:T(8,128)S(1)} %copy-done, f32[8,8,256]{2,1,0:T(8,128)S(1)} %near.4.near1, f32[8,8,256]{2,1,0:T(8,128)S(1)} %near.5.near2), custom_call_target="tpu_custom_call" | custom-call | tf_op jit(solution)/shard_map/final/pallas_call | solution.py:546
  (4 shorter events, 0.0 us)
Async XLA Ops:
  3.1 10.5 %copy-start.6 = (f32[48,256]{1,0:T(8,128)S(1)}, f32[48,256]{1,0:T(8,128)}, u32[]{:S(2)}) copy-start(f32[48,256]{1,0:T(8,128)} %get-tuple-element.29) | copy-start | bytes 147460
  3.2 14.4 %copy-start.2 = (f32[8,8,256]{2,1,0:T(8,128)S(1)}, f32[8,8,256]{2,1,0:T(8,128)}, u32[]{:S(2)}) copy-start(f32[8,8,256]{2,1,0:T(8,128)} %chg.2) | copy-start | bytes 196612
  3.2 14.4 %copy-start.3 = (f32[8,3,256]{2,0,1:T(8,128)S(1)}, f32[8,3,256]{2,0,1:T(8,128)}, u32[]{:S(2)}) copy-start(f32[8,3,256]{2,0,1:T(8,128)} %param.9) | copy-start | bytes 73732
  3.2 14.4 %copy-start.4 = (s32[8,9]{1,0:T(8,128)S(1)}, s32[8,9]{1,0:T(8,128)}, u32[]{:S(2)}) copy-start(s32[8,9]{1,0:T(8,128)} %ids.5) | copy-start | bytes 868
  3.2 21.9 %all-to-all-start = ((f32[8,40,128]{2,1,0:T(8,128)}), f32[8,40,128]{2,1,0:T(8,128)S(1)}, u32[]{:S(2)}, u32[]{:S(2)}) async-start(f32[8,40,128]{2,1,0:T(8,128)} %get-tuple-element.28), calls=%async_computation | async-start | bytes 327680 | tf_op jit(solution)/shard_map/all_to_all | solution.py:567
  13.7 11.5 %collective-permute-start = (f32[48,256]{1,0:T(8,128)S(1)}, f32[48,256]{1,0:T(8,128)S(1)}, u32[]{:S(2)}, u32[]{:S(2)}) collective-permute-start(f32[48,256]{1,0:T(8,128)S(1)} %copy-done.6), channel_id=1, source_target_pairs={{0,1},{1,2},{2,3},{3,4},{4,5},{5,6},{6,7},{7,8},{8,9},{9,10},{10,1... | collective-permute-start | bytes 147464 | tf_op jit(solution)/shard_map/ppermute | solution.py:578
  25.1 17.4 %all-to-all-start.1 = ((f32[8,104,128]{2,1,0:T(8,128)}), f32[8,104,128]{2,1,0:T(8,128)S(1)}, u32[]{:S(2)}, u32[]{:S(2)}) async-start(f32[8,104,128]{2,1,0:T(8,128)} %get-tuple-element.31), calls=%async_computation.1 | async-start | bytes 851968 | tf_op jit(solution)/shard_map/all_to_all | solution.py:567
  43.3 12.0 %all-to-all-start.2 = ((f32[8,88,128]{2,1,0:T(8,128)}), f32[8,88,128]{2,1,0:T(8,128)S(1)}, u32[]{:S(2)}, u32[]{:S(2)}) async-start(f32[8,88,128]{2,1,0:T(8,128)} %cells.1), calls=%async_computation.2 | async-start | bytes 720896 | tf_op jit(solution)/shard_map/all_to_all | solution.py:567
  57.7 5.0 %copy-start.5 = (f32[48,256]{1,0:T(8,128)S(1)}, f32[48,256]{1,0:T(8,128)}, u32[]{:S(2)}) copy-start(f32[48,256]{1,0:T(8,128)} %get-tuple-element.46) | copy-start | bytes 147460
  57.7 15.8 %all-to-all-start.3 = ((f32[8,9,8,128]{3,2,1,0:T(8,128)}), f32[8,9,8,128]{3,2,1,0:T(8,128)S(1)}, u32[]{:S(2)}, u32[]{:S(2)}) async-start(f32[8,9,8,128]{3,2,1,0:T(8,128)} %far_top.1), calls=%async_computation.3 | async-start | bytes 589824 | tf_op jit(solution)/shard_map/all_to_all | solution.py:567
  62.7 10.8 %copy-start = (f32[8,128,256]{2,1,0:T(8,128)S(1)}, f32[8,128,256]{2,1,0:T(8,128)}, u32[]{:S(2)}) copy-start(f32[8,128,256]{2,1,0:T(8,128)} %up.1) | copy-start | bytes 3145732
  62.7 10.8 %copy-start.1 = (f32[8,128,128]{2,1,0:T(8,128)S(1)}, f32[8,128,128]{2,1,0:T(8,128)}, u32[]{:S(2)}) copy-start(f32[8,128,128]{2,1,0:T(8,128)} %utm.1) | copy-start | bytes 1572868
  62.7 7.4 %collective-permute-start.1 = (f32[48,256]{1,0:T(8,128)S(1)}, f32[48,256]{1,0:T(8,128)S(1)}, u32[]{:S(2)}, u32[]{:S(2)}) collective-permute-start(f32[48,256]{1,0:T(8,128)S(1)} %copy-done.5), channel_id=1, source_target_pairs={{1,0},{2,1},{3,2},{4,3},{5,4},{6,5},{7,6},{8,7},{9,8},{10,9},{11,1... | collective-permute-start | bytes 147464 | tf_op jit(solution)/shard_map/ppermute | solution.py:591

commit v12 on v11

--- a/solution.py
+++ b/solution.py
@@ -21,7 +21,7 @@
 DUMMY = 64
 CHUNK = 16
 NEAR_DUMMY = 16
-FIRST_OWN = 16
+FIRST_OWN = 24
 
 SMEM = pl.BlockSpec(memory_space=pltpu.SMEM)
 HBM = pl.BlockSpec(memory_space=pltpu.HBM)
@@ -575,12 +575,13 @@
     m0, m1, first, last = pack(pts, charges, skel, cpts, leaf_list, top_list, up_op, utm)
     m0, charges1 = lax.optimization_barrier((m0, charges))
     got0 = exchange(m0, along_v)
+    near0 = near_part(FIRST, near_list, pts, charges1)
+    m1, got0, near0, last = lax.optimization_barrier((m1, got0, near0, last))
+    got1 = exchange(m1, along_u)
     before = lax.ppermute(last, "d", up)
-    near0 = near_part(FIRST, near_list, pts, charges1)
-    m1, got0, before, near0 = lax.optimization_barrier((m1, got0, before, near0))
-    got1 = exchange(m1, along_u)
     req = got0[:, 27:29, :].astype(jnp.int32)
     ft, ftop, leaf_flat, top_flat, counts = far_prep(req, got0)
+    ft, near0 = lax.optimization_barrier((ft, near0))
     near1 = near_part(MIDDLE, near_list, pts, charges, before, near0)
     got1, near1, ft, counts = lax.optimization_barrier((got1, near1, ft, counts))
     gotg = exchange(cells_message(got1, got0), along_g)

time: 75.3 us -> 79.3 us (1.053)
  the two profiles are of different devices: /device:TPU:2 before, /device:TPU:1 now
where the time goes in v12:
time: 79.3 us; the launch traced here: 78.7 us
  starting transfers between devices  38.9 us (49%)
  Pallas kernels  24.1 us (30%)
  waiting for transfers between devices  15.5 us (20%)
    all_to_all x4, starting transfers between devices, exchange(): return lax.all_to_all(x, 'd', 0, 0, axis_index_groups=groups, tiled=True)  33.5 us
    all_to_all x4, waiting for transfers between devices, exchange(): return lax.all_to_all(x, 'd', 0, 0, axis_index_groups=groups, tiled=True)  8.33 us
    pallas_call x3, Pallas kernels, near_part(): pl.pallas_call((near_first_kernel, near_middle_kernel, near_last_kernel)[...  7.97 us
    pallas_call x1, Pallas kernels, far_leaf(): pl.pallas_call(far_leaf_kernel, in_specs=[SMEM, SMEM, VMEM, VMEM], out_sp...  6.21 us
    ppermute x1, waiting for transfers between devices, body(): before = lax.ppermute(last, 'd', up)  3.96 us
    ppermute x1, starting transfers between devices, body(): before = lax.ppermute(last, 'd', up)  3.36 us
    ppermute x1, waiting for transfers between devices, body(): after = lax.ppermute(first, 'd', down)  3.22 us
    pallas_call x1, Pallas kernels, pack(): pl.pallas_call(pack_kernel, in_specs=[HBM] * 8, out_specs=[HBM] * 4, out_...  3.14 us
  transfers between devices with their start and end apart: 6, of which 5 were waited for; matrix products, arithmetic and copies ran while one was open for 0% of the time, Pallas kernels for 21%

profile of v12, /device:TPU:1, one launch (start us, length us, event | category | flops | bytes accessed | tf_op | source)
XLA Modules:
  0.0 78.7 jit_solution(8284339509014245774)
XLA Ops:
  0.0 3.1 %pack.1 = (f32[8,40,128]{2,1,0:T(8,128)}, f32[8,104,128]{2,1,0:T(8,128)}, f32[48,256]{1,0:T(8,128)}, f32[48,256]{1,0:T(8,128)}) custom-call(f32[3,8,256]{2,1,0:T(8,128)} %bitcast.5, f32[8,8,256]{2,1,0:T(8,128)} %chg.2, f32[3,8,128]{2,1,0:T(8,128)} %bitcast.9, f32[3,1,128]{2,1,0:T(1,128)} %bitcast.10, s32[8,16]{1,0:T(8,128)} %llist_h.1, s32[1,16]{1,0:T(1,128)} %tlist_h.1, ...), custom_call_target="tpu_custom_call" | custom-call | tf_op jit(solution)/shard_map/pack/pallas_call | solution.py:228
  3.1 0.0 copy-start.2
  3.2 0.0 copy-start.3
  3.2 0.0 copy-start.4
  3.2 7.8 %all-to-all-start = ((f32[8,40,128]{2,1,0:T(8,128)}), f32[8,40,128]{2,1,0:T(8,128)S(1)}, u32[]{:S(2)}, u32[]{:S(2)}) async-start(f32[8,40,128]{2,1,0:T(8,128)} %get-tuple-element.30), calls=%async_computation | async-start | bytes 327680 | tf_op jit(solution)/shard_map/all_to_all | solution.py:567
  11.0 0.0 copy-done.2
  11.0 0.0 copy-done.3
  11.0 0.0 copy-done.4
  11.0 3.9 %near.3.start = f32[8,8,256]{2,1,0:T(8,128)S(1)} custom-call(s32[8,9]{1,0:T(8,128)S(1)} %copy-done.4, f32[3,8,256]{2,1,0:T(8,128)S(1)} %bitcast.6, f32[8,8,256]{2,1,0:T(8,128)S(1)} %copy-done.2), custom_call_target="tpu_custom_call" | custom-call | flops 2000000000 | bytes 300000 | tf_op jit(solution)/shard_map/near/pallas_call | solution.py:340
  14.9 4.3 %all-to-all-done.along_v = f32[8,40,128]{2,1,0:T(8,128)S(1)} async-done(((f32[8,40,128]{2,1,0:T(8,128)}), f32[8,40,128]{2,1,0:T(8,128)S(1)}, u32[]{:S(2)}, u32[]{:S(2)}) %all-to-all-start) | async-done | bytes 163872 | tf_op jit(solution)/shard_map/all_to_all | solution.py:567
  19.3 10.2 %all-to-all-start.1 = ((f32[8,104,128]{2,1,0:T(8,128)}), f32[8,104,128]{2,1,0:T(8,128)S(1)}, u32[]{:S(2)}, u32[]{:S(2)}) async-start(f32[8,104,128]{2,1,0:T(8,128)} %get-tuple-element.33), calls=%async_computation.1 | async-start | bytes 851968 | tf_op jit(solution)/shard_map/all_to_all | solution.py:567
  29.4 0.0 copy-done.6
  29.4 3.4 %collective-permute-start = (f32[48,256]{1,0:T(8,128)S(1)}, f32[48,256]{1,0:T(8,128)S(1)}, u32[]{:S(2)}, u32[]{:S(2)}) collective-permute-start(f32[48,256]{1,0:T(8,128)S(1)} %copy-done.6), channel_id=1, source_target_pairs={{0,1},{1,2},{2,3},{3,4},{4,5},{5,6},{6,7},{7,8},{8,9},{9,10},{10,1... | collective-permute-start | bytes 147464 | tf_op jit(solution)/shard_map/ppermute | solution.py:581
  32.8 2.5 %far_prep.1 = (bf16[64,32,128]{2,1,0:T(8,128)(2,1)S(1)}, bf16[8,32,128]{2,1,0:T(8,128)(2,1)S(1)}, s32[1088]{0:T(1024)S(1)}, s32[256]{0:T(256)S(1)}, s32[2]{0:T(128)S(1)}) custom-call(s32[8,2,128]{2,1,0:T(2,128)S(1)} %slice_convert_fusion.req, f32[320,128]{1,0:T(8,128)S(1)} %bitcast.4), custom_call_target="tpu_custom_call" | custom-call | flops 100000000 | bytes 900000 | tf_op jit(solution)/shard_map/far_prep/pallas_call | solution.py:431
  35.3 4.0 %collective-permute-done.before = f32[48,256]{1,0:T(8,128)S(1)} collective-permute-done((f32[48,256]{1,0:T(8,128)S(1)}, f32[48,256]{1,0:T(8,128)S(1)}, u32[]{:S(2)}, u32[]{:S(2)}) %collective-permute-start) | collective-permute-done | bytes 49184 | tf_op jit(solution)/shard_map/ppermute | solution.py:581
  39.2 2.2 %near.4.near1 = f32[8,8,256]{2,1,0:T(8,128)S(1)} custom-call(s32[8,9]{1,0:T(8,128)S(1)} %copy-done.4, f32[3,8,256]{2,1,0:T(8,128)S(1)} %bitcast.7, f32[8,8,256]{2,1,0:T(8,128)S(1)} %copy-done.2, f32[48,256]{1,0:T(8,128)S(1)} %collective-permute-done.before, f32[8,8,256]{2,1,0:T(8,128)S(1)} %near.3.start), custom_call_target="tpu_custom_call" | custom-call | flops 2000000000 | bytes 300000 | tf_op jit(solution)/shard_map/near/pallas_call | solution.py:340
  41.4 0.0 all-to-all-done.1.along_u.src
  41.4 0.8 %cells.1 = f32[8,88,128]{2,1,0:T(8,128)} custom-call(f32[8,104,128]{2,1,0:T(8,128)S(1)} %all-to-all-done.1.along_u.src, f32[8,40,128]{2,1,0:T(8,128)S(1)} %all-to-all-done.along_v), custom_call_target="tpu_custom_call" | custom-call | tf_op jit(solution)/shard_map/cells/pallas_call | solution.py:497
  42.2 8.8 %all-to-all-start.2 = ((f32[8,88,128]{2,1,0:T(8,128)}), f32[8,88,128]{2,1,0:T(8,128)S(1)}, u32[]{:S(2)}, u32[]{:S(2)}) async-start(f32[8,88,128]{2,1,0:T(8,128)} %cells.1), calls=%async_computation.2 | async-start | bytes 720896 | tf_op jit(solution)/shard_map/all_to_all | solution.py:567
  51.0 6.2 %far_leaf.1.part = f32[8,9,8,128]{3,2,1,0:T(8,128)S(1)} custom-call(s32[2]{0:T(128)S(1)} %get-tuple-element.41.counts, s32[1088]{0:T(1024)S(1)} %get-tuple-element.45.flat, f32[8,104,128]{2,1,0:T(8,128)S(1)} %all-to-all-done.1.along_u.src, bf16[64,32,128]{2,1,0:T(8,128)(2,1)S(1)} %get-tuple-element.46.ft), custom_call_target="tpu_custom_call" | custom-call | flops 2097152000 | bytes 900000 | tf_op jit(solution)/shard_map/far_leaf/pallas_call | solution.py:472
  57.2 1.5 %all-to-all-done.2.src = f32[8,88,128]{2,1,0:T(8,128)S(1)} async-done(((f32[8,88,128]{2,1,0:T(8,128)}), f32[8,88,128]{2,1,0:T(8,128)S(1)}, u32[]{:S(2)}, u32[]{:S(2)}) %all-to-all-start.2) | async-done | bytes 360480 | tf_op jit(solution)/shard_map/all_to_all | solution.py:567
  58.7 2.4 %far_top.1 = f32[8,9,8,128]{3,2,1,0:T(8,128)} custom-call(s32[2]{0:T(128)S(1)} %get-tuple-element.41.counts, s32[256]{0:T(256)S(1)} %get-tuple-element.42.flat, f32[8,88,128]{2,1,0:T(8,128)S(1)} %all-to-all-done.2.src, bf16[8,32,128]{2,1,0:T(8,128)(2,1)S(1)} %get-tuple-element.44.ft, f32[8,9,8,128]{3,2,1,0:T(8,128)S(1)} %far_leaf.1.part), custom_call_target="tpu_custom_call" | custom-call | tf_op jit(solution)/shard_map/far_top/pallas_call | solution.py:524
  61.1 6.7 %all-to-all-start.3 = ((f32[8,9,8,128]{3,2,1,0:T(8,128)}), f32[8,9,8,128]{3,2,1,0:T(8,128)S(1)}, u32[]{:S(2)}, u32[]{:S(2)}) async-start(f32[8,9,8,128]{3,2,1,0:T(8,128)} %far_top.1), calls=%async_computation.3 | async-start | bytes 589824 | tf_op jit(solution)/shard_map/all_to_all | solution.py:567
  67.8 0.0 copy-done.5
  67.8 0.0 copy-start
  67.8 0.0 copy-start.1
  67.8 2.1 %collective-permute-start.1 = (f32[48,256]{1,0:T(8,128)S(1)}, f32[48,256]{1,0:T(8,128)S(1)}, u32[]{:S(2)}, u32[]{:S(2)}) collective-permute-start(f32[48,256]{1,0:T(8,128)S(1)} %copy-done.5), channel_id=1, source_target_pairs={{1,0},{2,1},{3,2},{4,3},{5,4},{6,5},{7,6},{8,7},{9,8},{10,9},{11,1... | collective-permute-start | bytes 147464 | tf_op jit(solution)/shard_map/ppermute | solution.py:592
  69.9 3.2 %collective-permute-done.1.after = f32[48,256]{1,0:T(8,128)S(1)} collective-permute-done((f32[48,256]{1,0:T(8,128)S(1)}, f32[48,256]{1,0:T(8,128)S(1)}, u32[]{:S(2)}, u32[]{:S(2)}) %collective-permute-start.1) | collective-permute-done | bytes 49184 | tf_op jit(solution)/shard_map/ppermute | solution.py:592
  73.1 1.9 %near.5.near2 = f32[8,8,256]{2,1,0:T(8,128)S(1)} custom-call(s32[8,9]{1,0:T(8,128)S(1)} %copy-done.4, f32[3,8,256]{2,1,0:T(8,128)S(1)} %bitcast.8, f32[48,256]{1,0:T(8,128)S(1)} %collective-permute-done.1.after), custom_call_target="tpu_custom_call" | custom-call | flops 2000000000 | bytes 300000 | tf_op jit(solution)/shard_map/near/pallas_call | solution.py:340
  75.0 2.5 %all-to-all-done.3.got = f32[8,9,8,128]{3,2,1,0:T(8,128)S(1)} async-done(((f32[8,9,8,128]{3,2,1,0:T(8,128)}), f32[8,9,8,128]{3,2,1,0:T(8,128)S(1)}, u32[]{:S(2)}, u32[]{:S(2)}) %all-to-all-start.3) | async-done | bytes 294944 | tf_op jit(solution)/shard_map/all_to_all | solution.py:567
  77.5 0.0 copy-done
  77.5 1.2 %final.1 = f32[8,8,256]{2,1,0:T(8,128)} custom-call(f32[8,9,8,128]{3,2,1,0:T(8,128)S(1)} %all-to-all-done.3.got, f32[8,128,128]{2,1,0:T(8,128)S(1)} %copy-done.1, f32[8,128,256]{2,1,0:T(8,128)S(1)} %copy-done, f32[8,8,256]{2,1,0:T(8,128)S(1)} %near.4.near1, f32[8,8,256]{2,1,0:T(8,128)S(1)} %near.5.near2), custom_call_target="tpu_custom_call" | custom-call | tf_op jit(solution)/shard_map/final/pallas_call | solution.py:546
  (4 shorter events, 0.0 us)
Async XLA Ops:
  3.1 7.8 %copy-start.2 = (f32[8,8,256]{2,1,0:T(8,128)S(1)}, f32[8,8,256]{2,1,0:T(8,128)}, u32[]{:S(2)}) copy-start(f32[8,8,256]{2,1,0:T(8,128)} %chg.2) | copy-start | bytes 196612
  3.2 7.8 %copy-start.3 = (f32[8,3,256]{2,0,1:T(8,128)S(1)}, f32[8,3,256]{2,0,1:T(8,128)}, u32[]{:S(2)}) copy-start(f32[8,3,256]{2,0,1:T(8,128)} %param.9) | copy-start | bytes 73732
  3.2 7.8 %copy-start.4 = (s32[8,9]{1,0:T(8,128)S(1)}, s32[8,9]{1,0:T(8,128)}, u32[]{:S(2)}) copy-start(s32[8,9]{1,0:T(8,128)} %ids.5) | copy-start | bytes 868
  3.2 16.1 %all-to-all-start = ((f32[8,40,128]{2,1,0:T(8,128)}), f32[8,40,128]{2,1,0:T(8,128)S(1)}, u32[]{:S(2)}, u32[]{:S(2)}) async-start(f32[8,40,128]{2,1,0:T(8,128)} %get-tuple-element.30), calls=%async_computation | async-start | bytes 327680 | tf_op jit(solution)/shard_map/all_to_all | solution.py:567
  19.3 10.2 %copy-start.6 = (f32[48,256]{1,0:T(8,128)S(1)}, f32[48,256]{1,0:T(8,128)}, u32[]{:S(2)}) copy-start(f32[48,256]{1,0:T(8,128)} %get-tuple-element.34) | copy-start | bytes 147460
  19.3 22.1 %all-to-all-start.1 = ((f32[8,104,128]{2,1,0:T(8,128)}), f32[8,104,128]{2,1,0:T(8,128)S(1)}, u32[]{:S(2)}, u32[]{:S(2)}) async-start(f32[8,104,128]{2,1,0:T(8,128)} %get-tuple-element.33), calls=%async_computation.1 | async-start | bytes 851968 | tf_op jit(solution)/shard_map/all_to_all | solution.py:567
  29.4 9.8 %collective-permute-start = (f32[48,256]{1,0:T(8,128)S(1)}, f32[48,256]{1,0:T(8,128)S(1)}, u32[]{:S(2)}, u32[]{:S(2)}) collective-permute-start(f32[48,256]{1,0:T(8,128)S(1)} %copy-done.6), channel_id=1, source_target_pairs={{0,1},{1,2},{2,3},{3,4},{4,5},{5,6},{6,7},{7,8},{8,9},{9,10},{10,1... | collective-permute-start | bytes 147464 | tf_op jit(solution)/shard_map/ppermute | solution.py:581
  42.2 16.5 %all-to-all-start.2 = ((f32[8,88,128]{2,1,0:T(8,128)}), f32[8,88,128]{2,1,0:T(8,128)S(1)}, u32[]{:S(2)}, u32[]{:S(2)}) async-start(f32[8,88,128]{2,1,0:T(8,128)} %cells.1), calls=%async_computation.2 | async-start | bytes 720896 | tf_op jit(solution)/shard_map/all_to_all | solution.py:567
  61.1 6.7 %copy-start.5 = (f32[48,256]{1,0:T(8,128)S(1)}, f32[48,256]{1,0:T(8,128)}, u32[]{:S(2)}) copy-start(f32[48,256]{1,0:T(8,128)} %get-tuple-element.50) | copy-start | bytes 147460
  61.1 16.4 %all-to-all-start.3 = ((f32[8,9,8,128]{3,2,1,0:T(8,128)}), f32[8,9,8,128]{3,2,1,0:T(8,128)S(1)}, u32[]{:S(2)}, u32[]{:S(2)}) async-start(f32[8,9,8,128]{3,2,1,0:T(8,128)} %far_top.1), calls=%async_computation.3 | async-start | bytes 589824 | tf_op jit(solution)/shard_map/all_to_all | solution.py:567
  67.8 9.7 %copy-start = (f32[8,128,256]{2,1,0:T(8,128)S(1)}, f32[8,128,256]{2,1,0:T(8,128)}, u32[]{:S(2)}) copy-start(f32[8,128,256]{2,1,0:T(8,128)} %up.1) | copy-start | bytes 3145732
  67.8 9.7 %copy-start.1 = (f32[8,128,128]{2,1,0:T(8,128)S(1)}, f32[8,128,128]{2,1,0:T(8,128)}, u32[]{:S(2)}) copy-start(f32[8,128,128]{2,1,0:T(8,128)} %utm.1) | copy-start | bytes 1572868
  67.8 5.3 %collective-permute-start.1 = (f32[48,256]{1,0:T(8,128)S(1)}, f32[48,256]{1,0:T(8,128)S(1)}, u32[]{:S(2)}, u32[]{:S(2)}) collective-permute-start(f32[48,256]{1,0:T(8,128)S(1)} %copy-done.5), channel_id=1, source_target_pairs={{1,0},{2,1},{3,2},{4,3},{5,4},{6,5},{7,6},{8,7},{9,8},{10,9},{11,1... | collective-permute-start | bytes 147464 | tf_op jit(solution)/shard_map/ppermute | solution.py:592

commit v13 on v11

--- a/solution.py
+++ b/solution.py
@@ -21,7 +21,7 @@
 DUMMY = 64
 CHUNK = 16
 NEAR_DUMMY = 16
-FIRST_OWN = 16
+FIRST_OWN = 32
 
 SMEM = pl.BlockSpec(memory_space=pltpu.SMEM)
 HBM = pl.BlockSpec(memory_space=pltpu.HBM)
@@ -573,22 +573,23 @@
     up = [(i, i + 1) for i in range(count - 1)]
     down = [(i + 1, i) for i in range(count - 1)]
     m0, m1, first, last = pack(pts, charges, skel, cpts, leaf_list, top_list, up_op, utm)
-    m0, charges1 = lax.optimization_barrier((m0, charges))
-    got0 = exchange(m0, along_v)
+    m1, charges1 = lax.optimization_barrier((m1, charges))
+    got1 = exchange(m1, along_u)
     before = lax.ppermute(last, "d", up)
     near0 = near_part(FIRST, near_list, pts, charges1)
-    m1, got0, before, near0 = lax.optimization_barrier((m1, got0, before, near0))
-    got1 = exchange(m1, along_u)
+    got1, before, near0, m0, first = lax.optimization_barrier((got1, before, near0, m0, first))
+    got0 = exchange(m0, along_v)
+    after = lax.ppermute(first, "d", down)
+    near1 = near_part(MIDDLE, near_list, pts, charges, before, near0)
+    got0, after, near1 = lax.optimization_barrier((got0, after, near1))
+    cells, got0 = lax.optimization_barrier((cells_message(got1, got0), got0))
+    gotg = exchange(cells, along_g)
     req = got0[:, 27:29, :].astype(jnp.int32)
     ft, ftop, leaf_flat, top_flat, counts = far_prep(req, got0)
-    near1 = near_part(MIDDLE, near_list, pts, charges, before, near0)
-    got1, near1, ft, counts = lax.optimization_barrier((got1, near1, ft, counts))
-    gotg = exchange(cells_message(got1, got0), along_g)
     part = far_leaf(counts, leaf_flat, got1, ft)
     part = far_top(counts, top_flat, gotg, ftop, part)
-    part, first = lax.optimization_barrier((part, first))
+    part, after = lax.optimization_barrier((part, after))
     gotr = exchange(part, along_v)
-    after = lax.ppermute(first, "d", down)
     near2 = near_part(LAST, near_list, pts, after)
     return final(gotr, utm, up_op, near1, near2)
 

time: 75.3 us -> 76 us (level)
  the two profiles are of different devices: /device:TPU:2 before, /device:TPU:1 now
where the time goes in v13:
time: 76 us; the launch traced here: 75.2 us
  starting transfers between devices  36.6 us (48%)
  Pallas kernels  23.7 us (31%)
  waiting for transfers between devices  14.7 us (19%)
    all_to_all x4, starting transfers between devices, exchange(): return lax.all_to_all(x, 'd', 0, 0, axis_index_groups=groups, tiled=True)  26.2 us
    pallas_call x3, Pallas kernels, near_part(): pl.pallas_call((near_first_kernel, near_middle_kernel, near_last_kernel)[...  8.77 us
    all_to_all x4, waiting for transfers between devices, exchange(): return lax.all_to_all(x, 'd', 0, 0, axis_index_groups=groups, tiled=True)  8.37 us
    ppermute x1, starting transfers between devices, body(): after = lax.ppermute(first, 'd', down)  7.09 us
    ppermute x1, waiting for transfers between devices, body(): before = lax.ppermute(last, 'd', up)  6.32 us
    pallas_call x1, Pallas kernels, far_leaf(): pl.pallas_call(far_leaf_kernel, in_specs=[SMEM, SMEM, VMEM, VMEM], out_sp...  5.04 us
    ppermute x1, starting transfers between devices, body(): before = lax.ppermute(last, 'd', up)  3.36 us
    pallas_call x1, Pallas kernels, pack(): pl.pallas_call(pack_kernel, in_specs=[HBM] * 8, out_specs=[HBM] * 4, out_...  3.14 us
  transfers between devices with their start and end apart: 6, of which 3 were waited for; matrix products, arithmetic and copies ran while one was open for 0% of the time, Pallas kernels for 22%

profile of v13, /device:TPU:1, one launch (start us, length us, event | category | flops | bytes accessed | tf_op | source)
XLA Modules:
  0.0 75.2 jit_solution(9898685858337942544)
XLA Ops:
  0.0 3.1 %pack.1 = (f32[8,40,128]{2,1,0:T(8,128)}, f32[8,104,128]{2,1,0:T(8,128)}, f32[48,256]{1,0:T(8,128)}, f32[48,256]{1,0:T(8,128)}) custom-call(f32[3,8,256]{2,1,0:T(8,128)} %bitcast.5, f32[8,8,256]{2,1,0:T(8,128)} %chg.2, f32[3,8,128]{2,1,0:T(8,128)} %bitcast.9, f32[3,1,128]{2,1,0:T(1,128)} %bitcast.10, s32[8,16]{1,0:T(8,128)} %llist_h.1, s32[1,16]{1,0:T(1,128)} %tlist_h.1, ...), custom_call_target="tpu_custom_call" | custom-call | tf_op jit(solution)/shard_map/pack/pallas_call | solution.py:228
  3.1 0.0 copy-start.6
  3.2 0.0 copy-start.2
  3.2 0.0 copy-start.3
  3.2 0.0 copy-start.4
  3.2 11.0 %all-to-all-start = ((f32[8,104,128]{2,1,0:T(8,128)}), f32[8,104,128]{2,1,0:T(8,128)S(1)}, u32[]{:S(2)}, u32[]{:S(2)}) async-start(f32[8,104,128]{2,1,0:T(8,128)} %get-tuple-element.29), calls=%async_computation | async-start | bytes 851968 | tf_op jit(solution)/shard_map/all_to_all | solution.py:567
  14.2 0.0 copy-done.6
  14.2 3.4 %collective-permute-start = (f32[48,256]{1,0:T(8,128)S(1)}, f32[48,256]{1,0:T(8,128)S(1)}, u32[]{:S(2)}, u32[]{:S(2)}) collective-permute-start(f32[48,256]{1,0:T(8,128)S(1)} %copy-done.6), channel_id=1, source_target_pairs={{0,1},{1,2},{2,3},{3,4},{4,5},{5,6},{6,7},{7,8},{8,9},{9,10},{10,1... | collective-permute-start | bytes 147464 | tf_op jit(solution)/shard_map/ppermute | solution.py:578
  17.6 0.0 copy-done.2
  17.6 0.0 copy-done.3
  17.6 0.0 copy-done.4
  17.6 4.7 %near.3.start = f32[8,8,256]{2,1,0:T(8,128)S(1)} custom-call(s32[8,9]{1,0:T(8,128)S(1)} %copy-done.4, f32[3,8,256]{2,1,0:T(8,128)S(1)} %bitcast.6, f32[8,8,256]{2,1,0:T(8,128)S(1)} %copy-done.2), custom_call_target="tpu_custom_call" | custom-call | flops 2000000000 | bytes 300000 | tf_op jit(solution)/shard_map/near/pallas_call | solution.py:340
  22.3 6.3 %collective-permute-done.before = f32[48,256]{1,0:T(8,128)S(1)} collective-permute-done((f32[48,256]{1,0:T(8,128)S(1)}, f32[48,256]{1,0:T(8,128)S(1)}, u32[]{:S(2)}, u32[]{:S(2)}) %collective-permute-start) | collective-permute-done | bytes 49184 | tf_op jit(solution)/shard_map/ppermute | solution.py:578
  28.7 0.0 all-to-all-done.along_u.src
  28.7 3.5 %all-to-all-start.1 = ((f32[8,40,128]{2,1,0:T(8,128)}), f32[8,40,128]{2,1,0:T(8,128)S(1)}, u32[]{:S(2)}, u32[]{:S(2)}) async-start(f32[8,40,128]{2,1,0:T(8,128)} %get-tuple-element.35), calls=%async_computation.1 | async-start | bytes 327680 | tf_op jit(solution)/shard_map/all_to_all | solution.py:567
  32.2 0.0 copy-done.5
  32.2 7.1 %collective-permute-start.1 = (f32[48,256]{1,0:T(8,128)S(1)}, f32[48,256]{1,0:T(8,128)S(1)}, u32[]{:S(2)}, u32[]{:S(2)}) collective-permute-start(f32[48,256]{1,0:T(8,128)S(1)} %copy-done.5), channel_id=1, source_target_pairs={{1,0},{2,1},{3,2},{4,3},{5,4},{6,5},{7,6},{8,7},{9,8},{10,9},{11,1... | collective-permute-start | bytes 147464 | tf_op jit(solution)/shard_map/ppermute | solution.py:582
  39.3 2.2 %near.4.near1 = f32[8,8,256]{2,1,0:T(8,128)S(1)} custom-call(s32[8,9]{1,0:T(8,128)S(1)} %copy-done.4, f32[3,8,256]{2,1,0:T(8,128)S(1)} %bitcast.7, f32[8,8,256]{2,1,0:T(8,128)S(1)} %copy-done.2, f32[48,256]{1,0:T(8,128)S(1)} %collective-permute-done.before, f32[8,8,256]{2,1,0:T(8,128)S(1)} %near.3.start), custom_call_target="tpu_custom_call" | custom-call | flops 2000000000 | bytes 300000 | tf_op jit(solution)/shard_map/near/pallas_call | solution.py:340
  41.4 0.0 collective-permute-done.1.after
  41.4 0.0 all-to-all-done.1.along_v
  41.5 0.8 %cells.1 = f32[8,88,128]{2,1,0:T(8,128)} custom-call(f32[8,104,128]{2,1,0:T(8,128)S(1)} %all-to-all-done.along_u.src, f32[8,40,128]{2,1,0:T(8,128)S(1)} %all-to-all-done.1.along_v), custom_call_target="tpu_custom_call" | custom-call | tf_op jit(solution)/shard_map/cells/pallas_call | solution.py:497
  42.3 6.9 %all-to-all-start.2 = ((f32[8,88,128]{2,1,0:T(8,128)}), f32[8,88,128]{2,1,0:T(8,128)S(1)}, u32[]{:S(2)}, u32[]{:S(2)}) async-start(f32[8,88,128]{2,1,0:T(8,128)} %cells.1), calls=%async_computation.2 | async-start | bytes 720896 | tf_op jit(solution)/shard_map/all_to_all | solution.py:567
  49.2 2.4 %far_prep.1 = (bf16[64,32,128]{2,1,0:T(8,128)(2,1)S(1)}, bf16[8,32,128]{2,1,0:T(8,128)(2,1)S(1)}, s32[1088]{0:T(1024)S(1)}, s32[256]{0:T(256)S(1)}, s32[2]{0:T(128)S(1)}) custom-call(s32[8,2,128]{2,1,0:T(2,128)S(1)} %slice_convert_fusion.req, f32[320,128]{1,0:T(8,128)S(1)} %bitcast.4), custom_call_target="tpu_custom_call" | custom-call | flops 100000000 | bytes 900000 | tf_op jit(solution)/shard_map/far_prep/pallas_call | solution.py:431
  51.6 5.0 %far_leaf.1.part = f32[8,9,8,128]{3,2,1,0:T(8,128)S(1)} custom-call(s32[2]{0:T(128)S(1)} %get-tuple-element.41.counts, s32[1088]{0:T(1024)S(1)} %get-tuple-element.45.flat, f32[8,104,128]{2,1,0:T(8,128)S(1)} %all-to-all-done.along_u.src, bf16[64,32,128]{2,1,0:T(8,128)(2,1)S(1)} %get-tuple-element.46.ft), custom_call_target="tpu_custom_call" | custom-call | flops 2097152000 | bytes 900000 | tf_op jit(solution)/shard_map/far_leaf/pallas_call | solution.py:472
  56.6 0.3 all-to-all-done.2.src
  56.9 2.4 %far_top.1 = f32[8,9,8,128]{3,2,1,0:T(8,128)} custom-call(s32[2]{0:T(128)S(1)} %get-tuple-element.41.counts, s32[256]{0:T(256)S(1)} %get-tuple-element.42.flat, f32[8,88,128]{2,1,0:T(8,128)S(1)} %all-to-all-done.2.src, bf16[8,32,128]{2,1,0:T(8,128)(2,1)S(1)} %get-tuple-element.44.ft, f32[8,9,8,128]{3,2,1,0:T(8,128)S(1)} %far_leaf.1.part), custom_call_target="tpu_custom_call" | custom-call | tf_op jit(solution)/shard_map/far_top/pallas_call | solution.py:524
  59.3 4.8 %all-to-all-start.3 = ((f32[8,9,8,128]{3,2,1,0:T(8,128)}), f32[8,9,8,128]{3,2,1,0:T(8,128)S(1)}, u32[]{:S(2)}, u32[]{:S(2)}) async-start(f32[8,9,8,128]{3,2,1,0:T(8,128)} %far_top.1), calls=%async_computation.3 | async-start | bytes 589824 | tf_op jit(solution)/shard_map/all_to_all | solution.py:567
  64.0 0.0 copy-start.1
  64.0 1.9 %near.5.near2 = f32[8,8,256]{2,1,0:T(8,128)S(1)} custom-call(s32[8,9]{1,0:T(8,128)S(1)} %copy-done.4, f32[3,8,256]{2,1,0:T(8,128)S(1)} %bitcast.8, f32[48,256]{1,0:T(8,128)S(1)} %collective-permute-done.1.after), custom_call_target="tpu_custom_call" | custom-call | flops 2000000000 | bytes 300000 | tf_op jit(solution)/shard_map/near/pallas_call | solution.py:340
  65.9 8.1 %all-to-all-done.3.got = f32[8,9,8,128]{3,2,1,0:T(8,128)S(1)} async-done(((f32[8,9,8,128]{3,2,1,0:T(8,128)}), f32[8,9,8,128]{3,2,1,0:T(8,128)S(1)}, u32[]{:S(2)}, u32[]{:S(2)}) %all-to-all-start.3) | async-done | bytes 294944 | tf_op jit(solution)/shard_map/all_to_all | solution.py:567
  74.0 0.0 copy-done.1
  74.0 1.2 %final.1 = f32[8,8,256]{2,1,0:T(8,128)} custom-call(f32[8,9,8,128]{3,2,1,0:T(8,128)S(1)} %all-to-all-done.3.got, f32[8,128,128]{2,1,0:T(8,128)S(1)} %copy-done.1, f32[8,128,256]{2,1,0:T(8,128)S(1)} %copy-done, f32[8,8,256]{2,1,0:T(8,128)S(1)} %near.4.near1, f32[8,8,256]{2,1,0:T(8,128)S(1)} %near.5.near2), custom_call_target="tpu_custom_call" | custom-call | tf_op jit(solution)/shard_map/final/pallas_call | solution.py:546
  (4 shorter events, 0.0 us)
Async XLA Ops:
  3.1 11.1 %copy-start.6 = (f32[48,256]{1,0:T(8,128)S(1)}, f32[48,256]{1,0:T(8,128)}, u32[]{:S(2)}) copy-start(f32[48,256]{1,0:T(8,128)} %get-tuple-element.30) | copy-start | bytes 147460
  3.2 14.4 %copy-start.2 = (f32[8,8,256]{2,1,0:T(8,128)S(1)}, f32[8,8,256]{2,1,0:T(8,128)}, u32[]{:S(2)}) copy-start(f32[8,8,256]{2,1,0:T(8,128)} %chg.2) | copy-start | bytes 196612
  3.2 14.4 %copy-start.3 = (f32[8,3,256]{2,0,1:T(8,128)S(1)}, f32[8,3,256]{2,0,1:T(8,128)}, u32[]{:S(2)}) copy-start(f32[8,3,256]{2,0,1:T(8,128)} %param.9) | copy-start | bytes 73732
  3.2 14.4 %copy-start.4 = (s32[8,9]{1,0:T(8,128)S(1)}, s32[8,9]{1,0:T(8,128)}, u32[]{:S(2)}) copy-start(s32[8,9]{1,0:T(8,128)} %ids.5) | copy-start | bytes 868
  3.2 25.5 %all-to-all-start = ((f32[8,104,128]{2,1,0:T(8,128)}), f32[8,104,128]{2,1,0:T(8,128)S(1)}, u32[]{:S(2)}, u32[]{:S(2)}) async-start(f32[8,104,128]{2,1,0:T(8,128)} %get-tuple-element.29), calls=%async_computation | async-start | bytes 851968 | tf_op jit(solution)/shard_map/all_to_all | solution.py:567
  14.2 14.5 %collective-permute-start = (f32[48,256]{1,0:T(8,128)S(1)}, f32[48,256]{1,0:T(8,128)S(1)}, u32[]{:S(2)}, u32[]{:S(2)}) collective-permute-start(f32[48,256]{1,0:T(8,128)S(1)} %copy-done.6), channel_id=1, source_target_pairs={{0,1},{1,2},{2,3},{3,4},{4,5},{5,6},{6,7},{7,8},{8,9},{9,10},{10,1... | collective-permute-start | bytes 147464 | tf_op jit(solution)/shard_map/ppermute | solution.py:578
  28.7 3.5 %copy-start.5 = (f32[48,256]{1,0:T(8,128)S(1)}, f32[48,256]{1,0:T(8,128)}, u32[]{:S(2)}) copy-start(f32[48,256]{1,0:T(8,128)} %get-tuple-element.36) | copy-start | bytes 147460
  28.7 12.8 %all-to-all-start.1 = ((f32[8,40,128]{2,1,0:T(8,128)}), f32[8,40,128]{2,1,0:T(8,128)S(1)}, u32[]{:S(2)}, u32[]{:S(2)}) async-start(f32[8,40,128]{2,1,0:T(8,128)} %get-tuple-element.35), calls=%async_computation.1 | async-start | bytes 327680 | tf_op jit(solution)/shard_map/all_to_all | solution.py:567
  32.2 9.3 %collective-permute-start.1 = (f32[48,256]{1,0:T(8,128)S(1)}, f32[48,256]{1,0:T(8,128)S(1)}, u32[]{:S(2)}, u32[]{:S(2)}) collective-permute-start(f32[48,256]{1,0:T(8,128)S(1)} %copy-done.5), channel_id=1, source_target_pairs={{1,0},{2,1},{3,2},{4,3},{5,4},{6,5},{7,6},{8,7},{9,8},{10,9},{11,1... | collective-permute-start | bytes 147464 | tf_op jit(solution)/shard_map/ppermute | solution.py:582
  42.3 14.6 %all-to-all-start.2 = ((f32[8,88,128]{2,1,0:T(8,128)}), f32[8,88,128]{2,1,0:T(8,128)S(1)}, u32[]{:S(2)}, u32[]{:S(2)}) async-start(f32[8,88,128]{2,1,0:T(8,128)} %cells.1), calls=%async_computation.2 | async-start | bytes 720896 | tf_op jit(solution)/shard_map/all_to_all | solution.py:567
  59.3 14.7 %all-to-all-start.3 = ((f32[8,9,8,128]{3,2,1,0:T(8,128)}), f32[8,9,8,128]{3,2,1,0:T(8,128)S(1)}, u32[]{:S(2)}, u32[]{:S(2)}) async-start(f32[8,9,8,128]{3,2,1,0:T(8,128)} %far_top.1), calls=%async_computation.3 | async-start | bytes 589824 | tf_op jit(solution)/shard_map/all_to_all | solution.py:567
  64.0 10.0 %copy-start = (f32[8,128,256]{2,1,0:T(8,128)S(1)}, f32[8,128,256]{2,1,0:T(8,128)}, u32[]{:S(2)}) copy-start(f32[8,128,256]{2,1,0:T(8,128)} %up.1) | copy-start | bytes 3145732
  64.0 10.0 %copy-start.1 = (f32[8,128,128]{2,1,0:T(8,128)S(1)}, f32[8,128,128]{2,1,0:T(8,128)}, u32[]{:S(2)}) copy-start(f32[8,128,128]{2,1,0:T(8,128)} %utm.1) | copy-start | bytes 1572868

commit v14 on v13

--- a/solution.py
+++ b/solution.py
@@ -21,7 +21,7 @@
 DUMMY = 64
 CHUNK = 16
 NEAR_DUMMY = 16
-FIRST_OWN = 32
+FIRST_OWN = 24
 
 SMEM = pl.BlockSpec(memory_space=pltpu.SMEM)
 HBM = pl.BlockSpec(memory_space=pltpu.HBM)
@@ -238,25 +238,19 @@
     )(*args)
 
 
-FIRST, MIDDLE, LAST = range(3)
-
-
-def near_blocks(ids, flat, base, first_leaf, stage):
+def near_blocks(ids, flat, base, first):
     pos = jnp.int32(0)
     seen = jnp.int32(0)
-    for l in range(first_leaf, OWN):
+    for l in range(OWN):
         for n in range(NBR):
             ident = ids[l, n]
             e = ident - base
             flat[pos] = l * 32 + e
-            if stage == LAST:
-                take = e >= REACH + OWN
-            else:
-                own = (e >= REACH) & (e < REACH + OWN)
-                take = own & (seen < FIRST_OWN)
-                if stage == MIDDLE:
-                    take = (ident >= 0) & (e < REACH + OWN) & jnp.logical_not(take)
-                seen = seen + own.astype(jnp.int32)
+            own = (e >= REACH) & (e < REACH + OWN)
+            take = own & (seen < FIRST_OWN)
+            if not first:
+                take = (ident >= 0) & jnp.logical_not(take)
+            seen = seen + own.astype(jnp.int32)
             pos = pos + take.astype(jnp.int32)
     for u in range(CHUNK):
         flat[pos + u] = (OWN - 1) * 32 + NEAR_DUMMY
@@ -298,7 +292,7 @@
 
 
 def near_first_kernel(ids, pts, chg, out, flat, fs, ft, vals, xyz, ts, tl):
-    count = near_blocks(ids, flat, near_base(), 0, FIRST)
+    count = near_blocks(ids, flat, near_base(), True)
     for c in range(3):
         xyz[c] = jnp.zeros((16, 256), F32)
         xyz[c, 4:12, :] = pts[c]
@@ -307,38 +301,27 @@
     near_run(count, flat, None, out, fs, ft, vals)
 
 
-def near_middle_kernel(ids, pts, chg, before, start, out, flat, fs, ft, vals, xyz, ts, tl):
-    count = near_blocks(ids, flat, near_base(), 0, MIDDLE)
+def near_rest_kernel(ids, pts, chg, before, after, start, out, flat, fs, ft, vals, xyz, ts, tl):
+    count = near_blocks(ids, flat, near_base(), False)
     for c in range(3):
         xyz[c, 0:4, :] = before[32 + 4 * c : 36 + 4 * c, :]
         xyz[c, 4:12, :] = pts[c]
-        xyz[c, 12:16, :] = jnp.zeros((4, 256), F32)
+        xyz[c, 12:16, :] = after[32 + 4 * c : 36 + 4 * c, :]
 
     def vals_of(e):
-        return before[8 * e : 8 * e + 8, :] if e < REACH else chg[e - REACH]
-
-    near_setup(range(REACH + OWN), range(OWN), [xyz[0], xyz[1], xyz[2]], vals_of, fs, ft, vals, ts, tl)
+        if e < REACH:
+            return before[8 * e : 8 * e + 8, :]
+        if e < REACH + OWN:
+            return chg[e - REACH]
+        return after[8 * (e - REACH - OWN) : 8 * (e - REACH - OWN) + 8, :]
+
+    near_setup(range(OWN + 2 * REACH), range(OWN), [xyz[0], xyz[1], xyz[2]], vals_of, fs, ft, vals, ts, tl)
     near_run(count, flat, start, out, fs, ft, vals)
 
 
-def near_last_kernel(ids, pts, after, out, flat, fs, ft, vals, xyz, ts, tl):
-    count = near_blocks(ids, flat, near_base(), OWN - REACH, LAST)
-    for c in range(3):
-        xyz[c, 0:4, :] = jnp.zeros((4, 256), F32)
-        xyz[c, 4:12, :] = pts[c]
-        xyz[c, 12:16, :] = after[32 + 4 * c : 36 + 4 * c, :]
-
-    def vals_of(e):
-        return after[8 * (e - REACH - OWN) : 8 * (e - REACH - OWN) + 8, :]
-
-    halo = range(REACH + OWN, 2 * REACH + OWN)
-    near_setup(halo, range(OWN - REACH, OWN), [xyz[0], xyz[1], xyz[2]], vals_of, fs, ft, vals, ts, tl)
-    near_run(count, flat, None, out, fs, ft, vals)
-
-
-def near_part(stage, *args):
-    return pl.pallas_call(
-        (near_first_kernel, near_middle_kernel, near_last_kernel)[stage],
+def near_part(kernel, *args):
+    return pl.pallas_call(
+        kernel,
         in_specs=[SMEM] + [VMEM] * (len(args) - 1),
         out_specs=VMEM,
         out_shape=jax.ShapeDtypeStruct((OWN, 8, 256), F32),
@@ -532,25 +515,25 @@
     )(counts, flat, src, ft, part)
 
 
-def final_kernel(got, utm, up, near1, near2, out):
+def final_kernel(got, utm, up, near, out):
     tot = got[0]
     for d in range(1, 8):
         tot = tot + got[d]
     cell = tot[8]
     for l in range(OWN):
         incoming = tot[l] + dot3(cell, utm[l])
-        out[l] = near1[l] + near2[l] + dot3(incoming, up[l])
-
-
-def final(got, utm, up, near1, near2):
+        out[l] = near[l] + dot3(incoming, up[l])
+
+
+def final(got, utm, up, near):
     return pl.pallas_call(
         final_kernel,
-        in_specs=[VMEM] * 5,
+        in_specs=[VMEM] * 4,
         out_specs=VMEM,
         out_shape=jax.ShapeDtypeStruct((8, 8, 256), F32),
         compiler_params=PARAMS,
         name="final",
-    )(got, utm, up, near1, near2)
+    )(got, utm, up, near)
 
 
 def device(g, u, v):
@@ -576,12 +559,11 @@
     m1, charges1 = lax.optimization_barrier((m1, charges))
     got1 = exchange(m1, along_u)
     before = lax.ppermute(last, "d", up)
-    near0 = near_part(FIRST, near_list, pts, charges1)
+    near0 = near_part(near_first_kernel, near_list, pts, charges1)
     got1, before, near0, m0, first = lax.optimization_barrier((got1, before, near0, m0, first))
     got0 = exchange(m0, along_v)
     after = lax.ppermute(first, "d", down)
-    near1 = near_part(MIDDLE, near_list, pts, charges, before, near0)
-    got0, after, near1 = lax.optimization_barrier((got0, after, near1))
+    got0, after = lax.optimization_barrier((got0, after))
     cells, got0 = lax.optimization_barrier((cells_message(got1, got0), got0))
     gotg = exchange(cells, along_g)
     req = got0[:, 27:29, :].astype(jnp.int32)
@@ -590,8 +572,8 @@
     part = far_top(counts, top_flat, gotg, ftop, part)
     part, after = lax.optimization_barrier((part, after))
     gotr = exchange(part, along_v)
-    near2 = near_part(LAST, near_list, pts, after)
-    return final(gotr, utm, up_op, near1, near2)
+    near = near_part(near_rest_kernel, near_list, pts, charges, before, after, near0)
+    return final(gotr, utm, up_op, near)
 
 
 def solution(mesh):

time: 76 us -> 76.3 us (level)
  starting transfers between devices: 36.6 us -> 38.2 us
    all_to_all x4, waiting for transfers between devices: 8.37 us -> 5.84 us  [exchange(): return lax.all_to_all(x, 'd', 0, 0, axis_index_groups=groups, tiled=True)]
    all_to_all x4, starting transfers between devices: 26.2 us -> 27.8 us  [exchange(): return lax.all_to_all(x, 'd', 0, 0, axis_index_groups=groups, tiled=True)]
    ppermute x1, waiting for transfers between devices: 0.01 us -> 1.16 us  [body(): after = lax.ppermute(first, 'd', down)]
    ppermute x1, waiting for transfers between devices: 6.32 us -> 7.12 us  [body(): before = lax.ppermute(last, 'd', up)]
    pallas_call x4 -> x3, Pallas kernels: 9.94 us -> 9.14 us  [the longest x2 7.98 us: near_part(): pl.pallas_call(kernel, in_specs=[SMEM] + [VMEM] * (len(args) - 1), out_sp...]
  transfers between devices with their start and end apart: 6 -> 6, of which waited for: 3 -> 3; matrix products, arithmetic and copies ran while one was open for 0% -> 0% of each run, Pallas kernels for 22% -> 21%
where the time goes in v14:
time: 76.3 us; the launch traced here: 75.7 us
  starting transfers between devices  38.2 us (50%)
  Pallas kernels  23.2 us (30%)
  waiting for transfers between devices  14.1 us (18%)
    all_to_all x4, starting transfers between devices, exchange(): return lax.all_to_all(x, 'd', 0, 0, axis_index_groups=groups, tiled=True)  27.8 us
    pallas_call x2, Pallas kernels, near_part(): pl.pallas_call(kernel, in_specs=[SMEM] + [VMEM] * (len(args) - 1), out_sp...  7.98 us
    ppermute x1, waiting for transfers between devices, body(): before = lax.ppermute(last, 'd', up)  7.12 us
    ppermute x1, starting transfers between devices, body(): after = lax.ppermute(first, 'd', down)  7.09 us
    all_to_all x4, waiting for transfers between devices, exchange(): return lax.all_to_all(x, 'd', 0, 0, axis_index_groups=groups, tiled=True)  5.84 us
    pallas_call x1, Pallas kernels, far_leaf(): pl.pallas_call(far_leaf_kernel, in_specs=[SMEM, SMEM, VMEM, VMEM], out_sp...  5.46 us
    ppermute x1, starting transfers between devices, body(): before = lax.ppermute(last, 'd', up)  3.36 us
    pallas_call x1, Pallas kernels, pack(): pl.pallas_call(pack_kernel, in_specs=[HBM] * 8, out_specs=[HBM] * 4, out_...  3.14 us
  transfers between devices with their start and end apart: 6, of which 3 were waited for; matrix products, arithmetic and copies ran while one was open for 0% of the time, Pallas kernels for 21%

profile of v14, /device:TPU:1, one launch (start us, length us, event | category | flops | bytes accessed | tf_op | source)
XLA Modules:
  0.0 75.7 jit_solution(6709551191399402604)
XLA Ops:
  0.0 3.1 %pack.1 = (f32[8,40,128]{2,1,0:T(8,128)}, f32[8,104,128]{2,1,0:T(8,128)}, f32[48,256]{1,0:T(8,128)}, f32[48,256]{1,0:T(8,128)}) custom-call(f32[3,8,256]{2,1,0:T(8,128)} %bitcast.5, f32[8,8,256]{2,1,0:T(8,128)} %chg.2, f32[3,8,128]{2,1,0:T(8,128)} %bitcast.8, f32[3,1,128]{2,1,0:T(1,128)} %bitcast.9, s32[8,16]{1,0:T(8,128)} %llist_h.1, s32[1,16]{1,0:T(1,128)} %tlist_h.1, ...), custom_call_target="tpu_custom_call" | custom-call | tf_op jit(solution)/shard_map/pack/pallas_call | solution.py:228
  3.1 0.0 copy-start.6
  3.2 0.0 copy-start.2
  3.2 0.0 copy-start.3
  3.2 0.0 copy-start.4
  3.2 11.0 %all-to-all-start = ((f32[8,104,128]{2,1,0:T(8,128)}), f32[8,104,128]{2,1,0:T(8,128)S(1)}, u32[]{:S(2)}, u32[]{:S(2)}) async-start(f32[8,104,128]{2,1,0:T(8,128)} %get-tuple-element.28), calls=%async_computation | async-start | bytes 851968 | tf_op jit(solution)/shard_map/all_to_all | solution.py:550
  14.2 0.0 copy-done.6
  14.2 3.4 %collective-permute-start = (f32[48,256]{1,0:T(8,128)S(1)}, f32[48,256]{1,0:T(8,128)S(1)}, u32[]{:S(2)}, u32[]{:S(2)}) collective-permute-start(f32[48,256]{1,0:T(8,128)S(1)} %copy-done.6), channel_id=1, source_target_pairs={{0,1},{1,2},{2,3},{3,4},{4,5},{5,6},{6,7},{7,8},{8,9},{9,10},{10,1... | collective-permute-start | bytes 147464 | tf_op jit(solution)/shard_map/ppermute | solution.py:561
  17.6 0.0 copy-done.2
  17.6 0.0 copy-done.3
  17.6 0.0 copy-done.4
  17.6 3.9 %near.2.start = f32[8,8,256]{2,1,0:T(8,128)S(1)} custom-call(s32[8,9]{1,0:T(8,128)S(1)} %copy-done.4, f32[3,8,256]{2,1,0:T(8,128)S(1)} %bitcast.6, f32[8,8,256]{2,1,0:T(8,128)S(1)} %copy-done.2), custom_call_target="tpu_custom_call" | custom-call | flops 2000000000 | bytes 300000 | tf_op jit(solution)/shard_map/near/pallas_call | solution.py:323
  21.5 7.1 %collective-permute-done.before = f32[48,256]{1,0:T(8,128)S(1)} collective-permute-done((f32[48,256]{1,0:T(8,128)S(1)}, f32[48,256]{1,0:T(8,128)S(1)}, u32[]{:S(2)}, u32[]{:S(2)}) %collective-permute-start) | collective-permute-done | bytes 49184 | tf_op jit(solution)/shard_map/ppermute | solution.py:561
  28.7 0.0 all-to-all-done.along_u.src
  28.7 3.5 %all-to-all-start.1 = ((f32[8,40,128]{2,1,0:T(8,128)}), f32[8,40,128]{2,1,0:T(8,128)S(1)}, u32[]{:S(2)}, u32[]{:S(2)}) async-start(f32[8,40,128]{2,1,0:T(8,128)} %get-tuple-element.34), calls=%async_computation.1 | async-start | bytes 327680 | tf_op jit(solution)/shard_map/all_to_all | solution.py:550
  32.2 0.0 copy-done.5
  32.2 7.1 %collective-permute-start.1 = (f32[48,256]{1,0:T(8,128)S(1)}, f32[48,256]{1,0:T(8,128)S(1)}, u32[]{:S(2)}, u32[]{:S(2)}) collective-permute-start(f32[48,256]{1,0:T(8,128)S(1)} %copy-done.5), channel_id=1, source_target_pairs={{1,0},{2,1},{3,2},{4,3},{5,4},{6,5},{7,6},{8,7},{9,8},{10,9},{11,1... | collective-permute-start | bytes 147464 | tf_op jit(solution)/shard_map/ppermute | solution.py:565
  39.3 1.2 %collective-permute-done.1.after = f32[48,256]{1,0:T(8,128)S(1)} collective-permute-done((f32[48,256]{1,0:T(8,128)S(1)}, f32[48,256]{1,0:T(8,128)S(1)}, u32[]{:S(2)}, u32[]{:S(2)}) %collective-permute-start.1) | collective-permute-done | bytes 49184 | tf_op jit(solution)/shard_map/ppermute | solution.py:565
  40.4 0.0 all-to-all-done.1.along_v
  40.4 0.8 %cells.1 = f32[8,88,128]{2,1,0:T(8,128)} custom-call(f32[8,104,128]{2,1,0:T(8,128)S(1)} %all-to-all-done.along_u.src, f32[8,40,128]{2,1,0:T(8,128)S(1)} %all-to-all-done.1.along_v), custom_call_target="tpu_custom_call" | custom-call | tf_op jit(solution)/shard_map/cells/pallas_call | solution.py:480
  41.3 7.9 %all-to-all-start.2 = ((f32[8,88,128]{2,1,0:T(8,128)}), f32[8,88,128]{2,1,0:T(8,128)S(1)}, u32[]{:S(2)}, u32[]{:S(2)}) async-start(f32[8,88,128]{2,1,0:T(8,128)} %cells.1), calls=%async_computation.2 | async-start | bytes 720896 | tf_op jit(solution)/shard_map/all_to_all | solution.py:550
  49.2 2.4 %far_prep.1 = (bf16[64,32,128]{2,1,0:T(8,128)(2,1)S(1)}, bf16[8,32,128]{2,1,0:T(8,128)(2,1)S(1)}, s32[1088]{0:T(1024)S(1)}, s32[256]{0:T(256)S(1)}, s32[2]{0:T(128)S(1)}) custom-call(s32[8,2,128]{2,1,0:T(2,128)S(1)} %slice_convert_fusion.req, f32[320,128]{1,0:T(8,128)S(1)} %bitcast.4), custom_call_target="tpu_custom_call" | custom-call | flops 100000000 | bytes 900000 | tf_op jit(solution)/shard_map/far_prep/pallas_call | solution.py:414
  51.6 5.5 %far_leaf.1.part = f32[8,9,8,128]{3,2,1,0:T(8,128)S(1)} custom-call(s32[2]{0:T(128)S(1)} %get-tuple-element.38.counts, s32[1088]{0:T(1024)S(1)} %get-tuple-element.42.flat, f32[8,104,128]{2,1,0:T(8,128)S(1)} %all-to-all-done.along_u.src, bf16[64,32,128]{2,1,0:T(8,128)(2,1)S(1)} %get-tuple-element.43.ft), custom_call_target="tpu_custom_call" | custom-call | flops 2097152000 | bytes 900000 | tf_op jit(solution)/shard_map/far_leaf/pallas_call | solution.py:455
  57.1 0.0 all-to-all-done.2.src
  57.1 2.2 %far_top.1 = f32[8,9,8,128]{3,2,1,0:T(8,128)} custom-call(s32[2]{0:T(128)S(1)} %get-tuple-element.38.counts, s32[256]{0:T(256)S(1)} %get-tuple-element.39.flat, f32[8,88,128]{2,1,0:T(8,128)S(1)} %all-to-all-done.2.src, bf16[8,32,128]{2,1,0:T(8,128)(2,1)S(1)} %get-tuple-element.41.ft, f32[8,9,8,128]{3,2,1,0:T(8,128)S(1)} %far_leaf.1.part), custom_call_target="tpu_custom_call" | custom-call | tf_op jit(solution)/shard_map/far_top/pallas_call | solution.py:507
  59.3 5.4 %all-to-all-start.3 = ((f32[8,9,8,128]{3,2,1,0:T(8,128)}), f32[8,9,8,128]{3,2,1,0:T(8,128)S(1)}, u32[]{:S(2)}, u32[]{:S(2)}) async-start(f32[8,9,8,128]{3,2,1,0:T(8,128)} %far_top.1), calls=%async_computation.3 | async-start | bytes 589824 | tf_op jit(solution)/shard_map/all_to_all | solution.py:550
  64.7 0.0 copy-start.1
  64.7 4.0 %near.3 = f32[8,8,256]{2,1,0:T(8,128)S(1)} custom-call(s32[8,9]{1,0:T(8,128)S(1)} %copy-done.4, f32[3,8,256]{2,1,0:T(8,128)S(1)} %bitcast.7, f32[8,8,256]{2,1,0:T(8,128)S(1)} %copy-done.2, f32[48,256]{1,0:T(8,128)S(1)} %collective-permute-done.before, f32[48,256]{1,0:T(8,128)S(1)} %collective-permute-done.1.after, f32[8,8,256]{2,1,0:T(8,128)S(1)} %near.2.start), custom_call_target="tpu_custom_call" | custom-call | flops 2000000000 | bytes 300000 | tf_op jit(solution)/shard_map/near/pallas_call | solution.py:323
  68.7 5.8 %all-to-all-done.3.got = f32[8,9,8,128]{3,2,1,0:T(8,128)S(1)} async-done(((f32[8,9,8,128]{3,2,1,0:T(8,128)}), f32[8,9,8,128]{3,2,1,0:T(8,128)S(1)}, u32[]{:S(2)}, u32[]{:S(2)}) %all-to-all-start.3) | async-done | bytes 294944 | tf_op jit(solution)/shard_map/all_to_all | solution.py:550
  74.6 0.0 copy-done
  74.6 0.0 copy-done.1
  74.6 1.2 %final.1 = f32[8,8,256]{2,1,0:T(8,128)} custom-call(f32[8,9,8,128]{3,2,1,0:T(8,128)S(1)} %all-to-all-done.3.got, f32[8,128,128]{2,1,0:T(8,128)S(1)} %copy-done.1, f32[8,128,256]{2,1,0:T(8,128)S(1)} %copy-done, f32[8,8,256]{2,1,0:T(8,128)S(1)} %near.3), custom_call_target="tpu_custom_call" | custom-call | tf_op jit(solution)/shard_map/final/pallas_call | solution.py:529
  (3 shorter events, 0.0 us)
Async XLA Ops:
  3.1 11.1 %copy-start.6 = (f32[48,256]{1,0:T(8,128)S(1)}, f32[48,256]{1,0:T(8,128)}, u32[]{:S(2)}) copy-start(f32[48,256]{1,0:T(8,128)} %get-tuple-element.29) | copy-start | bytes 147460
  3.2 14.4 %copy-start.2 = (f32[8,8,256]{2,1,0:T(8,128)S(1)}, f32[8,8,256]{2,1,0:T(8,128)}, u32[]{:S(2)}) copy-start(f32[8,8,256]{2,1,0:T(8,128)} %chg.2) | copy-start | bytes 196612
  3.2 14.4 %copy-start.3 = (f32[8,3,256]{2,0,1:T(8,128)S(1)}, f32[8,3,256]{2,0,1:T(8,128)}, u32[]{:S(2)}) copy-start(f32[8,3,256]{2,0,1:T(8,128)} %param.9) | copy-start | bytes 73732
  3.2 14.4 %copy-start.4 = (s32[8,9]{1,0:T(8,128)S(1)}, s32[8,9]{1,0:T(8,128)}, u32[]{:S(2)}) copy-start(s32[8,9]{1,0:T(8,128)} %ids.3) | copy-start | bytes 868
  3.2 25.5 %all-to-all-start = ((f32[8,104,128]{2,1,0:T(8,128)}), f32[8,104,128]{2,1,0:T(8,128)S(1)}, u32[]{:S(2)}, u32[]{:S(2)}) async-start(f32[8,104,128]{2,1,0:T(8,128)} %get-tuple-element.28), calls=%async_computation | async-start | bytes 851968 | tf_op jit(solution)/shard_map/all_to_all | solution.py:550
  14.2 14.5 %collective-permute-start = (f32[48,256]{1,0:T(8,128)S(1)}, f32[48,256]{1,0:T(8,128)S(1)}, u32[]{:S(2)}, u32[]{:S(2)}) collective-permute-start(f32[48,256]{1,0:T(8,128)S(1)} %copy-done.6), channel_id=1, source_target_pairs={{0,1},{1,2},{2,3},{3,4},{4,5},{5,6},{6,7},{7,8},{8,9},{9,10},{10,1... | collective-permute-start | bytes 147464 | tf_op jit(solution)/shard_map/ppermute | solution.py:561
  28.7 3.5 %copy-start.5 = (f32[48,256]{1,0:T(8,128)S(1)}, f32[48,256]{1,0:T(8,128)}, u32[]{:S(2)}) copy-start(f32[48,256]{1,0:T(8,128)} %get-tuple-element.35) | copy-start | bytes 147460
  28.7 11.8 %all-to-all-start.1 = ((f32[8,40,128]{2,1,0:T(8,128)}), f32[8,40,128]{2,1,0:T(8,128)S(1)}, u32[]{:S(2)}, u32[]{:S(2)}) async-start(f32[8,40,128]{2,1,0:T(8,128)} %get-tuple-element.34), calls=%async_computation.1 | async-start | bytes 327680 | tf_op jit(solution)/shard_map/all_to_all | solution.py:550
  32.2 8.3 %collective-permute-start.1 = (f32[48,256]{1,0:T(8,128)S(1)}, f32[48,256]{1,0:T(8,128)S(1)}, u32[]{:S(2)}, u32[]{:S(2)}) collective-permute-start(f32[48,256]{1,0:T(8,128)S(1)} %copy-done.5), channel_id=1, source_target_pairs={{1,0},{2,1},{3,2},{4,3},{5,4},{6,5},{7,6},{8,7},{9,8},{10,9},{11,1... | collective-permute-start | bytes 147464 | tf_op jit(solution)/shard_map/ppermute | solution.py:565
  41.3 15.8 %all-to-all-start.2 = ((f32[8,88,128]{2,1,0:T(8,128)}), f32[8,88,128]{2,1,0:T(8,128)S(1)}, u32[]{:S(2)}, u32[]{:S(2)}) async-start(f32[8,88,128]{2,1,0:T(8,128)} %cells.1), calls=%async_computation.2 | async-start | bytes 720896 | tf_op jit(solution)/shard_map/all_to_all | solution.py:550
  59.3 15.3 %all-to-all-start.3 = ((f32[8,9,8,128]{3,2,1,0:T(8,128)}), f32[8,9,8,128]{3,2,1,0:T(8,128)S(1)}, u32[]{:S(2)}, u32[]{:S(2)}) async-start(f32[8,9,8,128]{3,2,1,0:T(8,128)} %far_top.1), calls=%async_computation.3 | async-start | bytes 589824 | tf_op jit(solution)/shard_map/all_to_all | solution.py:550
  64.7 9.9 %copy-start = (f32[8,128,256]{2,1,0:T(8,128)S(1)}, f32[8,128,256]{2,1,0:T(8,128)}, u32[]{:S(2)}) copy-start(f32[8,128,256]{2,1,0:T(8,128)} %up.1) | copy-start | bytes 3145732
  64.7 9.9 %copy-start.1 = (f32[8,128,128]{2,1,0:T(8,128)S(1)}, f32[8,128,128]{2,1,0:T(8,128)}, u32[]{:S(2)}) copy-start(f32[8,128,128]{2,1,0:T(8,128)} %utm.1) | copy-start | bytes 1572868

commit v15 on v14

--- a/solution.py
+++ b/solution.py
@@ -21,7 +21,7 @@
 DUMMY = 64
 CHUNK = 16
 NEAR_DUMMY = 16
-FIRST_OWN = 24
+FIRST_OWN = 16
 
 SMEM = pl.BlockSpec(memory_space=pltpu.SMEM)
 HBM = pl.BlockSpec(memory_space=pltpu.HBM)

time: 76.3 us -> 75.7 us (level)
  starting transfers between devices: 38.2 us -> 36.3 us
  Pallas kernels: 23.2 us -> 24.1 us
    all_to_all x4, starting transfers between devices: 27.8 us -> 25.8 us  [exchange(): return lax.all_to_all(x, 'd', 0, 0, axis_index_groups=groups, tiled=True)]
    ppermute x1, waiting for transfers between devices: 7.12 us -> 8.19 us  [body(): before = lax.ppermute(last, 'd', up)]
    all_to_all x4, waiting for transfers between devices: 5.84 us -> 5.02 us  [exchange(): return lax.all_to_all(x, 'd', 0, 0, axis_index_groups=groups, tiled=True)]
  transfers between devices with their start and end apart: 6 -> 6, of which waited for: 3 -> 3; matrix products, arithmetic and copies ran while one was open for 0% -> 0% of each run, Pallas kernels for 21% -> 22%
where the time goes in v15:
time: 75.7 us; the launch traced here: 75 us
  starting transfers between devices  36.3 us (48%)
  Pallas kernels  24.1 us (32%)
  waiting for transfers between devices  14.4 us (19%)
    all_to_all x4, starting transfers between devices, exchange(): return lax.all_to_all(x, 'd', 0, 0, axis_index_groups=groups, tiled=True)  25.8 us
    ppermute x1, waiting for transfers between devices, body(): before = lax.ppermute(last, 'd', up)  8.19 us
    pallas_call x2, Pallas kernels, near_part(): pl.pallas_call(kernel, in_specs=[SMEM] + [VMEM] * (len(args) - 1), out_sp...  7.73 us
    ppermute x1, starting transfers between devices, body(): after = lax.ppermute(first, 'd', down)  7.09 us
    pallas_call x1, Pallas kernels, far_leaf(): pl.pallas_call(far_leaf_kernel, in_specs=[SMEM, SMEM, VMEM, VMEM], out_sp...  6.2 us
    all_to_all x4, waiting for transfers between devices, exchange(): return lax.all_to_all(x, 'd', 0, 0, axis_index_groups=groups, tiled=True)  5.02 us
    ppermute x1, starting transfers between devices, body(): before = lax.ppermute(last, 'd', up)  3.36 us
    pallas_call x1, Pallas kernels, pack(): pl.pallas_call(pack_kernel, in_specs=[HBM] * 8, out_specs=[HBM] * 4, out_...  3.14 us
  transfers between devices with their start and end apart: 6, of which 3 were waited for; matrix products, arithmetic and copies ran while one was open for 0% of the time, Pallas kernels for 22%

profile of v15, /device:TPU:1, one launch (start us, length us, event | category | flops | bytes accessed | tf_op | source)
XLA Modules:
  0.0 75.0 jit_solution(516967051896013714)
XLA Ops:
  0.0 3.1 %pack.1 = (f32[8,40,128]{2,1,0:T(8,128)}, f32[8,104,128]{2,1,0:T(8,128)}, f32[48,256]{1,0:T(8,128)}, f32[48,256]{1,0:T(8,128)}) custom-call(f32[3,8,256]{2,1,0:T(8,128)} %bitcast.5, f32[8,8,256]{2,1,0:T(8,128)} %chg.2, f32[3,8,128]{2,1,0:T(8,128)} %bitcast.8, f32[3,1,128]{2,1,0:T(1,128)} %bitcast.9, s32[8,16]{1,0:T(8,128)} %llist_h.1, s32[1,16]{1,0:T(1,128)} %tlist_h.1, ...), custom_call_target="tpu_custom_call" | custom-call | tf_op jit(solution)/shard_map/pack/pallas_call | solution.py:228
  3.1 0.0 copy-start.6
  3.2 0.0 copy-start.2
  3.2 0.0 copy-start.3
  3.2 0.0 copy-start.4
  3.2 11.0 %all-to-all-start = ((f32[8,104,128]{2,1,0:T(8,128)}), f32[8,104,128]{2,1,0:T(8,128)S(1)}, u32[]{:S(2)}, u32[]{:S(2)}) async-start(f32[8,104,128]{2,1,0:T(8,128)} %get-tuple-element.28), calls=%async_computation | async-start | bytes 851968 | tf_op jit(solution)/shard_map/all_to_all | solution.py:550
  14.2 0.0 copy-done.6
  14.2 3.4 %collective-permute-start = (f32[48,256]{1,0:T(8,128)S(1)}, f32[48,256]{1,0:T(8,128)S(1)}, u32[]{:S(2)}, u32[]{:S(2)}) collective-permute-start(f32[48,256]{1,0:T(8,128)S(1)} %copy-done.6), channel_id=1, source_target_pairs={{0,1},{1,2},{2,3},{3,4},{4,5},{5,6},{6,7},{7,8},{8,9},{9,10},{10,1... | collective-permute-start | bytes 147464 | tf_op jit(solution)/shard_map/ppermute | solution.py:561
  17.6 0.0 copy-done.2
  17.6 0.0 copy-done.3
  17.6 0.0 copy-done.4
  17.6 2.9 %near.2.start = f32[8,8,256]{2,1,0:T(8,128)S(1)} custom-call(s32[8,9]{1,0:T(8,128)S(1)} %copy-done.4, f32[3,8,256]{2,1,0:T(8,128)S(1)} %bitcast.6, f32[8,8,256]{2,1,0:T(8,128)S(1)} %copy-done.2), custom_call_target="tpu_custom_call" | custom-call | flops 2000000000 | bytes 300000 | tf_op jit(solution)/shard_map/near/pallas_call | solution.py:323
  20.5 8.2 %collective-permute-done.before = f32[48,256]{1,0:T(8,128)S(1)} collective-permute-done((f32[48,256]{1,0:T(8,128)S(1)}, f32[48,256]{1,0:T(8,128)S(1)}, u32[]{:S(2)}, u32[]{:S(2)}) %collective-permute-start) | collective-permute-done | bytes 49184 | tf_op jit(solution)/shard_map/ppermute | solution.py:561
  28.7 0.0 all-to-all-done.along_u.src
  28.7 3.5 %all-to-all-start.1 = ((f32[8,40,128]{2,1,0:T(8,128)}), f32[8,40,128]{2,1,0:T(8,128)S(1)}, u32[]{:S(2)}, u32[]{:S(2)}) async-start(f32[8,40,128]{2,1,0:T(8,128)} %get-tuple-element.34), calls=%async_computation.1 | async-start | bytes 327680 | tf_op jit(solution)/shard_map/all_to_all | solution.py:550
  32.2 0.0 copy-done.5
  32.2 7.1 %collective-permute-start.1 = (f32[48,256]{1,0:T(8,128)S(1)}, f32[48,256]{1,0:T(8,128)S(1)}, u32[]{:S(2)}, u32[]{:S(2)}) collective-permute-start(f32[48,256]{1,0:T(8,128)S(1)} %copy-done.5), channel_id=1, source_target_pairs={{1,0},{2,1},{3,2},{4,3},{5,4},{6,5},{7,6},{8,7},{9,8},{10,9},{11,1... | collective-permute-start | bytes 147464 | tf_op jit(solution)/shard_map/ppermute | solution.py:565
  39.3 1.2 %collective-permute-done.1.after = f32[48,256]{1,0:T(8,128)S(1)} collective-permute-done((f32[48,256]{1,0:T(8,128)S(1)}, f32[48,256]{1,0:T(8,128)S(1)}, u32[]{:S(2)}, u32[]{:S(2)}) %collective-permute-start.1) | collective-permute-done | bytes 49184 | tf_op jit(solution)/shard_map/ppermute | solution.py:565
  40.4 0.0 all-to-all-done.1.along_v
  40.4 0.8 %cells.1 = f32[8,88,128]{2,1,0:T(8,128)} custom-call(f32[8,104,128]{2,1,0:T(8,128)S(1)} %all-to-all-done.along_u.src, f32[8,40,128]{2,1,0:T(8,128)S(1)} %all-to-all-done.1.along_v), custom_call_target="tpu_custom_call" | custom-call | tf_op jit(solution)/shard_map/cells/pallas_call | solution.py:480
  41.3 7.9 %all-to-all-start.2 = ((f32[8,88,128]{2,1,0:T(8,128)}), f32[8,88,128]{2,1,0:T(8,128)S(1)}, u32[]{:S(2)}, u32[]{:S(2)}) async-start(f32[8,88,128]{2,1,0:T(8,128)} %cells.1), calls=%async_computation.2 | async-start | bytes 720896 | tf_op jit(solution)/shard_map/all_to_all | solution.py:550
  49.2 2.5 %far_prep.1 = (bf16[64,32,128]{2,1,0:T(8,128)(2,1)S(1)}, bf16[8,32,128]{2,1,0:T(8,128)(2,1)S(1)}, s32[1088]{0:T(1024)S(1)}, s32[256]{0:T(256)S(1)}, s32[2]{0:T(128)S(1)}) custom-call(s32[8,2,128]{2,1,0:T(2,128)S(1)} %slice_convert_fusion.req, f32[320,128]{1,0:T(8,128)S(1)} %bitcast.4), custom_call_target="tpu_custom_call" | custom-call | flops 100000000 | bytes 900000 | tf_op jit(solution)/shard_map/far_prep/pallas_call | solution.py:414
  51.7 6.2 %far_leaf.1.part = f32[8,9,8,128]{3,2,1,0:T(8,128)S(1)} custom-call(s32[2]{0:T(128)S(1)} %get-tuple-element.38.counts, s32[1088]{0:T(1024)S(1)} %get-tuple-element.42.flat, f32[8,104,128]{2,1,0:T(8,128)S(1)} %all-to-all-done.along_u.src, bf16[64,32,128]{2,1,0:T(8,128)(2,1)S(1)} %get-tuple-element.43.ft), custom_call_target="tpu_custom_call" | custom-call | flops 2097152000 | bytes 900000 | tf_op jit(solution)/shard_map/far_leaf/pallas_call | solution.py:455
  57.9 0.0 all-to-all-done.2.src
  57.9 2.6 %far_top.1 = f32[8,9,8,128]{3,2,1,0:T(8,128)} custom-call(s32[2]{0:T(128)S(1)} %get-tuple-element.38.counts, s32[256]{0:T(256)S(1)} %get-tuple-element.39.flat, f32[8,88,128]{2,1,0:T(8,128)S(1)} %all-to-all-done.2.src, bf16[8,32,128]{2,1,0:T(8,128)(2,1)S(1)} %get-tuple-element.41.ft, f32[8,9,8,128]{3,2,1,0:T(8,128)S(1)} %far_leaf.1.part), custom_call_target="tpu_custom_call" | custom-call | tf_op jit(solution)/shard_map/far_top/pallas_call | solution.py:507
  60.5 3.4 %all-to-all-start.3 = ((f32[8,9,8,128]{3,2,1,0:T(8,128)}), f32[8,9,8,128]{3,2,1,0:T(8,128)S(1)}, u32[]{:S(2)}, u32[]{:S(2)}) async-start(f32[8,9,8,128]{3,2,1,0:T(8,128)} %far_top.1), calls=%async_computation.3 | async-start | bytes 589824 | tf_op jit(solution)/shard_map/all_to_all | solution.py:550
  63.9 0.0 copy-start
  63.9 0.0 copy-start.1
  64.0 4.9 %near.3 = f32[8,8,256]{2,1,0:T(8,128)S(1)} custom-call(s32[8,9]{1,0:T(8,128)S(1)} %copy-done.4, f32[3,8,256]{2,1,0:T(8,128)S(1)} %bitcast.7, f32[8,8,256]{2,1,0:T(8,128)S(1)} %copy-done.2, f32[48,256]{1,0:T(8,128)S(1)} %collective-permute-done.before, f32[48,256]{1,0:T(8,128)S(1)} %collective-permute-done.1.after, f32[8,8,256]{2,1,0:T(8,128)S(1)} %near.2.start), custom_call_target="tpu_custom_call" | custom-call | flops 2000000000 | bytes 300000 | tf_op jit(solution)/shard_map/near/pallas_call | solution.py:323
  68.8 5.0 %all-to-all-done.3.got = f32[8,9,8,128]{3,2,1,0:T(8,128)S(1)} async-done(((f32[8,9,8,128]{3,2,1,0:T(8,128)}), f32[8,9,8,128]{3,2,1,0:T(8,128)S(1)}, u32[]{:S(2)}, u32[]{:S(2)}) %all-to-all-start.3) | async-done | bytes 294944 | tf_op jit(solution)/shard_map/all_to_all | solution.py:550
  73.8 0.0 copy-done
  73.8 1.2 %final.1 = f32[8,8,256]{2,1,0:T(8,128)} custom-call(f32[8,9,8,128]{3,2,1,0:T(8,128)S(1)} %all-to-all-done.3.got, f32[8,128,128]{2,1,0:T(8,128)S(1)} %copy-done.1, f32[8,128,256]{2,1,0:T(8,128)S(1)} %copy-done, f32[8,8,256]{2,1,0:T(8,128)S(1)} %near.3), custom_call_target="tpu_custom_call" | custom-call | tf_op jit(solution)/shard_map/final/pallas_call | solution.py:529
  (3 shorter events, 0.0 us)
Async XLA Ops:
  3.1 11.1 %copy-start.6 = (f32[48,256]{1,0:T(8,128)S(1)}, f32[48,256]{1,0:T(8,128)}, u32[]{:S(2)}) copy-start(f32[48,256]{1,0:T(8,128)} %get-tuple-element.29) | copy-start | bytes 147460
  3.2 14.4 %copy-start.2 = (f32[8,8,256]{2,1,0:T(8,128)S(1)}, f32[8,8,256]{2,1,0:T(8,128)}, u32[]{:S(2)}) copy-start(f32[8,8,256]{2,1,0:T(8,128)} %chg.2) | copy-start | bytes 196612
  3.2 14.4 %copy-start.3 = (f32[8,3,256]{2,0,1:T(8,128)S(1)}, f32[8,3,256]{2,0,1:T(8,128)}, u32[]{:S(2)}) copy-start(f32[8,3,256]{2,0,1:T(8,128)} %param.9) | copy-start | bytes 73732
  3.2 14.4 %copy-start.4 = (s32[8,9]{1,0:T(8,128)S(1)}, s32[8,9]{1,0:T(8,128)}, u32[]{:S(2)}) copy-start(s32[8,9]{1,0:T(8,128)} %ids.3) | copy-start | bytes 868
  3.2 25.5 %all-to-all-start = ((f32[8,104,128]{2,1,0:T(8,128)}), f32[8,104,128]{2,1,0:T(8,128)S(1)}, u32[]{:S(2)}, u32[]{:S(2)}) async-start(f32[8,104,128]{2,1,0:T(8,128)} %get-tuple-element.28), calls=%async_computation | async-start | bytes 851968 | tf_op jit(solution)/shard_map/all_to_all | solution.py:550
  14.2 14.5 %collective-permute-start = (f32[48,256]{1,0:T(8,128)S(1)}, f32[48,256]{1,0:T(8,128)S(1)}, u32[]{:S(2)}, u32[]{:S(2)}) collective-permute-start(f32[48,256]{1,0:T(8,128)S(1)} %copy-done.6), channel_id=1, source_target_pairs={{0,1},{1,2},{2,3},{3,4},{4,5},{5,6},{6,7},{7,8},{8,9},{9,10},{10,1... | collective-permute-start | bytes 147464 | tf_op jit(solution)/shard_map/ppermute | solution.py:561
  28.7 3.5 %copy-start.5 = (f32[48,256]{1,0:T(8,128)S(1)}, f32[48,256]{1,0:T(8,128)}, u32[]{:S(2)}) copy-start(f32[48,256]{1,0:T(8,128)} %get-tuple-element.35) | copy-start | bytes 147460
  28.7 11.8 %all-to-all-start.1 = ((f32[8,40,128]{2,1,0:T(8,128)}), f32[8,40,128]{2,1,0:T(8,128)S(1)}, u32[]{:S(2)}, u32[]{:S(2)}) async-start(f32[8,40,128]{2,1,0:T(8,128)} %get-tuple-element.34), calls=%async_computation.1 | async-start | bytes 327680 | tf_op jit(solution)/shard_map/all_to_all | solution.py:550
  32.2 8.3 %collective-permute-start.1 = (f32[48,256]{1,0:T(8,128)S(1)}, f32[48,256]{1,0:T(8,128)S(1)}, u32[]{:S(2)}, u32[]{:S(2)}) collective-permute-start(f32[48,256]{1,0:T(8,128)S(1)} %copy-done.5), channel_id=1, source_target_pairs={{1,0},{2,1},{3,2},{4,3},{5,4},{6,5},{7,6},{8,7},{9,8},{10,9},{11,1... | collective-permute-start | bytes 147464 | tf_op jit(solution)/shard_map/ppermute | solution.py:565
  41.3 16.6 %all-to-all-start.2 = ((f32[8,88,128]{2,1,0:T(8,128)}), f32[8,88,128]{2,1,0:T(8,128)S(1)}, u32[]{:S(2)}, u32[]{:S(2)}) async-start(f32[8,88,128]{2,1,0:T(8,128)} %cells.1), calls=%async_computation.2 | async-start | bytes 720896 | tf_op jit(solution)/shard_map/all_to_all | solution.py:550
  60.5 13.3 %all-to-all-start.3 = ((f32[8,9,8,128]{3,2,1,0:T(8,128)}), f32[8,9,8,128]{3,2,1,0:T(8,128)S(1)}, u32[]{:S(2)}, u32[]{:S(2)}) async-start(f32[8,9,8,128]{3,2,1,0:T(8,128)} %far_top.1), calls=%async_computation.3 | async-start | bytes 589824 | tf_op jit(solution)/shard_map/all_to_all | solution.py:550
  63.9 9.9 %copy-start = (f32[8,128,256]{2,1,0:T(8,128)S(1)}, f32[8,128,256]{2,1,0:T(8,128)}, u32[]{:S(2)}) copy-start(f32[8,128,256]{2,1,0:T(8,128)} %up.1) | copy-start | bytes 3145732
  63.9 9.9 %copy-start.1 = (f32[8,128,128]{2,1,0:T(8,128)S(1)}, f32[8,128,128]{2,1,0:T(8,128)}, u32[]{:S(2)}) copy-start(f32[8,128,128]{2,1,0:T(8,128)} %utm.1) | copy-start | bytes 1572868
